TPU v7x, 32 devices: a whole 2x2x4 slice. The times are simulated.
32 devices in a mesh: frame: 4 (over y, core), rows: 8 (over z, x).
Axes of the slice: x: 2, y: 2, z: 4, core: 2. Of those that a mesh axis runs over, the one named last changes fastest.
Arguments:
- latents: bfloat16 [16, 832, 640], P('frame', 'rows'), may hold values from -6 to 6
- cotangent: bfloat16 [16, 832, 640], P('frame', 'rows'), may hold values from -6 to 6
- timesteps: int32 [2], replicated, may hold values from 0 to 999
- prompt_ids: int32 [2, 77], replicated, may hold values from 0 to 49407
- embed_table: bfloat16 [49408, 768], P(('frame', 'rows')), may hold values from -6 to 6
- res_gain: bfloat16 [2, 640], replicated, may hold values from 0.5 to 1.5
- res_shift: bfloat16 [4, 640], replicated, may hold values from -4 to 4
- res_conv: bfloat16 [2, 3, 3, 640, 640], P(None, None, None, 'frame'), may hold values from -0.078125 to 0.078125
- temb_weight: bfloat16 [1280, 640], P('frame'), may hold values from -0.15625 to 0.15625
- st_gain: bfloat16 [4, 640], replicated, may hold values from 0.5 to 1.5
- st_shift: bfloat16 [9, 640], replicated, may hold values from -4 to 4
- st_proj: bfloat16 [2, 640, 640], P(None, 'frame'), may hold values from -0.25 to 0.25
- st_attn: bfloat16 [6, 640, 640], P(None, 'frame'), may hold values from -0.25 to 0.25
- st_cross_kv: bfloat16 [2, 768, 640], P(None, 'frame'), may hold values from -0.21875 to 0.21875
- st_ff_in: bfloat16 [640, 5120], P('frame'), may hold values from -0.25 to 0.25
- st_ff_bias: bfloat16 [5120], replicated, may hold values from -4 to 4
- st_ff_out: bfloat16 [2560, 640], P('frame'), may hold values from -0.125 to 0.125
- motion_gain: bfloat16 [4, 640], P(None, 'frame'), may hold values from 0.5 to 1.5
- motion_shift: bfloat16 [9, 640], P(None, 'frame'), may hold values from -4 to 4
- motion_proj: bfloat16 [2, 640, 640], P(None, 'frame'), may hold values from -0.25 to 0.25
- motion_attn: bfloat16 [2, 4, 640, 640], P(None, None, 'frame'), may hold values from -0.25 to 0.25
- motion_ff_in: bfloat16 [640, 2560], P('frame'), may hold values from -0.25 to 0.25
- motion_ff_bias: bfloat16 [2560], P('frame'), may hold values from -4 to 4
- motion_ff_out: bfloat16 [2560, 640], P('frame'), may hold values from -0.125 to 0.125
Outputs:
- output: bfloat16 [16, 832, 640], P('frame', 'rows')
- input_grad: float32 [16, 832, 640], P('frame', 'rows')
- motion_gain_grad: float32 [4, 640], P(None, 'frame')
- motion_shift_grad: float32 [9, 640], P(None, 'frame')
- motion_proj_grad: float32 [2, 640, 640], P(None, 'frame')
- motion_attn_grad: float32 [2, 4, 640, 640], P(None, None, 'frame')
- motion_ff_in_grad: float32 [640, 2560], P('frame')
- motion_ff_bias_grad: float32 [2560], P('frame')
- motion_ff_out_grad: float32 [2560, 640], P('frame')
All inputs are finite; a program needn't handle non-finite values.
Results may differ from a plain program's by a relative error of at most 0.024.
Values may be sent and summed in bfloat16 or wider, within the bound.
A program may use at most 512 MiB of HBM per device.

v0:
```python
import math

import jax
import jax.numpy as jnp
from jax import lax
from jax.sharding import PartitionSpec as P

HEADS = 8
GROUPS = 32
FF_ST = 2560
TEMB = 1280
SIDE_BIG = 32
SIDE_MID = 24
SIDE_SMALL = 16


HIGHEST = lax.Precision.HIGHEST
EPSILON = 1e-05


def from_behind(block, axis, distance):
    devices = range(lax.axis_size(axis))
    route = [(i - distance, i) for i in devices if i - distance in devices]
    return lax.ppermute(block, axis, route)


def to_low(value):
    return value.astype(jnp.bfloat16)


def matmul(left, weight):
    return jnp.dot(left, weight, preferred_element_type=jnp.float32)


def matmul_back(gradient, weight):
    return lax.dot_general(
        gradient,
        weight,
        (((gradient.ndim - 1,), (1,)), ((), ())),
        preferred_element_type=jnp.float32,
    )


def weight_grad(left, gradient):
    flat_left = left.reshape(-1, left.shape[-1])
    flat_grad = gradient.reshape(-1, gradient.shape[-1])
    return lax.dot_general(
        flat_left, flat_grad, (((0,), (0,)), ((), ())), preferred_element_type=jnp.float32
    )


def token_sum(gradient):
    return jnp.sum(gradient.reshape(-1, gradient.shape[-1]), axis=0)


def clip_layout(row_devices):
    grid_cols = min(8, row_devices // 2)
    grid_rows = row_devices // grid_cols
    sides = (
        [SIDE_BIG] * (3 * (row_devices // 64))
        + [SIDE_MID] * max(1, row_devices // 16)
        + [SIDE_SMALL] * max(1, row_devices // 16)
    )
    layout = []
    offset = 0
    for side in sides:
        layout.append((side, side // grid_rows, side // grid_cols, offset))
        offset = offset + side // grid_rows * (side // grid_cols)
    return (layout, grid_cols)


def cell_onehot(layout):
    pieces = [
        jnp.full((entry[1] * entry[2],), number, jnp.int32) for number, entry in enumerate(layout)
    ]
    clip_ids = jnp.concatenate(pieces)
    return (clip_ids[:, None] == jnp.arange(len(layout), dtype=jnp.int32)[None, :]).astype(
        jnp.float32
    )


def clip_slice(field, entry):
    return field[:, entry[3] : entry[3] + entry[1] * entry[2]]


def time_table(timesteps):
    half_count = TEMB // 2
    frequency = jnp.exp(
        jnp.arange(half_count, dtype=jnp.float32) * (-math.log(10000.0) / half_count)
    )
    angles = timesteps.astype(jnp.float32)[:, None] * frequency[None, :]
    return jnp.concatenate([jnp.cos(angles), jnp.sin(angles)], axis=1)


def frame_table(frame_ids, channels):
    channel = jnp.arange(channels, dtype=jnp.int32)
    even_index = (channel - channel % 2).astype(jnp.float32)
    frequency = jnp.exp(even_index * (-math.log(10000.0) / channels))
    angles = frame_ids.astype(jnp.float32)[:, None] * frequency[None, :]
    return jnp.where((channel % 2 == 0)[None, :], jnp.sin(angles), jnp.cos(angles))


def spread(stat, onehot):
    return jnp.einsum("fng,cn->fcg", stat, onehot, precision=HIGHEST)[..., None]


def clip_sums(first_term, second_term, onehot):
    sum_one = jnp.einsum("fcg,cn->fng", jnp.sum(first_term, axis=3), onehot, precision=HIGHEST)
    sum_two = jnp.einsum("fcg,cn->fng", jnp.sum(second_term, axis=3), onehot, precision=HIGHEST)
    return lax.psum((sum_one, sum_two), "rows")


def grouped_view(field):
    return field.reshape(field.shape[:-1] + (GROUPS, field.shape[-1] // GROUPS))


def norm_groups(field, gain, shift, onehot, counts):
    grouped = grouped_view(field)
    sum_one, sum_two = clip_sums(grouped, grouped * grouped, onehot)
    average = sum_one / counts[None, :, None]
    inv_std = lax.rsqrt(sum_two / counts[None, :, None] - average * average + EPSILON)
    normed = ((grouped - spread(average, onehot)) * spread(inv_std, onehot)).reshape(field.shape)
    return (normed * gain + shift, (normed, inv_std))


def norm_groups_back(gradient, saved, gain, onehot, counts):
    normed, inv_std = saved
    grad_normed = grouped_view(gradient * gain)
    normed_view = grouped_view(normed)
    sum_one, sum_two = clip_sums(grad_normed, grad_normed * normed_view, onehot)
    mean_one = spread(sum_one / counts[None, :, None], onehot)
    mean_two = spread(sum_two / counts[None, :, None], onehot)
    result = spread(inv_std, onehot) * (grad_normed - mean_one - normed_view * mean_two)
    return result.reshape(gradient.shape)


def layer_norm(field, gain, shift):
    average = jnp.mean(field, axis=-1, keepdims=True)
    centred = field - average
    variance = jnp.mean(centred * centred, axis=-1, keepdims=True)
    return centred * lax.rsqrt(variance + EPSILON) * gain + shift


def exact_gelu(field):
    return jax.nn.gelu(field, approximate=False)


def geglu(pre_act):
    return pre_act[..., :FF_ST] * jax.nn.gelu(pre_act[..., FF_ST:], approximate=False)


def split_rims(joined, sizes):
    pieces = []
    start = 0
    for count in sizes:
        pieces.append(joined[:, start : start + count])
        start = start + count
    return pieces


def conv_columns(field_low, layout, has_left, has_right, grid_cols):
    frame_count = field_low.shape[0]
    blocks = [
        clip_slice(field_low, entry).reshape(frame_count, entry[1], entry[2], field_low.shape[-1])
        for entry in layout
    ]
    received = []
    for distance, column in ((1, -1), (-1, 0)):
        rim_cells = jnp.concatenate([block[:, :, column] for block in blocks], axis=1)
        received.append(from_behind(rim_cells, "rows", distance))
    row_sizes = [entry[1] for entry in layout]
    from_left = split_rims(received[0] * has_left, row_sizes)
    from_right = split_rims(received[1] * has_right, row_sizes)
    widened = [
        jnp.concatenate([left_rim[:, :, None], block, right_rim[:, :, None]], axis=2)
        for left_rim, block, right_rim in zip(from_left, blocks, from_right)
    ]
    rims = []
    for distance, row_pick in ((grid_cols, -1), (-grid_cols, 0)):
        rim_cells = jnp.concatenate([wider[:, row_pick] for wider in widened], axis=1)
        rims.append(from_behind(rim_cells, "rows", distance))
    col_sizes = [entry[2] + 2 for entry in layout]
    above = split_rims(rims[0], col_sizes)
    below = split_rims(rims[1], col_sizes)
    columns = []
    for upper_rim, wider, lower_rim, entry in zip(above, widened, below, layout):
        padded = jnp.concatenate([upper_rim[:, None], wider, lower_rim[:, None]], axis=1)
        tap_list = [
            padded[:, row_tap : row_tap + entry[1], col_tap : col_tap + entry[2]]
            for row_tap in range(3)
            for col_tap in range(3)
        ]
        columns.append(
            jnp.concatenate(tap_list, axis=-1).reshape(frame_count, entry[1] * entry[2], -1)
        )
    return jnp.concatenate(columns, axis=1)


def forward_kernel(weight):
    return weight.reshape(9 * weight.shape[2], weight.shape[3])


def backward_kernel(weight):
    return jnp.transpose(weight[::-1, ::-1], (0, 1, 3, 2)).reshape(
        9 * weight.shape[3], weight.shape[2]
    )


def heads_view(field):
    return field.reshape(field.shape[:-1] + (HEADS, field.shape[-1] // HEADS))


def pixel_major(field):
    return jnp.transpose(heads_view(field), (1, 0, 2, 3))


def from_pixel_major(field, target_shape):
    return jnp.transpose(field, (1, 0, 2, 3)).reshape(target_shape)


def head_scores(queries, key_rows):
    return jnp.einsum(
        "bqhd,bkhd->bhqk", queries, key_rows, preferred_element_type=jnp.float32
    ) * queries.shape[-1] ** (-0.5)


def attend_forward(queries, key_rows, value_rows):
    scores = head_scores(queries, key_rows)
    top_score = jnp.max(scores, axis=-1, keepdims=True)
    powers = jnp.exp(scores - top_score)
    totals = jnp.sum(powers, axis=-1, keepdims=True)
    weights = to_low(powers / totals)
    result = jnp.einsum("bhqk,bkhd->bqhd", weights, value_rows, preferred_element_type=jnp.float32)
    return (result, top_score + jnp.log(totals))


def score_grads(queries, key_rows, value_rows, gradient, log_total, inner):
    probs = jnp.exp(head_scores(queries, key_rows) - log_total)
    grad_probs = jnp.einsum(
        "bqhd,bkhd->bhqk", gradient, value_rows, preferred_element_type=jnp.float32
    )
    inner = jnp.sum(probs * grad_probs, axis=-1, keepdims=True)
    return (probs, to_low(probs * (grad_probs - inner)), inner)


def query_grad(grad_scores, key_rows):
    return jnp.einsum(
        "bhqk,bkhd->bqhd", grad_scores, key_rows, preferred_element_type=jnp.float32
    ) * key_rows.shape[-1] ** (-0.5)


def key_value_grads(probs, grad_scores, queries, gradient):
    grad_key = jnp.einsum(
        "bhqk,bqhd->bkhd", grad_scores, queries, preferred_element_type=jnp.float32
    ) * queries.shape[-1] ** (-0.5)
    grad_value = jnp.einsum(
        "bhqk,bqhd->bkhd", to_low(probs), gradient, preferred_element_type=jnp.float32
    )
    return (grad_key, grad_value)


def temporal_forward(query_low, key_low, value_low):
    key_all, value_all = (
        lax.all_gather(key_low, "frame", axis=0, tiled=True),
        lax.all_gather(value_low, "frame", axis=0, tiled=True),
    )
    result, log_total = attend_forward(
        pixel_major(query_low), pixel_major(key_all), pixel_major(value_all)
    )
    return (to_low(from_pixel_major(result, query_low.shape)), (key_all, value_all, log_total))


def temporal_backward(grad_low, query_low, kept):
    key_all, value_all, log_total = kept
    queries = pixel_major(query_low)
    gradient = pixel_major(grad_low)
    probs, grad_scores, inner = score_grads(
        queries, pixel_major(key_all), pixel_major(value_all), gradient, log_total, None
    )
    grad_query = query_grad(grad_scores, pixel_major(key_all))
    grad_key, grad_value = key_value_grads(probs, grad_scores, queries, gradient)
    key_mine, value_mine = (
        lax.psum_scatter(
            from_pixel_major(grad_key, key_all.shape).astype(jnp.bfloat16),
            "frame",
            scatter_dimension=0,
            tiled=True,
        ).astype(jnp.float32),
        lax.psum_scatter(
            from_pixel_major(grad_value, value_all.shape).astype(jnp.bfloat16),
            "frame",
            scatter_dimension=0,
            tiled=True,
        ).astype(jnp.float32),
    )
    return (from_pixel_major(grad_query, query_low.shape), key_mine, value_mine)


def on_device(
    latents,
    cotangent,
    timesteps,
    prompt_ids,
    embed_table,
    res_gain,
    res_shift,
    res_conv,
    temb_weight,
    st_gain,
    st_shift,
    st_proj,
    st_attn,
    st_cross_kv,
    st_ff_in,
    st_ff_bias,
    st_ff_out,
    motion_gain,
    motion_shift,
    motion_proj,
    motion_attn,
    motion_ff_in,
    motion_ff_bias,
    motion_ff_out,
):
    (
        conv_all,
        temb_all,
        sproj_all,
        sattn_all,
        cross_all,
        sffin_all,
        sffout_all,
        mgain_all,
        mshift_all,
        mproj_all,
        mattn_all,
        mffin_all,
        mffbias_all,
        mffout_all,
    ) = (
        lax.all_gather(res_conv, "frame", axis=3, tiled=True),
        lax.all_gather(temb_weight, "frame", axis=0, tiled=True),
        lax.all_gather(st_proj, "frame", axis=1, tiled=True),
        lax.all_gather(st_attn, "frame", axis=1, tiled=True),
        lax.all_gather(st_cross_kv, "frame", axis=1, tiled=True),
        lax.all_gather(st_ff_in, "frame", axis=0, tiled=True),
        lax.all_gather(st_ff_out, "frame", axis=0, tiled=True),
        lax.all_gather(motion_gain, "frame", axis=1, tiled=True),
        lax.all_gather(motion_shift, "frame", axis=1, tiled=True),
        lax.all_gather(motion_proj, "frame", axis=1, tiled=True),
        lax.all_gather(motion_attn, "frame", axis=2, tiled=True),
        lax.all_gather(motion_ff_in, "frame", axis=0, tiled=True),
        lax.all_gather(motion_ff_bias, "frame", axis=0, tiled=True),
        lax.all_gather(motion_ff_out, "frame", axis=0, tiled=True),
    )
    frame_count, cell_count, channels = latents.shape
    row_devices = lax.axis_size("rows")
    layout, grid_cols = clip_layout(row_devices)
    onehot = cell_onehot(layout)
    counts = jnp.array(
        [float(entry[0] * entry[0] * (channels // GROUPS)) for entry in layout], jnp.float32
    )
    column_index = lax.axis_index("rows") % grid_cols
    has_left = (column_index != 0).astype(jnp.bfloat16)
    has_right = (column_index != grid_cols - 1).astype(jnp.bfloat16)
    rgain, rshift = (res_gain.astype(jnp.float32), res_shift.astype(jnp.float32))
    sgain, sshift, sffbias = (
        st_gain.astype(jnp.float32),
        st_shift.astype(jnp.float32),
        st_ff_bias.astype(jnp.float32),
    )
    mgain, mshift, mffbias = (
        mgain_all.astype(jnp.float32),
        mshift_all.astype(jnp.float32),
        mffbias_all.astype(jnp.float32),
    )
    temb_proj = matmul(to_low(jax.nn.silu(time_table(timesteps))), temb_all)
    time_cols = jnp.dot(onehot, temb_proj, precision=HIGHEST)
    vocab_rows = embed_table.shape[0]
    local_ids = prompt_ids - lax.axis_index(("frame", "rows")) * vocab_rows
    onehot_ids = (
        local_ids[:, :, None] == jnp.arange(vocab_rows, dtype=jnp.int32)[None, None, :]
    ).astype(jnp.bfloat16)
    context = lax.psum(
        jnp.einsum("ncv,ve->nce", onehot_ids, embed_table, preferred_element_type=jnp.float32),
        ("frame", "rows"),
    )
    clip_count, prompt_count = prompt_ids.shape
    context_low = to_low(context.reshape(clip_count * prompt_count, -1))
    cross_keys = heads_view(
        to_low(matmul(context_low, cross_all[0])).reshape(clip_count, prompt_count, channels)
    )
    cross_values = heads_view(
        to_low(matmul(context_low, cross_all[1])).reshape(clip_count, prompt_count, channels)
    )
    frame_ids = lax.axis_index("frame") * frame_count + jnp.arange(frame_count, dtype=jnp.int32)
    position = frame_table(frame_ids, channels)[:, None, :]
    field_shape = latents.shape
    field = latents.astype(jnp.float32)
    h_one, saved_one = norm_groups(field, rgain[0], rshift[0], onehot, counts)
    conv_one = (
        matmul(
            conv_columns(to_low(jax.nn.silu(h_one)), layout, has_left, has_right, grid_cols),
            forward_kernel(conv_all[0]),
        )
        + rshift[2]
        + time_cols
    )
    h_two, saved_two = norm_groups(conv_one, rgain[1], rshift[1], onehot, counts)
    resid = (
        field
        + matmul(
            conv_columns(to_low(jax.nn.silu(h_two)), layout, has_left, has_right, grid_cols),
            forward_kernel(conv_all[1]),
        )
        + rshift[3]
    )
    st_norm, saved_three = norm_groups(resid, sgain[0], sshift[0], onehot, counts)
    proj_one = matmul(to_low(st_norm), sproj_all[0]) + sshift[4]
    ln_one = to_low(layer_norm(proj_one, sgain[1], sshift[1]))
    space_query = to_low(matmul(ln_one, sattn_all[0]))
    key_low = to_low(matmul(ln_one, sattn_all[1]))
    value_low = to_low(matmul(ln_one, sattn_all[2]))
    space_parts = []
    space_kept = []
    for entry in layout:
        key_clip, value_clip = (
            lax.all_gather(clip_slice(key_low, entry), "rows", axis=1, tiled=True),
            lax.all_gather(clip_slice(value_low, entry), "rows", axis=1, tiled=True),
        )
        result, log_total = attend_forward(
            heads_view(clip_slice(space_query, entry)), heads_view(key_clip), heads_view(value_clip)
        )
        space_parts.append(result)
        space_kept.append((key_clip, value_clip, log_total))
    space_low = to_low(jnp.concatenate(space_parts, axis=1).reshape(field_shape))
    proj_two = proj_one + matmul(space_low, sattn_all[3]) + sshift[5]
    ln_two = to_low(layer_norm(proj_two, sgain[2], sshift[2]))
    cross_query = to_low(matmul(ln_two, sattn_all[4]))
    cross_parts = []
    cross_kept = []
    for number, entry in enumerate(layout):
        frame_keys = jnp.broadcast_to(
            cross_keys[number][None], (frame_count,) + cross_keys.shape[1:]
        )
        frame_values = jnp.broadcast_to(
            cross_values[number][None], (frame_count,) + cross_values.shape[1:]
        )
        result, log_total = attend_forward(
            heads_view(clip_slice(cross_query, entry)), frame_keys, frame_values
        )
        cross_parts.append(result)
        cross_kept.append((frame_keys, frame_values, log_total))
    cross_low = to_low(jnp.concatenate(cross_parts, axis=1).reshape(field_shape))
    proj_three = proj_two + matmul(cross_low, sattn_all[5]) + sshift[6]
    ln_three = to_low(layer_norm(proj_three, sgain[3], sshift[3]))
    st_pre = matmul(ln_three, sffin_all) + sffbias
    proj_four = proj_three + matmul(to_low(geglu(st_pre)), sffout_all) + sshift[7]
    st_out = matmul(to_low(proj_four), sproj_all[1]) + sshift[8] + resid
    motion_norm, saved_motion = norm_groups(st_out, mgain[0], mshift[0], onehot, counts)
    motion_in = to_low(motion_norm)
    zed = matmul(motion_in, mproj_all[0]) + mshift[4]
    zed_list = []
    block_saved = []
    for block in range(2):
        zed_list.append(zed)
        normed = to_low(layer_norm(zed, mgain[1 + block], mshift[1 + block]) + position)
        time_query = to_low(matmul(normed, mattn_all[block, 0]))
        time_key = to_low(matmul(normed, mattn_all[block, 1]))
        time_value = to_low(matmul(normed, mattn_all[block, 2]))
        time_low, kept = temporal_forward(time_query, time_key, time_value)
        block_saved.append((normed, time_query, kept, time_low))
        zed = zed + matmul(time_low, mattn_all[block, 3]) + mshift[5 + block]
    zed_last = zed
    ln_last = to_low(layer_norm(zed_last, mgain[3], mshift[3]))
    motion_pre = matmul(ln_last, mffin_all) + mffbias
    hidden_low = to_low(exact_gelu(motion_pre))
    zed = zed_last + matmul(hidden_low, mffout_all) + mshift[7]
    zed_low = to_low(zed)
    output = st_out + matmul(zed_low, mproj_all[1]) + mshift[8]
    grad_out = cotangent.astype(jnp.float32)
    grad_low = to_low(grad_out)
    d_shift = [None] * 9
    d_gain = [None] * 4
    d_proj_out = weight_grad(zed_low, grad_low)
    d_shift[8] = token_sum(grad_out)
    grad_zed = matmul_back(grad_low, mproj_all[1])
    grad_st = grad_out
    grad_low = to_low(grad_zed)
    d_ff_out = weight_grad(hidden_low, grad_low)
    d_shift[7] = token_sum(grad_zed)
    grad_pre = jax.vjp(exact_gelu, motion_pre)[1](matmul_back(grad_low, mffout_all))[0]
    pre_low = to_low(grad_pre)
    d_ff_in = weight_grad(ln_last, pre_low)
    d_ff_bias = token_sum(grad_pre)
    grad_in, d_gain[3], d_shift[3] = jax.vjp(layer_norm, zed_last, mgain[3], mshift[3])[1](
        matmul_back(pre_low, mffin_all)
    )
    grad_zed = grad_zed + grad_in
    d_attn = [[None] * 4, [None] * 4]
    for block in (1, 0):
        normed, time_query, kept, time_low = block_saved[block]
        grad_low = to_low(grad_zed)
        d_attn[block][3] = weight_grad(time_low, grad_low)
        d_shift[5 + block] = token_sum(grad_zed)
        grad_time = to_low(matmul_back(grad_low, mattn_all[block, 3]))
        grad_query, grad_key, grad_value = temporal_backward(grad_time, time_query, kept)
        grad_norm = jnp.zeros(field_shape, jnp.float32)
        for which, member in enumerate((grad_query, grad_key, grad_value)):
            member_low = to_low(member)
            d_attn[block][which] = weight_grad(normed, member_low)
            grad_norm = grad_norm + matmul_back(member_low, mattn_all[block, which])
        grad_in, d_gain[1 + block], d_shift[1 + block] = jax.vjp(
            layer_norm, zed_list[block], mgain[1 + block], mshift[1 + block]
        )[1](grad_norm)
        grad_zed = grad_zed + grad_in
    grad_low = to_low(grad_zed)
    d_proj_in = weight_grad(motion_in, grad_low)
    d_shift[4] = token_sum(grad_zed)
    grad_gn = matmul_back(grad_low, mproj_all[0])
    d_gain[0] = token_sum(grad_gn * saved_motion[0])
    d_shift[0] = token_sum(grad_gn)
    grad_st = grad_st + norm_groups_back(grad_gn, saved_motion, mgain[0], onehot, counts)
    grad_res = grad_st
    grad_four = matmul_back(to_low(grad_st), sproj_all[1])
    grad_act = matmul_back(to_low(grad_four), sffout_all)
    grad_pre_st = jax.vjp(geglu, st_pre)[1](grad_act)[0]
    grad_ln = matmul_back(to_low(grad_pre_st), sffin_all)
    grad_three = (
        grad_four
        + jax.vjp(lambda field_in: layer_norm(field_in, sgain[3], sshift[3]), proj_three)[1](
            grad_ln
        )[0]
    )
    grad_cross = to_low(matmul_back(to_low(grad_three), sattn_all[5]))
    cross_grad_parts = []
    for entry, kept in zip(layout, cross_kept):
        frame_keys, frame_values, log_total = kept
        probs, grad_scores, inner = score_grads(
            heads_view(clip_slice(cross_query, entry)),
            frame_keys,
            frame_values,
            heads_view(clip_slice(grad_cross, entry)),
            log_total,
            None,
        )
        cross_grad_parts.append(query_grad(grad_scores, frame_keys))
    grad_ln = matmul_back(
        to_low(jnp.concatenate(cross_grad_parts, axis=1).reshape(field_shape)), sattn_all[4]
    )
    grad_two = (
        grad_three
        + jax.vjp(lambda field_in: layer_norm(field_in, sgain[2], sshift[2]), proj_two)[1](grad_ln)[
            0
        ]
    )
    grad_space = to_low(matmul_back(to_low(grad_two), sattn_all[3]))
    query_parts, key_parts, value_parts = ([], [], [])
    for entry, kept in zip(layout, space_kept):
        key_clip, value_clip, log_total = kept
        query_heads = heads_view(clip_slice(space_query, entry))
        grad_heads = heads_view(clip_slice(grad_space, entry))
        probs, grad_scores, inner = score_grads(
            query_heads, heads_view(key_clip), heads_view(value_clip), grad_heads, log_total, None
        )
        query_parts.append(query_grad(grad_scores, heads_view(key_clip)))
        key_term, value_term = key_value_grads(probs, grad_scores, query_heads, grad_heads)
        key_grad, value_grad = (
            lax.psum_scatter(
                key_term.reshape(key_clip.shape), "rows", scatter_dimension=1, tiled=True
            ),
            lax.psum_scatter(
                value_term.reshape(value_clip.shape), "rows", scatter_dimension=1, tiled=True
            ),
        )
        key_parts.append(key_grad)
        value_parts.append(value_grad)
    grad_query_all = jnp.concatenate(query_parts, axis=1).reshape(field_shape)
    key_mine = jnp.concatenate(key_parts, axis=1)
    value_mine = jnp.concatenate(value_parts, axis=1)
    grad_ln = matmul_back(to_low(grad_query_all), sattn_all[0])
    grad_ln = (
        grad_ln
        + matmul_back(to_low(key_mine), sattn_all[1])
        + matmul_back(to_low(value_mine), sattn_all[2])
    )
    grad_one = (
        grad_two
        + jax.vjp(lambda field_in: layer_norm(field_in, sgain[1], sshift[1]), proj_one)[1](grad_ln)[
            0
        ]
    )
    grad_gn = matmul_back(to_low(grad_one), sproj_all[0])
    grad_res = grad_res + norm_groups_back(grad_gn, saved_three, sgain[0], onehot, counts)
    grad_field = grad_res
    grad_act = matmul(
        conv_columns(to_low(grad_res), layout, has_left, has_right, grid_cols),
        backward_kernel(conv_all[1]),
    )
    grad_h = jax.vjp(jax.nn.silu, h_two)[1](grad_act)[0]
    grad_conv = norm_groups_back(grad_h, saved_two, rgain[1], onehot, counts)
    grad_act = matmul(
        conv_columns(to_low(grad_conv), layout, has_left, has_right, grid_cols),
        backward_kernel(conv_all[0]),
    )
    grad_h = jax.vjp(jax.nn.silu, h_one)[1](grad_act)[0]
    grad_field = grad_field + norm_groups_back(grad_h, saved_one, rgain[0], onehot, counts)
    full_grads = (
        jnp.stack(d_gain),
        jnp.stack(d_shift),
        jnp.stack([d_proj_in, d_proj_out]),
        jnp.stack([jnp.stack(d_attn[0]), jnp.stack(d_attn[1])]),
        d_ff_in,
        d_ff_bias,
        d_ff_out,
    )
    shares = (
        lax.psum_scatter(
            full_grads[0].astype(jnp.bfloat16), "frame", scatter_dimension=1, tiled=True
        ).astype(jnp.float32),
        lax.psum_scatter(
            full_grads[1].astype(jnp.bfloat16), "frame", scatter_dimension=1, tiled=True
        ).astype(jnp.float32),
        lax.psum_scatter(
            full_grads[2].astype(jnp.bfloat16), "frame", scatter_dimension=1, tiled=True
        ).astype(jnp.float32),
        lax.psum_scatter(
            full_grads[3].astype(jnp.bfloat16), "frame", scatter_dimension=2, tiled=True
        ).astype(jnp.float32),
        lax.psum_scatter(
            full_grads[4].astype(jnp.bfloat16), "frame", scatter_dimension=0, tiled=True
        ).astype(jnp.float32),
        lax.psum_scatter(
            full_grads[5].astype(jnp.bfloat16), "frame", scatter_dimension=0, tiled=True
        ).astype(jnp.float32),
        lax.psum_scatter(
            full_grads[6].astype(jnp.bfloat16), "frame", scatter_dimension=0, tiled=True
        ).astype(jnp.float32),
    )
    totals = lax.psum(
        (shares[0], shares[1], shares[2], shares[3], shares[4], shares[5], shares[6]), "rows"
    )
    return (
        output.astype(jnp.bfloat16),
        grad_field,
        totals[0],
        totals[1],
        totals[2],
        totals[3],
        totals[4],
        totals[5],
        totals[6],
    )


def solution(mesh):
    return jax.shard_map(
        on_device,
        mesh=mesh,
        in_specs=(
            P("frame", "rows", None),
            P("frame", "rows", None),
            P(),
            P(),
            P(("frame", "rows"), None),
            P(),
            P(),
            P(None, None, None, "frame", None),
            P("frame", None),
            P(),
            P(),
            P(None, "frame", None),
            P(None, "frame", None),
            P(None, "frame", None),
            P("frame", None),
            P(),
            P("frame", None),
            P(None, "frame"),
            P(None, "frame"),
            P(None, "frame", None),
            P(None, None, "frame", None),
            P("frame", None),
            P("frame"),
            P("frame", None),
        ),
        out_specs=(
            P("frame", "rows", None),
            P("frame", "rows", None),
            P(None, "frame"),
            P(None, "frame"),
            P(None, "frame", None),
            P(None, None, "frame", None),
            P("frame", None),
            P("frame"),
            P("frame", None),
        ),
        check_vma=False,
    )
```

profile of v0, /device:TPU:0, one launch (start us, length us, event | category | flops | bytes accessed | tf_op | source)
XLA Modules:
  0.0 2020.6 jit_solution(1178766480867674208)
XLA Ops:
  8.0 6.7 copy.448
  20.2 23.3 %all-reduce.10 = (f32[4,2,32]{2,1,0:T(2,128)S(1)}, f32[4,2,32]{2,1,0:T(2,128)S(1)}) all-reduce(f32[4,2,32]{2,1,0:T(2,128)S(1)} %convolution_bitcast_fusion.30, f32[4,2,32]{2,1,0:T(2,128)S(1)} %convolution_bitcast_fusion.31), channel_id=1, replica_groups=mesh['frame'=4,'rows'=8] {'rows'}, use_global_device_ids=true, to_apply=%region_3.4 | all-reduce | flops 512 | bytes 4096 | tf_op jit(solution)/shard_map/psum | solution.py:110
  73.2 5.6 collective-permute-done.3
  95.2 33.2 %all-gather.23.cloned.1.call-done = bf16[2,3,3,640,640]{4,0,2,1,3:T(2,128)(2,1)} async-done(((bf16[2,3,3,160,640]{4,0,2,1,3:T(2,128)(2,1)}), bf16[2,3,3,640,640]{4,0,2,1,3:T(2,128)(2,1)}) %all-gather.23.cloned.1.call-update) | async-done | bytes 14745616 | tf_op jit(solution)/shard_map/all_gather | solution.py:341
  128.3 29.7 %fusion.477 = (bf16[1,3,3,640,640]{4,0,2,1,3:T(2,128)(2,1)}, bf16[1,3,3,640,640]{4,0,2,1,3:T(2,128)(2,1)}) fusion(bf16[2,3,3,640,640]{4,0,2,1,3:T(2,128)(2,1)} %all-gather.23.cloned.1.call-done), kind=kLoop, calls=%fused_computation.946 | loop fusion | bytes 29491200 | tf_op jit(solution)/shard_map/slice | solution.py:404
  158.0 10.8 copy.450
  168.8 8.3 fusion.137
  181.3 21.8 %all-reduce.9 = (f32[4,2,32]{2,1,0:T(2,128)S(1)}, f32[4,2,32]{2,1,0:T(2,128)S(1)}) all-reduce(f32[4,2,32]{2,1,0:T(2,128)S(1)} %convolution_bitcast_fusion.28, f32[4,2,32]{2,1,0:T(2,128)S(1)} %convolution_bitcast_fusion.29), channel_id=1, replica_groups=mesh['frame'=4,'rows'=8] {'rows'}, use_global_device_ids=true, to_apply=%region_7.8 | all-reduce | flops 512 | bytes 4096 | tf_op jit(solution)/shard_map/psum | solution.py:110
  222.9 9.6 copy.487
  242.3 5.3 collective-permute-done.7
  264.1 17.4 all-reduce.8
  314.7 5.2 all-gather.1
  324.4 44.6 %all-reduce.13 = bf16[2,77,768]{2,1,0:T(8,128)(2,1)S(1)} all-reduce(f32[2,77,768]{2,1,0:T(8,128)} %fusion.67), channel_id=1, replica_groups=mesh['frame'=4,'rows'=8] {'frame','rows'}, use_global_device_ids=true, to_apply=%region_18.19 | all-reduce | flops 118272 | bytes 709632 | tf_op jit(solution)/shard_map/psum | solution.py:384
  386.0 56.7 %all-gather.33.cloned.1.call-done = bf16[4,576,640]{2,1,0:T(8,128)(2,1)} async-done(((bf16[4,72,640]{2,1,0:T(8,128)(2,1)}), bf16[4,576,640]{2,1,0:T(8,128)(2,1)}) %all-gather.33.cloned.1.call-update) | async-done | bytes 2949136 | tf_op jit(solution)/shard_map/all_gather | solution.py:428
  454.5 47.8 %all-gather.31.cloned.1.call-done = bf16[4,576,640]{2,1,0:T(8,128)(2,1)} async-done(((bf16[4,72,640]{2,1,0:T(8,128)(2,1)}), bf16[4,576,640]{2,1,0:T(8,128)(2,1)}) %all-gather.31.cloned.1.call-update) | async-done | bytes 2949136 | tf_op jit(solution)/shard_map/all_gather | solution.py:429
  507.2 6.5 fusion.158
  528.0 22.3 %all-gather.41.cloned.1.call-done = bf16[640,5120]{1,0:T(8,128)(2,1)} async-done(((bf16[160,5120]{1,0:T(8,128)(2,1)}), bf16[640,5120]{1,0:T(8,128)(2,1)}) %all-gather.41.cloned.1.call-update) | async-done | bytes 6553616 | tf_op jit(solution)/shard_map/all_gather | solution.py:346
  550.2 5.9 convolution_add_fusion
  559.6 10.1 fusion.20
  569.7 11.4 all-gather.43.cloned.1.call-done
  581.1 9.2 fusion.89
  593.5 21.7 %all-reduce.7 = (f32[4,2,32]{2,1,0:T(2,128)S(1)}, f32[4,2,32]{2,1,0:T(2,128)S(1)}) all-reduce(f32[4,2,32]{2,1,0:T(2,128)S(1)} %convolution_bitcast_fusion.24, f32[4,2,32]{2,1,0:T(2,128)S(1)} %convolution_bitcast_fusion.25), channel_id=1, replica_groups=mesh['frame'=4,'rows'=8] {'rows'}, use_global_device_ids=true, to_apply=%region_30.31 | all-reduce | flops 512 | bytes 4096 | tf_op jit(solution)/shard_map/psum | solution.py:110
  628.4 23.7 %all-gather.47.cloned.1.call-done = bf16[2,4,640,640]{3,2,1,0:T(8,128)(2,1)} async-done(((bf16[2,4,160,640]{3,2,1,0:T(8,128)(2,1)}), bf16[2,4,640,640]{3,2,1,0:T(8,128)(2,1)}) %all-gather.47.cloned.1.call-update) | async-done | bytes 6553616 | tf_op jit(solution)/shard_map/all_gather | solution.py:351
  662.3 15.3 all-gather.49.cloned.1.call-done
  681.9 6.9 copy.521
  688.8 13.6 all-gather.51.cloned.1.call-done
  706.7 6.8 copy.524
  758.9 6.9 copy.529
  765.8 13.0 all-gather.55.cloned.1.call-done
  783.2 6.9 copy.532
  816.7 11.2 multiply_convert_fusion.3
  827.9 12.5 all-gather.59.cloned.1.call-done
  840.5 8.3 fusion.511
  871.6 6.1 copy.541
  877.7 7.4 convert_bitcast_fusion.1
  885.1 6.0 copy.544
  903.1 9.4 reduce-scatter.19.cloned.1.call-done
  915.9 34.0 %reduce-scatter.21.cloned.1.call-done = bf16[4,104,640]{1,2,0:T(8,128)(2,1)} async-done(((bf16[16,104,640]{1,2,0:T(8,128)(2,1)}), bf16[4,104,640]{1,2,0:T(8,128)(2,1)}) %reduce-scatter.21.cloned.1.call-update) | async-done | bytes 532496 | tf_op jit(solution)/shard_map/reduce_scatter | solution.py:289
  971.7 5.9 copy.551
  978.6 7.4 convert_bitcast_fusion
  985.9 5.9 copy.554
  993.1 5.3 bitcast_convert_fusion.1
  1023.3 26.6 %reduce-scatter.25.cloned.1.call-done = bf16[4,104,640]{1,2,0:T(8,128)(2,1)} async-done(((bf16[16,104,640]{1,2,0:T(8,128)(2,1)}), bf16[4,104,640]{1,2,0:T(8,128)(2,1)}) %reduce-scatter.25.cloned.1.call-update) | async-done | bytes 532496 | tf_op jit(solution)/shard_map/reduce_scatter | solution.py:289
  1062.0 21.6 %all-reduce.6 = (f32[4,2,32]{2,1,0:T(2,128)S(1)}, f32[4,2,32]{2,1,0:T(2,128)S(1)}) all-reduce(f32[4,2,32]{2,1,0:T(2,128)S(1)} %convolution_bitcast_fusion.22, f32[4,2,32]{2,1,0:T(2,128)S(1)} %convolution_bitcast_fusion.23), channel_id=1, replica_groups=mesh['frame'=4,'rows'=8] {'rows'}, use_global_device_ids=true, to_apply=%region_56.57 | all-reduce | flops 512 | bytes 4096 | tf_op jit(solution)/shard_map/psum | solution.py:110
  1096.0 10.0 multiply_add_fusion
  1106.0 7.5 multiply_reduce_fusion.19
  1155.1 6.9 fusion.62
  1161.9 6.6 copy.577
  1169.0 5.7 multiply_reduce_fusion
  1182.2 6.7 copy.573
  1190.8 29.1 %copy.716 = bf16[1,3,3,640,640]{3,4,2,1,0:T(8,128)(2,1)} copy(bf16[1,3,3,640,640]{4,0,2,1,3:T(2,128)(2,1)} %get-tuple-element.111) | data formatting | bytes 14745600
  1219.9 29.1 %copy.721 = bf16[1,3,3,640,640]{3,4,2,1,0:T(8,128)(2,1)} copy(bf16[1,3,3,640,640]{4,0,2,1,3:T(2,128)(2,1)} %get-tuple-element.112) | data formatting | bytes 14745600
  1249.0 6.9 rev.7
  1255.9 7.0 rev.6
  1262.9 6.0 all-reduce.2
  1303.6 52.2 %reduce-scatter.29.cloned.1.call-done = f32[4,32,640]{2,1,0:T(8,128)} async-done(((f32[4,256,640]{2,1,0:T(8,128)}), f32[4,32,640]{2,1,0:T(8,128)}) %reduce-scatter.29.cloned.1.call-update) | async-done | bytes 327696 | tf_op jit(solution)/shard_map/reduce_scatter | solution.py:569
  1356.8 113.9 %reduce-scatter.31.cloned.1.call-done = f32[4,72,640]{2,1,0:T(8,128)} async-done(((f32[4,576,640]{2,1,0:T(8,128)}), f32[4,72,640]{2,1,0:T(8,128)}) %reduce-scatter.31.cloned.1.call-update) | async-done | bytes 737296 | tf_op jit(solution)/shard_map/reduce_scatter | solution.py:572
  1472.6 113.9 %reduce-scatter.27.cloned.1.call-done = f32[4,72,640]{2,1,0:T(8,128)} async-done(((f32[4,576,640]{2,1,0:T(8,128)}), f32[4,72,640]{2,1,0:T(8,128)}) %reduce-scatter.27.cloned.1.call-update) | async-done | bytes 737296 | tf_op jit(solution)/shard_map/reduce_scatter | solution.py:569
  1601.2 20.5 %all-reduce.5 = (f32[4,2,32]{2,1,0:T(2,128)S(1)}, f32[4,2,32]{2,1,0:T(2,128)S(1)}) all-reduce(f32[4,2,32]{2,1,0:T(2,128)S(1)} %convolution_bitcast_fusion.20, f32[4,2,32]{2,1,0:T(2,128)S(1)} %convolution_bitcast_fusion.21), channel_id=1, replica_groups=mesh['frame'=4,'rows'=8] {'rows'}, use_global_device_ids=true, to_apply=%region_74.75 | all-reduce | flops 512 | bytes 4096 | tf_op jit(solution)/shard_map/psum | solution.py:110
  1647.3 6.0 collective-permute-done.11
  1667.2 18.5 all-reduce.4
  1709.6 6.0 collective-permute-done.15
  1720.2 5.2 fusion.172
  1730.9 274.1 %all-reduce.14 = (f32[4,2,32]{2,1,0:T(2,128)S(1)}, f32[4,2,32]{2,1,0:T(2,128)S(1)}, f32[4,160]{1,0:T(4,128)}, f32[9,160]{1,0:T(8,128)}, f32[2,160,640]{2,1,0:T(8...) all-reduce(f32[4,2,32]{2,1,0:T(2,128)S(1)} %convolution_bitcast_fus, ...), channel_id=1, replica_groups=mesh['frame'=4,'rows'=8] {'rows'}, use_global_device_ids=true, to_apply=%region_82.83 | all-reduce | flops 1846432 | bytes 11080896 | tf_op jit(solution)/shard_map/psum | solution.py:110
  (1179 shorter events, 594.9 us)
Async XLA Ops:
  7.2 315.8 %copy-start = (bf16[1544,768]{1,0:T(8,128)(2,1)S(1)}, bf16[1544,768]{1,0:T(8,128)(2,1)}, u32[]{:S(2)}) copy-start(bf16[1544,768]{1,0:T(8,128)(2,1)} %param.29) | copy-start | bytes 7114756
  7.2 85.1 %all-gather.25.cloned.1.call-start = ((), (), s32[]{:S(2)}) async-start(), calls=%async_computation.15 | async-start | bytes 2048000 | tf_op jit(solution)/shard_map/all_gather | solution.py:342
  7.9 120.4 %all-gather.23.cloned.1.call-start = ((), (), s32[]{:S(2)}) async-start(), calls=%async_computation.14 | async-start | bytes 18432000 | tf_op jit(solution)/shard_map/all_gather | solution.py:341
  14.7 275.5 %all-gather.27.cloned.1.call-start = ((), (), s32[]{:S(2)}) async-start(), calls=%async_computation.16 | async-start | bytes 2048000 | tf_op jit(solution)/shard_map/all_gather | solution.py:343
  15.5 279.1 %all-gather.29.cloned.1.call-start = ((), (), s32[]{:S(2)}) async-start(), calls=%async_computation.17 | async-start | bytes 6144000 | tf_op jit(solution)/shard_map/all_gather | solution.py:344
  16.1 353.2 %all-gather.39.cloned.1.call-start = ((), (), s32[]{:S(2)}) async-start(), calls=%async_computation.22 | async-start | bytes 2457600 | tf_op jit(solution)/shard_map/all_gather | solution.py:345
  16.2 27.3 %copy-start.224 = (f32[2]{0:T(128)S(1)}, f32[2]{0:T(128)}, u32[]{:S(2)}) copy-start(f32[2]{0:T(128)} %constant.175) | copy-start | bytes 28
  55.8 7.7 collective-permute-start.1
  57.2 6.8 collective-permute-start
  61.8 317.6 %all-gather.37.cloned.1.call-start = ((), (), s32[]{:S(2)}) async-start(), calls=%async_computation.21 | async-start | bytes 1474560 | tf_op jit(solution)/shard_map/all_gather | solution.py:428
  67.2 5.2 collective-permute-start.2
  70.5 8.2 collective-permute-start.3
  177.2 25.9 %copy-start.225 = (f32[2]{0:T(128)S(1)}, f32[2]{0:T(128)}, u32[]{:S(2)}) copy-start(f32[2]{0:T(128)} %constant.175) | copy-start | bytes 28
  217.0 15.5 collective-permute-start.5
  218.4 15.7 collective-permute-start.4
  236.9 4.7 collective-permute-start.6
  239.5 8.2 collective-permute-start.7
  293.2 221.1 %copy-start.3 = (f32[4,104,640]{2,1,0:T(8,128)}, f32[4,104,640]{2,1,0:T(8,128)S(1)}, u32[]{:S(2)}) copy-start(f32[4,104,640]{2,1,0:T(8,128)S(1)} %get-tuple-element.247) | copy-start | bytes 3194884
  298.1 84.9 %all-gather.35.cloned.1.call-start = ((), (), s32[]{:S(2)}) async-start(), calls=%async_computation.20 | async-start | bytes 1474560 | tf_op jit(solution)/shard_map/all_gather | solution.py:429
  301.6 141.1 %all-gather.33.cloned.1.call-start = ((), (), s32[]{:S(2)}) async-start(), calls=%async_computation.19 | async-start | bytes 3317760 | tf_op jit(solution)/shard_map/all_gather | solution.py:428
  303.6 198.7 %all-gather.31.cloned.1.call-start = ((), (), s32[]{:S(2)}) async-start(), calls=%async_computation.18 | async-start | bytes 3317760 | tf_op jit(solution)/shard_map/all_gather | solution.py:429
  305.5 244.8 %all-gather.41.cloned.1.call-start = ((), (), s32[]{:S(2)}) async-start(), calls=%async_computation.23 | async-start | bytes 8192000 | tf_op jit(solution)/shard_map/all_gather | solution.py:346
  306.1 275.0 %all-gather.43.cloned.1.call-start = ((), (), s32[]{:S(2)}) async-start(), calls=%async_computation.24 | async-start | bytes 4096000 | tf_op jit(solution)/shard_map/all_gather | solution.py:347
  306.8 318.7 %all-gather.45.cloned.1.call-start = ((), (), s32[]{:S(2)}) async-start(), calls=%async_computation.25 | async-start | bytes 2048000 | tf_op jit(solution)/shard_map/all_gather | solution.py:350
  307.4 344.6 %all-gather.47.cloned.1.call-start = ((), (), s32[]{:S(2)}) async-start(), calls=%async_computation.26 | async-start | bytes 8192000 | tf_op jit(solution)/shard_map/all_gather | solution.py:351
  308.2 369.5 %all-gather.49.cloned.1.call-start = ((), (), s32[]{:S(2)}) async-start(), calls=%async_computation.27 | async-start | bytes 2662400 | tf_op jit(solution)/shard_map/all_gather | solution.py:265
  322.9 46.1 %copy-start.219 = (f32[4]{0:T(128)S(1)}, f32[4]{0:T(128)}, u32[]{:S(2)}) copy-start(f32[4]{0:T(128)} %add_convert_fusion.21) | copy-start | bytes 52
  386.0 61.4 %copy-start.57 = (bf16[4,72,8,80]{3,2,1,0:T(8,128)(2,1)S(1)}, bf16[4,72,8,80]{3,2,1,0:T(8,128)(2,1)}, u32[]{:S(2)}) copy-start(bf16[4,72,8,80]{3,2,1,0:T(8,128)(2,1)} %reshape.734) | copy-start | bytes 1105924
  450.5 56.7 %copy-start.150 = (f32[4,8,72]{2,1,0:T(8,128)}, f32[4,8,72]{2,1,0:T(8,128)S(1)}, u32[]{:S(2)}) copy-start(f32[4,8,72]{2,1,0:T(8,128)S(1)} %get-tuple-element.250) | copy-start | bytes 27652
  454.5 52.6 %copy-start.154 = (f32[4,8,72]{2,1,0:T(8,128)}, f32[4,8,72]{2,1,0:T(8,128)S(1)}, u32[]{:S(2)}) copy-start(f32[4,8,72]{2,1,0:T(8,128)S(1)} %fusion.3) | copy-start | bytes 27652
  527.9 28.2 %copy-start.174 = (f32[4,104]{1,0:T(4,128)}, f32[4,104]{1,0:T(4,128)S(1)}, u32[]{:S(2)}) copy-start(f32[4,104]{1,0:T(4,128)S(1)} %multiply_reduce_fusion.26) | copy-start | bytes 4996
  528.0 28.2 %copy-start.196 = (f32[4,104]{1,0:T(4,128)}, f32[4,104]{1,0:T(4,128)S(1)}, u32[]{:S(2)}) copy-start(f32[4,104]{1,0:T(4,128)S(1)} %fusion.401) | copy-start | bytes 4996
  590.3 24.8 %copy-start.226 = (f32[2]{0:T(128)S(1)}, f32[2]{0:T(128)}, u32[]{:S(2)}) copy-start(f32[2]{0:T(128)} %constant.175) | copy-start | bytes 28
  592.3 24.9 %copy-start.32 = (f32[4,104,640]{1,0,2:T(4,128)}, f32[4,104,640]{1,0,2:T(4,128)S(1)}, u32[]{:S(2)}) copy-start(f32[4,104,640]{1,0,2:T(4,128)S(1)} %copy.511) | copy-start | bytes 3194884
  628.4 29.0 %copy-start.136 = (bf16[4,104,640]{2,1,0:T(8,128)(2,1)}, bf16[4,104,640]{2,1,0:T(8,128)(2,1)S(1)}, u32[]{:S(2)}) copy-start(bf16[4,104,640]{2,1,0:T(8,128)(2,1)S(1)} %add_convert_fusion.7) | copy-start | bytes 1597444
  654.7 47.7 %all-gather.51.cloned.1.call-start = ((), (), s32[]{:S(2)}) async-start(), calls=%async_computation.28 | async-start | bytes 2662400 | tf_op jit(solution)/shard_map/all_gather | solution.py:264
  657.4 97.2 %all-gather.53.cloned.1.call-start = ((), (), s32[]{:S(2)}) async-start(), calls=%async_computation.29 | async-start | bytes 2662400 | tf_op jit(solution)/shard_map/all_gather | solution.py:265
  662.3 51.3 %copy-start.54 = (bf16[104,4,8,80]{3,1,2,0:T(4,128)(2,1)}, bf16[104,4,8,80]{3,1,2,0:T(4,128)(2,1)S(1)}, u32[]{:S(2)}) copy-start(bf16[104,4,8,80]{3,1,2,0:T(4,128)(2,1)S(1)} %copy.525) | copy-start | bytes 1597444
  731.7 47.1 %all-gather.55.cloned.1.call-start = ((), (), s32[]{:S(2)}) async-start(), calls=%async_computation.30 | async-start | bytes 2662400 | tf_op jit(solution)/shard_map/all_gather | solution.py:264
  734.6 75.0 %all-gather.57.cloned.1.call-start = ((), (), s32[]{:S(2)}) async-start(), calls=%async_computation.31 | async-start | bytes 4096000 | tf_op jit(solution)/shard_map/all_gather | solution.py:352
  735.2 105.3 %all-gather.59.cloned.1.call-start = ((), (), s32[]{:S(2)}) async-start(), calls=%async_computation.32 | async-start | bytes 4096000 | tf_op jit(solution)/shard_map/all_gather | solution.py:354
  735.9 176.6 %reduce-scatter.19.cloned.1.call-start = ((), (), s32[]{:S(2)}) async-start(), calls=%async_computation.33 | async-start | bytes 3276800 | tf_op jit(solution)/shard_map/reduce_scatter | solution.py:283
  877.7 72.3 %reduce-scatter.21.cloned.1.call-start = ((), (), s32[]{:S(2)}) async-start(), calls=%async_computation.34 | async-start | bytes 3276800 | tf_op jit(solution)/shard_map/reduce_scatter | solution.py:289
  891.2 129.7 %reduce-scatter.23.cloned.1.call-start = ((), (), s32[]{:S(2)}) async-start(), calls=%async_computation.35 | async-start | bytes 3276800 | tf_op jit(solution)/shard_map/reduce_scatter | solution.py:283
  977.6 72.3 %reduce-scatter.25.cloned.1.call-start = ((), (), s32[]{:S(2)}) async-start(), calls=%async_computation.36 | async-start | bytes 3276800 | tf_op jit(solution)/shard_map/reduce_scatter | solution.py:289
  991.9 289.3 %reduce-scatter.39.cloned.1.call-start = ((), (), s32[]{:S(2)}) async-start(), calls=%async_computation.43 | async-start | bytes 4096000 | tf_op jit(solution)/shard_map/reduce_scatter | solution.py:630
  998.5 282.8 %reduce-scatter.41.cloned.1.call-start = ((), (), s32[]{:S(2)}) async-start(), calls=%async_computation.44 | async-start | bytes 4096000 | tf_op jit(solution)/shard_map/reduce_scatter | solution.py:636
  1010.8 290.1 %reduce-scatter.43.cloned.1.call-start = ((), (), s32[]{:S(2)}) async-start(), calls=%async_computation.45 | async-start | bytes 204800
  1058.9 24.7 %copy-start.227 = (f32[2]{0:T(128)S(1)}, f32[2]{0:T(128)}, u32[]{:S(2)}) copy-start(f32[2]{0:T(128)} %constant.175) | copy-start | bytes 28
  1115.2 186.6 %reduce-scatter.45.cloned.1.call-start = ((), (), s32[]{:S(2)}) async-start(), calls=%async_computation.46 | async-start | bytes 204800
  1117.9 184.7 %reduce-scatter.35.cloned.1.call-start = ((), (), s32[]{:S(2)}) async-start(), calls=%async_computation.41 | async-start | bytes 2048000 | tf_op jit(solution)/shard_map/reduce_scatter | solution.py:624
  1120.5 182.1 %reduce-scatter.33.cloned.1.call-start = ((), (), s32[]{:S(2)}) async-start(), calls=%async_computation.40 | async-start | bytes 2949120 | tf_op jit(solution)/shard_map/reduce_scatter | solution.py:572
  1144.4 211.5 %reduce-scatter.29.cloned.1.call-start = ((), (), s32[]{:S(2)}) async-start(), calls=%async_computation.38 | async-start | bytes 2949120 | tf_op jit(solution)/shard_map/reduce_scatter | solution.py:569
  1153.4 317.3 %reduce-scatter.31.cloned.1.call-start = ((), (), s32[]{:S(2)}) async-start(), calls=%async_computation.39 | async-start | bytes 6635520 | tf_op jit(solution)/shard_map/reduce_scatter | solution.py:572
  1168.5 418.0 %reduce-scatter.27.cloned.1.call-start = ((), (), s32[]{:S(2)}) async-start(), calls=%async_computation.37 | async-start | bytes 6635520 | tf_op jit(solution)/shard_map/reduce_scatter | solution.py:569
  1189.0 541.9 %reduce-scatter.37.cloned.1.call-start = ((), (), s32[]{:S(2)}) async-start(), calls=%async_computation.42 | async-start | bytes 8192000 | tf_op jit(solution)/shard_map/reduce_scatter | solution.py:627
  1634.3 6.6 collective-permute-start.9
  1635.7 6.8 collective-permute-start.8
  1643.4 3.9 collective-permute-start.10
  1645.4 7.9 collective-permute-start.11
  1694.9 6.6 collective-permute-start.13
  1696.3 6.8 collective-permute-start.12
  1703.9 5.7 collective-permute-start.14
  1707.7 7.9 collective-permute-start.15
  (224 other events, 736.2 us)
Sparse Core Ops, SparseCore 0:
  9.6 22.7 all-gather.24
  33.9 94.3 all-gather.22
  129.9 20.0 all-gather.26
  151.4 38.5 all-gather.28
  191.4 21.8 all-gather.38
  298.2 41.3 all-gather.36
  341.8 41.1 all-gather.34
  385.7 56.9 all-gather.32
  445.5 56.7 all-gather.30
  503.7 46.4 all-gather.40
  551.8 29.2 all-gather.42
  582.5 20.0 all-gather.44
  604.1 47.8 all-gather.46
  654.8 22.7 all-gather.48
  679.6 22.7 all-gather.50
  731.8 22.7 all-gather.52
  756.0 22.7 all-gather.54
  780.3 29.2 all-gather.56
  811.1 29.2 all-gather.58
  877.8 34.6 reduce-scatter.18
  915.2 34.6 reduce-scatter.20
  977.7 34.6 reduce-scatter.22
  1015.1 34.6 reduce-scatter.24
  1052.3 38.7 reduce-scatter.38
  1093.8 38.7 reduce-scatter.40
  1134.9 19.6 reduce-scatter.42
  1156.9 19.6 reduce-scatter.44
  1179.7 28.5 reduce-scatter.34
  1212.2 70.5 reduce-scatter.32
  1286.5 69.2 reduce-scatter.28
  1360.0 110.7 reduce-scatter.30
  1474.8 111.6 reduce-scatter.26
  1589.1 59.9 reduce-scatter.36
where the time goes:
time: 2040 us; the launch traced here: 2020 us
  waiting for transfers between devices  638 us (31%)
  blocking collectives  485 us (24%)
  local copies, waits for them, and re-layouts  421 us (21%)
  matrix products  293 us (14%)
  other arithmetic  121 us (6%)
  starting transfers between devices  42.8 us (2%)
    psum x8, blocking collectives, clip_sums(): return lax.psum((sum_one, sum_two), 'rows')  419 us
    reduce_scatter x2, waiting for transfers between devices, on_device(): lax.psum_scatter(key_term.reshape(key_clip.shape), 'rows', scatter_dimens...  166 us
    unnamed x555, local copies, waits for them, and re-layouts  124 us
    reduce_scatter x2, waiting for transfers between devices, on_device(): lax.psum_scatter(value_term.reshape(value_clip.shape), 'rows', scatter_di...  114 us
    dot_general x28, matrix products, matmul(): return jnp.dot(left, weight, preferred_element_type=jnp.float32)  88.1 us
    dot_general x22, matrix products, matmul_back(): lax.dot_general(gradient, weight, (((gradient.ndim - 1,), (1,)), ((), ())...  71.7 us
    reduce_scatter x2, waiting for transfers between devices, temporal_backward(): lax.psum_scatter(from_pixel_major(grad_value, value_all.shape).astype(jnp...  60.6 us
    all_gather x2, waiting for transfers between devices, on_device(): lax.all_gather(clip_slice(key_low, entry), 'rows', axis=1, tiled=True)  56.7 us
  transfers between devices with their start and end apart: 49, of which 29 were waited for; matrix products, arithmetic and copies ran while one was open for 34% of the time, Pallas kernels for 0%

commit v1 on v0

v1 whole, which is shorter than its diff:
```python
import math

import jax
import jax.numpy as jnp
from jax import lax
from jax.sharding import PartitionSpec as P

HEADS = 8
GROUPS = 32
FF_ST = 2560
TEMB = 1280
SIDE_BIG = 32
SIDE_MID = 24
SIDE_SMALL = 16


HIGHEST = lax.Precision.HIGHEST
EPSILON = 1e-05
FAR = -1e30


def to_low(value):
    return value.astype(jnp.bfloat16)


def matmul(left, weight):
    return jnp.dot(left, weight, preferred_element_type=jnp.float32)


def matmul_back(gradient, weight):
    return lax.dot_general(
        gradient, weight, (((1,), (1,)), ((), ())), preferred_element_type=jnp.float32
    )


def matmul_left(left, right):
    return lax.dot_general(left, right, (((0,), (0,)), ((), ())), preferred_element_type=jnp.float32)


def token_sum(gradient):
    return jnp.sum(gradient, axis=0)


def clip_layout(row_devices):
    grid_cols = min(8, row_devices // 2)
    grid_rows = row_devices // grid_cols
    sides = (
        [SIDE_BIG] * (3 * (row_devices // 64))
        + [SIDE_MID] * max(1, row_devices // 16)
        + [SIDE_SMALL] * max(1, row_devices // 16)
    )
    layout = []
    offset = 0
    for side in sides:
        layout.append((side, side // grid_rows, side // grid_cols, offset))
        offset = offset + side // grid_rows * (side // grid_cols)
    return (layout, grid_rows, grid_cols)


def time_table(timesteps):
    half_count = TEMB // 2
    frequency = jnp.exp(
        jnp.arange(half_count, dtype=jnp.float32) * (-math.log(10000.0) / half_count)
    )
    angles = timesteps.astype(jnp.float32)[:, None] * frequency[None, :]
    return jnp.concatenate([jnp.cos(angles), jnp.sin(angles)], axis=1)


def frame_table(frame_ids, channels):
    channel = jnp.arange(channels, dtype=jnp.int32)
    even_index = (channel - channel % 2).astype(jnp.float32)
    frequency = jnp.exp(even_index * (-math.log(10000.0) / channels))
    angles = frame_ids.astype(jnp.float32)[:, None] * frequency[None, :]
    return jnp.where((channel % 2 == 0)[None, :], jnp.sin(angles), jnp.cos(angles))


def exact_gelu(field):
    return jax.nn.gelu(field, approximate=False)


def geglu(pre_act):
    return pre_act[..., :FF_ST] * jax.nn.gelu(pre_act[..., FF_ST:], approximate=False)


def layer_norm(field, gain, shift):
    average = jnp.mean(field, axis=-1, keepdims=True)
    centred = field - average
    variance = jnp.mean(centred * centred, axis=-1, keepdims=True)
    return centred * lax.rsqrt(variance + EPSILON) * gain + shift


def group_table(channels):
    which = jnp.arange(channels, dtype=jnp.int32) // (channels // GROUPS)
    return (which[:, None] == jnp.arange(GROUPS, dtype=jnp.int32)[None, :]).astype(jnp.float32)


def group_means(first, second, table, count):
    sums = jnp.stack([jnp.sum(first, axis=0), jnp.sum(second, axis=0)])
    means = jnp.dot(sums, table, precision=HIGHEST) / count
    return means


def spread(stats, table):
    return jnp.dot(stats, table.T, precision=HIGHEST)


def norm_groups(field, gain, shift, valid, table, count):
    kept = field * valid
    means = group_means(kept, kept * field, table, count)
    inv_std = lax.rsqrt(means[1] - means[0] * means[0] + EPSILON)
    average, inv_std = spread(jnp.stack([means[0], inv_std]), table)
    normed = (field - average[None]) * inv_std[None]
    return (normed * gain + shift, (normed, inv_std))


def norm_groups_back(gradient, saved, gain, valid, table, count):
    normed, inv_std = saved
    grad_normed = gradient * gain * valid
    means = spread(group_means(grad_normed, grad_normed * normed, table, count), table)
    return inv_std[None] * (grad_normed - means[0][None] - normed * means[1][None]) * valid


def shifted_taps(field, side):
    image = field.reshape(side, side, field.shape[-1])
    padded = jnp.pad(image, ((1, 1), (1, 1), (0, 0)))
    return [
        padded[row_tap : row_tap + side, col_tap : col_tap + side].reshape(field.shape)
        for row_tap in range(3)
        for col_tap in range(3)
    ]


def convolve(field_low, weight, side):
    columns = jnp.concatenate(shifted_taps(field_low, side), axis=1)
    return matmul(columns, weight.reshape(-1, weight.shape[-1]))


def convolve_back(field_low, weight, side):
    total = None
    for tap, shifted in enumerate(shifted_taps(field_low, side)):
        part = matmul_back(shifted, weight[8 - tap])
        total = part if total is None else total + part
    return total


def heads_view(field):
    return field.reshape(field.shape[:-1] + (HEADS, field.shape[-1] // HEADS))


def attend_forward(queries, key_rows, value_rows, bias):
    scale = queries.shape[-1] ** (-0.5)
    scores = (
        jnp.einsum("gqhd,gkhd->ghqk", queries, key_rows, preferred_element_type=jnp.float32) * scale
        + bias
    )
    top_score = jnp.max(scores, axis=-1, keepdims=True)
    powers = jnp.exp(scores - top_score)
    totals = jnp.sum(powers, axis=-1, keepdims=True)
    weights = to_low(powers / totals)
    result = jnp.einsum("ghqk,gkhd->gqhd", weights, value_rows, preferred_element_type=jnp.float32)
    return (result, top_score + jnp.log(totals))


def attend_backward(queries, key_rows, value_rows, bias, log_total, gradient, keys_too):
    scale = queries.shape[-1] ** (-0.5)
    scores = (
        jnp.einsum("gqhd,gkhd->ghqk", queries, key_rows, preferred_element_type=jnp.float32) * scale
        + bias
    )
    probs = jnp.exp(scores - log_total)
    grad_probs = jnp.einsum(
        "gqhd,gkhd->ghqk", gradient, value_rows, preferred_element_type=jnp.float32
    )
    inner = jnp.sum(probs * grad_probs, axis=-1, keepdims=True)
    grad_scores = to_low(probs * (grad_probs - inner))
    grad_query = (
        jnp.einsum("ghqk,gkhd->gqhd", grad_scores, key_rows, preferred_element_type=jnp.float32)
        * scale
    )
    if not keys_too:
        return grad_query
    grad_key = (
        jnp.einsum("ghqk,gqhd->gkhd", grad_scores, queries, preferred_element_type=jnp.float32)
        * scale
    )
    grad_value = jnp.einsum(
        "ghqk,gqhd->gkhd", to_low(probs), gradient, preferred_element_type=jnp.float32
    )
    return (grad_query, grad_key, grad_value)


def onehot(indices, width):
    return (indices[:, None] == jnp.arange(width, dtype=jnp.int32)[None, :]).astype(jnp.bfloat16)


class Places:
    def __init__(self, frames_here, channels):
        self.rows = lax.axis_size("rows")
        self.frames = lax.axis_size("frame")
        self.row = lax.axis_index("rows")
        self.frame = lax.axis_index("frame")
        self.frames_here = frames_here
        self.layout, self.grid_rows, self.grid_cols = clip_layout(self.rows)
        self.clips = len(self.layout)
        self.units = frames_here * self.clips
        assert self.units <= self.rows
        self.channels = channels
        self.side = max(entry[0] for entry in self.layout)
        self.block_max = max(entry[1] * entry[2] for entry in self.layout)
        self.shares = [-(-entry[1] * entry[2] // self.frames) for entry in self.layout]
        self.share_max = max(self.shares)
        self.share_total = sum(self.shares)
        self.clip = self.row % self.clips
        sides = jnp.array([entry[0] for entry in self.layout], jnp.int32)
        self.my_side = jnp.where(self.row < self.units, sides[self.clip], 0)
        self.safe_side = jnp.maximum(self.my_side, self.grid_rows * self.grid_cols)
        cells = jnp.arange(self.side * self.side, dtype=jnp.int32)
        self.cell_row, self.cell_col = cells // self.side, cells % self.side
        self.valid = (self.cell_row < self.my_side) & (self.cell_col < self.my_side)
        block_rows = sides[self.clip] // self.grid_rows
        block_cols = sides[self.clip] // self.grid_cols
        self.device = self.cell_row // block_rows * self.grid_cols + self.cell_col // block_cols
        self.in_block = self.cell_row % block_rows * block_cols + self.cell_col % block_cols
        shares = jnp.array(self.shares, jnp.int32)
        share = shares[self.clip]
        block_index = jnp.where(self.valid, self.device * self.block_max + self.in_block, -1)
        self.block_table = onehot(block_index, self.rows * self.block_max)
        column_index = (
            (self.in_block // share * self.rows + self.device) * self.share_max
            + self.in_block % share
        )
        column_index = jnp.where(self.valid, column_index, -1)
        self.column_table = onehot(column_index, self.frames * self.rows * self.share_max)
        picks = []
        for number in range(self.clips):
            cell = jnp.arange(self.shares[number], dtype=jnp.int32)[:, None]
            when = jnp.arange(self.frames * frames_here, dtype=jnp.int32)[None, :]
            source = (
                when // frames_here * self.rows + when % frames_here * self.clips + number
            ) * self.share_max + cell
            picks.append(source.reshape(-1))
        self.pick_table = onehot(
            jnp.concatenate(picks), self.frames * self.rows * self.share_max
        )

    def blocks_to_unit(self, blocks):
        pieces = []
        for frame in range(self.frames_here):
            for side, height, width, offset in self.layout:
                piece = blocks[frame, offset : offset + height * width]
                pieces.append(jnp.pad(piece, ((0, self.block_max - height * width), (0, 0))))
        for _ in range(self.units, self.rows):
            pieces.append(jnp.zeros_like(pieces[0]))
        received = lax.all_to_all(jnp.stack(pieces), "rows", 0, 0)
        return matmul(self.block_table, received.reshape(-1, self.channels))

    def unit_to_blocks(self, field_low):
        send = to_low(matmul_left(self.block_table, field_low))
        send = send.reshape(self.rows, self.block_max, self.channels)
        received = lax.all_to_all(send, "rows", 0, 0)
        frames = []
        for frame in range(self.frames_here):
            frames.append(
                jnp.concatenate(
                    [
                        received[frame * self.clips + number, : entry[1] * entry[2]]
                        for number, entry in enumerate(self.layout)
                    ]
                )
            )
        return jnp.stack(frames)

    def unit_to_columns(self, fields_low):
        width = sum(field.shape[-1] for field in fields_low)
        joined = jnp.concatenate(fields_low, axis=1)
        send = to_low(matmul_left(self.column_table, joined))
        send = send.reshape(self.frames * self.rows, self.share_max, width)
        received = lax.all_to_all(send, ("frame", "rows"), 0, 0)
        return matmul(self.pick_table, received.reshape(-1, width))

    def columns_to_unit(self, field_low):
        send = to_low(matmul_left(self.pick_table, field_low))
        send = send.reshape(self.frames * self.rows, self.share_max, self.channels)
        received = lax.all_to_all(send, ("frame", "rows"), 0, 0)
        return matmul(self.column_table, received.reshape(-1, self.channels))

    def blocks_to_columns(self, blocks):
        parts = []
        for number, (side, height, width, offset) in enumerate(self.layout):
            share = self.shares[number]
            part = blocks[:, offset : offset + height * width]
            part = jnp.pad(part, ((0, 0), (0, share * self.frames - height * width), (0, 0)))
            parts.append(part.reshape(self.frames_here, self.frames, share, self.channels))
        send = jnp.transpose(jnp.concatenate(parts, axis=2), (1, 0, 2, 3))
        received = lax.all_to_all(send, "frame", 0, 0)
        received = received.reshape(-1, self.share_total, self.channels)
        return jnp.transpose(received, (1, 0, 2)).reshape(-1, self.channels)

    def columns_to_blocks(self, field_low):
        send = jnp.transpose(field_low.reshape(self.share_total, -1, self.channels), (1, 0, 2))
        send = send.reshape(self.frames, self.frames_here, self.share_total, self.channels)
        received = lax.all_to_all(send, "frame", 0, 0)
        parts = []
        start = 0
        for number, (side, height, width, offset) in enumerate(self.layout):
            share = self.shares[number]
            part = jnp.transpose(received[:, :, start : start + share], (1, 0, 2, 3))
            part = part.reshape(self.frames_here, self.frames * share, self.channels)
            parts.append(part[:, : height * width])
            start = start + share
        return jnp.concatenate(parts, axis=1)


def gather_rows(shard, lead):
    gathered = lax.all_gather(shard, "frame", axis=0, tiled=False)
    if lead == 0:
        return gathered.reshape(-1, shard.shape[-1])
    return jnp.moveaxis(gathered, 0, lead).reshape(
        shard.shape[:lead] + (-1, shard.shape[-1])
    )


def on_device(
    latents,
    cotangent,
    timesteps,
    prompt_ids,
    embed_table,
    res_gain,
    res_shift,
    res_conv,
    temb_weight,
    st_gain,
    st_shift,
    st_proj,
    st_attn,
    st_cross_kv,
    st_ff_in,
    st_ff_bias,
    st_ff_out,
    motion_gain,
    motion_shift,
    motion_proj,
    motion_attn,
    motion_ff_in,
    motion_ff_bias,
    motion_ff_out,
):
    frames_here, cell_count, channels = latents.shape
    places = Places(frames_here, channels)
    side = places.side
    valid = places.valid.astype(jnp.float32)[:, None]
    table = group_table(channels)
    count = (places.safe_side * places.safe_side * (channels // GROUPS)).astype(jnp.float32)

    conv_one_all = gather_rows(res_conv[0].reshape(9, -1, channels), 1)
    conv_two_all = gather_rows(res_conv[1].reshape(9, -1, channels), 1)
    sproj_all = [gather_rows(st_proj[i], 0) for i in range(2)]
    sattn_all = [gather_rows(st_attn[i], 0) for i in range(6)]
    cross_all = [gather_rows(st_cross_kv[i], 0) for i in range(2)]
    sffin_all = gather_rows(st_ff_in, 0)
    sffout_all = gather_rows(st_ff_out, 0)
    mproj_all = [gather_rows(motion_proj[i], 0) for i in range(2)]
    mattn_all = [[gather_rows(motion_attn[b, i], 0) for i in range(4)] for b in range(2)]
    mffin_all = gather_rows(motion_ff_in, 0)
    mffout_all = gather_rows(motion_ff_out, 0)
    small = jnp.concatenate(
        [motion_gain.reshape(-1), motion_shift.reshape(-1), motion_ff_bias.reshape(-1)]
    )
    small_all = lax.all_gather(small, "frame", axis=0, tiled=False)
    own = channels // places.frames
    mgain = jnp.transpose(
        small_all[:, : 4 * own].reshape(places.frames, 4, own), (1, 0, 2)
    ).reshape(4, channels).astype(jnp.float32)
    mshift = jnp.transpose(
        small_all[:, 4 * own : 13 * own].reshape(places.frames, 9, own), (1, 0, 2)
    ).reshape(9, channels).astype(jnp.float32)
    mffbias = small_all[:, 13 * own :].reshape(-1).astype(jnp.float32)

    field = places.blocks_to_unit(latents)
    grad_unit = places.blocks_to_unit(cotangent)
    grad_columns = places.blocks_to_columns(cotangent)

    rgain, rshift = (res_gain.astype(jnp.float32), res_shift.astype(jnp.float32))
    sgain, sshift, sffbias = (
        st_gain.astype(jnp.float32),
        st_shift.astype(jnp.float32),
        st_ff_bias.astype(jnp.float32),
    )
    own_temb = TEMB // places.frames
    time_low = to_low(jax.nn.silu(time_table(timesteps)))
    time_mine = lax.dynamic_slice_in_dim(time_low, places.frame * own_temb, own_temb, 1)
    temb_proj = lax.psum(matmul(time_mine, temb_weight), "frame")
    time_row = lax.dynamic_index_in_dim(temb_proj, places.clip, 0, keepdims=False)

    vocab_rows = embed_table.shape[0]
    local_ids = prompt_ids - lax.axis_index(("frame", "rows")) * vocab_rows
    clip_count, prompt_count = prompt_ids.shape
    ids_table = onehot(local_ids.reshape(-1), vocab_rows)
    context = lax.psum(to_low(matmul(ids_table, embed_table)), ("frame", "rows"))
    context = context.reshape(clip_count, prompt_count, -1)
    context_low = lax.dynamic_index_in_dim(context, places.clip, 0, keepdims=False)
    cross_keys = to_low(matmul(context_low, cross_all[0]))
    cross_values = to_low(matmul(context_low, cross_all[1]))

    h_one, saved_one = norm_groups(field, rgain[0], rshift[0], valid, table, count)
    conv_one = (
        convolve(to_low(jax.nn.silu(h_one) * valid), conv_one_all, side) + rshift[2] + time_row
    )
    h_two, saved_two = norm_groups(conv_one, rgain[1], rshift[1], valid, table, count)
    resid = (
        field
        + convolve(to_low(jax.nn.silu(h_two) * valid), conv_two_all, side)
        + rshift[3]
    )
    st_norm, saved_three = norm_groups(resid, sgain[0], sshift[0], valid, table, count)
    proj_one = matmul(to_low(st_norm), sproj_all[0]) + sshift[4]
    ln_one = to_low(layer_norm(proj_one, sgain[1], sshift[1]))
    key_bias = jnp.where(places.valid, 0.0, FAR)[None, None, None, :]
    space_query, space_key, space_value = (
        heads_view(to_low(matmul(ln_one, sattn_all[i])))[None] for i in range(3)
    )
    space_out, space_total = attend_forward(space_query, space_key, space_value, key_bias)
    space_low = to_low(space_out.reshape(-1, channels))
    proj_two = proj_one + matmul(space_low, sattn_all[3]) + sshift[5]
    ln_two = to_low(layer_norm(proj_two, sgain[2], sshift[2]))
    cross_query = heads_view(to_low(matmul(ln_two, sattn_all[4])))[None]
    cross_key, cross_value = (heads_view(cross_keys)[None], heads_view(cross_values)[None])
    cross_out, cross_total = attend_forward(cross_query, cross_key, cross_value, 0.0)
    cross_low = to_low(cross_out.reshape(-1, channels))
    proj_three = proj_two + matmul(cross_low, sattn_all[5]) + sshift[6]
    ln_three = to_low(layer_norm(proj_three, sgain[3], sshift[3]))
    st_pre = matmul(ln_three, sffin_all) + sffbias
    proj_four = proj_three + matmul(to_low(geglu(st_pre)), sffout_all) + sshift[7]
    st_out = matmul(to_low(proj_four), sproj_all[1]) + sshift[8] + resid
    motion_norm, saved_motion = norm_groups(st_out, mgain[0], mshift[0], valid, table, count)

    moved = places.unit_to_columns([to_low(motion_norm), to_low(st_out)])
    motion_in = to_low(moved[:, :channels])
    st_columns = moved[:, channels:]
    frame_total = places.frames * frames_here
    position = frame_table(jnp.arange(frame_total, dtype=jnp.int32), channels)
    position = jnp.broadcast_to(
        position[None], (places.share_total, frame_total, channels)
    ).reshape(-1, channels)
    per_group = max(n for n in range(1, 14) if places.share_total % n == 0)
    group_len = per_group * frame_total
    cell_of = jnp.arange(group_len, dtype=jnp.int32) // frame_total
    cell_bias = jnp.where(cell_of[:, None] == cell_of[None, :], 0.0, FAR)[None, None]

    def grouped(tokens):
        return heads_view(tokens.reshape(-1, group_len, channels))

    zed = matmul(motion_in, mproj_all[0]) + mshift[4]
    zed_list = []
    block_saved = []
    for block in range(2):
        zed_list.append(zed)
        normed = to_low(layer_norm(zed, mgain[1 + block], mshift[1 + block]) + position)
        queries, key_rows, value_rows = (
            grouped(to_low(matmul(normed, mattn_all[block][i]))) for i in range(3)
        )
        result, log_total = attend_forward(queries, key_rows, value_rows, cell_bias)
        time_out = to_low(result.reshape(-1, channels))
        block_saved.append((normed, queries, key_rows, value_rows, log_total, time_out))
        zed = zed + matmul(time_out, mattn_all[block][3]) + mshift[5 + block]
    zed_last = zed
    ln_last = to_low(layer_norm(zed_last, mgain[3], mshift[3]))
    motion_pre = matmul(ln_last, mffin_all) + mffbias
    hidden_low = to_low(exact_gelu(motion_pre))
    zed = zed_last + matmul(hidden_low, mffout_all) + mshift[7]
    zed_low = to_low(zed)
    out_columns = to_low(st_columns + matmul(zed_low, mproj_all[1]) + mshift[8])
    output = places.columns_to_blocks(out_columns)

    grad_low = grad_columns
    grad_out = grad_columns.astype(jnp.float32)
    d_shift = [None] * 9
    d_gain = [None] * 4
    d_proj_out = matmul_left(zed_low, grad_low)
    d_shift[8] = token_sum(grad_out)
    grad_zed = matmul_back(grad_low, mproj_all[1])
    grad_low = to_low(grad_zed)
    d_ff_out = matmul_left(hidden_low, grad_low)
    d_shift[7] = token_sum(grad_zed)
    grad_pre = jax.vjp(exact_gelu, motion_pre)[1](matmul_back(grad_low, mffout_all))[0]
    pre_low = to_low(grad_pre)
    d_ff_in = matmul_left(ln_last, pre_low)
    d_ff_bias = token_sum(grad_pre)
    grad_in, d_gain[3], d_shift[3] = jax.vjp(layer_norm, zed_last, mgain[3], mshift[3])[1](
        matmul_back(pre_low, mffin_all)
    )
    grad_zed = grad_zed + grad_in
    d_attn = [[None] * 4, [None] * 4]
    for block in (1, 0):
        normed, queries, key_rows, value_rows, log_total, time_out = block_saved[block]
        grad_low = to_low(grad_zed)
        d_attn[block][3] = matmul_left(time_out, grad_low)
        d_shift[5 + block] = token_sum(grad_zed)
        grad_time = grouped(to_low(matmul_back(grad_low, mattn_all[block][3])))
        members = attend_backward(
            queries, key_rows, value_rows, cell_bias, log_total, grad_time, True
        )
        grad_norm = 0.0
        for which, member in enumerate(members):
            member_low = to_low(member.reshape(-1, channels))
            d_attn[block][which] = matmul_left(normed, member_low)
            grad_norm = grad_norm + matmul_back(member_low, mattn_all[block][which])
        grad_in, d_gain[1 + block], d_shift[1 + block] = jax.vjp(
            layer_norm, zed_list[block], mgain[1 + block], mshift[1 + block]
        )[1](grad_norm)
        grad_zed = grad_zed + grad_in
    grad_low = to_low(grad_zed)
    d_proj_in = matmul_left(motion_in, grad_low)
    d_shift[4] = token_sum(grad_zed)
    grad_motion = matmul_back(grad_low, mproj_all[0])

    def share_rows(gradient):
        mine = lax.psum_scatter(to_low(gradient), "frame", scatter_dimension=0, tiled=True)
        return lax.psum(mine, "rows").astype(jnp.float32)

    ff_out_grad = share_rows(d_ff_out)
    ff_in_grad = share_rows(d_ff_in)
    proj_grad = jnp.stack([share_rows(d_proj_in), share_rows(d_proj_out)])
    attn_grad = jnp.stack([jnp.stack([share_rows(d) for d in d_attn[b]]) for b in range(2)])

    grad_gn = places.columns_to_unit(to_low(grad_motion))
    d_gain[0] = token_sum(grad_gn * saved_motion[0])
    d_shift[0] = token_sum(grad_gn)
    small_grads = jnp.concatenate(
        [
            jnp.stack(d_gain).reshape(4, places.frames, own),
            jnp.stack(d_shift).reshape(9, places.frames, own),
            jnp.transpose(
                d_ff_bias.reshape(places.frames, -1, own), (1, 0, 2)
            ),
        ]
    )
    small_grads = lax.psum(small_grads, ("frame", "rows"))
    small_mine = lax.dynamic_index_in_dim(small_grads, places.frame, 1, keepdims=False)
    gain_grad, shift_grad = (small_mine[:4], small_mine[4:13])
    ff_bias_grad = small_mine[13:].reshape(-1)

    grad_st = grad_unit + norm_groups_back(grad_gn, saved_motion, mgain[0], valid, table, count)
    grad_res = grad_st
    grad_four = matmul_back(to_low(grad_st), sproj_all[1])
    grad_act = matmul_back(to_low(grad_four), sffout_all)
    grad_pre_st = jax.vjp(geglu, st_pre)[1](grad_act)[0]
    grad_ln = matmul_back(to_low(grad_pre_st), sffin_all)
    grad_three = (
        grad_four
        + jax.vjp(lambda field_in: layer_norm(field_in, sgain[3], sshift[3]), proj_three)[1](
            grad_ln
        )[0]
    )
    grad_cross = heads_view(to_low(matmul_back(to_low(grad_three), sattn_all[5])))[None]
    grad_query = attend_backward(
        cross_query, cross_key, cross_value, 0.0, cross_total, grad_cross, False
    )
    grad_ln = matmul_back(to_low(grad_query.reshape(-1, channels)), sattn_all[4])
    grad_two = (
        grad_three
        + jax.vjp(lambda field_in: layer_norm(field_in, sgain[2], sshift[2]), proj_two)[1](grad_ln)[
            0
        ]
    )
    grad_space = heads_view(to_low(matmul_back(to_low(grad_two), sattn_all[3])))[None]
    members = attend_backward(
        space_query, space_key, space_value, key_bias, space_total, grad_space, True
    )
    grad_ln = 0.0
    for which, member in enumerate(members):
        grad_ln = grad_ln + matmul_back(to_low(member.reshape(-1, channels)), sattn_all[which])
    grad_one = (
        grad_two
        + jax.vjp(lambda field_in: layer_norm(field_in, sgain[1], sshift[1]), proj_one)[1](grad_ln)[
            0
        ]
    )
    grad_gn = matmul_back(to_low(grad_one), sproj_all[0])
    grad_res = grad_res + norm_groups_back(grad_gn, saved_three, sgain[0], valid, table, count)
    grad_act = convolve_back(to_low(grad_res), conv_two_all, side)
    grad_h = jax.vjp(jax.nn.silu, h_two)[1](grad_act)[0]
    grad_conv = norm_groups_back(grad_h, saved_two, rgain[1], valid, table, count)
    grad_act = convolve_back(to_low(grad_conv), conv_one_all, side)
    grad_h = jax.vjp(jax.nn.silu, h_one)[1](grad_act)[0]
    grad_field = grad_res + norm_groups_back(grad_h, saved_one, rgain[0], valid, table, count)
    input_grad = places.unit_to_blocks(to_low(grad_field)).astype(jnp.float32)

    return (
        output,
        input_grad,
        gain_grad,
        shift_grad,
        proj_grad,
        attn_grad,
        ff_in_grad,
        ff_bias_grad,
        ff_out_grad,
    )
def solution(mesh):
    return jax.shard_map(
        on_device,
        mesh=mesh,
        in_specs=(
            P("frame", "rows", None),
            P("frame", "rows", None),
            P(),
            P(),
            P(("frame", "rows"), None),
            P(),
            P(),
            P(None, None, None, "frame", None),
            P("frame", None),
            P(),
            P(),
            P(None, "frame", None),
            P(None, "frame", None),
            P(None, "frame", None),
            P("frame", None),
            P(),
            P("frame", None),
            P(None, "frame"),
            P(None, "frame"),
            P(None, "frame", None),
            P(None, None, "frame", None),
            P("frame", None),
            P("frame"),
            P("frame", None),
        ),
        out_specs=(
            P("frame", "rows", None),
            P("frame", "rows", None),
            P(None, "frame"),
            P(None, "frame"),
            P(None, "frame", None),
            P(None, None, "frame", None),
            P("frame", None),
            P("frame"),
            P("frame", None),
        ),
        check_vma=False,
    )
```

time: 2040 us -> 1230 us (0.60)
  waiting for transfers between devices: 638 us -> 290 us
  local copies, waits for them, and re-layouts: 421 us -> 196 us
  blocking collectives: 485 us -> 319 us
  other arithmetic: 121 us -> 56.3 us
    psum x9 -> x2, blocking collectives: 464 us -> 62.3 us  [the longest x1 55.4 us: on_device(): small_grads = lax.psum(small_grads, ('frame', 'rows'))]
    all_gather x19 -> x6, waiting for transfers between devices: 255 us -> 0.11 us  [gather_rows(): gathered = lax.all_gather(shard, 'frame', axis=0, tiled=False)]
    reduce_scatter x12, waiting for transfers between devices: 350 us -> 115 us  [share_rows(): lax.psum_scatter(to_low(gradient), 'frame', scatter_dimension=0, tiled=True)]
    all_gather x3 -> x20, blocking collectives: 15.5 us -> 244 us  [gather_rows(): gathered = lax.all_gather(shard, 'frame', axis=0, tiled=False)]
    psum x0 -> x2, waiting for transfers between devices: none -> 153 us  [the longest x1 83.5 us: share_rows(): return lax.psum(mine, 'rows').astype(jnp.float32)]
    unnamed x555 -> x501, local copies, waits for them, and re-layouts: 124 us -> 61.1 us
    reshape x24 -> x13, local copies, waits for them, and re-layouts: 53.1 us -> 10.3 us  [the longest x1 2.16 us: columns_to_unit(): send = send.reshape(self.frames * self.rows, self.share_max, self.channels)]
    another operation x14 -> x53, local copies, waits for them, and re-layouts: 0.14 us -> 40.8 us  [the longest x16 37.2 us: heads_view(): return field.reshape(field.shape[:-1] + (HEADS, field.shape[-1] // HEADS))]
  transfers between devices with their start and end apart: 49 -> 27, of which waited for: 29 -> 8; matrix products, arithmetic and copies ran while one was open for 34% -> 36% of each run, Pallas kernels for 0% -> 0%
where the time goes in v1:
time: 1230 us; the launch traced here: 1220 us
  blocking collectives  319 us (26%)
  matrix products  299 us (24%)
  waiting for transfers between devices  290 us (24%)
  local copies, waits for them, and re-layouts  196 us (16%)
  other arithmetic  56.3 us (5%)
  starting transfers between devices  36.8 us (3%)
  between operations  24.9 us (2%)
    all_gather x20, blocking collectives, gather_rows(): gathered = lax.all_gather(shard, 'frame', axis=0, tiled=False)  244 us
    reduce_scatter x12, waiting for transfers between devices, share_rows(): lax.psum_scatter(to_low(gradient), 'frame', scatter_dimension=0, tiled=True)  115 us
    dot_general x31, matrix products, matmul(): return jnp.dot(left, weight, preferred_element_type=jnp.float32)  102 us
    dot_general x39, matrix products, matmul_back(): lax.dot_general(gradient, weight, (((1,), (1,)), ((), ())), preferred_ele...  91.2 us
    psum x1, waiting for transfers between devices, share_rows(): return lax.psum(mine, 'rows').astype(jnp.float32)  83.5 us
    psum x1, waiting for transfers between devices, on_device(): lax.psum(to_low(matmul(ids_table, embed_table)), ('frame', 'rows'))  69.5 us
    unnamed x501, local copies, waits for them, and re-layouts  61.1 us
    psum x1, blocking collectives, on_device(): small_grads = lax.psum(small_grads, ('frame', 'rows'))  55.4 us
  transfers between devices with their start and end apart: 27, of which 8 were waited for; matrix products, arithmetic and copies ran while one was open for 36% of the time, Pallas kernels for 0%

profile of v1, /device:TPU:0, one launch (start us, length us, event | category | flops | bytes accessed | tf_op | source)
XLA Modules:
  0.0 1221.4 jit_solution(7647023262704292761)
XLA Ops:
  11.2 4.2 fusion.303
  23.3 7.3 all-to-all-start
  37.8 12.1 all-reduce.14
  53.5 13.9 %all_gather.98 = bf16[4,160,640]{2,1,0:T(8,128)(2,1)} all-gather(bf16[1,160,640]{2,1,0:T(8,128)(2,1)S(1)} %get-tuple-element.245), channel_id=1, replica_groups=mesh['frame'=4,'rows'=8] {'frame'}, dimensions={0}, use_global_device_ids=true | all-gather | bytes 1024000 | tf_op jit(solution)/shard_map/all_gather | solution.py:315
  67.5 11.8 all_gather.100
  79.4 9.3 all_gather.101
  88.7 14.0 %all_gather.99 = bf16[4,160,640]{2,1,0:T(8,128)(2,1)} all-gather(bf16[1,160,640]{2,1,0:T(8,128)(2,1)S(1)} %get-tuple-element.190), channel_id=1, replica_groups=mesh['frame'=4,'rows'=8] {'frame'}, dimensions={0}, use_global_device_ids=true | all-gather | bytes 1024000 | tf_op jit(solution)/shard_map/all_gather | solution.py:315
  102.7 14.1 %all_gather.102 = bf16[4,160,640]{2,1,0:T(8,128)(2,1)} all-gather(bf16[1,160,640]{2,1,0:T(8,128)(2,1)S(1)} %get-tuple-element.187), channel_id=1, replica_groups=mesh['frame'=4,'rows'=8] {'frame'}, dimensions={0}, use_global_device_ids=true | all-gather | bytes 1024000 | tf_op jit(solution)/shard_map/all_gather | solution.py:315
  116.8 14.1 %all_gather.104 = bf16[4,160,640]{2,1,0:T(8,128)(2,1)} all-gather(bf16[1,160,640]{2,1,0:T(8,128)(2,1)S(1)} %get-tuple-element.191), channel_id=1, replica_groups=mesh['frame'=4,'rows'=8] {'frame'}, dimensions={0}, use_global_device_ids=true | all-gather | bytes 1024000 | tf_op jit(solution)/shard_map/all_gather | solution.py:315
  131.7 14.1 %all_gather.106 = bf16[4,160,640]{2,1,0:T(8,128)(2,1)} all-gather(bf16[1,160,640]{2,1,0:T(8,128)(2,1)S(1)} %get-tuple-element.186), channel_id=1, replica_groups=mesh['frame'=4,'rows'=8] {'frame'}, dimensions={0}, use_global_device_ids=true | all-gather | bytes 1024000 | tf_op jit(solution)/shard_map/all_gather | solution.py:315
  145.8 9.5 all_gather.111
  158.7 13.7 %all_gather.114 = bf16[4,160,640]{2,1,0:T(8,128)(2,1)} all-gather(bf16[1,160,640]{2,1,0:T(8,128)(2,1)S(1)} %get-tuple-element.244), channel_id=1, replica_groups=mesh['frame'=4,'rows'=8] {'frame'}, dimensions={0}, use_global_device_ids=true | all-gather | bytes 1024000 | tf_op jit(solution)/shard_map/all_gather | solution.py:315
  173.5 14.2 %all-gather.4 = bf16[4,1,160,640]{3,2,1,0:T(8,128)(2,1)} all-gather(bf16[1,1,160,640]{3,2,1,0:T(8,128)(2,1)S(1)} %get-tuple-element.181), channel_id=6, replica_groups=mesh['frame'=4,'rows'=8] {'frame'}, dimensions={0}, use_global_device_ids=true | all-gather | bytes 1024000 | tf_op jit(solution)/shard_map/all_gather | solution.py:315
  191.3 6.8 psum.105
  198.2 14.5 %all_gather.105 = bf16[4,192,640]{2,1,0:T(8,128)(2,1)S(1)} all-gather(bf16[1,192,640]{2,1,0:T(8,128)(2,1)} %get-tuple-element.242), channel_id=1, replica_groups=mesh['frame'=4,'rows'=8] {'frame'}, dimensions={0}, use_global_device_ids=true | all-gather | bytes 1228800 | tf_op jit(solution)/shard_map/all_gather | solution.py:315
  212.7 9.8 all_gather.103
  222.5 69.5 %all-reduce.19.cloned.1.call-done = bf16[2,77,768]{2,1,0:T(8,128)(2,1)} async-done(((bf16[2,77,768]{2,1,0:T(8,128)(2,1)}), bf16[2,77,768]{2,1,0:T(8,128)(2,1)}) %all-reduce.19.cloned.1.call-update) | async-done | bytes 236560 | tf_op jit(solution)/shard_map/psum | solution.py:400
  296.1 4.4 all-to-all-start.4
  316.6 9.7 multiply_reduce_fusion.5
  340.4 10.2 multiply_reduce_fusion.4
  358.9 3.1 convolution_convert_fusion.18
  363.5 3.3 convolution_convert_fusion.20
  388.9 7.5 convolution_add_fusion
  396.5 4.3 copy-done.96
  400.8 13.2 %fusion.2 = f32[576,2560]{1,0:T(8,128)} fusion(f32[576,5120]{1,0:T(8,128)S(1)} %convolution_add_fusion), kind=kLoop, calls=%fused_computation.12 | loop fusion | flops 91422720 | bytes 11796480 | tf_op jit(solution)/shard_map/erfc | solution.py:82
  414.0 11.7 multiply_reduce_fusion.3
  433.0 5.1 all-to-all-start.1
  439.2 25.0 %all-gather.5 = bf16[4,1,160,640]{3,2,1,0:T(8,128)(2,1)} all-gather(bf16[1,1,160,640]{3,2,1,0:T(8,128)(2,1)S(1)} %copy-done.118), channel_id=7, replica_groups=mesh['frame'=4,'rows'=8] {'frame'}, dimensions={0}, use_global_device_ids=true | all-gather | bytes 1024000 | tf_op jit(solution)/shard_map/all_gather | solution.py:315
  464.2 10.4 all-gather.3
  474.6 9.0 all-gather.6
  483.6 9.5 all-gather.8
  493.1 9.5 all-gather.9
  502.5 9.3 all-gather.7
  511.9 9.3 all-gather.10
  521.2 9.3 all_gather.127
  560.7 3.1 reshape.1206
  587.8 3.7 fusion.321
  605.7 14.6 %multiply_convert_fusion.2 = (bf16[416,2560]{1,0:T(8,128)(2,1)}, f32[416,2560]{1,0:T(8,128)}, f32[416,2560]{1,0:T(8,128)}) fusion(f32[2560]{0:T(1024)S(1)} %reshape.1173, bf16[640,2560]{1,0:T(8,128)(2,1)} %all-gather.28.cloned.1.call-done, f32[416,640]{1,0:T(8,128)S(1)} %get-tuple-element.284, f32[640]{0:T(1024)S(1)} %add.1010, f32[640]{0:T(1024)S(1)} %mul.1103, ...), kind=kOutput, calls=%fused_computation.39 | convolution fusion | flops 1434767360 | bytes 15010048 | tf_op jit(solution)/shard_map/dot_general | solution.py:27
  620.3 8.3 fusion.323
  655.5 3.3 convert_element_type.586
  677.6 3.4 multiply_reduce_fusion.1
  736.6 4.5 fusion.77
  742.8 5.3 convolution_convert_fusion.1
  753.7 5.7 all-to-all-start.5
  759.5 6.2 fusion.302
  765.7 6.3 fusion.301
  773.8 11.8 all-to-all-done.5
  785.6 3.5 all-to-all-start.3
  789.2 5.5 convolution_convert_fusion
  795.5 3.5 multiply_reduce_fusion.8
  801.1 7.1 all-to-all-done.3
  808.2 4.1 all-to-all-start.2
  818.4 11.8 multiply_add_fusion.1
  830.2 11.3 multiply_reduce_fusion.14
  857.1 11.2 multiply_reduce_fusion
  869.3 6.3 multiply_convert_fusion
  926.1 5.3 reduce-scatter.13.cloned.1.call-done
  931.4 26.1 %reduce-scatter.15.cloned.1.call-done = bf16[160,640]{1,0:T(8,128)(2,1)} async-done(((bf16[640,640]{1,0:T(8,128)(2,1)}), bf16[160,640]{1,0:T(8,128)(2,1)}) %reduce-scatter.15.cloned.1.call-update) | async-done | bytes 204816 | tf_op jit(solution)/shard_map/reduce_scatter | solution.py:519
  957.6 41.9 %reduce-scatter.33.cloned.1.call-done = bf16[160,2560]{1,0:T(8,128)(2,1)} async-done(((bf16[640,2560]{1,0:T(8,128)(2,1)}), bf16[160,2560]{1,0:T(8,128)(2,1)}) %reduce-scatter.33.cloned.1.call-update) | async-done | bytes 819216 | tf_op jit(solution)/shard_map/reduce_scatter | solution.py:519
  999.5 41.4 %reduce-scatter.35.cloned.1.call-done = bf16[640,640]{1,0:T(8,128)(2,1)} async-done(((bf16[2560,640]{1,0:T(8,128)(2,1)}), bf16[640,640]{1,0:T(8,128)(2,1)}) %reduce-scatter.35.cloned.1.call-update) | async-done | bytes 819216 | tf_op jit(solution)/shard_map/reduce_scatter | solution.py:519
  1042.5 6.5 fusion.287
  1053.4 5.4 all-to-all-start.6
  1063.8 55.4 %psum.107 = f32[17,4,160]{2,0,1:T(8,128)S(1)} all-reduce(f32[17,4,160]{2,0,1:T(8,128)S(1)} %concatenate.54), channel_id=1, replica_groups=mesh['frame'=4,'rows'=8] {'frame','rows'}, use_global_device_ids=true, to_apply=%region_68.69 | all-reduce | flops 10880 | bytes 87040 | tf_op jit(solution)/shard_map/psum | solution.py:539
  1122.3 83.5 %all-reduce.21.cloned.1.call-done = (bf16[1,160,640]{2,1,0:T(8,128)(2,1)}, bf16[1,160,640]{2,1,0:T(8,128)(2,1)}, bf16[1,160,640]{2,1,0:T(8,128)(2,1)}, bf16[1,16...) async-done(((bf16[1,160,640]{2,1,0:T(8,128)(2,1)}, ...) | async-done | bytes 3686416 | tf_op jit(solution)/shard_map/psum | solution.py:520
  (916 shorter events, 373.4 us)
Async XLA Ops:
  8.0 283.9 %all-reduce.19.cloned.1.call-start = ((), (), s32[]{:S(2)}) async-start(), calls=%async_computation.21 | async-start | bytes 491520 | tf_op jit(solution)/shard_map/psum | solution.py:400
  11.2 305.4 %all-gather.20.cloned.1.call-start = ((), (), s32[]{:S(2)}) async-start(), calls=%async_computation.19 | async-start | bytes 9216000 | tf_op jit(solution)/shard_map/all_gather | solution.py:315
  15.4 324.9 %all-gather.22.cloned.1.call-start = ((), (), s32[]{:S(2)}) async-start(), calls=%async_computation.20 | async-start | bytes 9216000 | tf_op jit(solution)/shard_map/all_gather | solution.py:315
  16.1 372.9 %all-gather.24.cloned.1.call-start = ((), (), s32[]{:S(2)}) async-start(), calls=%async_computation.34 | async-start | bytes 8192000 | tf_op jit(solution)/shard_map/all_gather | solution.py:315
  16.6 397.4 %all-gather.26.cloned.1.call-start = ((), (), s32[]{:S(2)}) async-start(), calls=%async_computation.35 | async-start | bytes 4096000 | tf_op jit(solution)/shard_map/all_gather | solution.py:315
  17.4 588.3 %all-gather.28.cloned.1.call-start = ((), (), s32[]{:S(2)}) async-start(), calls=%async_computation.36 | async-start | bytes 4096000 | tf_op jit(solution)/shard_map/all_gather | solution.py:315
  21.4 16.0 %copy-start.219 = (bf16[640]{0:T(1024)(128)(2,1)S(1)}, bf16[640]{0:T(1024)(128)(2,1)}, u32[]{:S(2)}) copy-start(bf16[640]{0:T(1024)(128)(2,1)} %param.48) | copy-start | bytes 3844
  22.0 28.0 %copy-start.225 = (s32[2]{0:T(128)S(1)}, s32[2]{0:T(128)}, u32[]{:S(2)}) copy-start(s32[2]{0:T(128)} %constant.337.clone) | copy-start | bytes 28
  23.3 272.7 %all-to-all-start = ((bf16[8,72,640]{2,1,0:T(8,128)(2,1)}), bf16[8,72,640]{2,1,0:T(8,128)(2,1)}, u32[]{:S(2)}, u32[]{:S(2)}) async-start(bf16[8,72,640]{2,1,0:T(8,128)(2,1)} %bitcast_dynamic-update-slice_fusion.4), calls=%async_computation | async-start | bytes 1474560 | tf_op jit(solution)/shard_map/all_to_all | solution.py:254
  30.6 22.0 %copy-start.212 = (bf16[4,640]{1,0:T(4,128)(2,1)S(1)}, bf16[4,640]{1,0:T(4,128)(2,1)}, u32[]{:S(2)}) copy-start(bf16[4,640]{1,0:T(4,128)(2,1)} %param.32) | copy-start | bytes 15364
  30.6 22.0 %copy-start.218 = (bf16[2,640]{1,0:T(2,128)(2,1)S(1)}, bf16[2,640]{1,0:T(2,128)(2,1)}, u32[]{:S(2)}) copy-start(bf16[2,640]{1,0:T(2,128)(2,1)} %param.31) | copy-start | bytes 7684
  30.6 22.1 %copy-start.224 = (s32[2]{0:T(128)S(1)}, s32[2]{0:T(128)}, u32[]{:S(2)}) copy-start(s32[2]{0:T(128)} %param.28) | copy-start | bytes 28
  30.6 22.1 %copy-start.187 = (bf16[9,640]{1,0:T(8,128)(2,1)S(1)}, bf16[9,640]{1,0:T(8,128)(2,1)}, u32[]{:S(2)}) copy-start(bf16[9,640]{1,0:T(8,128)(2,1)} %param.36) | copy-start | bytes 34564
  30.6 22.2 %copy-start.213 = (bf16[4,640]{1,0:T(4,128)(2,1)S(1)}, bf16[4,640]{1,0:T(4,128)(2,1)}, u32[]{:S(2)}) copy-start(bf16[4,640]{1,0:T(4,128)(2,1)} %param.35) | copy-start | bytes 15364
  30.6 22.8 %copy-start.129 = (bf16[2,160,640]{2,1,0:T(8,128)(2,1)S(1)}, bf16[2,160,640]{2,1,0:T(8,128)(2,1)}, u32[]{:S(2)}) copy-start(bf16[2,160,640]{2,1,0:T(8,128)(2,1)} %param.37) | copy-start | bytes 1228804
  30.7 589.6 %all-gather.30.cloned.1.call-start = ((), (), s32[]{:S(2)}) async-start(), calls=%async_computation.37 | async-start | bytes 4096000 | tf_op jit(solution)/shard_map/all_gather | solution.py:315
  35.9 378.1 %copy-start.131 = (f32[576]{0:T(1024)}, f32[576]{0:T(1024)S(1)}, u32[]{:S(2)}) copy-start(f32[576]{0:T(1024)S(1)} %fusion.245) | copy-start | bytes 6916
  52.6 258.5 %copy-start.167 = (f32[640]{0:T(1024)}, f32[640]{0:T(1024)S(1)}, u32[]{:S(2)}) copy-start(f32[640]{0:T(1024)S(1)} %get-tuple-element.101) | copy-start | bytes 7684
  52.6 282.3 %copy-start.169 = (f32[640]{0:T(1024)}, f32[640]{0:T(1024)S(1)}, u32[]{:S(2)}) copy-start(f32[640]{0:T(1024)S(1)} %get-tuple-element.99) | copy-start | bytes 7684
  52.7 258.4 %copy-start.159 = (f32[640]{0:T(1024)}, f32[640]{0:T(1024)S(1)}, u32[]{:S(2)}) copy-start(f32[640]{0:T(1024)S(1)} %get-tuple-element.117) | copy-start | bytes 7684
  52.7 282.2 %copy-start.161 = (f32[640]{0:T(1024)}, f32[640]{0:T(1024)S(1)}, u32[]{:S(2)}) copy-start(f32[640]{0:T(1024)S(1)} %get-tuple-element.116) | copy-start | bytes 7684
  53.5 299.3 %copy-start.205 = (f32[640]{0:T(1024)}, f32[640]{0:T(1024)S(1)}, u32[]{:S(2)}) copy-start(f32[640]{0:T(1024)S(1)} %get-tuple-element.97) | copy-start | bytes 7684
  53.5 300.7 %copy-start.171 = (f32[640]{0:T(1024)}, f32[640]{0:T(1024)S(1)}, u32[]{:S(2)}) copy-start(f32[640]{0:T(1024)S(1)} %get-tuple-element.96) | copy-start | bytes 7684
  53.5 326.6 %copy-start.207 = (f32[640]{0:T(1024)}, f32[640]{0:T(1024)S(1)}, u32[]{:S(2)}) copy-start(f32[640]{0:T(1024)S(1)} %get-tuple-element.95) | copy-start | bytes 7684
  79.4 275.4 %copy-start.78 = (bf16[4,160,640]{2,1,0:T(8,128)(2,1)}, bf16[4,160,640]{2,1,0:T(8,128)(2,1)S(1)}, u32[]{:S(2)}) copy-start(bf16[4,160,640]{2,1,0:T(8,128)(2,1)S(1)} %all_gather.100) | copy-start | bytes 2457604
  88.7 42.2 %copy-start.128 = (bf16[2,192,640]{2,1,0:T(8,128)(2,1)S(1)}, bf16[2,192,640]{2,1,0:T(8,128)(2,1)}, u32[]{:S(2)}) copy-start(bf16[2,192,640]{2,1,0:T(8,128)(2,1)} %param.39) | copy-start | bytes 1474564
  145.8 26.6 %copy-start.105 = (bf16[2,4,160,640]{3,2,1,0:T(8,128)(2,1)S(1)}, bf16[2,4,160,640]{3,2,1,0:T(8,128)(2,1)}, u32[]{:S(2)}) copy-start(bf16[2,4,160,640]{3,2,1,0:T(8,128)(2,1)} %param.46) | copy-start | bytes 4915204
  172.4 15.5 %slice-start.3 = ((bf16[4,104,640]{2,1,0:T(8,128)(2,1)}), bf16[4,72,640]{2,1,0:T(8,128)(2,1)S(1)}, s32[]{:S(2)}) async-start(bf16[4,104,640]{2,1,0:T(8,128)(2,1)} %param.27), calls=%async_computation.42 | async-start | bytes 737280 | tf_op jit(solution)/shard_map/slice | solution.py:291
  173.5 16.4 %copy-start.130 = (bf16[320,640]{1,0:T(8,128)(2,1)S(1)}, bf16[320,640]{1,0:T(8,128)(2,1)}, u32[]{:S(2)}) copy-start(bf16[320,640]{1,0:T(8,128)(2,1)} %param.34) | copy-start | bytes 1228804
  189.9 110.5 %copy-start.214 = (s32[576]{0:T(1024)}, s32[576]{0:T(1024)S(1)}, u32[]{:S(2)}) copy-start(s32[576]{0:T(1024)S(1)} %add_select_fusion.9) | copy-start | bytes 6916
  191.3 236.5 %copy-start.188 = (f32[640]{0:T(1024)}, f32[640]{0:T(1024)S(1)}, u32[]{:S(2)}) copy-start(f32[640]{0:T(1024)S(1)} %mul.1079) | copy-start | bytes 7684
  296.1 136.9 %all-to-all-start.4 = ((bf16[4,4,26,640]{3,1,2,0:T(4,128)(2,1)}), bf16[4,4,26,640]{3,1,2,0:T(4,128)(2,1)}, u32[]{:S(2)}, u32[]{:S(2)}) async-start(bf16[4,4,26,640]{3,1,2,0:T(4,128)(2,1)} %maximum_bitcast_fusion.2), calls=%async_computation.4 | async-start | bytes 1064960 | tf_op jit(solution)/shard_map/all_to_all | solution.py:295
  353.7 24.9 %copy-start.7 = (f32[576,640]{1,0:T(8,128)}, f32[576,640]{1,0:T(8,128)S(1)}, u32[]{:S(2)}) copy-start(f32[576,640]{1,0:T(8,128)S(1)} %get-tuple-element.265) | copy-start | bytes 4423684
  433.0 31.2 %copy-start.117 = (bf16[1,1,160,640]{3,2,1,0:T(8,128)(2,1)S(1)}, bf16[1,1,160,640]{3,2,1,0:T(8,128)(2,1)}, u32[]{:S(2)}) copy-start(bf16[1,1,160,640]{3,2,1,0:T(8,128)(2,1)} %get-tuple-element.182) | copy-start | bytes 614404
  433.0 104.5 %all-to-all-start.1 = ((bf16[32,18,1280]{2,1,0:T(8,128)(2,1)}), bf16[32,18,1280]{2,1,0:T(8,128)(2,1)S(1)}, u32[]{:S(2)}, u32[]{:S(2)}) async-start(bf16[32,18,1280]{2,1,0:T(8,128)(2,1)} %reshape.1124), calls=%async_computation.1 | async-start | bytes 3932160 | tf_op jit(solution)/shard_map/all_to_all | solution.py:278
  438.1 36.5 %copy-start.116 = (bf16[1,1,160,640]{3,2,1,0:T(8,128)(2,1)S(1)}, bf16[1,1,160,640]{3,2,1,0:T(8,128)(2,1)}, u32[]{:S(2)}) copy-start(bf16[1,1,160,640]{3,2,1,0:T(8,128)(2,1)} %get-tuple-element.179) | copy-start | bytes 614404
  438.1 487.8 %reduce-scatter.17.cloned.1.call-start = ((), (), s32[]{:S(2)}) async-start(), calls=%async_computation.24 | async-start | bytes 1024000 | tf_op jit(solution)/shard_map/reduce_scatter | solution.py:519
  439.2 44.4 %copy-start.115 = (bf16[1,1,160,640]{3,2,1,0:T(8,128)(2,1)S(1)}, bf16[1,1,160,640]{3,2,1,0:T(8,128)(2,1)}, u32[]{:S(2)}) copy-start(bf16[1,1,160,640]{3,2,1,0:T(8,128)(2,1)} %get-tuple-element.177) | copy-start | bytes 614404
  464.2 28.9 %copy-start.114 = (bf16[1,1,160,640]{3,2,1,0:T(8,128)(2,1)S(1)}, bf16[1,1,160,640]{3,2,1,0:T(8,128)(2,1)}, u32[]{:S(2)}) copy-start(bf16[1,1,160,640]{3,2,1,0:T(8,128)(2,1)} %get-tuple-element.183) | copy-start | bytes 614404
  474.6 28.0 %copy-start.113 = (bf16[1,1,160,640]{3,2,1,0:T(8,128)(2,1)S(1)}, bf16[1,1,160,640]{3,2,1,0:T(8,128)(2,1)}, u32[]{:S(2)}) copy-start(bf16[1,1,160,640]{3,2,1,0:T(8,128)(2,1)} %get-tuple-element.178) | copy-start | bytes 614404
  483.6 88.8 %copy-start.40 = (bf16[4,1,160,640]{3,2,1,0:T(8,128)(2,1)}, bf16[4,1,160,640]{3,2,1,0:T(8,128)(2,1)S(1)}, u32[]{:S(2)}) copy-start(bf16[4,1,160,640]{3,2,1,0:T(8,128)(2,1)S(1)} %all-gather.6) | copy-start | bytes 2457604
  483.6 28.3 %copy-start.112 = (bf16[1,1,160,640]{3,2,1,0:T(8,128)(2,1)S(1)}, bf16[1,1,160,640]{3,2,1,0:T(8,128)(2,1)}, u32[]{:S(2)}) copy-start(bf16[1,1,160,640]{3,2,1,0:T(8,128)(2,1)} %get-tuple-element.176) | copy-start | bytes 614404
  493.1 28.1 %copy-start.119 = (bf16[1,160,640]{2,1,0:T(8,128)(2,1)S(1)}, bf16[1,160,640]{2,1,0:T(8,128)(2,1)}, u32[]{:S(2)}) copy-start(bf16[1,160,640]{2,1,0:T(8,128)(2,1)} %get-tuple-element.243) | copy-start | bytes 614404
  550.1 16.1 %copy-start.45 = (bf16[2,208,8,80]{1,3,2,0:T(8,128)(2,1)}, bf16[2,208,8,80]{1,3,2,0:T(8,128)(2,1)S(1)}, u32[]{:S(2)}) copy-start(bf16[2,208,8,80]{1,3,2,0:T(8,128)(2,1)S(1)} %copy.266) | copy-start | bytes 1597444
  605.3 25.9 %copy-start.32 = (f32[416,640]{1,0:T(8,128)}, f32[416,640]{1,0:T(8,128)S(1)}, u32[]{:S(2)}) copy-start(f32[416,640]{1,0:T(8,128)S(1)} %get-tuple-element.284) | copy-start | bytes 3194884
  690.9 235.1 %reduce-scatter.19.cloned.1.call-start = ((), (), s32[]{:S(2)}) async-start(), calls=%async_computation.25 | async-start | bytes 1024000 | tf_op jit(solution)/shard_map/reduce_scatter | solution.py:519
  700.7 225.3 %reduce-scatter.21.cloned.1.call-start = ((), (), s32[]{:S(2)}) async-start(), calls=%async_computation.26 | async-start | bytes 1024000 | tf_op jit(solution)/shard_map/reduce_scatter | solution.py:519
  710.9 215.1 %reduce-scatter.23.cloned.1.call-start = ((), (), s32[]{:S(2)}) async-start(), calls=%async_computation.27 | async-start | bytes 1024000 | tf_op jit(solution)/shard_map/reduce_scatter | solution.py:519
  713.7 212.3 %reduce-scatter.25.cloned.1.call-start = ((), (), s32[]{:S(2)}) async-start(), calls=%async_computation.28 | async-start | bytes 1024000 | tf_op jit(solution)/shard_map/reduce_scatter | solution.py:519
  716.7 209.3 %reduce-scatter.27.cloned.1.call-start = ((), (), s32[]{:S(2)}) async-start(), calls=%async_computation.29 | async-start | bytes 1024000 | tf_op jit(solution)/shard_map/reduce_scatter | solution.py:519
  719.8 206.3 %reduce-scatter.29.cloned.1.call-start = ((), (), s32[]{:S(2)}) async-start(), calls=%async_computation.30 | async-start | bytes 1024000 | tf_op jit(solution)/shard_map/reduce_scatter | solution.py:519
  722.8 203.3 %reduce-scatter.31.cloned.1.call-start = ((), (), s32[]{:S(2)}) async-start(), calls=%async_computation.31 | async-start | bytes 1024000 | tf_op jit(solution)/shard_map/reduce_scatter | solution.py:519
  729.7 201.7 %reduce-scatter.13.cloned.1.call-start = ((), (), s32[]{:S(2)}) async-start(), calls=%async_computation.22 | async-start | bytes 1024000 | tf_op jit(solution)/shard_map/reduce_scatter | solution.py:519
  736.5 221.1 %reduce-scatter.15.cloned.1.call-start = ((), (), s32[]{:S(2)}) async-start(), calls=%async_computation.23 | async-start | bytes 1024000 | tf_op jit(solution)/shard_map/reduce_scatter | solution.py:519
  742.7 256.7 %reduce-scatter.33.cloned.1.call-start = ((), (), s32[]{:S(2)}) async-start(), calls=%async_computation.32 | async-start | bytes 4096000 | tf_op jit(solution)/shard_map/reduce_scatter | solution.py:519
  753.7 31.9 %all-to-all-start.5 = ((bf16[32,18,640]{2,1,0:T(8,128)(2,1)}), bf16[32,18,640]{2,1,0:T(8,128)(2,1)S(1)}, u32[]{:S(2)}, u32[]{:S(2)}) async-start(bf16[32,18,640]{2,1,0:T(8,128)(2,1)} %reshape.1148), calls=%async_computation.5 | async-start | bytes 1966080 | tf_op jit(solution)/shard_map/all_to_all | solution.py:284
  772.8 16.4 %copy-start.56 = (f32[416,640]{1,0:T(8,128)S(1)}, f32[416,640]{1,0:T(8,128)}, u32[]{:S(2)}) copy-start(f32[416,640]{1,0:T(8,128)} %fusion.324) | copy-start | bytes 3194884
  785.6 22.6 %all-to-all-start.3 = ((bf16[8,72,640]{2,1,0:T(8,128)(2,1)}), bf16[8,72,640]{2,1,0:T(8,128)(2,1)S(1)}, u32[]{:S(2)}, u32[]{:S(2)}) async-start(bf16[8,72,640]{2,1,0:T(8,128)(2,1)} %copy-done.110), calls=%async_computation.3 | async-start | bytes 1474560 | tf_op jit(solution)/shard_map/all_to_all | solution.py:254
  789.2 251.8 %reduce-scatter.35.cloned.1.call-start = ((), (), s32[]{:S(2)}) async-start(), calls=%async_computation.33 | async-start | bytes 4096000 | tf_op jit(solution)/shard_map/reduce_scatter | solution.py:519
  795.5 16.9 %copy-start.215 = (s32[576]{0:T(1024)S(1)}, s32[576]{0:T(1024)}, u32[]{:S(2)}) copy-start(s32[576]{0:T(1024)} %copy-done.214) | copy-start | bytes 6916
  808.2 245.2 %all-to-all-start.2 = ((bf16[4,4,26,640]{3,1,2,0:T(4,128)(2,1)}), bf16[4,4,26,640]{3,1,2,0:T(4,128)(2,1)}, u32[]{:S(2)}, u32[]{:S(2)}) async-start(bf16[4,4,26,640]{3,1,2,0:T(4,128)(2,1)} %copy.279), calls=%async_computation.2 | async-start | bytes 1064960 | tf_op jit(solution)/shard_map/all_to_all | solution.py:302
  812.4 393.4 %all-reduce.21.cloned.1.call-start = ((), (), s32[]{:S(2)}) async-start(), calls=%async_computation.38 | async-start | bytes 7372800 | tf_op jit(solution)/shard_map/psum | solution.py:520
  818.4 23.7 %copy-start.18 = (f32[576,640]{1,0:T(8,128)}, f32[576,640]{1,0:T(8,128)S(1)}, u32[]{:S(2)}) copy-start(f32[576,640]{1,0:T(8,128)S(1)} %fusion.107) | copy-start | bytes 4423684
  1053.4 67.7 %all-to-all-start.6 = ((bf16[8,72,640]{2,1,0:T(8,128)(2,1)}), bf16[8,72,640]{2,1,0:T(8,128)(2,1)S(1)}, u32[]{:S(2)}, u32[]{:S(2)}) async-start(bf16[8,72,640]{2,1,0:T(8,128)(2,1)} %bitcast.148), calls=%async_computation.6 | async-start | bytes 1474560 | tf_op jit(solution)/shard_map/all_to_all | solution.py:260
  (199 other events, 716.6 us)
Sparse Core Ops, SparseCore 0:
  14.9 276.9 all-reduce.18
  1041.1 164.6 all-reduce.20
Sparse Core Ops, SparseCore 1:
  15.5 63.2 all-gather.19
  80.8 69.6 all-gather.21
  151.9 60.4 all-gather.23
  213.9 29.1 all-gather.25
  244.7 29.2 all-gather.27
  275.5 29.2 all-gather.29
  691.0 24.6 reduce-scatter.16
  718.2 23.3 reduce-scatter.18
  744.0 32.9 reduce-scatter.20
  779.7 21.7 reduce-scatter.22
  803.9 23.4 reduce-scatter.24
  830.1 23.4 reduce-scatter.26
  855.9 23.4 reduce-scatter.28
  882.0 23.4 reduce-scatter.30
  908.0 23.4 reduce-scatter.12
  934.2 23.4 reduce-scatter.14
  960.7 38.7 reduce-scatter.32
  1002.2 38.6 reduce-scatter.34

commit v2 on v1

v2 whole, which is shorter than its diff:
```python
import functools
import math

import jax
import jax.numpy as jnp
from jax import lax
from jax.experimental import pallas as pl
from jax.experimental.pallas import tpu as pltpu
from jax.sharding import PartitionSpec as P

HEADS = 8
GROUPS = 32
FF_ST = 2560
TEMB = 1280
SIDE_BIG = 32
SIDE_MID = 24
SIDE_SMALL = 16


HIGHEST = lax.Precision.HIGHEST
EPSILON = 1e-05
FAR = -1e30
MESH = pl.DeviceIdType.MESH


def to_low(value):
    return value.astype(jnp.bfloat16)


def matmul(left, weight):
    return jnp.dot(left, weight, preferred_element_type=jnp.float32)


def matmul_back(gradient, weight):
    return lax.dot_general(
        gradient, weight, (((1,), (1,)), ((), ())), preferred_element_type=jnp.float32
    )


def matmul_left(left, right):
    return lax.dot_general(left, right, (((0,), (0,)), ((), ())), preferred_element_type=jnp.float32)


def token_sum(gradient):
    return jnp.sum(gradient, axis=0)


def clip_layout(row_devices):
    grid_cols = min(8, row_devices // 2)
    grid_rows = row_devices // grid_cols
    sides = (
        [SIDE_BIG] * (3 * (row_devices // 64))
        + [SIDE_MID] * max(1, row_devices // 16)
        + [SIDE_SMALL] * max(1, row_devices // 16)
    )
    layout = []
    offset = 0
    for side in sides:
        layout.append((side, side // grid_rows, side // grid_cols, offset))
        offset = offset + side // grid_rows * (side // grid_cols)
    return (layout, grid_rows, grid_cols)


def time_table(timesteps):
    half_count = TEMB // 2
    frequency = jnp.exp(
        jnp.arange(half_count, dtype=jnp.float32) * (-math.log(10000.0) / half_count)
    )
    angles = timesteps.astype(jnp.float32)[:, None] * frequency[None, :]
    return jnp.concatenate([jnp.cos(angles), jnp.sin(angles)], axis=1)


def frame_table(frame_ids, channels):
    channel = jnp.arange(channels, dtype=jnp.int32)
    even_index = (channel - channel % 2).astype(jnp.float32)
    frequency = jnp.exp(even_index * (-math.log(10000.0) / channels))
    angles = frame_ids.astype(jnp.float32)[:, None] * frequency[None, :]
    return jnp.where((channel % 2 == 0)[None, :], jnp.sin(angles), jnp.cos(angles))


def group_table(channels):
    which = jnp.arange(channels, dtype=jnp.int32) // (channels // GROUPS)
    return (which[:, None] == which[None, :]).astype(jnp.float32)


def onehot(indices, width):
    return (indices[:, None] == jnp.arange(width, dtype=jnp.int32)[None, :]).astype(jnp.bfloat16)


class Places:
    def __init__(self, frames_here, channels):
        self.rows = lax.axis_size("rows")
        self.frames = lax.axis_size("frame")
        self.row = lax.axis_index("rows")
        self.frame = lax.axis_index("frame")
        self.frames_here = frames_here
        self.layout, self.grid_rows, self.grid_cols = clip_layout(self.rows)
        self.clips = len(self.layout)
        self.units = frames_here * self.clips
        assert self.units <= self.rows
        self.channels = channels
        self.side = max(entry[0] for entry in self.layout)
        self.block_max = max(entry[1] * entry[2] for entry in self.layout)
        self.shares = [-(-entry[1] * entry[2] // self.frames) for entry in self.layout]
        self.share_max = max(self.shares)
        self.share_total = sum(self.shares)
        self.clip = self.row % self.clips
        sides = jnp.array([entry[0] for entry in self.layout], jnp.int32)
        self.my_side = jnp.where(self.row < self.units, sides[self.clip], 0)
        self.safe_side = jnp.maximum(self.my_side, self.grid_rows * self.grid_cols)
        cells = jnp.arange(self.side * self.side, dtype=jnp.int32)
        self.cell_row, self.cell_col = cells // self.side, cells % self.side
        self.valid = (self.cell_row < self.my_side) & (self.cell_col < self.my_side)
        block_rows = sides[self.clip] // self.grid_rows
        block_cols = sides[self.clip] // self.grid_cols
        self.device = self.cell_row // block_rows * self.grid_cols + self.cell_col // block_cols
        self.in_block = self.cell_row % block_rows * block_cols + self.cell_col % block_cols
        shares = jnp.array(self.shares, jnp.int32)
        share = shares[self.clip]
        block_index = jnp.where(self.valid, self.device * self.block_max + self.in_block, -1)
        self.block_table = onehot(block_index, self.rows * self.block_max)
        column_index = (
            (self.in_block // share * self.rows + self.device) * self.share_max
            + self.in_block % share
        )
        column_index = jnp.where(self.valid, column_index, -1)
        self.column_table = onehot(column_index, self.frames * self.rows * self.share_max)
        picks = []
        for number in range(self.clips):
            cell = jnp.arange(self.shares[number], dtype=jnp.int32)[:, None]
            when = jnp.arange(self.frames * frames_here, dtype=jnp.int32)[None, :]
            source = (
                when // frames_here * self.rows + when % frames_here * self.clips + number
            ) * self.share_max + cell
            picks.append(source.reshape(-1))
        self.pick_table = onehot(
            jnp.concatenate(picks), self.frames * self.rows * self.share_max
        )

    def blocks_to_unit(self, blocks):
        pieces = []
        for frame in range(self.frames_here):
            for side, height, width, offset in self.layout:
                piece = blocks[frame, offset : offset + height * width]
                pieces.append(jnp.pad(piece, ((0, self.block_max - height * width), (0, 0))))
        for _ in range(self.units, self.rows):
            pieces.append(jnp.zeros_like(pieces[0]))
        received = lax.all_to_all(jnp.stack(pieces), "rows", 0, 0)
        return matmul(self.block_table, received.reshape(-1, self.channels))

    def unit_to_blocks(self, field_low):
        send = to_low(matmul_left(self.block_table, field_low))
        send = send.reshape(self.rows, self.block_max, self.channels)
        received = lax.all_to_all(send, "rows", 0, 0)
        frames = []
        for frame in range(self.frames_here):
            frames.append(
                jnp.concatenate(
                    [
                        received[frame * self.clips + number, : entry[1] * entry[2]]
                        for number, entry in enumerate(self.layout)
                    ]
                )
            )
        return jnp.stack(frames)

    def unit_to_columns(self, fields_low):
        width = sum(field.shape[-1] for field in fields_low)
        joined = jnp.concatenate(fields_low, axis=1)
        send = to_low(matmul_left(self.column_table, joined))
        send = send.reshape(self.frames * self.rows, self.share_max, width)
        received = lax.all_to_all(send, ("frame", "rows"), 0, 0)
        return matmul(self.pick_table, received.reshape(-1, width))

    def columns_to_unit(self, field_low):
        send = to_low(matmul_left(self.pick_table, field_low))
        send = send.reshape(self.frames * self.rows, self.share_max, self.channels)
        received = lax.all_to_all(send, ("frame", "rows"), 0, 0)
        return matmul(self.column_table, received.reshape(-1, self.channels))

    def blocks_to_columns(self, blocks):
        parts = []
        for number, (side, height, width, offset) in enumerate(self.layout):
            share = self.shares[number]
            part = blocks[:, offset : offset + height * width]
            part = jnp.pad(part, ((0, 0), (0, share * self.frames - height * width), (0, 0)))
            parts.append(part.reshape(self.frames_here, self.frames, share, self.channels))
        send = jnp.transpose(jnp.concatenate(parts, axis=2), (1, 0, 2, 3))
        received = lax.all_to_all(send, "frame", 0, 0)
        received = received.reshape(-1, self.share_total, self.channels)
        return jnp.transpose(received, (1, 0, 2)).reshape(-1, self.channels)

    def columns_to_blocks(self, field_low):
        send = jnp.transpose(field_low.reshape(self.share_total, -1, self.channels), (1, 0, 2))
        send = send.reshape(self.frames, self.frames_here, self.share_total, self.channels)
        received = lax.all_to_all(send, "frame", 0, 0)
        parts = []
        start = 0
        for number, (side, height, width, offset) in enumerate(self.layout):
            share = self.shares[number]
            part = jnp.transpose(received[:, :, start : start + share], (1, 0, 2, 3))
            part = part.reshape(self.frames_here, self.frames * share, self.channels)
            parts.append(part[:, : height * width])
            start = start + share
        return jnp.concatenate(parts, axis=1)


def swap(value, axis, bit):
    count = lax.axis_size(axis)
    return lax.ppermute(value, axis, [(i, i ^ bit) for i in range(count)])


def exchange_pieces(shard, near, half):
    first = swap(half, "frame", 2)
    second = swap(first, "rows", 1)
    return (shard, near, first, second, swap(first, "frame", 1), swap(second, "frame", 1))


def piece_places():
    frame = lax.axis_index("frame")
    odd_row = lax.axis_index("rows") % 2
    far, corner = 2 * (frame ^ 2), 2 * (frame ^ 3)
    return jnp.stack(
        [
            2 * frame,
            2 * (frame ^ 1),
            far + odd_row,
            far + 1 - odd_row,
            corner + odd_row,
            corner + 1 - odd_row,
        ]
    ).astype(jnp.int32)


def start_load(places_ref, pieces, lead, target, sem):
    if len(pieces) == 1:
        source = pieces[0] if lead is None else pieces[0].at[lead]
        pltpu.make_async_copy(source, target, sem).start()
        return
    half = pieces[0].shape[-2] // 2
    for number, piece in enumerate(pieces):
        start = pl.multiple_of(places_ref[number] * half, 16)
        source = piece if lead is None else piece.at[lead]
        where = target.at[pl.ds(start, piece.shape[-2])]
        pltpu.make_async_copy(source, where, sem).start()


def pair_load(places_ref, groups, lead, target, sem):
    if lead < 2:
        start_load(places_ref, groups[0], lead, target, sem)
    else:
        start_load(places_ref, groups[1], lead - 2, target, sem)


def finish_load(target, sem):
    pltpu.make_async_copy(target, target, sem).wait()


def run_kernel(body, places_row, arrays, groups, outs, scratch, flops):
    count, pieces = len(arrays), sum(len(group) for group in groups)
    out_count = len(outs)

    def kernel(*refs):
        held = list(refs[1 + count : 1 + count + pieces])
        grouped = [[held.pop(0) for _ in group] for group in groups]
        outputs = refs[1 + count + pieces : 1 + count + pieces + out_count]
        body(
            refs[0],
            refs[1 : 1 + count],
            grouped,
            outputs,
            refs[1 + count + pieces + out_count :],
        )

    whole = pl.BlockSpec(memory_space=pltpu.VMEM)
    flat = [piece for group in groups for piece in group]
    moved = sum(a.size * a.dtype.itemsize for a in list(arrays) + flat)
    moved += sum(math.prod(o.shape) * o.dtype.itemsize for o in outs)
    return pl.pallas_call(
        kernel,
        out_shape=outs,
        in_specs=[pl.BlockSpec(memory_space=pltpu.SMEM)]
        + [whole] * count
        + [pl.BlockSpec(memory_space=pl.ANY)] * pieces,
        out_specs=[whole] * out_count,
        scratch_shapes=scratch,
        compiler_params=pltpu.CompilerParams(vmem_limit_bytes=56 * 2**20),
        cost_estimate=pl.CostEstimate(flops=flops, bytes_accessed=moved, transcendentals=0),
    )(places_row, *arrays, *flat)


def f32(*shape):
    return jax.ShapeDtypeStruct(shape, jnp.float32)


def b16(*shape):
    return jax.ShapeDtypeStruct(shape, jnp.bfloat16)


def dot_nn(left, right):
    return jnp.dot(left, right, preferred_element_type=jnp.float32)


def dot_nt(left, right):
    return lax.dot_general(left, right, (((1,), (1,)), ((), ())), preferred_element_type=jnp.float32)


def dot_tn(left, right):
    return lax.dot_general(left, right, (((0,), (0,)), ((), ())), preferred_element_type=jnp.float32)


def spread_means(first, second, table, inv_count):
    rows = jnp.concatenate(
        [
            jnp.sum(first, axis=0, keepdims=True),
            jnp.sum(second, axis=0, keepdims=True),
            jnp.zeros((6, first.shape[1]), jnp.float32),
        ]
    )
    means = jnp.dot(rows, table, precision=HIGHEST, preferred_element_type=jnp.float32) * inv_count
    return (means[0:1], means[1:2])


def group_normed(field, valid, table, inv_count):
    kept = field * valid
    average, square = spread_means(kept, kept * field, table, inv_count)
    inv_std = lax.rsqrt(square - average * average + EPSILON)
    return ((field - average) * inv_std, inv_std)


def group_back(gradient, normed, inv_std, gain, valid, table, inv_count):
    scaled = gradient * gain * valid
    mean_one, mean_two = spread_means(scaled, scaled * normed, table, inv_count)
    return inv_std * (scaled - mean_one - normed * mean_two) * valid


def layer_normed(field):
    centred = field - jnp.mean(field, axis=1, keepdims=True)
    inv_std = lax.rsqrt(jnp.mean(centred * centred, axis=1, keepdims=True) + EPSILON)
    return (centred * inv_std, inv_std)


def layer_back(gradient, normed, inv_std, gain):
    scaled = gradient * gain
    mean_one = jnp.mean(scaled, axis=1, keepdims=True)
    mean_two = jnp.mean(scaled * normed, axis=1, keepdims=True)
    return inv_std * (scaled - mean_one - normed * mean_two)


def half_erf(field):
    return 0.5 + 0.5 * lax.erf(field * (0.5**0.5))


def gelu_slope(field, half):
    return half + field * (jnp.exp(-0.5 * field * field) * (1.0 / math.sqrt(2.0 * math.pi)))


def head_windows(channels):
    width = channels // HEADS
    windows = []
    for head in range(HEADS):
        start = head * width // 128 * 128
        stop = -(-(head + 1) * width // 128) * 128
        windows.append((start, stop, head * width - start, (head + 1) * width - start))
    return windows


def head_mask(window):
    start, stop, low, high = window
    lane = lax.broadcasted_iota(jnp.int32, (1, stop - start), 1)
    return ((lane >= low) & (lane < high)).astype(jnp.float32).astype(jnp.bfloat16)


def attend_into(query_ref, key_ref, value_ref, bias, out_ref, rows):
    channels = query_ref.shape[1]
    factor = (channels // HEADS) ** (-0.5) * math.log2(math.e)
    out_ref[rows, :] = jnp.zeros((query_ref[rows, :].shape[0], channels), jnp.float32)
    for window in head_windows(channels):
        lanes = slice(window[0], window[1])
        mask = head_mask(window)
        scores = dot_nt(query_ref[rows, lanes] * mask, key_ref[rows if bias.shape[0] > 1 else slice(None), lanes])
        scores = scores * factor + bias
        powers = jnp.exp2(scores - jnp.max(scores, axis=1, keepdims=True))
        inverse = 1.0 / jnp.sum(powers, axis=1, keepdims=True)
        values = value_ref[rows if bias.shape[0] > 1 else slice(None), lanes] * mask
        out_ref[rows, lanes] += dot_nn(to_low(powers), values) * inverse


def attend_back_into(query_ref, key_ref, value_ref, grad_ref, bias, outs, rows, key_rows):
    channels = query_ref.shape[1]
    scale = (channels // HEADS) ** (-0.5)
    factor = scale * math.log2(math.e)
    for number, out_ref in enumerate(outs):
        size = (rows if number == 0 else key_rows)
        out_ref[size, :] = jnp.zeros(
            ((query_ref if number == 0 else key_ref)[size, :].shape[0], channels), jnp.float32
        )
    for window in head_windows(channels):
        lanes = slice(window[0], window[1])
        mask = head_mask(window)
        queries = query_ref[rows, lanes] * mask
        keys = key_ref[key_rows, lanes] * mask
        grads = grad_ref[rows, lanes] * mask
        scores = dot_nt(keys, queries) * factor + bias
        powers = jnp.exp2(scores - jnp.max(scores, axis=0, keepdims=True))
        probs = powers * (1.0 / jnp.sum(powers, axis=0, keepdims=True))
        grad_probs = dot_nt(value_ref[key_rows, lanes], grads)
        inner = jnp.sum(probs * grad_probs, axis=0, keepdims=True)
        grad_scores = to_low(probs * (grad_probs - inner))
        outs[0][rows, lanes] += dot_tn(grad_scores, keys) * scale
        if len(outs) > 1:
            outs[1][key_rows, lanes] += dot_nn(grad_scores, queries) * scale
            outs[2][key_rows, lanes] += dot_nn(to_low(probs), grads)


ALL = slice(None)


def fill_taps(field, masks, pads, side):
    cells = field.shape[0]
    border = jnp.zeros((side, field.shape[1]), jnp.float32)
    left = pltpu.roll(field, 1, 0) * masks[:, 1:2]
    right = pltpu.roll(field, cells - 1, 0) * masks[:, 2:3]
    for number, moved in enumerate((left, field, right)):
        pads[number, :side, :] = border
        pads[number, side : side + cells, :] = moved
        pads[number, side + cells :, :] = border


def conv_forward(places_row, side, field, masks, vectors, table, weights, which, residual):
    cells, channels = field.shape

    def body(places_ref, ins, groups, outs, scratch):
        field_ref, masks_ref, vec_ref, table_ref = ins[:4]
        weight, pads, sem = scratch
        (out_ref,) = outs
        start_load(places_ref, groups[0], pl.ds(9 * which, 9), weight, sem.at[0])
        masks = masks_ref[...]
        valid = masks[:, 0:1]
        vec = vec_ref[...]
        normed, _ = group_normed(
            field_ref[...].astype(jnp.float32), valid, table_ref[...], vec[3:4]
        )
        pre = normed * vec[0:1] + vec[1:2]
        act = pre / (1.0 + jnp.exp(-pre)) * valid
        fill_taps(act, masks, pads, side)
        out_ref[...] = jnp.broadcast_to(vec[2:3], (cells, channels))
        if residual:
            out_ref[...] += field_resid(ins)
        finish_load(weight, sem.at[0])

        def row_tap(step, carry):
            rows = pl.ds(pl.multiple_of(step * side, 8), cells)
            total = out_ref[...]
            for col in range(3):
                total += dot_nn(to_low(pads[col, rows, :]), weight[step * 3 + col])
            out_ref[...] = total
            return carry

        lax.fori_loop(0, 3, row_tap, 0)

    def field_resid(ins):
        return ins[4][...].astype(jnp.float32)

    arrays = [field, masks, vectors, table] + ([residual[0]] if residual else [])
    return run_kernel(
        body,
        places_row,
        arrays,
        [(weights,)],
        [f32(cells, channels)],
        [
            pltpu.VMEM((9, channels, channels), jnp.bfloat16),
            pltpu.VMEM((3, cells + 2 * side, channels), jnp.float32),
            pltpu.SemaphoreType.DMA((1,)),
        ],
        18 * cells * channels * channels,
    )[0]


def conv_backward(places_row, side, gradient, field, masks, vectors, table, weights, which, extra):
    cells, channels = field.shape

    def body(places_ref, ins, groups, outs, scratch):
        grad_ref, field_ref, masks_ref, vec_ref, table_ref = ins[:5]
        weight, pads, total_ref, sem = scratch
        (out_ref,) = outs
        start_load(places_ref, groups[0], pl.ds(9 * which, 9), weight, sem.at[0])
        masks = masks_ref[...]
        valid = masks[:, 0:1]
        vec = vec_ref[...]
        fill_taps(grad_ref[...], masks, pads, side)
        total_ref[...] = jnp.zeros((cells, channels), jnp.float32)
        finish_load(weight, sem.at[0])

        def row_tap(step, carry):
            rows = pl.ds(pl.multiple_of(step * side, 8), cells)
            total = total_ref[...]
            for col in range(3):
                total += dot_nt(to_low(pads[col, rows, :]), weight[8 - (step * 3 + col)])
            total_ref[...] = total
            return carry

        lax.fori_loop(0, 3, row_tap, 0)
        normed, inv_std = group_normed(
            field_ref[...].astype(jnp.float32), valid, table_ref[...], vec[3:4]
        )
        pre = normed * vec[0:1] + vec[1:2]
        gate = 1.0 / (1.0 + jnp.exp(-pre))
        grad_pre = total_ref[...] * (gate * (1.0 + pre * (1.0 - gate)))
        result = group_back(
            grad_pre, normed, inv_std, vec[0:1], valid, table_ref[...], vec[3:4]
        )
        if extra:
            result += ins[5][...]
        out_ref[...] = result

    return run_kernel(
        body,
        places_row,
        [gradient, field, masks, vectors, table] + list(extra),
        [(weights,)],
        [f32(cells, channels)],
        [
            pltpu.VMEM((9, channels, channels), jnp.bfloat16),
            pltpu.VMEM((3, cells + 2 * side, channels), jnp.float32),
            pltpu.VMEM((cells, channels), jnp.float32),
            pltpu.SemaphoreType.DMA((1,)),
        ],
        18 * cells * channels * channels,
    )[0]


def self_forward(places_row, resid, masks, bias, vectors, table, proj, attn):
    cells, channels = resid.shape
    needed = (0, 2, 3, 4, 5)

    def body(places_ref, ins, groups, outs, scratch):
        resid_ref, masks_ref, bias_ref, vec_ref, table_ref = ins
        proj_ref, query_ref, key_ref, value_ref, two_ref = outs
        weight, att, sem = scratch
        for slot, lead in enumerate(needed):
            pair_load(places_ref, groups, lead, weight.at[slot], sem.at[slot])
        vec = vec_ref[...]
        normed, _ = group_normed(resid_ref[...], masks_ref[:, 0:1], table_ref[...], vec[7:8])
        low = to_low(normed * vec[0:1] + vec[1:2])
        finish_load(weight.at[0], sem.at[0])
        entered = dot_nn(low, weight[0]) + vec[2:3]
        proj_ref[...] = entered
        normed, _ = layer_normed(entered)
        low = to_low(normed * vec[3:4] + vec[4:5])
        for slot, out_ref in ((1, query_ref), (2, key_ref), (3, value_ref)):
            finish_load(weight.at[slot], sem.at[slot])
            out_ref[...] = to_low(dot_nn(low, weight[slot]))
        attend_into(query_ref, key_ref, value_ref, bias_ref[0:1, :], att, ALL)
        finish_load(weight.at[4], sem.at[4])
        two_ref[...] = proj_ref[...] + dot_nn(to_low(att[...]), weight[4]) + vec[5:6]

    return run_kernel(
        body,
        places_row,
        [resid, masks, bias, vectors, table],
        [(proj,), (attn,)],
        [f32(cells, channels)] + [b16(cells, channels)] * 3 + [f32(cells, channels)],
        [
            pltpu.VMEM((5, channels, channels), jnp.bfloat16),
            pltpu.VMEM((cells, channels), jnp.float32),
            pltpu.SemaphoreType.DMA((5,)),
        ],
        10 * cells * channels * channels + 4 * cells * cells * channels,
    )


def self_backward(places_row, grad_two, proj_one, query, key, value, resid, grad_st, masks, vectors, table, proj, attn):
    cells, channels = resid.shape
    needed = (5, 2, 3, 4, 0)

    def body(places_ref, ins, groups, outs, scratch):
        grad_ref, proj_ref, query_ref, key_ref, value_ref, resid_ref, st_ref, masks_ref, vec_ref, table_ref = ins
        (out_ref,) = outs
        weight, grad_att, grad_q, grad_k, grad_v, sem = scratch
        for slot, lead in enumerate(needed):
            pair_load(places_ref, groups, lead, weight.at[slot], sem.at[slot])
        vec = vec_ref[...]
        valid = masks_ref[:, 0:1]
        finish_load(weight.at[0], sem.at[0])
        grad_att[...] = to_low(dot_nt(to_low(grad_ref[...]), weight[0]))
        attend_back_into(
            query_ref, key_ref, value_ref, grad_att, (valid - 1.0) * -FAR,
            (grad_q, grad_k, grad_v), ALL, ALL,
        )
        total = None
        for slot, member in ((1, grad_q), (2, grad_k), (3, grad_v)):
            finish_load(weight.at[slot], sem.at[slot])
            part = dot_nt(to_low(member[...]), weight[slot])
            total = part if total is None else total + part
        normed, inv_std = layer_normed(proj_ref[...])
        grad_one = grad_ref[...] + layer_back(total, normed, inv_std, vec[3:4])
        finish_load(weight.at[4], sem.at[4])
        grad_gn = dot_nt(to_low(grad_one), weight[4])
        normed, inv_std = group_normed(resid_ref[...], valid, table_ref[...], vec[7:8])
        out_ref[...] = st_ref[...] + group_back(
            grad_gn, normed, inv_std, vec[0:1], valid, table_ref[...], vec[7:8]
        )

    return run_kernel(
        body,
        places_row,
        [grad_two, proj_one, query, key, value, resid, grad_st, masks, vectors, table],
        [(proj,), (attn,)],
        [f32(cells, channels)],
        [
            pltpu.VMEM((5, channels, channels), jnp.bfloat16),
            pltpu.VMEM((cells, channels), jnp.bfloat16),
            pltpu.VMEM((cells, channels), jnp.float32),
            pltpu.VMEM((cells, channels), jnp.float32),
            pltpu.VMEM((cells, channels), jnp.float32),
            pltpu.SemaphoreType.DMA((5,)),
        ],
        10 * cells * channels * channels + 10 * cells * cells * channels,
    )[0]


CHUNK = 512


def cross_forward(places_row, two, resid, context, masks, bias, vectors, wide_bias, table, proj, attn, cross, w_in_all, w_out_all):
    cells, channels = resid.shape
    prompt, width = context.shape

    def body(places_ref, ins, groups, outs, scratch):
        two_ref, resid_ref, context_ref, masks_ref, bias_ref, vec_ref, wide_ref, table_ref = ins
        query_ref, key_ref, value_ref, three_ref, out_ref, motion_ref = outs
        weight, kv, w_in, w_out, att, total, sem = scratch
        for slot, lead in enumerate((6, 7, 1)):
            pair_load(places_ref, groups, lead, weight.at[slot], sem.at[slot])
        for slot in range(2):
            start_load(places_ref, groups[2], slot, kv.at[slot], sem.at[3 + slot])
        start_load(places_ref, groups[3], None, w_in, sem.at[5])
        start_load(places_ref, groups[4], None, w_out, sem.at[6])
        vec = vec_ref[...]
        normed, _ = layer_normed(two_ref[...])
        low = to_low(normed * vec[0:1] + vec[1:2])
        finish_load(weight.at[0], sem.at[0])
        query_ref[...] = to_low(dot_nn(low, weight[0]))
        for slot, ref in ((0, key_ref), (1, value_ref)):
            finish_load(kv.at[slot], sem.at[3 + slot])
            ref[...] = to_low(dot_nn(context_ref[...], kv[slot]))
        attend_into(query_ref, key_ref, value_ref, bias_ref[0:1, :], att, ALL)
        finish_load(weight.at[1], sem.at[1])
        three_ref[...] = two_ref[...] + dot_nn(to_low(att[...]), weight[1]) + vec[2:3]
        normed, _ = layer_normed(three_ref[...])
        low = to_low(normed * vec[3:4] + vec[4:5])
        finish_load(w_in, sem.at[5])
        finish_load(w_out, sem.at[6])
        total[...] = three_ref[...] + vec[5:6]

        def chunk(step, carry):
            lanes = pl.ds(pl.multiple_of(step * CHUNK, 128), CHUNK)
            gates = pl.ds(pl.multiple_of(FF_ST + step * CHUNK, 128), CHUNK)
            hidden = dot_nn(low_ref(att), w_in[:, lanes]) + wide_ref[0:1, lanes]
            gate = dot_nn(low_ref(att), w_in[:, gates]) + wide_ref[0:1, gates]
            act = to_low(hidden * (gate * half_erf(gate)))
            total[...] += dot_nn(act, w_out[lanes, :])
            return carry

        def low_ref(ref):
            return to_low(ref[...])

        att[...] = low.astype(jnp.float32)
        lax.fori_loop(0, FF_ST // CHUNK, chunk, 0)
        finish_load(weight.at[2], sem.at[2])
        st_out = dot_nn(to_low(total[...]), weight[2]) + vec[6:7] + resid_ref[...]
        out_ref[...] = st_out
        normed, _ = group_normed(st_out, masks_ref[:, 0:1], table_ref[...], vec[9:10])
        motion_ref[...] = to_low(normed * vec[7:8] + vec[8:9])

    return run_kernel(
        body,
        places_row,
        [two, resid, context, masks, bias, vectors, wide_bias, table],
        [(proj,), (attn,), (cross,), (w_in_all,), (w_out_all,)],
        [
            b16(cells, channels),
            b16(prompt, channels),
            b16(prompt, channels),
            f32(cells, channels),
            f32(cells, channels),
            b16(cells, channels),
        ],
        [
            pltpu.VMEM((3, channels, channels), jnp.bfloat16),
            pltpu.VMEM((2, width, channels), jnp.bfloat16),
            pltpu.VMEM((channels, 2 * FF_ST), jnp.bfloat16),
            pltpu.VMEM((FF_ST, channels), jnp.bfloat16),
            pltpu.VMEM((cells, channels), jnp.float32),
            pltpu.VMEM((cells, channels), jnp.float32),
            pltpu.SemaphoreType.DMA((7,)),
        ],
        2 * cells * channels * (3 * channels + 3 * FF_ST),
    )


def cross_backward(places_row, grad_gn, grad_out, st_out, three, two, query, key, value, masks, bias_col, vectors, wide_bias, table, proj, attn, w_in_all, w_out_all):
    cells, channels = st_out.shape
    prompt = key.shape[0]

    def body(places_ref, ins, groups, outs, scratch):
        gn_ref, cot_ref, st_ref, three_ref, two_ref, query_ref, key_ref, value_ref, masks_ref, bias_ref, vec_ref, wide_ref, table_ref = ins
        grad_two_ref, grad_st_ref, small_ref = outs
        weight, w_in, w_out, low, grad_low, total, grad_att, grad_q, sem = scratch
        pair_load(places_ref, groups, 1, weight.at[0], sem.at[0])
        start_load(places_ref, groups[3], None, w_out, sem.at[4])
        start_load(places_ref, groups[2], None, w_in, sem.at[3])
        pair_load(places_ref, groups, 7, weight.at[1], sem.at[1])
        pair_load(places_ref, groups, 6, weight.at[2], sem.at[2])
        vec = vec_ref[...]
        valid = masks_ref[:, 0:1]
        grad_motion = gn_ref[...].astype(jnp.float32)
        normed, inv_std = group_normed(st_ref[...], valid, table_ref[...], vec[9:10])
        small_ref[...] = jnp.concatenate(
            [
                jnp.sum(grad_motion * normed, axis=0, keepdims=True),
                jnp.sum(grad_motion, axis=0, keepdims=True),
                jnp.zeros((6, channels), jnp.float32),
            ]
        )
        grad_st_ref[...] = cot_ref[...].astype(jnp.float32) + group_back(
            grad_motion, normed, inv_std, vec[7:8], valid, table_ref[...], vec[9:10]
        )
        finish_load(weight.at[0], sem.at[0])
        grad_two_ref[...] = dot_nt(to_low(grad_st_ref[...]), weight[0])
        grad_low[...] = to_low(grad_two_ref[...])
        normed, inv_std = layer_normed(three_ref[...])
        low[...] = to_low(normed * vec[3:4] + vec[4:5])
        total[...] = jnp.zeros((cells, channels), jnp.float32)
        finish_load(w_out, sem.at[4])
        finish_load(w_in, sem.at[3])

        def chunk(step, carry):
            lanes = pl.ds(pl.multiple_of(step * CHUNK, 128), CHUNK)
            gates = pl.ds(pl.multiple_of(FF_ST + step * CHUNK, 128), CHUNK)
            hidden = dot_nn(low[...], w_in[:, lanes]) + wide_ref[0:1, lanes]
            gate = dot_nn(low[...], w_in[:, gates]) + wide_ref[0:1, gates]
            grad_act = dot_nt(grad_low[...], w_out[lanes, :])
            half = half_erf(gate)
            grad_hidden = to_low(grad_act * (gate * half))
            grad_gate = to_low(grad_act * hidden * gelu_slope(gate, half))
            total[...] += dot_nt(grad_hidden, w_in[:, lanes]) + dot_nt(grad_gate, w_in[:, gates])
            return carry

        lax.fori_loop(0, FF_ST // CHUNK, chunk, 0)
        normed, inv_std = layer_normed(three_ref[...])
        grad_two_ref[...] += layer_back(total[...], normed, inv_std, vec[3:4])
        finish_load(weight.at[1], sem.at[1])
        grad_att[...] = to_low(dot_nt(to_low(grad_two_ref[...]), weight[1]))
        attend_back_into(
            query_ref, key_ref, value_ref, grad_att, bias_ref[:, 0:1], (grad_q,), ALL, ALL
        )
        finish_load(weight.at[2], sem.at[2])
        grad_ln = dot_nt(to_low(grad_q[...]), weight[2])
        normed, inv_std = layer_normed(two_ref[...])
        grad_two_ref[...] += layer_back(grad_ln, normed, inv_std, vec[0:1])

    return run_kernel(
        body,
        places_row,
        [grad_gn, grad_out, st_out, three, two, query, key, value, masks, bias_col, vectors, wide_bias, table],
        [(proj,), (attn,), (w_in_all,), (w_out_all,)],
        [f32(cells, channels), f32(cells, channels), f32(8, channels)],
        [
            pltpu.VMEM((3, channels, channels), jnp.bfloat16),
            pltpu.VMEM((channels, 2 * FF_ST), jnp.bfloat16),
            pltpu.VMEM((FF_ST, channels), jnp.bfloat16),
            pltpu.VMEM((cells, channels), jnp.bfloat16),
            pltpu.VMEM((cells, channels), jnp.bfloat16),
            pltpu.VMEM((cells, channels), jnp.float32),
            pltpu.VMEM((cells, channels), jnp.bfloat16),
            pltpu.VMEM((cells, channels), jnp.float32),
            pltpu.SemaphoreType.DMA((5,)),
        ],
        2 * cells * channels * (3 * channels + 6 * FF_ST),
    )


def group_rows(step, group_len):
    return pl.ds(pl.multiple_of(step * group_len, 16), group_len)


def motion_forward(places_row, motion_in, position, bias, vectors, proj, attn):
    tokens, channels = motion_in.shape
    group_len = bias.shape[0]

    def body(places_ref, ins, groups, outs, scratch):
        in_ref, pos_ref, bias_ref, vec_ref = ins
        weight, att, sem = scratch
        for slot, lead in enumerate((0, 2, 3, 4, 5, 6, 7, 8, 9)):
            pair_load(places_ref, groups, lead, weight.at[slot], sem.at[slot])
        vec = vec_ref[...]
        finish_load(weight.at[0], sem.at[0])
        outs[0][...] = dot_nn(in_ref[...], weight[0]) + vec[0:1]
        for block in range(2):
            zed_ref, next_ref = outs[block], outs[block + 1]
            qkv = outs[3 + 4 * block : 6 + 4 * block]
            time_ref = outs[6 + 4 * block]
            normed, _ = layer_normed(zed_ref[...])
            low = to_low(normed * vec[1 + 3 * block : 2 + 3 * block] + vec[2 + 3 * block : 3 + 3 * block] + pos_ref[...])
            for which in range(3):
                slot = 1 + 4 * block + which
                finish_load(weight.at[slot], sem.at[slot])
                qkv[which][...] = to_low(dot_nn(low, weight[slot]))

            def group(step, carry):
                attend_into(*qkv, bias_ref[...], att, group_rows(step, group_len))
                return carry

            lax.fori_loop(0, tokens // group_len, group, 0)
            time_ref[...] = to_low(att[...])
            slot = 4 + 4 * block
            finish_load(weight.at[slot], sem.at[slot])
            next_ref[...] = zed_ref[...] + dot_nn(time_ref[...], weight[slot]) + vec[3 + 3 * block : 4 + 3 * block]

    return run_kernel(
        body,
        places_row,
        [motion_in, position, bias, vectors],
        [proj, attn],
        [f32(tokens, channels)] * 3 + [b16(tokens, channels)] * 8,
        [
            pltpu.VMEM((9, channels, channels), jnp.bfloat16),
            pltpu.VMEM((tokens, channels), jnp.float32),
            pltpu.SemaphoreType.DMA((9,)),
        ],
        18 * tokens * channels * channels,
    )


def motion_ff(places_row, zed, st_columns, cotangent, vectors, wide_bias, proj, in_pieces, out_pieces):
    tokens, channels = zed.shape
    hidden_width = wide_bias.shape[1]

    def body(places_ref, ins, groups, outs, scratch):
        zed_ref, st_ref, cot_ref, vec_ref, wide_ref = ins
        out_ref, grad_ref, d_proj, d_in, d_out, small_ref, wide_out = outs
        weight, w_in, w_out, pre, low, grad_low, total, sem = scratch
        start_load(places_ref, groups[1], None, w_in, sem.at[0])
        start_load(places_ref, groups[2], None, w_out, sem.at[1])
        start_load(places_ref, groups[0], 1, weight, sem.at[2])
        vec = vec_ref[...]
        normed, inv_std = layer_normed(zed_ref[...])
        low[...] = to_low(normed * vec[0:1] + vec[1:2])
        total[...] = zed_ref[...] + vec[2:3]
        finish_load(w_in, sem.at[0])
        finish_load(w_out, sem.at[1])

        def forward(step, carry):
            lanes = pl.ds(pl.multiple_of(step * CHUNK, 128), CHUNK)
            before = dot_nn(low[...], w_in[:, lanes]) + wide_ref[0:1, lanes]
            pre[:, lanes] = before
            total[...] += dot_nn(to_low(before * half_erf(before)), w_out[lanes, :])
            return carry

        lax.fori_loop(0, hidden_width // CHUNK, forward, 0)
        finish_load(weight, sem.at[2])
        zed_low = to_low(total[...])
        out_ref[...] = to_low(st_ref[...].astype(jnp.float32) + dot_nn(zed_low, weight[...]) + vec[3:4])
        d_proj[...] = to_low(dot_tn(zed_low, cot_ref[...]))
        grad_ref[...] = dot_nt(cot_ref[...], weight[...])
        grad_low[...] = to_low(grad_ref[...])
        total[...] = jnp.zeros((tokens, channels), jnp.float32)

        def backward(step, carry):
            lanes = pl.ds(pl.multiple_of(step * CHUNK, 128), CHUNK)
            before = pre[:, lanes]
            half = half_erf(before)
            d_out[lanes, :] = to_low(dot_tn(to_low(before * half), grad_low[...]))
            grad_pre = dot_nt(grad_low[...], w_out[lanes, :]) * gelu_slope(before, half)
            wide_out[0:1, lanes] = jnp.sum(grad_pre, axis=0, keepdims=True)
            pre_low = to_low(grad_pre)
            d_in[:, lanes] = to_low(dot_tn(low[...], pre_low))
            total[...] += dot_nt(pre_low, w_in[:, lanes])
            return carry

        wide_out[...] = jnp.zeros((8, hidden_width), jnp.float32)
        lax.fori_loop(0, hidden_width // CHUNK, backward, 0)
        normed, inv_std = layer_normed(zed_ref[...])
        grad_ln = total[...]
        small_ref[...] = jnp.concatenate(
            [
                jnp.sum(cot_ref[...].astype(jnp.float32), axis=0, keepdims=True),
                jnp.sum(grad_ref[...], axis=0, keepdims=True),
                jnp.sum(grad_ln * normed, axis=0, keepdims=True),
                jnp.sum(grad_ln, axis=0, keepdims=True),
                jnp.zeros((4, channels), jnp.float32),
            ]
        )
        grad_ref[...] += layer_back(grad_ln, normed, inv_std, vec[0:1])

    return run_kernel(
        body,
        places_row,
        [zed, st_columns, cotangent, vectors, wide_bias],
        [proj, in_pieces, out_pieces],
        [
            b16(tokens, channels),
            f32(tokens, channels),
            b16(channels, channels),
            b16(channels, hidden_width),
            b16(hidden_width, channels),
            f32(8, channels),
            f32(8, hidden_width),
        ],
        [
            pltpu.VMEM((channels, channels), jnp.bfloat16),
            pltpu.VMEM((channels, hidden_width), jnp.bfloat16),
            pltpu.VMEM((hidden_width, channels), jnp.bfloat16),
            pltpu.VMEM((tokens, hidden_width), jnp.float32),
            pltpu.VMEM((tokens, channels), jnp.bfloat16),
            pltpu.VMEM((tokens, channels), jnp.bfloat16),
            pltpu.VMEM((tokens, channels), jnp.float32),
            pltpu.SemaphoreType.DMA((3,)),
        ],
        12 * tokens * channels * hidden_width,
    )


def motion_back(places_row, block, grad_zed, zed, query, key, value, time_out, motion_in, position, bias, vectors, proj, attn):
    tokens, channels = zed.shape
    group_len = bias.shape[0]
    leads = [5 + 4 * block, 2 + 4 * block, 3 + 4 * block, 4 + 4 * block] + ([0] if motion_in is not None else [])
    last = motion_in is not None

    def body(places_ref, ins, groups, outs, scratch):
        grad_ref, zed_ref, query_ref, key_ref, value_ref, time_ref, pos_ref, bias_ref, vec_ref = ins[:9]
        out_ref, d_query, d_key, d_value, d_output, small_ref = outs[:6]
        weight, grad_att, grad_q, grad_k, grad_v, sem = scratch
        for slot, lead in enumerate(leads):
            pair_load(places_ref, groups, lead, weight.at[slot], sem.at[slot])
        vec = vec_ref[...]
        grad_low = to_low(grad_ref[...])
        d_output[...] = to_low(dot_tn(time_ref[...], grad_low))
        finish_load(weight.at[0], sem.at[0])
        grad_att[...] = to_low(dot_nt(grad_low, weight[0]))

        def group(step, carry):
            rows = group_rows(step, group_len)
            attend_back_into(
                query_ref, key_ref, value_ref, grad_att, bias_ref[...], (grad_q, grad_k, grad_v), rows, rows
            )
            return carry

        lax.fori_loop(0, tokens // group_len, group, 0)
        normed, inv_std = layer_normed(zed_ref[...])
        low = to_low(normed * vec[0:1] + vec[1:2] + pos_ref[...])
        grad_ln = None
        for slot, member, d_ref in ((1, grad_q, d_query), (2, grad_k, d_key), (3, grad_v, d_value)):
            member_low = to_low(member[...])
            d_ref[...] = to_low(dot_tn(low, member_low))
            finish_load(weight.at[slot], sem.at[slot])
            part = dot_nt(member_low, weight[slot])
            grad_ln = part if grad_ln is None else grad_ln + part
        total = grad_ref[...] + layer_back(grad_ln, normed, inv_std, vec[0:1])
        small_ref[...] = jnp.concatenate(
            [
                jnp.sum(grad_ref[...], axis=0, keepdims=True),
                jnp.sum(grad_ln * normed, axis=0, keepdims=True),
                jnp.sum(grad_ln, axis=0, keepdims=True),
                jnp.sum(total, axis=0, keepdims=True),
                jnp.zeros((4, channels), jnp.float32),
            ]
        )
        if last:
            total_low = to_low(total)
            outs[6][...] = to_low(dot_tn(ins[9][...], total_low))
            finish_load(weight.at[4], sem.at[4])
            out_ref[...] = to_low(dot_nt(total_low, weight[4]))
        else:
            out_ref[...] = total

    arrays = [grad_zed, zed, query, key, value, time_out, position, bias, vectors]
    outs = [b16(tokens, channels) if last else f32(tokens, channels)] + [b16(channels, channels)] * 4 + [f32(8, channels)]
    if last:
        arrays.append(motion_in)
        outs.append(b16(channels, channels))
    return run_kernel(
        body,
        places_row,
        arrays,
        [proj, attn],
        outs,
        [
            pltpu.VMEM((len(leads), channels, channels), jnp.bfloat16),
            pltpu.VMEM((tokens, channels), jnp.bfloat16),
            pltpu.VMEM((tokens, channels), jnp.float32),
            pltpu.VMEM((tokens, channels), jnp.float32),
            pltpu.VMEM((tokens, channels), jnp.float32),
            pltpu.SemaphoreType.DMA((len(leads),)),
        ],
        18 * tokens * channels * channels,
    )


def part_rows(count, turn):
    units = count // 16
    sizes = [units // 3 + (1 if (part - turn) % 3 < units % 3 else 0) for part in range(3)]
    starts = [16 * sum(sizes[:part]) for part in range(3)]
    return [(start, 16 * size) for start, size in zip(starts, sizes)]


def gather_plan(shards):
    plan = []
    for number, (shape, pieces) in enumerate(shards):
        if len(shape) == 2:
            plan.append((number, None, None, part_rows(shape[0], len(plan))))
            continue
        step = shape[0] // pieces
        for piece in range(pieces):
            if step % 3 == 0:
                third = step // 3
                parts = [(piece * step + part * third, third) for part in range(3)]
                plan.append((number, "lead", None, parts))
            else:
                plan.append((number, "rows", (piece * step, step), part_rows(shape[1], len(plan))))
    return plan


def gather_all(shards, small, carried):
    arrays = [array for array, _ in shards]
    plan = gather_plan([(array.shape, pieces) for array, pieces in shards])
    frames = lax.axis_size("frame")
    count, extra = len(arrays), len(carried)
    steps = len(plan)
    roles = ((0, 1, 2), (1, 0, 2), (2, 1, 0), (2, 0, 1))

    def kernel(*refs):
        sources, small_ref = refs[:count], refs[count]
        carried_in = refs[count + 1 : count + 1 + extra]
        base = count + 1 + extra
        targets, small_out = refs[base : base + count], refs[base + count]
        near_out = refs[base + count + 1 : base + count + 1 + extra]
        half_out = refs[base + count + 1 + extra : base + count + 1 + 2 * extra]
        send, recv, small_send, small_recv, near_send, near_recv, own_sem, half_sem = refs[
            base + count + 1 + 2 * extra :
        ]
        frame, row = lax.axis_index("frame"), lax.axis_index("rows")
        frame_bit, core_bit = frame // 2, frame % 2
        across = (1 - frame_bit) * 2 + core_bit
        beside = frame_bit * 2 + 1 - core_bit
        corner = (1 - frame_bit) * 2 + 1 - core_bit
        x_bit, z_bit = row % 2, row // 2 % 2
        over_x = row + 1 - 2 * x_bit
        over_z = row + 2 - 4 * z_bit
        over = {
            "y": (across, row),
            "core": (beside, row),
            "corner": (corner, row),
            "x": (frame, over_x),
            "z": (frame, over_z),
        }
        barrier = pltpu.get_barrier_semaphore()
        for place in over.values():
            pl.semaphore_signal(barrier, inc=1, device_id=place, device_id_type=MESH)
        pl.semaphore_wait(barrier, len(over))

        def view(ref, step, part, shard):
            number, kind, leads, parts = plan[step]
            rows = arrays[number].shape[-2]
            begin = 0 if shard is None else pl.multiple_of(shard * rows, 16)
            if kind == "lead":
                first, size = parts[0][0], sum(length for _, length in parts)
                if part is not None:
                    first, size = parts[part]
                where = pl.ds(first, size)
                return ref.at[where] if shard is None else ref.at[where, pl.ds(begin, rows)]
            start, size = (0, rows) if part is None else parts[part]
            where = pl.ds(begin + start, size)
            if kind is None:
                return ref.at[where]
            return ref.at[pl.ds(*leads), where]

        def move(step, part, shard, source, target, way, slot):
            number = plan[step][0]
            return pltpu.make_async_remote_copy(
                src_ref=source,
                dst_ref=view(targets[number], step, part, shard),
                send_sem=send.at[step, slot],
                recv_sem=recv.at[step, slot],
                device_id=over[way],
                device_id_type=MESH,
            )

        own = [
            pltpu.make_async_copy(
                view(sources[plan[step][0]], step, None, None),
                view(targets[plan[step][0]], step, None, frame),
                own_sem.at[step],
            )
            for step in range(steps)
        ]
        smalls = [
            pltpu.make_async_remote_copy(
                src_ref=small_ref,
                dst_ref=small_out.at[frame],
                send_sem=small_send.at[slot],
                recv_sem=small_recv.at[slot],
                device_id=over[way],
                device_id_type=MESH,
            )
            for slot, way in enumerate(("y", "core", "corner"))
        ]
        small_own = pltpu.make_async_copy(small_ref, small_out.at[frame], half_sem.at[extra])
        nears = [
            pltpu.make_async_remote_copy(
                src_ref=carried_in[number],
                dst_ref=near_out[number],
                send_sem=near_send.at[number],
                recv_sem=near_recv.at[number],
                device_id=over["core"],
                device_id_type=MESH,
            )
            for number in range(extra)
        ]
        halves = []
        for number, array in enumerate(carried):
            half = array.shape[-2] // 2
            where = pl.ds(pl.multiple_of(x_bit * half, 16), half)
            source = carried_in[number]
            source = source.at[where] if array.ndim == 2 else source.at[:, where]
            halves.append(pltpu.make_async_copy(source, half_out[number], half_sem.at[number]))

        def run(role):
            part_y, part_x, part_z = roles[role]
            forward = role >= 2

            def first(step):
                number = plan[step][0]
                return [
                    move(step, part_y, frame, view(sources[number], step, part_y, None), None, "y", 0),
                    move(step, None, frame, view(sources[number], step, None, None), None, "core", 3),
                ]

            def passed(step, part, way, slot):
                number = plan[step][0]
                return move(
                    step, part, across, view(targets[number], step, part, across), None, way, slot
                )

            started = [first(step) for step in range(steps)]
            for step in range(steps):
                started[step][0].start()
            for copy in smalls:
                copy.start()
            small_own.start()
            for step in range(steps):
                started[step][1].start()
                own[step].start()
            for copy in nears + halves:
                copy.start()
            later = []
            for turn in range(steps + 2):
                if turn < steps:
                    started[turn][0].wait_recv()
                    sends = [passed(turn, part_y, "z", 2), passed(turn, part_y, "core", 4)]
                    if not forward:
                        sends.insert(1, passed(turn, part_y, "x", 1))
                    for copy in sends:
                        copy.start()
                    later.append(sends)
                if 1 <= turn <= steps:
                    step = turn - 1
                    arrival = passed(step, part_z, "z", 2)
                    arrival.wait_recv()
                    sends = [passed(step, part_z, "core", 6)]
                    if forward:
                        sends.insert(0, passed(step, part_z, "x", 1))
                    for copy in sends:
                        copy.start()
                    later.append(sends)
                if turn >= 2:
                    step = turn - 2
                    arrival = passed(step, part_x, "x", 1)
                    arrival.wait_recv()
                    sends = [passed(step, part_x, "core", 5)]
                    for copy in sends:
                        copy.start()
                    later.append(sends)
            for step in range(steps):
                for copy in started[step]:
                    copy.wait_send()
                move(step, None, frame, view(sources[plan[step][0]], step, None, None), None, "core", 3).wait_recv()
                for part, slot in ((part_y, 4), (part_x, 5), (part_z, 6)):
                    passed(step, part, "core", slot).wait_recv()
                own[step].wait()
            for sends in later:
                for copy in sends:
                    copy.wait_send()
            for copy in smalls + nears:
                copy.wait()
            for copy in halves + [small_own]:
                copy.wait()

        for role in range(4):
            pl.when((z_bit == role // 2) & (x_bit == role % 2))(functools.partial(run, role))

    anywhere = pl.BlockSpec(memory_space=pl.ANY)
    outs = [
        b16(*array.shape[:-2], array.shape[-2] * frames, array.shape[-1]) for array in arrays
    ]
    outs.append(jax.ShapeDtypeStruct((frames,) + small.shape, small.dtype))
    outs += [b16(*array.shape) for array in carried]
    outs += [b16(*array.shape[:-2], array.shape[-2] // 2, array.shape[-1]) for array in carried]
    dma = pltpu.SemaphoreType.DMA
    results = pl.pallas_call(
        kernel,
        out_shape=outs,
        in_specs=[anywhere] * (count + 1 + extra),
        out_specs=[anywhere] * len(outs),
        scratch_shapes=[
            dma((steps, 7)),
            dma((steps, 7)),
            dma((3,)),
            dma((3,)),
            dma((extra,)),
            dma((extra,)),
            dma((steps,)),
            dma((extra + 1,)),
        ],
        compiler_params=pltpu.CompilerParams(collective_id=0, has_side_effects=True),
        cost_estimate=pl.CostEstimate(
            flops=0, bytes_accessed=200 * 2**20, transcendentals=0
        ),
    )(*arrays, small, *carried)
    return (
        results[:count],
        results[count],
        results[count + 1 : count + 1 + extra],
        results[count + 1 + extra :],
    )


def stack_rows(rows):
    filler = [jnp.zeros_like(rows[0])] * (-len(rows) % 8)
    return jnp.stack(list(rows) + filler)


def on_device(
    latents,
    cotangent,
    timesteps,
    prompt_ids,
    embed_table,
    res_gain,
    res_shift,
    res_conv,
    temb_weight,
    st_gain,
    st_shift,
    st_proj,
    st_attn,
    st_cross_kv,
    st_ff_in,
    st_ff_bias,
    st_ff_out,
    motion_gain,
    motion_shift,
    motion_proj,
    motion_attn,
    motion_ff_in,
    motion_ff_bias,
    motion_ff_out,
):
    frames_here, cell_count, channels = latents.shape
    places = Places(frames_here, channels)
    side = places.side
    cells = side * side
    valid = places.valid.astype(jnp.float32)
    table = group_table(channels)
    count = (places.safe_side * places.safe_side * (channels // GROUPS)).astype(jnp.float32)
    inv_count = jnp.broadcast_to(1.0 / count, (channels,))
    lanes = jnp.arange(128, dtype=jnp.int32)[None, :]
    masks = jnp.where(
        lanes == 0,
        valid[:, None],
        jnp.where(lanes == 1, places.cell_col[:, None] > 0, places.cell_col[:, None] < side - 1),
    ).astype(jnp.float32)
    key_bias = jnp.broadcast_to(((valid - 1.0) * -FAR)[None, :], (8, cells))
    places_row = piece_places()

    own = channels // places.frames
    clip_count, prompt_count = prompt_ids.shape
    own_temb = TEMB // places.frames
    time_low = to_low(jax.nn.silu(time_table(timesteps)))
    time_mine = lax.dynamic_slice_in_dim(time_low, places.frame * own_temb, own_temb, 1)
    time_part = matmul(time_mine, temb_weight)
    small = jnp.concatenate(
        [
            motion_gain.astype(jnp.float32),
            motion_shift.astype(jnp.float32),
            motion_ff_bias.astype(jnp.float32).reshape(-1, own),
            time_part.reshape(-1, own),
        ]
    )
    small_count = small.shape[0]
    small = jnp.pad(small, ((0, -small_count % 8), (0, -own % 128)))
    flat_attn = motion_attn.reshape((-1,) + motion_attn.shape[2:])
    carried = [motion_proj, flat_attn, motion_ff_in, motion_ff_out]
    whole, small_all, near, half = gather_all(
        [
            (res_conv.reshape((-1,) + res_conv.shape[3:]), 2),
            (st_proj, 1),
            (st_attn, 1),
            (st_cross_kv, 1),
            (st_ff_in, 1),
            (st_ff_out, 1),
        ],
        small,
        carried,
    )
    conv_all, sproj_all, sattn_all, cross_all, sffin_all, sffout_all = whole
    mproj_pieces, mattn_pieces, mffin_pieces, mffout_pieces = (
        exchange_pieces(*triple) for triple in zip(carried, near, half)
    )
    small_all = small_all[:, :small_count, :own]

    def gathered_rows(first, last):
        rows = jnp.transpose(small_all[:, first:last], (1, 0, 2))
        return rows.reshape(last - first, channels)

    bias_rows = motion_ff_bias.shape[0] // own
    mgain, mshift = (gathered_rows(0, 4), gathered_rows(4, 13))
    mffbias = small_all[:, 13 : 13 + bias_rows].reshape(-1)
    temb_proj = jnp.sum(small_all[:, 13 + bias_rows :], axis=0).reshape(clip_count, channels)
    time_row = lax.dynamic_index_in_dim(temb_proj, places.clip, 0, keepdims=False)

    field = to_low(places.blocks_to_unit(latents))
    grad_unit = to_low(places.blocks_to_unit(cotangent))
    grad_columns = places.blocks_to_columns(cotangent)

    rgain, rshift = (res_gain.astype(jnp.float32), res_shift.astype(jnp.float32))
    sgain, sshift, sffbias = (
        st_gain.astype(jnp.float32),
        st_shift.astype(jnp.float32),
        st_ff_bias.astype(jnp.float32),
    )
    vocab_rows = embed_table.shape[0]
    local_ids = prompt_ids - lax.axis_index(("frame", "rows")) * vocab_rows
    ids_table = onehot(local_ids.reshape(-1), vocab_rows)
    context = lax.psum(to_low(matmul(ids_table, embed_table)), ("frame", "rows"))
    context = context.reshape(clip_count, prompt_count, -1)
    context_low = lax.dynamic_index_in_dim(context, places.clip, 0, keepdims=False)
    prompt_pad = -(-prompt_count // 128) * 128
    context_low = jnp.pad(context_low, ((0, prompt_pad - prompt_count), (0, 0)))
    prompt_bias = jnp.where(jnp.arange(prompt_pad) < prompt_count, 0.0, FAR)
    prompt_row = jnp.broadcast_to(prompt_bias[None, :], (8, prompt_pad))
    prompt_col = jnp.broadcast_to(prompt_bias[:, None], (prompt_pad, 128))

    def wide(row):
        return jnp.broadcast_to(row[None, :], (8, row.shape[0]))

    vec_one = stack_rows([rgain[0], rshift[0], rshift[2] + time_row, inv_count])
    vec_two = stack_rows([rgain[1], rshift[1], rshift[3], inv_count])
    conv_one = conv_forward(
        places_row, side, field, masks, vec_one, table, conv_all, 0, None
    )
    resid = conv_forward(
        places_row, side, conv_one, masks, vec_two, table, conv_all, 1, [field]
    )
    vec_self = stack_rows(
        [
            sgain[0], sshift[0], sshift[4], sgain[1], sshift[1], sshift[5], sshift[5], inv_count,
        ]
    )
    proj_one, query, key, value, proj_two = self_forward(
        places_row, resid, masks, key_bias, vec_self, table, sproj_all, sattn_all
    )
    vec_cross = stack_rows(
        [
            sgain[2], sshift[2], sshift[6], sgain[3], sshift[3], sshift[7], sshift[8],
            mgain[0], mshift[0], inv_count,
        ]
    )
    cross_query, cross_key, cross_value, proj_three, st_out, motion_low = cross_forward(
        places_row, proj_two, resid, context_low, masks, prompt_row, vec_cross, wide(sffbias),
        table, sproj_all, sattn_all, cross_all, sffin_all, sffout_all,
    )

    moved = to_low(places.unit_to_columns([motion_low, to_low(st_out)]))
    motion_in, st_columns = (moved[:, :channels], moved[:, channels:])
    frame_total = places.frames * frames_here
    position = frame_table(jnp.arange(frame_total, dtype=jnp.int32), channels)
    position = jnp.broadcast_to(
        position[None], (places.share_total, frame_total, channels)
    ).reshape(-1, channels)
    per_group = max(n for n in range(1, 14) if places.share_total % n == 0)
    cell_of = jnp.arange(per_group * frame_total, dtype=jnp.int32) // frame_total
    cell_bias = jnp.where(cell_of[:, None] == cell_of[None, :], 0.0, FAR)
    vec_motion = stack_rows(
        [mshift[4], mgain[1], mshift[1], mshift[5], mgain[2], mshift[2], mshift[6]]
    )
    kept = motion_forward(
        places_row, motion_in, position, cell_bias, vec_motion, mproj_pieces, mattn_pieces
    )
    zeds = kept[:3]
    out_columns, grad_zed, d_proj_out, d_ff_in, d_ff_out, small_ff, wide_ff = motion_ff(
        places_row, zeds[2], st_columns, grad_columns,
        stack_rows([mgain[3], mshift[3], mshift[7], mshift[8]]), wide(mffbias),
        mproj_pieces, mffin_pieces, mffout_pieces,
    )
    output = places.columns_to_blocks(out_columns)
    d_attn = [None, None]
    small_back = [None, None]
    for block in (1, 0):
        results = motion_back(
            places_row, block, grad_zed, zeds[block], *kept[3 + 4 * block : 7 + 4 * block],
            motion_in if block == 0 else None, position, cell_bias,
            stack_rows([mgain[1 + block], mshift[1 + block]]), mproj_pieces, mattn_pieces,
        )
        grad_zed, d_attn[block], small_back[block] = (results[0], results[1:5], results[5])
    grad_motion, d_proj_in = (grad_zed, results[6])

    def share_rows(gradients):
        joined = jnp.concatenate(
            [d.reshape(places.frames, -1, channels) for d in gradients], axis=1
        )
        mine = lax.psum_scatter(joined, "frame", scatter_dimension=0, tiled=False)
        mine = lax.psum(mine, "rows").astype(jnp.float32)
        shares = []
        start = 0
        for d in gradients:
            size = d.size // places.frames // channels
            shares.append(mine[start : start + size].reshape(-1, d.shape[1]))
            start = start + size
        return shares

    ff_in_grad, ff_out_grad, share_out = share_rows([d_ff_in, d_ff_out, d_proj_out])
    shares = share_rows([*d_attn[0], *d_attn[1], d_proj_in])
    attn_grad = jnp.stack(shares[:8]).reshape(motion_attn.shape)
    proj_grad = jnp.stack([shares[8], share_out])

    grad_gn = to_low(places.columns_to_unit(grad_motion))
    grad_two, grad_st, small_gn = cross_backward(
        places_row, grad_gn, grad_unit, st_out, proj_three, proj_two, cross_query, cross_key,
        cross_value, masks, prompt_col, vec_cross, wide(sffbias), table, sproj_all, sattn_all,
        sffin_all, sffout_all,
    )
    grad_res = self_backward(
        places_row, grad_two, proj_one, query, key, value, resid, grad_st, masks, vec_self, table,
        sproj_all, sattn_all,
    )
    grad_conv = conv_backward(
        places_row, side, grad_res, conv_one, masks, vec_two, table, conv_all, 1, []
    )
    grad_field = conv_backward(
        places_row, side, grad_conv, field, masks, vec_one, table, conv_all, 0, [grad_res]
    )
    input_grad = places.unit_to_blocks(to_low(grad_field)).astype(jnp.float32)

    gain_rows = [small_gn[0], small_back[0][1], small_back[1][1], small_ff[2]]
    shift_rows = [
        small_gn[1], small_back[0][2], small_back[1][2], small_ff[3], small_back[0][3],
        small_back[0][0], small_back[1][0], small_ff[1], small_ff[0],
    ]
    small_grads = jnp.concatenate(
        [
            jnp.stack(gain_rows + shift_rows).reshape(13, places.frames, own),
            jnp.transpose(wide_ff[0].reshape(places.frames, -1, own), (1, 0, 2)),
        ]
    )
    small_grads = lax.psum(small_grads, ("frame", "rows"))
    small_mine = lax.dynamic_index_in_dim(small_grads, places.frame, 1, keepdims=False)
    gain_grad, shift_grad = (small_mine[:4], small_mine[4:13])
    ff_bias_grad = small_mine[13:].reshape(-1)
    return (
        output,
        input_grad,
        gain_grad,
        shift_grad,
        proj_grad,
        attn_grad,
        ff_in_grad,
        ff_bias_grad,
        ff_out_grad,
    )


def solution(mesh):
    return jax.shard_map(
        on_device,
        mesh=mesh,
        in_specs=(
            P("frame", "rows", None),
            P("frame", "rows", None),
            P(),
            P(),
            P(("frame", "rows"), None),
            P(),
            P(),
            P(None, None, None, "frame", None),
            P("frame", None),
            P(),
            P(),
            P(None, "frame", None),
            P(None, "frame", None),
            P(None, "frame", None),
            P("frame", None),
            P(),
            P("frame", None),
            P(None, "frame"),
            P(None, "frame"),
            P(None, "frame", None),
            P(None, None, "frame", None),
            P("frame", None),
            P("frame"),
            P("frame", None),
        ),
        out_specs=(
            P("frame", "rows", None),
            P("frame", "rows", None),
            P(None, "frame"),
            P(None, "frame"),
            P(None, "frame", None),
            P(None, None, "frame", None),
            P("frame", None),
            P("frame"),
            P("frame", None),
        ),
        check_vma=False,
    )
```

time: 1230 us -> 954 us (0.78)
  Pallas kernels: 0 us -> 534 us
  matrix products: 299 us -> 17.1 us
  blocking collectives: 319 us -> 42 us
  waiting for transfers between devices: 290 us -> 172 us
  local copies, waits for them, and re-layouts: 196 us -> 92.4 us
  other arithmetic: 56.3 us -> 23.7 us
    pallas_call x0 -> x13, Pallas kernels: none -> 534 us  [the longest x1 312 us: gather_all(): pl.pallas_call(kernel, out_shape=outs, in_specs=[anywhere] * (count + 1 +...]
    all_gather x20 -> x0, blocking collectives: 244 us -> none  [gather_rows(): gathered = lax.all_gather(shard, 'frame', axis=0, tiled=False)]
    dot_general x77 -> x0, matrix products: 154 us -> none  [the longest x39 91.2 us: matmul_back(): lax.dot_general(gradient, weight, (((1,), (1,)), ((), ())), preferred_ele...]
    dot_general x31 -> x6, matrix products: 102 us -> 10.3 us  [matmul(): return jnp.dot(left, weight, preferred_element_type=jnp.float32)]
    reduce_scatter x12 -> x2, waiting for transfers between devices: 115 us -> 37.1 us  [share_rows(): mine = lax.psum_scatter(joined, 'frame', scatter_dimension=0, tiled=False)]
    psum x1, waiting for transfers between devices: 69.5 us -> 0.02 us  [on_device(): lax.psum(to_low(matmul(ids_table, embed_table)), ('frame', 'rows'))]
    ppermute x0 -> x16, waiting for transfers between devices: none -> 57.1 us  [swap(): return lax.ppermute(value, axis, [(i, i ^ bit) for i in range(count)])]
    psum x1, waiting for transfers between devices: 83.5 us -> 38.2 us  [share_rows(): mine = lax.psum(mine, 'rows').astype(jnp.float32)]
  transfers between devices with their start and end apart: 27 -> 27, of which waited for: 8 -> 8; matrix products, arithmetic and copies ran while one was open for 36% -> 10% of each run, Pallas kernels for 0% -> 50%
where the time goes in v2:
time: 954 us; the launch traced here: 946 us
  Pallas kernels  534 us (56%)
  waiting for transfers between devices  172 us (18%)
  local copies, waits for them, and re-layouts  92.4 us (10%)
  starting transfers between devices  43.8 us (5%)
  blocking collectives  42 us (4%)
  other arithmetic  23.7 us (2%)
  between operations  20.1 us (2%)
  matrix products  17.1 us (2%)
    pallas_call x1, Pallas kernels, gather_all(): pl.pallas_call(kernel, out_shape=outs, in_specs=[anywhere] * (count + 1 +...  312 us
    pallas_call x12, Pallas kernels, run_kernel(): pl.pallas_call(kernel, out_shape=outs, in_specs=[pl.BlockSpec(memory_spac...  223 us
    ppermute x16, waiting for transfers between devices, swap(): return lax.ppermute(value, axis, [(i, i ^ bit) for i in range(count)])  57.1 us
    psum x1, blocking collectives, on_device(): small_grads = lax.psum(small_grads, ('frame', 'rows'))  42 us
    psum x1, waiting for transfers between devices, share_rows(): mine = lax.psum(mine, 'rows').astype(jnp.float32)  38.2 us
    reduce_scatter x2, waiting for transfers between devices, share_rows(): mine = lax.psum_scatter(joined, 'frame', scatter_dimension=0, tiled=False)  37.1 us
    unnamed x125, local copies, waits for them, and re-layouts  28.5 us
    all_to_all x1, waiting for transfers between devices, columns_to_unit(): received = lax.all_to_all(send, ('frame', 'rows'), 0, 0)  22.3 us
  transfers between devices with their start and end apart: 27, of which 8 were waited for; matrix products, arithmetic and copies ran while one was open for 10% of the time, Pallas kernels for 50%

profile of v2, /device:TPU:0, one launch (start us, length us, event | category | flops | bytes accessed | tf_op | source)
XLA Modules:
  0.0 945.9 jit_solution(9011745731622989284)
XLA Ops:
  8.2 1.5 slice_dynamic-update-slice_fusion.7
  10.4 1.5 slice_dynamic-update-slice_fusion.6
  12.6 1.5 slice_dynamic-update-slice_fusion.5
  14.8 1.6 slice_dynamic-update-slice_fusion.4
  17.0 7.3 all-to-all-start
  24.4 1.4 convolution_convert_fusion.3
  25.8 1.7 reshape.498
  28.8 311.7 %shard_map.313 = (bf16[18,640,640]{2,1,0:T(8,128)(2,1)}, bf16[2,640,640]{2,1,0:T(8,128)(2,1)}, bf16[6,640,640]{2,1,0:T(8,128)(2,1)}, bf16[2,768,640]{2,1,0:T(8,1...) custom-call(bf16[18,160,640]{2,1,0:T(8,128)(2,1)} %bitcast.169, ...), custom_call_target="tpu_custom_call" | custom-call | bytes 209715200 | tf_op jit(solution)/shard_map/pallas_call | solution.py:1213
  351.4 1.3 compare_convert_fusion.refs_4_.refs_5_.refs_8_.refs_13_.refs_10_
  362.6 4.0 all-to-all-start.2
  366.6 2.9 fusion.8.refs_1_.refs_5_.refs_2_
  369.4 12.4 %shard_map.314.refs_1_.refs_2_ = f32[576,640]{1,0:T(8,128)} custom-call(s32[6]{0:T(128)} %stack.144.refs_0_, bf16[576,640]{1,0:T(8,128)(2,1)} %fusion.8.refs_1_.refs_5_.refs_2_, f32[576,128]{1,0:T(8,128)} %convert_select_fusion.refs_2_.refs_4_.refs_9_.refs_8_.refs_3_, f32[8,640]{1,0:T(8,128)} %stack.150.refs_3_.refs_4_, ...), custom_call_target="tpu_custom_call" | custom-call | flops 4246732800 | bytes 18911232 | tf_op jit(solution)/shard_map/pallas_call | solution.py:279
  381.8 12.9 %shard_map.315.refs_1_.refs_2_.refs_6_ = f32[576,640]{1,0:T(8,128)} custom-call(s32[6]{0:T(128)} %stack.144.refs_0_, f32[576,640]{1,0:T(8,128)} %shard_map.314.refs_1_.refs_2_, f32[576,128]{1,0:T(8,128)} %convert_select_fusion.refs_2_.refs_4_.refs_9_.refs_8_.refs_3_, f32[8,640]{1,0:T(8,128)} %stack.151.refs_3_.refs_4_, ...), custom_call_target="tpu_custom_call" | custom-call | flops 4246732800 | bytes 20385792 | tf_op jit(solution)/shard_map/pallas_call | solution.py:279
  395.4 14.7 %shard_map.316 = (f32[576,640]{1,0:T(8,128)}, bf16[576,640]{1,0:T(8,128)(2,1)}, bf16[576,640]{1,0:T(8,128)(2,1)}, bf16[576,640]{1,0:T(8,128)(2,1)}, f32[576,640]{1,0:T(8,128)}) custom-call(s32[6]{0:T(128)} %stack.144.refs_0_, f32[576,640]{1,0:T(8,128)} %shard_map.315.refs_1_.refs_2_.refs_6_, ...), custom_call_target="tpu_custom_call" | custom-call | flops 3208642560 | bytes 15161344 | tf_op jit(solution)/shard_map/pallas_call | solution.py:279
  411.4 20.0 %shard_map.317 = (bf16[576,640]{1,0:T(8,128)(2,1)}, bf16[128,640]{1,0:T(8,128)(2,1)}, bf16[128,640]{1,0:T(8,128)(2,1)}, f32[576,640]{1,0:T(8,128)}, f32[576,640]{1,0:T(8,128)}, /*index=5*/bf16[576,640]{1,0:T(8,128)(2,1)}) custom-call(s32[6]{0:T(128)} %stack.144.refs_0_, f32[576,640]{1,0:T(8,128)} %get-tuple-element.73.refs_1_.refs_5_, ...), custom_call_target="tpu_custom_call" | custom-call | flops 7077888000 | bytes 28389376 | tf_op jit(solution)/shard_map/pallas_call | solution.py:279
  431.4 1.5 convert_element_type.156
  432.9 2.6 convolution_convert_fusion
  435.5 1.5 reshape.499
  437.0 6.0 all-to-all-start.1
  443.0 1.8 collective-permute-start.4
  445.1 1.8 collective-permute-start.8
  447.1 37.1 %collective-permute-done.4.refs_13_.refs_18_.refs_19_ = bf16[8,80,640]{2,1,0:T(8,128)(2,1)S(1)} collective-permute-done((bf16[8,80,640]{2,1,0:T(8,128)(2,1)}, bf16[8,80,640]{2,1,0:T(8,128)(2,1)S(1)}, u32[]{:S(2)}, u32[]{:S(2)}) %collective-permute-start.4) | collective-permute-done | bytes 819232 | tf_op jit(solution)/shard_map/ppermute | solution.py:210
  486.5 2.1 collective-permute-done.refs_7_.refs_8_.refs_12_.refs_13_
  489.8 17.1 %collective-permute-done.5.refs_14_.refs_19_.refs_20_ = bf16[8,80,640]{2,1,0:T(8,128)(2,1)} collective-permute-done((bf16[8,80,640]{2,1,0:T(8,128)(2,1)S(1)}, bf16[8,80,640]{2,1,0:T(8,128)(2,1)}, u32[]{:S(2)}, u32[]{:S(2)}) %collective-permute-start.5) | collective-permute-done | bytes 819232 | tf_op jit(solution)/shard_map/ppermute | solution.py:210
  506.9 1.4 add.359
  509.6 1.8 collective-permute-start.9
  511.6 1.3 pad_add_fusion
  513.7 1.4 slice.385
  516.4 1.3 slice.381
  517.7 1.3 slice.387
  519.1 1.3 slice.377
  529.0 1.3 stack.154.refs_4_
  530.4 1.4 pad_maximum_fusion.4
  532.7 2.0 reshape.504
  534.7 1.7 reshape.500
  536.6 2.4 convolution_convert_fusion.1
  542.2 16.7 %shard_map.318 = (f32[416,640]{1,0:T(8,128)}, f32[416,640]{1,0:T(8,128)}, f32[416,640]{1,0:T(8,128)}, bf16[416,640]{1,0:T(8,128)(2,1)}, bf16[416,640]{1,0:T(8,12...) custom-call(s32[6]{0:T(128)} %stack.144.refs_0_, ...), custom_call_target="tpu_custom_call" | custom-call | flops 3067084800 | bytes 17437696 | tf_op jit(solution)/shard_map/pallas_call | solution.py:279
  560.2 23.0 %shard_map.319 = (bf16[416,640]{1,0:T(8,128)(2,1)}, f32[416,640]{1,0:T(8,128)}, bf16[640,640]{1,0:T(8,128)(2,1)}, bf16[640,2560]{1,0:T(8,128)(2,1)}, bf16[2560,6...) custom-call(s32[6]{0:T(128)} %stack.144.refs_0_, f32[416,640]{1,0:T(8,128)} %get-tuple-element.83.refs_1_, ...), custom_call_target="tpu_custom_call" | custom-call | flops 8178892800 | bytes 19496960 | tf_op jit(solution)/shard_map/pallas_call | solution.py:279
  583.1 17.1 %shard_map.320 = (f32[416,640]{1,0:T(8,128)}, bf16[640,640]{1,0:T(8,128)(2,1)}, bf16[640,640]{1,0:T(8,128)(2,1)}, bf16[640,640]{1,0:T(8,128)(2,1)}, bf16[640,640]{1,0:T(8,128)(2,1)}, /*index=5*/f32[8,640]{1,0:T(8,128)}) custom-call(s32[6]{0:T(128)} %stack.144.refs_0_, f32[416,640]{1,0:T(8,128)} %get-tuple-element.89.refs_1_, ...), custom_call_target="tpu_custom_call" | custom-call | flops 3067084800 | bytes 18072576 | tf_op jit(solution)/shard_map/pallas_call | solution.py:279
  600.2 19.4 %shard_map.321 = (bf16[416,640]{1,0:T(8,128)(2,1)}, bf16[640,640]{1,0:T(8,128)(2,1)}, bf16[640,640]{1,0:T(8,128)(2,1)}, bf16[640,640]{1,0:T(8,128)(2,1)}, bf16[6...) custom-call(s32[6]{0:T(128)} %stack.144.refs_0_, f32[416,640]{1,0:T(8,128)} %get-tuple-element.95.refs_1_, ...), custom_call_target="tpu_custom_call" | custom-call | flops 3067084800 | bytes 18891776 | tf_op jit(solution)/shard_map/pallas_call | solution.py:279
  619.6 2.3 constant_dynamic-update-slice_fusion.8
  622.0 2.2 constant_dynamic-update-slice_fusion.7
  631.2 5.1 reshape.524
  636.4 6.4 pad_maximum_fusion
  649.0 5.1 all-to-all-start.5
  656.1 17.6 %all-to-all-done.5 = bf16[8,72,640]{2,1,0:T(8,128)(2,1)S(1)} async-done(((bf16[8,72,640]{2,1,0:T(8,128)(2,1)}), bf16[8,72,640]{2,1,0:T(8,128)(2,1)S(1)}, u32[]{:S(2)}, u32[]{:S(2)}) %all-to-all-start.5) | async-done | bytes 737312 | tf_op jit(solution)/shard_map/all_to_all | solution.py:148
  673.8 3.0 all-to-all-start.4
  676.8 1.7 fusion.9.refs_2_
  680.6 22.3 %all-to-all-done.4 = bf16[32,18,640]{2,1,0:T(8,128)(2,1)S(1)} async-done(((bf16[32,18,640]{2,1,0:T(8,128)(2,1)}), bf16[32,18,640]{2,1,0:T(8,128)(2,1)S(1)}, u32[]{:S(2)}, u32[]{:S(2)}) %all-to-all-start.4) | async-done | bytes 737312 | tf_op jit(solution)/shard_map/all_to_all | solution.py:178
  702.9 3.5 all-to-all-start.3
  707.1 1.7 fusion.7.refs_1_
  709.6 29.1 %shard_map.322 = (f32[576,640]{1,0:T(8,128)}, f32[576,640]{1,0:T(8,128)}, f32[8,640]{1,0:T(8,128)}) custom-call(s32[6]{0:T(128)} %stack.144.refs_0_, bf16[576,640]{1,0:T(8,128)(2,1)} %fusion.7.refs_1_, bf16[576,640]{1,0:T(8,128)(2,1)} %fusion.9.refs_2_, f32[576,640]{1,0:T(8,128)} %get-tuple-element.78.refs_3_, f32[576,640]{1,0:T(8,128)} %get-tuple-element.102.refs_4_, ...), custom_call_target="tpu_custom_call" | custom-call | flops 12740198400 | bytes 28520448 | tf_op jit(solution)/shard_map/pallas_call | solution.py:279
  738.7 37.1 %reduce-scatter.5.cloned.1.call-done = bf16[1,1440,640]{2,1,0:T(8,128)(2,1)} async-done(((bf16[4,1440,640]{2,1,0:T(8,128)(2,1)}), bf16[1,1440,640]{2,1,0:T(8,128)(2,1)}) %reduce-scatter.5.cloned.1.call-update) | async-done | bytes 1843216 | tf_op jit(solution)/shard_map/reduce_scatter | solution.py:1425
  775.8 24.8 %shard_map.323.refs_1_.refs_6_ = f32[576,640]{1,0:T(8,128)} custom-call(s32[6]{0:T(128)} %stack.144.refs_0_, f32[576,640]{1,0:T(8,128)} %get-tuple-element.106.refs_1_, f32[576,640]{1,0:T(8,128)} %get-tuple-element.107.refs_2_, bf16[576,640]{1,0:T(8,128)(2,1)} %get-tuple-element.108.refs_3_, bf16[576,640]{1,0:T(8,128)(2,1)} %get-tuple-element.109.refs_4_, ...), custom_call_target="tpu_custom_call" | custom-call | flops 4482662400 | bytes 18092032 | tf_op jit(solution)/shard_map/pallas_call | solution.py:279
  800.6 16.3 %shard_map.324.refs_1_ = f32[576,640]{1,0:T(8,128)} custom-call(s32[6]{0:T(128)} %stack.144.refs_0_, f32[576,640]{1,0:T(8,128)} %shard_map.323.refs_1_.refs_6_, f32[576,640]{1,0:T(8,128)} %shard_map.314.refs_1_.refs_2_, f32[576,128]{1,0:T(8,128)} %convert_select_fusion.refs_2_.refs_4_.refs_9_.refs_8_.refs_3_, f32[8,640]{1,0:T(8,128)} %stack.151.refs_3_.refs_4_, ...), custom_call_target="tpu_custom_call" | custom-call | flops 4246732800 | bytes 21123072 | tf_op jit(solution)/shard_map/pallas_call | solution.py:279
  816.9 16.3 %shard_map.325 = f32[576,640]{1,0:T(8,128)} custom-call(s32[6]{0:T(128)} %stack.144.refs_0_, f32[576,640]{1,0:T(8,128)} %shard_map.324.refs_1_, bf16[576,640]{1,0:T(8,128)(2,1)} %fusion.8.refs_1_.refs_5_.refs_2_, f32[576,128]{1,0:T(8,128)} %convert_select_fusion.refs_2_.refs_4_.refs_9_.refs_8_.refs_3_, f32[8,640]{1,0:T(8,128)} %stack.150.refs_3_.refs_4_, ...), custom_call_target="tpu_custom_call" | custom-call | flops 4246732800 | bytes 21860352 | tf_op jit(solution)/shard_map/pallas_call | solution.py:279
  833.2 3.3 fusion.10
  836.5 5.9 all-to-all-start.6
  846.0 42.0 %psum.29 = f32[17,4,160]{2,0,1:T(8,128)S(1)} all-reduce(f32[17,4,160]{2,0,1:T(8,128)S(1)} %pad_maximum_fusion.3), channel_id=1, replica_groups=mesh['frame'=4,'rows'=8] {'frame','rows'}, use_global_device_ids=true, to_apply=%region_2.3 | all-reduce | flops 10880 | bytes 87040 | tf_op jit(solution)/shard_map/psum | solution.py:1469
  891.1 38.2 %all-reduce.16.cloned.1.call-done = (bf16[1440,640]{1,0:T(8,128)(2,1)}, bf16[1440,640]{1,0:T(8,128)(2,1)}) async-done(((bf16[1440,640]{1,0:T(8,128)(2,1)}, bf16[1440,640]{1,0:T(8,128)(2,1)}), (bf16[1440,640]{1,0:T(8,128)(2,1)}, bf16[1440,640]{1,0:T(8,128)(2,1)})) %all-reduce.16.cloned.1.call-update) | async-done | bytes 3686416 | tf_op jit(solution)/shard_map/psum | solution.py:1426
  929.3 1.9 convert_element_type.167
  931.6 2.0 fusion.82
  933.9 1.7 copy-done.18
  935.5 2.7 reshape.528
  (278 shorter events, 70.8 us)
Async XLA Ops:
  7.2 17.2 %copy-start = (bf16[1544,768]{1,0:T(8,128)(2,1)S(1)}, bf16[1544,768]{1,0:T(8,128)(2,1)}, u32[]{:S(2)}) copy-start(bf16[1544,768]{1,0:T(8,128)(2,1)} %param.30) | copy-start | bytes 7114756
  7.2 17.1 %copy-start.38 = (s32[2,77]{1,0:T(2,128)S(1)}, s32[2,77]{1,0:T(2,128)}, u32[]{:S(2)}) copy-start(s32[2,77]{1,0:T(2,128)} %param.29) | copy-start | bytes 1852
  11.9 15.6 %copy-start.44 = (s32[2]{0:T(128)S(1)}, s32[2]{0:T(128)}, u32[]{:S(2)}) copy-start(s32[2]{0:T(128)} %param.28) | copy-start | bytes 28
  11.9 15.8 %copy-start.16 = (bf16[320,640]{1,0:T(8,128)(2,1)S(1)}, bf16[320,640]{1,0:T(8,128)(2,1)}, u32[]{:S(2)}) copy-start(bf16[320,640]{1,0:T(8,128)(2,1)} %param.34) | copy-start | bytes 1228804
  14.8 13.3 %copy-start.26 = (bf16[9,160]{1,0:T(8,128)(2,1)S(1)}, bf16[9,160]{1,0:T(8,128)(2,1)}, u32[]{:S(2)}) copy-start(bf16[9,160]{1,0:T(8,128)(2,1)} %param.44) | copy-start | bytes 8644
  14.8 13.3 %copy-start.35 = (bf16[4,160]{1,0:T(4,128)(2,1)S(1)}, bf16[4,160]{1,0:T(4,128)(2,1)}, u32[]{:S(2)}) copy-start(bf16[4,160]{1,0:T(4,128)(2,1)} %param.43) | copy-start | bytes 3844
  14.8 13.3 %copy-start.36 = (bf16[640]{0:T(1024)(128)(2,1)S(1)}, bf16[640]{0:T(1024)(128)(2,1)}, u32[]{:S(2)}) copy-start(bf16[640]{0:T(1024)(128)(2,1)} %param.48) | copy-start | bytes 3844
  17.0 344.7 %all-to-all-start = ((bf16[8,72,640]{2,1,0:T(8,128)(2,1)}), bf16[8,72,640]{2,1,0:T(8,128)(2,1)S(1)}, u32[]{:S(2)}, u32[]{:S(2)}) async-start(bf16[8,72,640]{2,1,0:T(8,128)(2,1)} %bitcast_dynamic-update-slice_fusion.4), calls=%async_computation | async-start | bytes 1474560 | tf_op jit(solution)/shard_map/all_to_all | solution.py:148
  24.3 335.8 %all-reduce.14.cloned.1.call-start = ((), (), s32[]{:S(2)}) async-start(), calls=%async_computation.9 | async-start | bytes 491520 | tf_op jit(solution)/shard_map/psum | solution.py:1348
  28.8 314.4 %copy-start.46 = (s32[2]{0:T(128)S(1)}, s32[2]{0:T(128)}, u32[]{:S(2)}) copy-start(s32[2]{0:T(128)} %constant.218.clone) | copy-start | bytes 28
  28.8 319.8 %copy-start.21 = (bf16[4,640]{1,0:T(4,128)(2,1)S(1)}, bf16[4,640]{1,0:T(4,128)(2,1)}, u32[]{:S(2)}) copy-start(bf16[4,640]{1,0:T(4,128)(2,1)} %param.32) | copy-start | bytes 15364
  28.8 319.8 %slice-start = ((bf16[4,104,640]{2,1,0:T(8,128)(2,1)}), bf16[4,72,640]{2,1,0:T(8,128)(2,1)S(1)}, s32[]{:S(2)}) async-start(bf16[4,104,640]{2,1,0:T(8,128)(2,1)} %param.27), calls=%async_computation.13 | async-start | bytes 737280 | tf_op jit(solution)/shard_map/slice | solution.py:185
  28.8 320.0 %slice-start.1 = ((bf16[4,104,640]{2,1,0:T(8,128)(2,1)}), bf16[4,32,640]{2,1,0:T(8,128)(2,1)S(1)}, s32[]{:S(2)}) async-start(bf16[4,104,640]{2,1,0:T(8,128)(2,1)} %param.27), calls=%async_computation.14 | async-start | bytes 327680 | tf_op jit(solution)/shard_map/slice | solution.py:185
  340.6 9.7 %copy-start.24 = (bf16[2,640]{1,0:T(2,128)(2,1)S(1)}, bf16[2,640]{1,0:T(2,128)(2,1)}, u32[]{:S(2)}) copy-start(bf16[2,640]{1,0:T(2,128)(2,1)} %param.31) | copy-start | bytes 7684
  340.6 9.8 %copy-start.22 = (bf16[9,640]{1,0:T(8,128)(2,1)S(1)}, bf16[9,640]{1,0:T(8,128)(2,1)}, u32[]{:S(2)}) copy-start(bf16[9,640]{1,0:T(8,128)(2,1)} %param.36) | copy-start | bytes 34564
  340.6 9.8 %copy-start.23 = (bf16[4,640]{1,0:T(4,128)(2,1)S(1)}, bf16[4,640]{1,0:T(4,128)(2,1)}, u32[]{:S(2)}) copy-start(bf16[4,640]{1,0:T(4,128)(2,1)} %param.35) | copy-start | bytes 15364
  340.6 12.2 %copy-start.45 = (s32[2]{0:T(128)S(1)}, s32[2]{0:T(128)}, u32[]{:S(2)}) copy-start(s32[2]{0:T(128)} %constant.219.clone) | copy-start | bytes 28
  350.3 19.1 %copy-start.29 = (s32[576]{0:T(1024)}, s32[576]{0:T(1024)S(1)}, u32[]{:S(2)}) copy-start(s32[576]{0:T(1024)S(1)} %add_select_fusion.9) | copy-start | bytes 6916
  352.8 58.1 %copy-start.33 = (f32[128]{0:T(128)}, f32[128]{0:T(128)S(1)}, u32[]{:S(2)}) copy-start(f32[128]{0:T(128)S(1)} %compare_select_fusion.1) | copy-start | bytes 1540
  360.0 72.8 %copy-start.31 = (s32[576]{0:T(1024)}, s32[576]{0:T(1024)S(1)}, u32[]{:S(2)}) copy-start(s32[576]{0:T(1024)S(1)} %fusion.41) | copy-start | bytes 6916
  362.6 74.4 %all-to-all-start.2 = ((bf16[4,4,26,640]{3,1,2,0:T(4,128)(2,1)}), bf16[4,4,26,640]{3,1,2,0:T(4,128)(2,1)S(1)}, u32[]{:S(2)}, u32[]{:S(2)}) async-start(bf16[4,4,26,640]{3,1,2,0:T(4,128)(2,1)} %maximum_bitcast_fusion), calls=%async_computation.2 | async-start | bytes 1064960 | tf_op jit(solution)/shard_map/all_to_all | solution.py:189
  395.4 14.8 %copy-start.25 = (bf16[5120]{0:T(1024)(128)(2,1)S(1)}, bf16[5120]{0:T(1024)(128)(2,1)}, u32[]{:S(2)}) copy-start(bf16[5120]{0:T(1024)(128)(2,1)} %param.41) | copy-start | bytes 30724
  437.0 97.7 %all-to-all-start.1 = ((bf16[32,18,1280]{2,1,0:T(8,128)(2,1)}), bf16[32,18,1280]{2,1,0:T(8,128)(2,1)S(1)}, u32[]{:S(2)}, u32[]{:S(2)}) async-start(bf16[32,18,1280]{2,1,0:T(8,128)(2,1)} %reshape.499), calls=%async_computation.1 | async-start | bytes 3932160 | tf_op jit(solution)/shard_map/all_to_all | solution.py:172
  443.0 295.7 %reduce-scatter.3.cloned.1.call-start = ((), (), s32[]{:S(2)}) async-start(), calls=%async_computation.10 | async-start | bytes 9216000 | tf_op jit(solution)/shard_map/reduce_scatter | solution.py:1425
  443.0 41.2 %collective-permute-start.4 = (bf16[8,80,640]{2,1,0:T(8,128)(2,1)}, bf16[8,80,640]{2,1,0:T(8,128)(2,1)S(1)}, u32[]{:S(2)}, u32[]{:S(2)}) collective-permute-start(bf16[8,80,640]{2,1,0:T(8,128)(2,1)} %get-tuple-element.82), channel_id=1, source_target_pairs={{0,16},{8,24},{16,0},{24,8},{1,17},{9,25},{17,1},{25,9},{2,18},{10... | collective-permute-start | bytes 2457608 | tf_op jit(solution)/shard_map/ppermute | solution.py:210
  444.8 43.8 %collective-permute-start = (bf16[2,80,640]{2,1,0:T(8,128)(2,1)}, bf16[2,80,640]{2,1,0:T(8,128)(2,1)S(1)}, u32[]{:S(2)}, u32[]{:S(2)}) collective-permute-start(bf16[2,80,640]{2,1,0:T(8,128)(2,1)} %get-tuple-element.80), channel_id=1, source_target_pairs={{0,16},{8,24},{16,0},{24,8},{1,17},{9,25},{17,1},{25,9},{2,18},{10... | collective-permute-start | bytes 614408 | tf_op jit(solution)/shard_map/ppermute | solution.py:210
  445.1 64.5 %collective-permute-start.8 = (bf16[80,2560]{1,0:T(8,128)(2,1)}, bf16[80,2560]{1,0:T(8,128)(2,1)}, u32[]{:S(2)}, u32[]{:S(2)}) collective-permute-start(bf16[80,2560]{1,0:T(8,128)(2,1)} %get-tuple-element.85), channel_id=1, source_target_pairs={{0,16},{8,24},{16,0},{24,8},{1,17},{9,25},{17,1},{25,9},{2,18},{10... | collective-permute-start | bytes 1228808 | tf_op jit(solution)/shard_map/ppermute | solution.py:210
  446.9 64.5 %collective-permute-start.12 = (bf16[320,640]{1,0:T(8,128)(2,1)}, bf16[320,640]{1,0:T(8,128)(2,1)}, u32[]{:S(2)}, u32[]{:S(2)}) collective-permute-start(bf16[320,640]{1,0:T(8,128)(2,1)} %get-tuple-element.87), channel_id=1, source_target_pairs={{0,16},{8,24},{16,0},{24,8},{1,17},{9,25},{17,1},{25,9},{2,18},{10... | collective-permute-start | bytes 1228808 | tf_op jit(solution)/shard_map/ppermute | solution.py:210
  484.2 52.2 %copy-start.3 = (bf16[8,80,640]{2,1,0:T(8,128)(2,1)}, bf16[8,80,640]{2,1,0:T(8,128)(2,1)S(1)}, u32[]{:S(2)}) copy-start(bf16[8,80,640]{2,1,0:T(8,128)(2,1)S(1)} %collective-permute-done.4.refs_13_.refs_18_.refs_19_) | copy-start | bytes 2457604
  484.2 22.6 %collective-permute-start.5 = (bf16[8,80,640]{2,1,0:T(8,128)(2,1)S(1)}, bf16[8,80,640]{2,1,0:T(8,128)(2,1)}, u32[]{:S(2)}, u32[]{:S(2)}) collective-permute-start(bf16[8,80,640]{2,1,0:T(8,128)(2,1)S(1)} %collective-permute-done.4.refs_13_.refs_18_.refs_19_), channel_id=1, source_target_pairs={{0,1},{1,0},{2,3},{3,2},{4,5},{5,4},{6,7},{7,6},{8,9},{9,8},{10,11... | collective-permute-start | bytes 2457608 | tf_op jit(solution)/shard_map/ppermute | solution.py:210
  485.9 54.1 %collective-permute-start.6 = (bf16[8,80,640]{2,1,0:T(8,128)(2,1)S(1)}, bf16[8,80,640]{2,1,0:T(8,128)(2,1)}, u32[]{:S(2)}, u32[]{:S(2)}) collective-permute-start(bf16[8,80,640]{2,1,0:T(8,128)(2,1)S(1)} %collective-permute-done.4.refs_13_.refs_18_.refs_19_), channel_id=1, source_target_pairs={{0,8},{8,0},{16,24},{24,16},{1,9},{9,1},{17,25},{25,17},{2,10},{10... | collective-permute-start | bytes 2457608 | tf_op jit(solution)/shard_map/ppermute | solution.py:210
  488.6 50.3 %copy-start.12 = (bf16[2,80,640]{2,1,0:T(8,128)(2,1)}, bf16[2,80,640]{2,1,0:T(8,128)(2,1)S(1)}, u32[]{:S(2)}) copy-start(bf16[2,80,640]{2,1,0:T(8,128)(2,1)S(1)} %collective-permute-done.refs_7_.refs_8_.refs_12_.refs_13_) | copy-start | bytes 614404
  488.6 20.9 %collective-permute-start.1 = (bf16[2,80,640]{2,1,0:T(8,128)(2,1)S(1)}, bf16[2,80,640]{2,1,0:T(8,128)(2,1)}, u32[]{:S(2)}, u32[]{:S(2)}) collective-permute-start(bf16[2,80,640]{2,1,0:T(8,128)(2,1)S(1)} %collective-permute-done.refs_7_.refs_8_.refs_12_.refs_13_), channel_id=1, source_target_pairs={{0,1},{1,0},{2,3},{3,2},{4,5},{5,4},{6,7},{7,6},{8,9},{9,8},{10,11... | collective-permute-start | bytes 614408 | tf_op jit(solution)/shard_map/ppermute | solution.py:210
  506.8 34.3 %collective-permute-start.7 = (bf16[8,80,640]{2,1,0:T(8,128)(2,1)}, bf16[8,80,640]{2,1,0:T(8,128)(2,1)}, u32[]{:S(2)}, u32[]{:S(2)}) collective-permute-start(bf16[8,80,640]{2,1,0:T(8,128)(2,1)} %collective-permute-done.5.refs_14_.refs_19_.refs_20_), channel_id=1, source_target_pairs={{0,8},{8,0},{16,24},{24,16},{1,9},{9,1},{17,25},{25,17},{2,10},{10... | collective-permute-start | bytes 2457608 | tf_op jit(solution)/shard_map/ppermute | solution.py:210
  509.6 26.9 %collective-permute-start.2 = (bf16[2,80,640]{2,1,0:T(8,128)(2,1)S(1)}, bf16[2,80,640]{2,1,0:T(8,128)(2,1)}, u32[]{:S(2)}, u32[]{:S(2)}) collective-permute-start(bf16[2,80,640]{2,1,0:T(8,128)(2,1)S(1)} %collective-permute-done.refs_7_.refs_8_.refs_12_.refs_13_), channel_id=1, source_target_pairs={{0,8},{8,0},{16,24},{24,16},{1,9},{9,1},{17,25},{25,17},{2,10},{10... | collective-permute-start | bytes 614408 | tf_op jit(solution)/shard_map/ppermute | solution.py:210
  509.6 30.0 %collective-permute-start.9 = (bf16[80,2560]{1,0:T(8,128)(2,1)}, bf16[80,2560]{1,0:T(8,128)(2,1)}, u32[]{:S(2)}, u32[]{:S(2)}) collective-permute-start(bf16[80,2560]{1,0:T(8,128)(2,1)} %collective-permute-done.8.refs_14_), channel_id=1, source_target_pairs={{0,1},{1,0},{2,3},{3,2},{4,5},{5,4},{6,7},{7,6},{8,9},{9,8},{10,11... | collective-permute-start | bytes 1228808 | tf_op jit(solution)/shard_map/ppermute | solution.py:210
  511.4 28.3 %collective-permute-start.13 = (bf16[320,640]{1,0:T(8,128)(2,1)}, bf16[320,640]{1,0:T(8,128)(2,1)}, u32[]{:S(2)}, u32[]{:S(2)}) collective-permute-start(bf16[320,640]{1,0:T(8,128)(2,1)} %collective-permute-done.12.refs_20_), channel_id=1, source_target_pairs={{0,1},{1,0},{2,3},{3,2},{4,5},{5,4},{6,7},{7,6},{8,9},{9,8},{10,11... | collective-permute-start | bytes 1228808 | tf_op jit(solution)/shard_map/ppermute | solution.py:210
  527.7 8.9 copy-start.37
  536.4 4.8 copy-start.17
  536.4 2.6 collective-permute-start.3
  539.0 19.9 %collective-permute-start.10 = (bf16[80,2560]{1,0:T(8,128)(2,1)}, bf16[80,2560]{1,0:T(8,128)(2,1)S(1)}, u32[]{:S(2)}, u32[]{:S(2)}) collective-permute-start(bf16[80,2560]{1,0:T(8,128)(2,1)} %collective-permute-done.8.refs_14_), channel_id=1, source_target_pairs={{0,8},{8,0},{16,24},{24,16},{1,9},{9,1},{17,25},{25,17},{2,10},{10... | collective-permute-start | bytes 1228808 | tf_op jit(solution)/shard_map/ppermute | solution.py:210
  539.5 19.4 %collective-permute-start.14 = (bf16[320,640]{1,0:T(8,128)(2,1)}, bf16[320,640]{1,0:T(8,128)(2,1)S(1)}, u32[]{:S(2)}, u32[]{:S(2)}) collective-permute-start(bf16[320,640]{1,0:T(8,128)(2,1)} %collective-permute-done.12.refs_20_), channel_id=1, source_target_pairs={{0,8},{8,0},{16,24},{24,16},{1,9},{9,1},{17,25},{25,17},{2,10},{10... | collective-permute-start | bytes 1228808 | tf_op jit(solution)/shard_map/ppermute | solution.py:210
  539.6 19.3 %collective-permute-start.11 = (bf16[80,2560]{1,0:T(8,128)(2,1)}, bf16[80,2560]{1,0:T(8,128)(2,1)S(1)}, u32[]{:S(2)}, u32[]{:S(2)}) collective-permute-start(bf16[80,2560]{1,0:T(8,128)(2,1)} %collective-permute-done.9.refs_15_), channel_id=1, source_target_pairs={{0,8},{8,0},{16,24},{24,16},{1,9},{9,1},{17,25},{25,17},{2,10},{10... | collective-permute-start | bytes 1228808 | tf_op jit(solution)/shard_map/ppermute | solution.py:210
  540.0 18.9 %collective-permute-start.15 = (bf16[320,640]{1,0:T(8,128)(2,1)}, bf16[320,640]{1,0:T(8,128)(2,1)S(1)}, u32[]{:S(2)}, u32[]{:S(2)}) collective-permute-start(bf16[320,640]{1,0:T(8,128)(2,1)} %collective-permute-done.13.refs_21_), channel_id=1, source_target_pairs={{0,8},{8,0},{16,24},{24,16},{1,9},{9,1},{17,25},{25,17},{2,10},{10... | collective-permute-start | bytes 1228808 | tf_op jit(solution)/shard_map/ppermute | solution.py:210
  542.2 16.8 %copy-start.19 = (f32[2560]{0:T(1024)S(1)}, f32[2560]{0:T(1024)}, u32[]{:S(2)}) copy-start(f32[2560]{0:T(1024)} %broadcast_in_dim.154) | copy-start | bytes 30724
  619.6 4.6 copy-start.11
  619.6 5.6 copy-start.10
  619.6 6.6 copy-start.8
  622.0 5.2 copy-start.7
  624.2 4.0 copy-start.6
  631.2 144.6 %reduce-scatter.5.cloned.1.call-start = ((), (), s32[]{:S(2)}) async-start(), calls=%async_computation.11 | async-start | bytes 9216000 | tf_op jit(solution)/shard_map/reduce_scatter | solution.py:1425
  643.9 10.3 %copy-start.39 = (bf16[416,640]{1,0:T(8,128)(2,1)S(1)}, bf16[416,640]{1,0:T(8,128)(2,1)}, u32[]{:S(2)}) copy-start(bf16[416,640]{1,0:T(8,128)(2,1)} %get-tuple-element.101) | copy-start | bytes 1597444
  649.0 24.7 %all-to-all-start.5 = ((bf16[8,72,640]{2,1,0:T(8,128)(2,1)}), bf16[8,72,640]{2,1,0:T(8,128)(2,1)S(1)}, u32[]{:S(2)}, u32[]{:S(2)}) async-start(bf16[8,72,640]{2,1,0:T(8,128)(2,1)} %bitcast_dynamic-update-slice_fusion), calls=%async_computation.5 | async-start | bytes 1474560 | tf_op jit(solution)/shard_map/all_to_all | solution.py:148
  654.1 22.6 %copy-start.30 = (s32[576]{0:T(1024)S(1)}, s32[576]{0:T(1024)}, u32[]{:S(2)}) copy-start(s32[576]{0:T(1024)} %copy-done.29) | copy-start | bytes 6916
  655.0 24.6 %copy-start.15 = (bf16[416,640]{1,0:T(8,128)(2,1)S(1)}, bf16[416,640]{1,0:T(8,128)(2,1)}, u32[]{:S(2)}) copy-start(bf16[416,640]{1,0:T(8,128)(2,1)} %get-tuple-element.88) | copy-start | bytes 1597444
  673.8 29.2 %all-to-all-start.4 = ((bf16[32,18,640]{2,1,0:T(8,128)(2,1)}), bf16[32,18,640]{2,1,0:T(8,128)(2,1)S(1)}, u32[]{:S(2)}, u32[]{:S(2)}) async-start(bf16[32,18,640]{2,1,0:T(8,128)(2,1)} %reshape.510), calls=%async_computation.4 | async-start | bytes 1966080 | tf_op jit(solution)/shard_map/all_to_all | solution.py:178
  678.5 28.6 %copy-start.32 = (s32[576]{0:T(1024)S(1)}, s32[576]{0:T(1024)}, u32[]{:S(2)}) copy-start(s32[576]{0:T(1024)} %copy-done.31) | copy-start | bytes 6916
  680.6 28.2 %copy-start.34 = (f32[128]{0:T(128)S(1)}, f32[128]{0:T(128)}, u32[]{:S(2)}) copy-start(f32[128]{0:T(128)} %copy-done.33) | copy-start | bytes 1540
  702.9 133.6 %all-to-all-start.3 = ((bf16[4,4,26,640]{3,1,2,0:T(4,128)(2,1)}), bf16[4,4,26,640]{3,1,2,0:T(4,128)(2,1)S(1)}, u32[]{:S(2)}, u32[]{:S(2)}) async-start(bf16[4,4,26,640]{3,1,2,0:T(4,128)(2,1)} %copy.59), calls=%async_computation.3 | async-start | bytes 1064960 | tf_op jit(solution)/shard_map/all_to_all | solution.py:196
  706.4 222.9 %all-reduce.16.cloned.1.call-start = ((), (), s32[]{:S(2)}) async-start(), calls=%async_computation.12 | async-start | bytes 7372800 | tf_op jit(solution)/shard_map/psum | solution.py:1426
  833.2 10.1 %copy-start.28 = (f32[8,640]{1,0:T(8,128)S(1)}, f32[8,640]{1,0:T(8,128)}, u32[]{:S(2)}) copy-start(f32[8,640]{1,0:T(8,128)} %get-tuple-element.113) | copy-start | bytes 61444
  833.2 10.1 %copy-start.27 = (f32[8,640]{1,0:T(8,128)S(1)}, f32[8,640]{1,0:T(8,128)}, u32[]{:S(2)}) copy-start(f32[8,640]{1,0:T(8,128)} %get-tuple-element.115) | copy-start | bytes 61444
  836.5 53.4 %all-to-all-start.6 = ((bf16[8,72,640]{2,1,0:T(8,128)(2,1)}), bf16[8,72,640]{2,1,0:T(8,128)(2,1)S(1)}, u32[]{:S(2)}, u32[]{:S(2)}) async-start(bf16[8,72,640]{2,1,0:T(8,128)(2,1)} %bitcast.43), calls=%async_computation.6 | async-start | bytes 1474560 | tf_op jit(solution)/shard_map/all_to_all | solution.py:154
  933.8 5.4 copy-start.1
  (12 other events, 24.7 us)
Sparse Core Ops, SparseCore 0:
  31.2 126.9 all-reduce.13
  631.3 76.0 reduce-scatter.2
  710.1 65.6 reduce-scatter.4
  779.3 149.9 all-reduce.15

commit v3 on v2

--- a/solution.py
+++ b/solution.py
@@ -3,6 +3,7 @@
 
 import jax
 import jax.numpy as jnp
+import numpy as np
 from jax import lax
 from jax.experimental import pallas as pl
 from jax.experimental.pallas import tpu as pltpu
@@ -70,17 +71,16 @@
     return jnp.concatenate([jnp.cos(angles), jnp.sin(angles)], axis=1)
 
 
-def frame_table(frame_ids, channels):
-    channel = jnp.arange(channels, dtype=jnp.int32)
-    even_index = (channel - channel % 2).astype(jnp.float32)
-    frequency = jnp.exp(even_index * (-math.log(10000.0) / channels))
-    angles = frame_ids.astype(jnp.float32)[:, None] * frequency[None, :]
-    return jnp.where((channel % 2 == 0)[None, :], jnp.sin(angles), jnp.cos(angles))
+def frame_table(frames, channels):
+    channel = np.arange(channels)
+    frequency = np.exp((channel - channel % 2) * (-math.log(10000.0) / channels))
+    angles = np.arange(frames)[:, None] * frequency[None, :]
+    return np.where((channel % 2 == 0)[None, :], np.sin(angles), np.cos(angles)).astype(np.float32)
 
 
 def group_table(channels):
-    which = jnp.arange(channels, dtype=jnp.int32) // (channels // GROUPS)
-    return (which[:, None] == which[None, :]).astype(jnp.float32)
+    which = np.arange(channels) // (channels // GROUPS)
+    return jnp.asarray((which[:, None] == which[None, :]).astype(np.float32))
 
 
 def onehot(indices, width):
@@ -127,15 +127,15 @@
         self.column_table = onehot(column_index, self.frames * self.rows * self.share_max)
         picks = []
         for number in range(self.clips):
-            cell = jnp.arange(self.shares[number], dtype=jnp.int32)[:, None]
-            when = jnp.arange(self.frames * frames_here, dtype=jnp.int32)[None, :]
+            cell = np.arange(self.shares[number])[:, None]
+            when = np.arange(self.frames * frames_here)[None, :]
             source = (
                 when // frames_here * self.rows + when % frames_here * self.clips + number
             ) * self.share_max + cell
             picks.append(source.reshape(-1))
-        self.pick_table = onehot(
-            jnp.concatenate(picks), self.frames * self.rows * self.share_max
-        )
+        picks = np.concatenate(picks)
+        slots = np.arange(self.frames * self.rows * self.share_max)
+        self.pick_table = jnp.asarray((picks[:, None] == slots[None, :]).astype(jnp.bfloat16))
 
     def blocks_to_unit(self, blocks):
         pieces = []
@@ -170,7 +170,7 @@
         send = to_low(matmul_left(self.column_table, joined))
         send = send.reshape(self.frames * self.rows, self.share_max, width)
         received = lax.all_to_all(send, ("frame", "rows"), 0, 0)
-        return matmul(self.pick_table, received.reshape(-1, width))
+        return received.reshape(-1, width)
 
     def columns_to_unit(self, field_low):
         send = to_low(matmul_left(self.pick_table, field_low))
@@ -205,58 +205,38 @@
         return jnp.concatenate(parts, axis=1)
 
 
-def swap(value, axis, bit):
-    count = lax.axis_size(axis)
-    return lax.ppermute(value, axis, [(i, i ^ bit) for i in range(count)])
-
-
-def exchange_pieces(shard, near, half):
-    first = swap(half, "frame", 2)
-    second = swap(first, "rows", 1)
-    return (shard, near, first, second, swap(first, "frame", 1), swap(second, "frame", 1))
-
-
-def piece_places():
+def shard_order():
     frame = lax.axis_index("frame")
-    odd_row = lax.axis_index("rows") % 2
-    far, corner = 2 * (frame ^ 2), 2 * (frame ^ 3)
-    return jnp.stack(
-        [
-            2 * frame,
-            2 * (frame ^ 1),
-            far + odd_row,
-            far + 1 - odd_row,
-            corner + odd_row,
-            corner + 1 - odd_row,
-        ]
-    ).astype(jnp.int32)
-
-
-def start_load(places_ref, pieces, lead, target, sem):
-    if len(pieces) == 1:
-        source = pieces[0] if lead is None else pieces[0].at[lead]
-        pltpu.make_async_copy(source, target, sem).start()
-        return
-    half = pieces[0].shape[-2] // 2
-    for number, piece in enumerate(pieces):
-        start = pl.multiple_of(places_ref[number] * half, 16)
-        source = piece if lead is None else piece.at[lead]
-        where = target.at[pl.ds(start, piece.shape[-2])]
-        pltpu.make_async_copy(source, where, sem).start()
-
-
-def pair_load(places_ref, groups, lead, target, sem):
+    return jnp.stack([frame, frame ^ 1, frame ^ 2, frame ^ 3]).astype(jnp.int32)
+
+
+def start_load(order_ref, pieces, lead, target, sem):
+    whole, own = pieces
+    rows = own.shape[-2]
+    for number in range(4):
+        where = pl.ds(pl.multiple_of(order_ref[number] * rows, 16), rows)
+        if lead is None:
+            source = own if number == 0 else whole.at[where]
+        elif number == 0:
+            source = own.at[lead]
+        else:
+            source = whole.at[lead, where]
+        goal = target.at[where] if len(target.shape) == 2 else target.at[:, where]
+        pltpu.make_async_copy(source, goal, sem).start()
+
+
+def pair_load(order_ref, groups, lead, target, sem):
     if lead < 2:
-        start_load(places_ref, groups[0], lead, target, sem)
+        start_load(order_ref, groups[0], lead, target, sem)
     else:
-        start_load(places_ref, groups[1], lead - 2, target, sem)
+        start_load(order_ref, groups[1], lead - 2, target, sem)
 
 
 def finish_load(target, sem):
     pltpu.make_async_copy(target, target, sem).wait()
 
 
-def run_kernel(body, places_row, arrays, groups, outs, scratch, flops):
+def run_kernel(body, order_row, arrays, groups, outs, scratch, flops):
     count, pieces = len(arrays), sum(len(group) for group in groups)
     out_count = len(outs)
 
@@ -274,8 +254,6 @@
 
     whole = pl.BlockSpec(memory_space=pltpu.VMEM)
     flat = [piece for group in groups for piece in group]
-    moved = sum(a.size * a.dtype.itemsize for a in list(arrays) + flat)
-    moved += sum(math.prod(o.shape) * o.dtype.itemsize for o in outs)
     return pl.pallas_call(
         kernel,
         out_shape=outs,
@@ -285,8 +263,13 @@
         out_specs=[whole] * out_count,
         scratch_shapes=scratch,
         compiler_params=pltpu.CompilerParams(vmem_limit_bytes=56 * 2**20),
-        cost_estimate=pl.CostEstimate(flops=flops, bytes_accessed=moved, transcendentals=0),
-    )(places_row, *arrays, *flat)
+        cost_estimate=pl.CostEstimate(flops=flops // 1000, bytes_accessed=4096, transcendentals=0),
+    )(order_row, *arrays, *flat)
+
+
+def rows_of(ref):
+    value = ref[...].astype(jnp.float32)
+    return [value[number : number + 1] for number in range(value.shape[0])]
 
 
 def f32(*shape):
@@ -427,24 +410,30 @@
         pads[number, side + cells :, :] = border
 
 
-def conv_forward(places_row, side, field, masks, vectors, table, weights, which, residual):
+def conv_rows(gains_ref, shifts_ref, stats_ref, which):
+    gains, shifts, stats = rows_of(gains_ref), rows_of(shifts_ref), rows_of(stats_ref)
+    bias = shifts[2 + which] + stats[1] if which == 0 else shifts[2 + which]
+    return [gains[which], shifts[which], bias, stats[0]]
+
+
+def conv_forward(order_row, side, field, masks, gains, shifts, stats, table, weights, which, residual, early):
     cells, channels = field.shape
 
-    def body(places_ref, ins, groups, outs, scratch):
-        field_ref, masks_ref, vec_ref, table_ref = ins[:4]
+    def body(order_ref, ins, groups, outs, scratch):
+        field_ref, masks_ref, gains_ref, shifts_ref, stats_ref, table_ref = ins[:6]
         weight, pads, sem = scratch
         (out_ref,) = outs
-        start_load(places_ref, groups[0], pl.ds(9 * which, 9), weight, sem.at[0])
+        start_load(order_ref, groups[0], pl.ds(9 * which, 9), weight, sem.at[0])
         masks = masks_ref[...]
         valid = masks[:, 0:1]
-        vec = vec_ref[...]
+        vec = conv_rows(gains_ref, shifts_ref, stats_ref, which)
         normed, _ = group_normed(
-            field_ref[...].astype(jnp.float32), valid, table_ref[...], vec[3:4]
+            field_ref[...].astype(jnp.float32), valid, table_ref[...], vec[3]
         )
-        pre = normed * vec[0:1] + vec[1:2]
+        pre = normed * vec[0] + vec[1]
         act = pre / (1.0 + jnp.exp(-pre)) * valid
         fill_taps(act, masks, pads, side)
-        out_ref[...] = jnp.broadcast_to(vec[2:3], (cells, channels))
+        out_ref[...] = jnp.broadcast_to(vec[2], (cells, channels))
         if residual:
             out_ref[...] += field_resid(ins)
         finish_load(weight, sem.at[0])
@@ -460,14 +449,14 @@
         lax.fori_loop(0, 3, row_tap, 0)
 
     def field_resid(ins):
-        return ins[4][...].astype(jnp.float32)
-
-    arrays = [field, masks, vectors, table] + ([residual[0]] if residual else [])
+        return ins[6][...].astype(jnp.float32)
+
+    arrays = [field, masks, gains, shifts, stats, table] + ([residual[0]] if residual else [])
     return run_kernel(
         body,
-        places_row,
+        order_row,
         arrays,
-        [(weights,)],
+        [weights, early],
         [f32(cells, channels)],
         [
             pltpu.VMEM((9, channels, channels), jnp.bfloat16),
@@ -478,17 +467,17 @@
     )[0]
 
 
-def conv_backward(places_row, side, gradient, field, masks, vectors, table, weights, which, extra):
+def conv_backward(order_row, side, gradient, field, masks, gains, shifts, stats, table, weights, which, extra):
     cells, channels = field.shape
 
-    def body(places_ref, ins, groups, outs, scratch):
-        grad_ref, field_ref, masks_ref, vec_ref, table_ref = ins[:5]
+    def body(order_ref, ins, groups, outs, scratch):
+        grad_ref, field_ref, masks_ref, gains_ref, shifts_ref, stats_ref, table_ref = ins[:7]
         weight, pads, total_ref, sem = scratch
         (out_ref,) = outs
-        start_load(places_ref, groups[0], pl.ds(9 * which, 9), weight, sem.at[0])
+        start_load(order_ref, groups[0], pl.ds(9 * which, 9), weight, sem.at[0])
         masks = masks_ref[...]
         valid = masks[:, 0:1]
-        vec = vec_ref[...]
+        vec = conv_rows(gains_ref, shifts_ref, stats_ref, which)
         fill_taps(grad_ref[...], masks, pads, side)
         total_ref[...] = jnp.zeros((cells, channels), jnp.float32)
         finish_load(weight, sem.at[0])
@@ -503,23 +492,23 @@
 
         lax.fori_loop(0, 3, row_tap, 0)
         normed, inv_std = group_normed(
-            field_ref[...].astype(jnp.float32), valid, table_ref[...], vec[3:4]
+            field_ref[...].astype(jnp.float32), valid, table_ref[...], vec[3]
         )
-        pre = normed * vec[0:1] + vec[1:2]
+        pre = normed * vec[0] + vec[1]
         gate = 1.0 / (1.0 + jnp.exp(-pre))
         grad_pre = total_ref[...] * (gate * (1.0 + pre * (1.0 - gate)))
         result = group_back(
-            grad_pre, normed, inv_std, vec[0:1], valid, table_ref[...], vec[3:4]
+            grad_pre, normed, inv_std, vec[0], valid, table_ref[...], vec[3]
         )
         if extra:
-            result += ins[5][...]
+            result += ins[7][...]
         out_ref[...] = result
 
     return run_kernel(
         body,
-        places_row,
-        [gradient, field, masks, vectors, table] + list(extra),
-        [(weights,)],
+        order_row,
+        [gradient, field, masks, gains, shifts, stats, table] + list(extra),
+        [weights],
         [f32(cells, channels)],
         [
             pltpu.VMEM((9, channels, channels), jnp.bfloat16),
@@ -531,36 +520,41 @@
     )[0]
 
 
-def self_forward(places_row, resid, masks, bias, vectors, table, proj, attn):
+def self_rows(gains_ref, shifts_ref, stats_ref):
+    gains, shifts, stats = rows_of(gains_ref), rows_of(shifts_ref), rows_of(stats_ref)
+    return [gains[0], shifts[0], shifts[4], gains[1], shifts[1], shifts[5], None, stats[0]]
+
+
+def self_forward(order_row, resid, masks, bias, gains, shifts, stats, table, proj, attn):
     cells, channels = resid.shape
     needed = (0, 2, 3, 4, 5)
 
-    def body(places_ref, ins, groups, outs, scratch):
-        resid_ref, masks_ref, bias_ref, vec_ref, table_ref = ins
+    def body(order_ref, ins, groups, outs, scratch):
+        resid_ref, masks_ref, bias_ref, gains_ref, shifts_ref, stats_ref, table_ref = ins
         proj_ref, query_ref, key_ref, value_ref, two_ref = outs
         weight, att, sem = scratch
         for slot, lead in enumerate(needed):
-            pair_load(places_ref, groups, lead, weight.at[slot], sem.at[slot])
-        vec = vec_ref[...]
-        normed, _ = group_normed(resid_ref[...], masks_ref[:, 0:1], table_ref[...], vec[7:8])
-        low = to_low(normed * vec[0:1] + vec[1:2])
+            pair_load(order_ref, groups, lead, weight.at[slot], sem.at[slot])
+        vec = self_rows(gains_ref, shifts_ref, stats_ref)
+        normed, _ = group_normed(resid_ref[...], masks_ref[:, 0:1], table_ref[...], vec[7])
+        low = to_low(normed * vec[0] + vec[1])
         finish_load(weight.at[0], sem.at[0])
-        entered = dot_nn(low, weight[0]) + vec[2:3]
+        entered = dot_nn(low, weight[0]) + vec[2]
         proj_ref[...] = entered
         normed, _ = layer_normed(entered)
-        low = to_low(normed * vec[3:4] + vec[4:5])
+        low = to_low(normed * vec[3] + vec[4])
         for slot, out_ref in ((1, query_ref), (2, key_ref), (3, value_ref)):
             finish_load(weight.at[slot], sem.at[slot])
             out_ref[...] = to_low(dot_nn(low, weight[slot]))
         attend_into(query_ref, key_ref, value_ref, bias_ref[0:1, :], att, ALL)
         finish_load(weight.at[4], sem.at[4])
-        two_ref[...] = proj_ref[...] + dot_nn(to_low(att[...]), weight[4]) + vec[5:6]
+        two_ref[...] = proj_ref[...] + dot_nn(to_low(att[...]), weight[4]) + vec[5]
 
     return run_kernel(
         body,
-        places_row,
-        [resid, masks, bias, vectors, table],
-        [(proj,), (attn,)],
+        order_row,
+        [resid, masks, bias, gains, shifts, stats, table],
+        [proj, attn],
         [f32(cells, channels)] + [b16(cells, channels)] * 3 + [f32(cells, channels)],
         [
             pltpu.VMEM((5, channels, channels), jnp.bfloat16),
@@ -571,17 +565,17 @@
     )
 
 
-def self_backward(places_row, grad_two, proj_one, query, key, value, resid, grad_st, masks, vectors, table, proj, attn):
+def self_backward(order_row, early, grad_two, proj_one, query, key, value, resid, grad_st, masks, gains, shifts, stats, table, proj, attn):
     cells, channels = resid.shape
     needed = (5, 2, 3, 4, 0)
 
-    def body(places_ref, ins, groups, outs, scratch):
-        grad_ref, proj_ref, query_ref, key_ref, value_ref, resid_ref, st_ref, masks_ref, vec_ref, table_ref = ins
+    def body(order_ref, ins, groups, outs, scratch):
+        grad_ref, proj_ref, query_ref, key_ref, value_ref, resid_ref, st_ref, masks_ref, gains_ref, shifts_ref, stats_ref, table_ref = ins
         (out_ref,) = outs
         weight, grad_att, grad_q, grad_k, grad_v, sem = scratch
         for slot, lead in enumerate(needed):
-            pair_load(places_ref, groups, lead, weight.at[slot], sem.at[slot])
-        vec = vec_ref[...]
+            pair_load(order_ref, groups, lead, weight.at[slot], sem.at[slot])
+        vec = self_rows(gains_ref, shifts_ref, stats_ref)
         valid = masks_ref[:, 0:1]
         finish_load(weight.at[0], sem.at[0])
         grad_att[...] = to_low(dot_nt(to_low(grad_ref[...]), weight[0]))
@@ -595,19 +589,19 @@
             part = dot_nt(to_low(member[...]), weight[slot])
             total = part if total is None else total + part
         normed, inv_std = layer_normed(proj_ref[...])
-        grad_one = grad_ref[...] + layer_back(total, normed, inv_std, vec[3:4])
+        grad_one = grad_ref[...] + layer_back(total, normed, inv_std, vec[3])
         finish_load(weight.at[4], sem.at[4])
         grad_gn = dot_nt(to_low(grad_one), weight[4])
-        normed, inv_std = group_normed(resid_ref[...], valid, table_ref[...], vec[7:8])
+        normed, inv_std = group_normed(resid_ref[...], valid, table_ref[...], vec[7])
         out_ref[...] = st_ref[...] + group_back(
-            grad_gn, normed, inv_std, vec[0:1], valid, table_ref[...], vec[7:8]
+            grad_gn, normed, inv_std, vec[0], valid, table_ref[...], vec[7]
         )
 
     return run_kernel(
         body,
-        places_row,
-        [grad_two, proj_one, query, key, value, resid, grad_st, masks, vectors, table],
-        [(proj,), (attn,)],
+        order_row,
+        [grad_two, proj_one, query, key, value, resid, grad_st, masks, gains, shifts, stats, table],
+        [proj, attn, early],
         [f32(cells, channels)],
         [
             pltpu.VMEM((5, channels, channels), jnp.bfloat16),
@@ -624,23 +618,32 @@
 CHUNK = 512
 
 
-def cross_forward(places_row, two, resid, context, masks, bias, vectors, wide_bias, table, proj, attn, cross, w_in_all, w_out_all):
+def cross_rows(gains_ref, shifts_ref, motion_rows_ref, stats_ref):
+    gains, shifts = rows_of(gains_ref), rows_of(shifts_ref)
+    motion, stats = rows_of(motion_rows_ref), rows_of(stats_ref)
+    return [
+        gains[2], shifts[2], shifts[6], gains[3], shifts[3], shifts[7], shifts[8],
+        motion[0], motion[4], stats[0],
+    ]
+
+
+def cross_forward(order_row, early, two, resid, context, masks, bias, gains, shifts, motion_rows, stats, wide_bias, table, proj, attn, cross, w_in_all, w_out_all):
     cells, channels = resid.shape
     prompt, width = context.shape
 
-    def body(places_ref, ins, groups, outs, scratch):
-        two_ref, resid_ref, context_ref, masks_ref, bias_ref, vec_ref, wide_ref, table_ref = ins
+    def body(order_ref, ins, groups, outs, scratch):
+        two_ref, resid_ref, context_ref, masks_ref, bias_ref, gains_ref, shifts_ref, motion_rows_ref, stats_ref, wide_ref, table_ref = ins
         query_ref, key_ref, value_ref, three_ref, out_ref, motion_ref = outs
         weight, kv, w_in, w_out, att, total, sem = scratch
         for slot, lead in enumerate((6, 7, 1)):
-            pair_load(places_ref, groups, lead, weight.at[slot], sem.at[slot])
+            pair_load(order_ref, groups, lead, weight.at[slot], sem.at[slot])
         for slot in range(2):
-            start_load(places_ref, groups[2], slot, kv.at[slot], sem.at[3 + slot])
-        start_load(places_ref, groups[3], None, w_in, sem.at[5])
-        start_load(places_ref, groups[4], None, w_out, sem.at[6])
-        vec = vec_ref[...]
+            start_load(order_ref, groups[2], slot, kv.at[slot], sem.at[3 + slot])
+        start_load(order_ref, groups[3], None, w_in, sem.at[5])
+        start_load(order_ref, groups[4], None, w_out, sem.at[6])
+        vec = cross_rows(gains_ref, shifts_ref, motion_rows_ref, stats_ref)
         normed, _ = layer_normed(two_ref[...])
-        low = to_low(normed * vec[0:1] + vec[1:2])
+        low = to_low(normed * vec[0] + vec[1])
         finish_load(weight.at[0], sem.at[0])
         query_ref[...] = to_low(dot_nn(low, weight[0]))
         for slot, ref in ((0, key_ref), (1, value_ref)):
@@ -648,12 +651,12 @@
             ref[...] = to_low(dot_nn(context_ref[...], kv[slot]))
         attend_into(query_ref, key_ref, value_ref, bias_ref[0:1, :], att, ALL)
         finish_load(weight.at[1], sem.at[1])
-        three_ref[...] = two_ref[...] + dot_nn(to_low(att[...]), weight[1]) + vec[2:3]
+        three_ref[...] = two_ref[...] + dot_nn(to_low(att[...]), weight[1]) + vec[2]
         normed, _ = layer_normed(three_ref[...])
-        low = to_low(normed * vec[3:4] + vec[4:5])
+        low = to_low(normed * vec[3] + vec[4])
         finish_load(w_in, sem.at[5])
         finish_load(w_out, sem.at[6])
-        total[...] = three_ref[...] + vec[5:6]
+        total[...] = three_ref[...] + vec[5]
 
         def chunk(step, carry):
             lanes = pl.ds(pl.multiple_of(step * CHUNK, 128), CHUNK)
@@ -670,16 +673,16 @@
         att[...] = low.astype(jnp.float32)
         lax.fori_loop(0, FF_ST // CHUNK, chunk, 0)
         finish_load(weight.at[2], sem.at[2])
-        st_out = dot_nn(to_low(total[...]), weight[2]) + vec[6:7] + resid_ref[...]
+        st_out = dot_nn(to_low(total[...]), weight[2]) + vec[6] + resid_ref[...]
         out_ref[...] = st_out
-        normed, _ = group_normed(st_out, masks_ref[:, 0:1], table_ref[...], vec[9:10])
-        motion_ref[...] = to_low(normed * vec[7:8] + vec[8:9])
+        normed, _ = group_normed(st_out, masks_ref[:, 0:1], table_ref[...], vec[9])
+        motion_ref[...] = to_low(normed * vec[7] + vec[8])
 
     return run_kernel(
         body,
-        places_row,
-        [two, resid, context, masks, bias, vectors, wide_bias, table],
-        [(proj,), (attn,), (cross,), (w_in_all,), (w_out_all,)],
+        order_row,
+        [two, resid, context, masks, bias, gains, shifts, motion_rows, stats, wide_bias, table],
+        [proj, attn, cross, w_in_all, w_out_all, early],
         [
             b16(cells, channels),
             b16(prompt, channels),
@@ -701,38 +704,31 @@
     )
 
 
-def cross_backward(places_row, grad_gn, grad_out, st_out, three, two, query, key, value, masks, bias_col, vectors, wide_bias, table, proj, attn, w_in_all, w_out_all):
+def cross_backward(order_row, grad_gn, grad_out, st_out, three, two, query, key, value, masks, bias_col, gains, shifts, motion_rows, stats, wide_bias, table, proj, attn, w_in_all, w_out_all):
     cells, channels = st_out.shape
     prompt = key.shape[0]
 
-    def body(places_ref, ins, groups, outs, scratch):
-        gn_ref, cot_ref, st_ref, three_ref, two_ref, query_ref, key_ref, value_ref, masks_ref, bias_ref, vec_ref, wide_ref, table_ref = ins
-        grad_two_ref, grad_st_ref, small_ref = outs
+    def body(order_ref, ins, groups, outs, scratch):
+        gn_ref, cot_ref, st_ref, three_ref, two_ref, query_ref, key_ref, value_ref, masks_ref, bias_ref, gains_ref, shifts_ref, motion_rows_ref, stats_ref, wide_ref, table_ref = ins
+        grad_two_ref, grad_st_ref = outs
         weight, w_in, w_out, low, grad_low, total, grad_att, grad_q, sem = scratch
-        pair_load(places_ref, groups, 1, weight.at[0], sem.at[0])
-        start_load(places_ref, groups[3], None, w_out, sem.at[4])
-        start_load(places_ref, groups[2], None, w_in, sem.at[3])
-        pair_load(places_ref, groups, 7, weight.at[1], sem.at[1])
-        pair_load(places_ref, groups, 6, weight.at[2], sem.at[2])
-        vec = vec_ref[...]
+        pair_load(order_ref, groups, 1, weight.at[0], sem.at[0])
+        start_load(order_ref, groups[3], None, w_out, sem.at[4])
+        start_load(order_ref, groups[2], None, w_in, sem.at[3])
+        pair_load(order_ref, groups, 7, weight.at[1], sem.at[1])
+        pair_load(order_ref, groups, 6, weight.at[2], sem.at[2])
+        vec = cross_rows(gains_ref, shifts_ref, motion_rows_ref, stats_ref)
         valid = masks_ref[:, 0:1]
         grad_motion = gn_ref[...].astype(jnp.float32)
-        normed, inv_std = group_normed(st_ref[...], valid, table_ref[...], vec[9:10])
-        small_ref[...] = jnp.concatenate(
-            [
-                jnp.sum(grad_motion * normed, axis=0, keepdims=True),
-                jnp.sum(grad_motion, axis=0, keepdims=True),
-                jnp.zeros((6, channels), jnp.float32),
-            ]
-        )
+        normed, inv_std = group_normed(st_ref[...], valid, table_ref[...], vec[9])
         grad_st_ref[...] = cot_ref[...].astype(jnp.float32) + group_back(
-            grad_motion, normed, inv_std, vec[7:8], valid, table_ref[...], vec[9:10]
+            grad_motion, normed, inv_std, vec[7], valid, table_ref[...], vec[9]
         )
         finish_load(weight.at[0], sem.at[0])
         grad_two_ref[...] = dot_nt(to_low(grad_st_ref[...]), weight[0])
         grad_low[...] = to_low(grad_two_ref[...])
         normed, inv_std = layer_normed(three_ref[...])
-        low[...] = to_low(normed * vec[3:4] + vec[4:5])
+        low[...] = to_low(normed * vec[3] + vec[4])
         total[...] = jnp.zeros((cells, channels), jnp.float32)
         finish_load(w_out, sem.at[4])
         finish_load(w_in, sem.at[3])
@@ -751,7 +747,7 @@
 
         lax.fori_loop(0, FF_ST // CHUNK, chunk, 0)
         normed, inv_std = layer_normed(three_ref[...])
-        grad_two_ref[...] += layer_back(total[...], normed, inv_std, vec[3:4])
+        grad_two_ref[...] += layer_back(total[...], normed, inv_std, vec[3])
         finish_load(weight.at[1], sem.at[1])
         grad_att[...] = to_low(dot_nt(to_low(grad_two_ref[...]), weight[1]))
         attend_back_into(
@@ -760,14 +756,14 @@
         finish_load(weight.at[2], sem.at[2])
         grad_ln = dot_nt(to_low(grad_q[...]), weight[2])
         normed, inv_std = layer_normed(two_ref[...])
-        grad_two_ref[...] += layer_back(grad_ln, normed, inv_std, vec[0:1])
+        grad_two_ref[...] += layer_back(grad_ln, normed, inv_std, vec[0])
 
     return run_kernel(
         body,
-        places_row,
-        [grad_gn, grad_out, st_out, three, two, query, key, value, masks, bias_col, vectors, wide_bias, table],
-        [(proj,), (attn,), (w_in_all,), (w_out_all,)],
-        [f32(cells, channels), f32(cells, channels), f32(8, channels)],
+        order_row,
+        [grad_gn, grad_out, st_out, three, two, query, key, value, masks, bias_col, gains, shifts, motion_rows, stats, wide_bias, table],
+        [proj, attn, w_in_all, w_out_all],
+        [f32(cells, channels), f32(cells, channels)],
         [
             pltpu.VMEM((3, channels, channels), jnp.bfloat16),
             pltpu.VMEM((channels, 2 * FF_ST), jnp.bfloat16),
@@ -787,24 +783,27 @@
     return pl.ds(pl.multiple_of(step * group_len, 16), group_len)
 
 
-def motion_forward(places_row, motion_in, position, bias, vectors, proj, attn):
-    tokens, channels = motion_in.shape
+def motion_forward(order_row, moved, picks, position, bias, vectors, proj, attn):
+    tokens, channels = position.shape
     group_len = bias.shape[0]
 
-    def body(places_ref, ins, groups, outs, scratch):
-        in_ref, pos_ref, bias_ref, vec_ref = ins
+    def body(order_ref, ins, groups, outs, scratch):
+        moved_ref, picks_ref, pos_ref, bias_ref, vec_ref = ins
         weight, att, sem = scratch
         for slot, lead in enumerate((0, 2, 3, 4, 5, 6, 7, 8, 9)):
-            pair_load(places_ref, groups, lead, weight.at[slot], sem.at[slot])
-        vec = vec_ref[...]
+            pair_load(order_ref, groups, lead, weight.at[slot], sem.at[slot])
+        rows = rows_of(vec_ref)
+        vec = [rows[number] for number in (8, 1, 5, 9, 2, 6, 10)]
         finish_load(weight.at[0], sem.at[0])
-        outs[0][...] = dot_nn(in_ref[...], weight[0]) + vec[0:1]
+        entered = to_low(dot_nn(picks_ref[...], moved_ref[...]))
+        outs[11][...] = entered
+        outs[0][...] = dot_nn(entered, weight[0]) + vec[0]
         for block in range(2):
             zed_ref, next_ref = outs[block], outs[block + 1]
             qkv = outs[3 + 4 * block : 6 + 4 * block]
             time_ref = outs[6 + 4 * block]
             normed, _ = layer_normed(zed_ref[...])
-            low = to_low(normed * vec[1 + 3 * block : 2 + 3 * block] + vec[2 + 3 * block : 3 + 3 * block] + pos_ref[...])
+            low = to_low(normed * vec[1 + 3 * block] + vec[2 + 3 * block] + pos_ref[...])
             for which in range(3):
                 slot = 1 + 4 * block + which
                 finish_load(weight.at[slot], sem.at[slot])
@@ -818,14 +817,14 @@
             time_ref[...] = to_low(att[...])
             slot = 4 + 4 * block
             finish_load(weight.at[slot], sem.at[slot])
-            next_ref[...] = zed_ref[...] + dot_nn(time_ref[...], weight[slot]) + vec[3 + 3 * block : 4 + 3 * block]
+            next_ref[...] = zed_ref[...] + dot_nn(time_ref[...], weight[slot]) + vec[3 + 3 * block]
 
     return run_kernel(
         body,
-        places_row,
-        [motion_in, position, bias, vectors],
+        order_row,
+        [moved, picks, position, bias, vectors],
         [proj, attn],
-        [f32(tokens, channels)] * 3 + [b16(tokens, channels)] * 8,
+        [f32(tokens, channels)] * 3 + [b16(tokens, channels)] * 9,
         [
             pltpu.VMEM((9, channels, channels), jnp.bfloat16),
             pltpu.VMEM((tokens, channels), jnp.float32),
@@ -835,54 +834,65 @@
     )
 
 
-def motion_ff(places_row, zed, st_columns, cotangent, vectors, wide_bias, proj, in_pieces, out_pieces):
+def motion_ff(order_row, zed, st_moved, picks, cotangent, vectors, wide_bias, proj, in_pieces, out_pieces):
     tokens, channels = zed.shape
     hidden_width = wide_bias.shape[1]
-
-    def body(places_ref, ins, groups, outs, scratch):
-        zed_ref, st_ref, cot_ref, vec_ref, wide_ref = ins
-        out_ref, grad_ref, d_proj, d_in, d_out, small_ref, wide_out = outs
+    frames = 4
+    own = channels // frames
+    joined = hidden_width // frames + own * (hidden_width // channels) + own
+    second, third = own * (hidden_width // channels), joined - own
+    assert hidden_width == frames * channels
+
+    def body(order_ref, ins, groups, outs, scratch):
+        zed_ref, st_ref, picks_ref, cot_ref, vec_ref, wide_ref = ins
+        out_ref, grad_ref, d_all, small_ref, wide_out = outs
         weight, w_in, w_out, pre, low, grad_low, total, sem = scratch
-        start_load(places_ref, groups[1], None, w_in, sem.at[0])
-        start_load(places_ref, groups[2], None, w_out, sem.at[1])
-        start_load(places_ref, groups[0], 1, weight, sem.at[2])
-        vec = vec_ref[...]
+        start_load(order_ref, groups[1], None, w_in, sem.at[0])
+        start_load(order_ref, groups[2], None, w_out, sem.at[1])
+        start_load(order_ref, groups[0], 1, weight, sem.at[2])
+        rows = rows_of(vec_ref)
+        vec = [rows[3], rows[7], rows[11], rows[12]]
         normed, inv_std = layer_normed(zed_ref[...])
-        low[...] = to_low(normed * vec[0:1] + vec[1:2])
-        total[...] = zed_ref[...] + vec[2:3]
+        low[...] = to_low(normed * vec[0] + vec[1])
+        total[...] = zed_ref[...] + vec[2]
         finish_load(w_in, sem.at[0])
         finish_load(w_out, sem.at[1])
 
         def forward(step, carry):
-            lanes = pl.ds(pl.multiple_of(step * CHUNK, 128), CHUNK)
+            lanes = pl.ds(pl.multiple_of(step * channels, 128), channels)
             before = dot_nn(low[...], w_in[:, lanes]) + wide_ref[0:1, lanes]
             pre[:, lanes] = before
             total[...] += dot_nn(to_low(before * half_erf(before)), w_out[lanes, :])
             return carry
 
-        lax.fori_loop(0, hidden_width // CHUNK, forward, 0)
+        lax.fori_loop(0, hidden_width // channels, forward, 0)
         finish_load(weight, sem.at[2])
         zed_low = to_low(total[...])
-        out_ref[...] = to_low(st_ref[...].astype(jnp.float32) + dot_nn(zed_low, weight[...]) + vec[3:4])
-        d_proj[...] = to_low(dot_tn(zed_low, cot_ref[...]))
+        out_ref[...] = to_low(dot_nn(picks_ref[...], st_ref[...]) + dot_nn(zed_low, weight[...]) + vec[3])
+        d_proj = to_low(dot_tn(zed_low, cot_ref[...]))
+        for shard in range(frames):
+            d_all[shard, third:, :] = d_proj[shard * own : (shard + 1) * own]
         grad_ref[...] = dot_nt(cot_ref[...], weight[...])
         grad_low[...] = to_low(grad_ref[...])
         total[...] = jnp.zeros((tokens, channels), jnp.float32)
 
         def backward(step, carry):
-            lanes = pl.ds(pl.multiple_of(step * CHUNK, 128), CHUNK)
+            lanes = pl.ds(pl.multiple_of(step * channels, 128), channels)
             before = pre[:, lanes]
             half = half_erf(before)
-            d_out[lanes, :] = to_low(dot_tn(to_low(before * half), grad_low[...]))
+            d_all[step, second:third, :] = to_low(dot_tn(to_low(before * half), grad_low[...]))
             grad_pre = dot_nt(grad_low[...], w_out[lanes, :]) * gelu_slope(before, half)
             wide_out[0:1, lanes] = jnp.sum(grad_pre, axis=0, keepdims=True)
             pre_low = to_low(grad_pre)
-            d_in[:, lanes] = to_low(dot_tn(low[...], pre_low))
+            d_in = to_low(dot_tn(low[...], pre_low))
+            for shard in range(frames):
+                rows_in = pl.ds(pl.multiple_of(step * own, 16), own)
+                d_all[shard, rows_in, :] = d_in[shard * own : (shard + 1) * own]
             total[...] += dot_nt(pre_low, w_in[:, lanes])
             return carry
 
         wide_out[...] = jnp.zeros((8, hidden_width), jnp.float32)
-        lax.fori_loop(0, hidden_width // CHUNK, backward, 0)
+        lax.fori_loop(0, hidden_width // channels, backward, 0)
         normed, inv_std = layer_normed(zed_ref[...])
         grad_ln = total[...]
         small_ref[...] = jnp.concatenate(
@@ -894,19 +904,17 @@
                 jnp.zeros((4, channels), jnp.float32),
             ]
         )
-        grad_ref[...] += layer_back(grad_ln, normed, inv_std, vec[0:1])
+        grad_ref[...] += layer_back(grad_ln, normed, inv_std, vec[0])
 
     return run_kernel(
         body,
-        places_row,
-        [zed, st_columns, cotangent, vectors, wide_bias],
+        order_row,
+        [zed, st_moved, picks, cotangent, vectors, wide_bias],
         [proj, in_pieces, out_pieces],
         [
             b16(tokens, channels),
             f32(tokens, channels),
-            b16(channels, channels),
-            b16(channels, hidden_width),
-            b16(hidden_width, channels),
+            b16(frames, joined, channels),
             f32(8, channels),
             f32(8, hidden_width),
         ],
@@ -924,21 +932,30 @@
     )
 
 
-def motion_back(places_row, block, grad_zed, zed, query, key, value, time_out, motion_in, position, bias, vectors, proj, attn):
+def motion_back(order_row, block, grad_zed, zed, query, key, value, time_out, motion_in, small, position, bias, vectors, proj, attn):
     tokens, channels = zed.shape
     group_len = bias.shape[0]
     leads = [5 + 4 * block, 2 + 4 * block, 3 + 4 * block, 4 + 4 * block] + ([0] if motion_in is not None else [])
     last = motion_in is not None
-
-    def body(places_ref, ins, groups, outs, scratch):
-        grad_ref, zed_ref, query_ref, key_ref, value_ref, time_ref, pos_ref, bias_ref, vec_ref = ins[:9]
-        out_ref, d_query, d_key, d_value, d_output, small_ref = outs[:6]
+    frames = 4
+    own = channels // frames
+
+    def body(order_ref, ins, groups, outs, scratch):
+        grad_ref, zed_ref, query_ref, key_ref, value_ref, time_ref, pos_ref, bias_ref, vec_ref, small_in = ins[:10]
+        out_ref, d_all, small_ref = outs
         weight, grad_att, grad_q, grad_k, grad_v, sem = scratch
         for slot, lead in enumerate(leads):
-            pair_load(places_ref, groups, lead, weight.at[slot], sem.at[slot])
-        vec = vec_ref[...]
+            pair_load(order_ref, groups, lead, weight.at[slot], sem.at[slot])
+        rows = rows_of(vec_ref)
+        vec = [rows[1 + block], rows[5 + block]]
+
+        def put(slot, value):
+            low_value = to_low(value)
+            for shard in range(frames):
+                d_all[shard, slot * own : (slot + 1) * own, :] = low_value[shard * own : (shard + 1) * own]
+
         grad_low = to_low(grad_ref[...])
-        d_output[...] = to_low(dot_tn(time_ref[...], grad_low))
+        put(3, dot_tn(time_ref[...], grad_low))
         finish_load(weight.at[0], sem.at[0])
         grad_att[...] = to_low(dot_nt(grad_low, weight[0]))
 
@@ -951,40 +968,53 @@
 
         lax.fori_loop(0, tokens // group_len, group, 0)
         normed, inv_std = layer_normed(zed_ref[...])
-        low = to_low(normed * vec[0:1] + vec[1:2] + pos_ref[...])
+        low = to_low(normed * vec[0] + vec[1] + pos_ref[...])
         grad_ln = None
-        for slot, member, d_ref in ((1, grad_q, d_query), (2, grad_k, d_key), (3, grad_v, d_value)):
+        for slot, member in ((1, grad_q), (2, grad_k), (3, grad_v)):
             member_low = to_low(member[...])
-            d_ref[...] = to_low(dot_tn(low, member_low))
+            put(slot - 1, dot_tn(low, member_low))
             finish_load(weight.at[slot], sem.at[slot])
             part = dot_nt(member_low, weight[slot])
             grad_ln = part if grad_ln is None else grad_ln + part
-        total = grad_ref[...] + layer_back(grad_ln, normed, inv_std, vec[0:1])
-        small_ref[...] = jnp.concatenate(
-            [
-                jnp.sum(grad_ref[...], axis=0, keepdims=True),
-                jnp.sum(grad_ln * normed, axis=0, keepdims=True),
-                jnp.sum(grad_ln, axis=0, keepdims=True),
-                jnp.sum(total, axis=0, keepdims=True),
-                jnp.zeros((4, channels), jnp.float32),
-            ]
-        )
-        if last:
-            total_low = to_low(total)
-            outs[6][...] = to_low(dot_tn(ins[9][...], total_low))
-            finish_load(weight.at[4], sem.at[4])
-            out_ref[...] = to_low(dot_nt(total_low, weight[4]))
-        else:
+        total = grad_ref[...] + layer_back(grad_ln, normed, inv_std, vec[0])
+        before = rows_of(small_in)
+        mine = [
+            jnp.sum(grad_ref[...], axis=0, keepdims=True),
+            jnp.sum(grad_ln * normed, axis=0, keepdims=True),
+            jnp.sum(grad_ln, axis=0, keepdims=True),
+        ]
+        filler = [jnp.zeros((1, channels), jnp.float32)]
+        if not last:
+            small_ref[...] = jnp.concatenate(before[:4] + mine + filler * 9)
             out_ref[...] = total
-
-    arrays = [grad_zed, zed, query, key, value, time_out, position, bias, vectors]
-    outs = [b16(tokens, channels) if last else f32(tokens, channels)] + [b16(channels, channels)] * 4 + [f32(8, channels)]
+            return
+        total_low = to_low(total)
+        put(4, dot_tn(ins[10][...], total_low))
+        finish_load(weight.at[4], sem.at[4])
+        entered = dot_nt(total_low, weight[4])
+        out_ref[...] = to_low(entered)
+        shift_sum = jnp.sum(entered, axis=0, keepdims=True)
+        product = jnp.sum(entered * ins[10][...].astype(jnp.float32), axis=0, keepdims=True)
+        gain_sum = (product - rows[4] * shift_sum) / rows[0]
+        gains = [gain_sum, mine[1], before[5], before[2]]
+        shifts = [
+            shift_sum, mine[2], before[6], before[3], jnp.sum(total, axis=0, keepdims=True),
+            mine[0], before[4], before[1], before[0],
+        ]
+        small_ref[...] = jnp.concatenate(gains + shifts + filler * 3)
+
+    arrays = [grad_zed, zed, query, key, value, time_out, position, bias, vectors, small]
+    extra_rows = 16 if last else 0
+    outs = [
+        b16(tokens, channels) if last else f32(tokens, channels),
+        b16(frames, own * len(leads) + extra_rows, channels),
+        f32(16, channels),
+    ]
     if last:
         arrays.append(motion_in)
-        outs.append(b16(channels, channels))
     return run_kernel(
         body,
-        places_row,
+        order_row,
         arrays,
         [proj, attn],
         outs,
@@ -1024,24 +1054,19 @@
     return plan
 
 
-def gather_all(shards, small, carried):
+def gather_all(shards, small):
     arrays = [array for array, _ in shards]
     plan = gather_plan([(array.shape, pieces) for array, pieces in shards])
     frames = lax.axis_size("frame")
-    count, extra = len(arrays), len(carried)
+    count = len(arrays)
     steps = len(plan)
     roles = ((0, 1, 2), (1, 0, 2), (2, 1, 0), (2, 0, 1))
 
     def kernel(*refs):
         sources, small_ref = refs[:count], refs[count]
-        carried_in = refs[count + 1 : count + 1 + extra]
-        base = count + 1 + extra
+        base = count + 1
         targets, small_out = refs[base : base + count], refs[base + count]
-        near_out = refs[base + count + 1 : base + count + 1 + extra]
-        half_out = refs[base + count + 1 + extra : base + count + 1 + 2 * extra]
-        send, recv, small_send, small_recv, near_send, near_recv, own_sem, half_sem = refs[
-            base + count + 1 + 2 * extra :
-        ]
+        send, recv, small_send, small_recv, own_sem = refs[base + count + 1 :]
         frame, row = lax.axis_index("frame"), lax.axis_index("rows")
         frame_bit, core_bit = frame // 2, frame % 2
         across = (1 - frame_bit) * 2 + core_bit
@@ -1089,14 +1114,6 @@
                 device_id_type=MESH,
             )
 
-        own = [
-            pltpu.make_async_copy(
-                view(sources[plan[step][0]], step, None, None),
-                view(targets[plan[step][0]], step, None, frame),
-                own_sem.at[step],
-            )
-            for step in range(steps)
-        ]
         smalls = [
             pltpu.make_async_remote_copy(
                 src_ref=small_ref,
@@ -1108,25 +1125,7 @@
             )
             for slot, way in enumerate(("y", "core", "corner"))
         ]
-        small_own = pltpu.make_async_copy(small_ref, small_out.at[frame], half_sem.at[extra])
-        nears = [
-            pltpu.make_async_remote_copy(
-                src_ref=carried_in[number],
-                dst_ref=near_out[number],
-                send_sem=near_send.at[number],
-                recv_sem=near_recv.at[number],
-                device_id=over["core"],
-                device_id_type=MESH,
-            )
-            for number in range(extra)
-        ]
-        halves = []
-        for number, array in enumerate(carried):
-            half = array.shape[-2] // 2
-            where = pl.ds(pl.multiple_of(x_bit * half, 16), half)
-            source = carried_in[number]
-            source = source.at[where] if array.ndim == 2 else source.at[:, where]
-            halves.append(pltpu.make_async_copy(source, half_out[number], half_sem.at[number]))
+        small_own = pltpu.make_async_copy(small_ref, small_out.at[frame], own_sem.at[0])
 
         def run(role):
             part_y, part_x, part_z = roles[role]
@@ -1153,9 +1152,6 @@
             small_own.start()
             for step in range(steps):
                 started[step][1].start()
-                own[step].start()
-            for copy in nears + halves:
-                copy.start()
             later = []
             for turn in range(steps + 2):
                 if turn < steps:
@@ -1190,13 +1186,10 @@
                 move(step, None, frame, view(sources[plan[step][0]], step, None, None), None, "core", 3).wait_recv()
                 for part, slot in ((part_y, 4), (part_x, 5), (part_z, 6)):
                     passed(step, part, "core", slot).wait_recv()
-                own[step].wait()
             for sends in later:
                 for copy in sends:
                     copy.wait_send()
-            for copy in smalls + nears:
-                copy.wait()
-            for copy in halves + [small_own]:
+            for copy in smalls + [small_own]:
                 copy.wait()
 
         for role in range(4):
@@ -1207,40 +1200,233 @@
         b16(*array.shape[:-2], array.shape[-2] * frames, array.shape[-1]) for array in arrays
     ]
     outs.append(jax.ShapeDtypeStruct((frames,) + small.shape, small.dtype))
-    outs += [b16(*array.shape) for array in carried]
-    outs += [b16(*array.shape[:-2], array.shape[-2] // 2, array.shape[-1]) for array in carried]
     dma = pltpu.SemaphoreType.DMA
     results = pl.pallas_call(
         kernel,
         out_shape=outs,
-        in_specs=[anywhere] * (count + 1 + extra),
+        in_specs=[anywhere] * (count + 1),
         out_specs=[anywhere] * len(outs),
         scratch_shapes=[
             dma((steps, 7)),
             dma((steps, 7)),
             dma((3,)),
             dma((3,)),
-            dma((extra,)),
-            dma((extra,)),
-            dma((steps,)),
-            dma((extra + 1,)),
+            dma((1,)),
         ],
         compiler_params=pltpu.CompilerParams(collective_id=0, has_side_effects=True),
         cost_estimate=pl.CostEstimate(
-            flops=0, bytes_accessed=200 * 2**20, transcendentals=0
+            flops=0, bytes_accessed=4096, transcendentals=0
         ),
-    )(*arrays, small, *carried)
-    return (
-        results[:count],
-        results[count],
-        results[count + 1 : count + 1 + extra],
-        results[count + 1 + extra :],
-    )
-
-
-def stack_rows(rows):
-    filler = [jnp.zeros_like(rows[0])] * (-len(rows) % 8)
-    return jnp.stack(list(rows) + filler)
+    )(*arrays, small)
+    return ([(whole, own) for whole, own in zip(results[:count], arrays)], results[count])
+
+
+def reduce_piece(row_devices):
+    return max(256, 16 * row_devices)
+
+
+def reduce_all(parts, row_devices):
+    frames, channels = parts[0].shape[0], parts[0].shape[2]
+    sizes = [part.shape[1] for part in parts]
+    piece = reduce_piece(row_devices)
+    count = -(-sum(sizes) // piece)
+    total = count * piece
+    group = row_devices // 2
+    half = piece // 2
+    share = half // group
+
+    def kernel(*refs):
+        sources = refs[: len(parts)]
+        out_ref = refs[len(parts)]
+        (
+            held, from_core, from_y, from_x, halves, from_z,
+            load_sem, core_send, core_recv, y_send, y_recv, x_send, x_recv, z_send, z_recv,
+            back_send, back_recv, last_send, last_recv,
+        ) = refs[len(parts) + 1 :]
+        frame, row = lax.axis_index("frame"), lax.axis_index("rows")
+        frame_bit, core_bit = frame // 2, frame % 2
+        across = (1 - frame_bit) * 2 + core_bit
+        beside = frame_bit * 2 + 1 - core_bit
+        corner = (1 - frame_bit) * 2 + 1 - core_bit
+        x_bit, level = row % 2, row // 2
+        over_x = (frame, row + 1 - 2 * x_bit)
+        peers = [(level + step) % group for step in range(1, group)]
+        barrier = pltpu.get_barrier_semaphore()
+        places = [(beside, row), (across, row), over_x]
+        places += [(frame, peer * 2 + x_bit) for peer in peers]
+        for place in places:
+            pl.semaphore_signal(barrier, inc=1, device_id=place, device_id_type=MESH)
+        loads = []
+        start = 0
+        for number, source in enumerate(sources):
+            loads.append(
+                pltpu.make_async_copy(
+                    source, held.at[:, pl.ds(start, sizes[number])], load_sem.at[number]
+                )
+            )
+            loads[-1].start()
+            start = start + sizes[number]
+        if start < total:
+            held[:, start:, :] = jnp.zeros((frames, total - start, channels), jnp.bfloat16)
+        for load in loads:
+            load.wait()
+        pl.semaphore_wait(barrier, len(places))
+
+        def send(source, target, send_sem, recv_sem, place):
+            return pltpu.make_async_remote_copy(
+                src_ref=source,
+                dst_ref=target,
+                send_sem=send_sem,
+                recv_sem=recv_sem,
+                device_id=place,
+                device_id_type=MESH,
+            )
+
+        def add(first, second):
+            return to_low(first.astype(jnp.float32) + second.astype(jnp.float32))
+
+        def rows(number):
+            return pl.ds(number * piece, piece)
+
+        keep_start = pl.multiple_of(x_bit * half, 16)
+        give_start = pl.multiple_of((1 - x_bit) * half, 16)
+
+        def over_core(number):
+            return [
+                send(
+                    held.at[shard, rows(number)],
+                    from_core.at[slot, rows(number)],
+                    core_send.at[number, slot],
+                    core_recv.at[number, slot],
+                    (beside, row),
+                )
+                for slot, shard in enumerate((beside, corner))
+            ]
+
+        def over_y(number):
+            return send(
+                held.at[across, rows(number)], from_y.at[rows(number)], y_send.at[number],
+                y_recv.at[number], (across, row),
+            )
+
+        def along_x(number):
+            return send(
+                held.at[frame, pl.ds(number * piece + give_start, half)],
+                from_x.at[pl.ds(number * half, half)],
+                x_send.at[number],
+                x_recv.at[number],
+                over_x,
+            )
+
+        def along_z(number, step):
+            peer = peers[step]
+            start = pl.multiple_of(number * half + peer * share, 16)
+            return send(
+                halves.at[pl.ds(start, share)],
+                from_z.at[number, step],
+                z_send.at[number, step],
+                z_recv.at[number, step],
+                (frame, peer * 2 + x_bit),
+            )
+
+        def own_share(number):
+            return pl.ds(
+                pl.multiple_of(number * piece + keep_start + level * share, 16), share
+            )
+
+        def back_z(number, step):
+            return send(
+                out_ref.at[own_share(number)], out_ref.at[own_share(number)],
+                back_send.at[number, step], back_recv.at[number, step],
+                (frame, peers[step] * 2 + x_bit),
+            )
+
+        def back_x(number):
+            keep = pl.ds(pl.multiple_of(number * piece + keep_start, 16), half)
+            return send(
+                out_ref.at[keep], out_ref.at[keep], last_send.at[number], last_recv.at[number],
+                over_x,
+            )
+
+        for number in range(count):
+            for copy in over_core(number):
+                copy.start()
+        for turn in range(count + 4):
+            if turn < count:
+                for copy in over_core(turn):
+                    copy.wait_recv()
+                held[across, rows(turn), :] = add(held[across, rows(turn), :], from_core[1, rows(turn), :])
+                over_y(turn).start()
+                held[frame, rows(turn), :] = add(held[frame, rows(turn), :], from_core[0, rows(turn), :])
+            if 0 <= turn - 1 < count:
+                number = turn - 1
+                over_y(number).wait_recv()
+                held[frame, rows(number), :] = add(held[frame, rows(number), :], from_y[rows(number), :])
+                along_x(number).start()
+            if 0 <= turn - 2 < count:
+                number = turn - 2
+                along_x(number).wait_recv()
+                mine = held[frame, pl.ds(number * piece + keep_start, half), :]
+                where = pl.ds(number * half, half)
+                halves[where, :] = add(mine, from_x[where, :])
+                for step in range(group - 1):
+                    along_z(number, step).start()
+            if 0 <= turn - 3 < count:
+                number = turn - 3
+                start = pl.multiple_of(number * half + level * share, 16)
+                value = halves[pl.ds(start, share), :].astype(jnp.float32)
+                for step in range(group - 1):
+                    along_z(number, step).wait_recv()
+                    value += from_z[number, step].astype(jnp.float32)
+                out_ref[own_share(number), :] = to_low(value)
+                for step in range(group - 1):
+                    back_z(number, step).start()
+            if 0 <= turn - 4 < count:
+                number = turn - 4
+                for step in range(group - 1):
+                    back_z(number, step).wait_recv()
+                back_x(number).start()
+        for number in range(count):
+            back_x(number).wait_recv()
+            for copy in over_core(number) + [over_y(number), along_x(number), back_x(number)]:
+                copy.wait_send()
+            for step in range(group - 1):
+                along_z(number, step).wait_send()
+                back_z(number, step).wait_send()
+
+    dma = pltpu.SemaphoreType.DMA
+    low_type = jnp.bfloat16
+    return pl.pallas_call(
+        kernel,
+        out_shape=b16(total, channels),
+        in_specs=[pl.BlockSpec(memory_space=pl.ANY)] * len(parts),
+        out_specs=pl.BlockSpec(memory_space=pltpu.VMEM),
+        scratch_shapes=[
+            pltpu.VMEM((frames, total, channels), low_type),
+            pltpu.VMEM((2, total, channels), low_type),
+            pltpu.VMEM((total, channels), low_type),
+            pltpu.VMEM((total // 2, channels), low_type),
+            pltpu.VMEM((total // 2, channels), low_type),
+            pltpu.VMEM((count, group - 1, share, channels), low_type),
+            dma((len(parts),)),
+            dma((count, 2)),
+            dma((count, 2)),
+            dma((count,)),
+            dma((count,)),
+            dma((count,)),
+            dma((count,)),
+            dma((count, group - 1)),
+            dma((count, group - 1)),
+            dma((count, group - 1)),
+            dma((count, group - 1)),
+            dma((count,)),
+            dma((count,)),
+        ],
+        compiler_params=pltpu.CompilerParams(
+            collective_id=1, has_side_effects=True, vmem_limit_bytes=40 * 2**20
+        ),
+        cost_estimate=pl.CostEstimate(flops=0, bytes_accessed=4096, transcendentals=0),
+    )(*parts)
 
 
 def on_device(
@@ -1276,7 +1462,6 @@
     valid = places.valid.astype(jnp.float32)
     table = group_table(channels)
     count = (places.safe_side * places.safe_side * (channels // GROUPS)).astype(jnp.float32)
-    inv_count = jnp.broadcast_to(1.0 / count, (channels,))
     lanes = jnp.arange(128, dtype=jnp.int32)[None, :]
     masks = jnp.where(
         lanes == 0,
@@ -1284,7 +1469,7 @@
         jnp.where(lanes == 1, places.cell_col[:, None] > 0, places.cell_col[:, None] < side - 1),
     ).astype(jnp.float32)
     key_bias = jnp.broadcast_to(((valid - 1.0) * -FAR)[None, :], (8, cells))
-    places_row = piece_places()
+    order_row = shard_order()
 
     own = channels // places.frames
     clip_count, prompt_count = prompt_ids.shape
@@ -1303,8 +1488,7 @@
     small_count = small.shape[0]
     small = jnp.pad(small, ((0, -small_count % 8), (0, -own % 128)))
     flat_attn = motion_attn.reshape((-1,) + motion_attn.shape[2:])
-    carried = [motion_proj, flat_attn, motion_ff_in, motion_ff_out]
-    whole, small_all, near, half = gather_all(
+    whole, small_all = gather_all(
         [
             (res_conv.reshape((-1,) + res_conv.shape[3:]), 2),
             (st_proj, 1),
@@ -1312,23 +1496,19 @@
             (st_cross_kv, 1),
             (st_ff_in, 1),
             (st_ff_out, 1),
+            (motion_proj, 1),
+            (flat_attn, 1),
+            (motion_ff_in, 1),
+            (motion_ff_out, 1),
         ],
         small,
-        carried,
-    )
-    conv_all, sproj_all, sattn_all, cross_all, sffin_all, sffout_all = whole
-    mproj_pieces, mattn_pieces, mffin_pieces, mffout_pieces = (
-        exchange_pieces(*triple) for triple in zip(carried, near, half)
-    )
+    )
+    conv_all, sproj_all, sattn_all, cross_all, sffin_all, sffout_all = whole[:6]
+    mproj_all, mattn_all, mffin_all, mffout_all = whole[6:]
     small_all = small_all[:, :small_count, :own]
-
-    def gathered_rows(first, last):
-        rows = jnp.transpose(small_all[:, first:last], (1, 0, 2))
-        return rows.reshape(last - first, channels)
-
     bias_rows = motion_ff_bias.shape[0] // own
-    mgain, mshift = (gathered_rows(0, 4), gathered_rows(4, 13))
-    mffbias = small_all[:, 13 : 13 + bias_rows].reshape(-1)
+    motion_rows = jnp.transpose(small_all[:, :13], (1, 0, 2)).reshape(13, channels)
+    mffbias = small_all[:, 13 : 13 + bias_rows].reshape(1, -1)
     temb_proj = jnp.sum(small_all[:, 13 + bias_rows :], axis=0).reshape(clip_count, channels)
     time_row = lax.dynamic_index_in_dim(temb_proj, places.clip, 0, keepdims=False)
 
@@ -1336,12 +1516,8 @@
     grad_unit = to_low(places.blocks_to_unit(cotangent))
     grad_columns = places.blocks_to_columns(cotangent)
 
-    rgain, rshift = (res_gain.astype(jnp.float32), res_shift.astype(jnp.float32))
-    sgain, sshift, sffbias = (
-        st_gain.astype(jnp.float32),
-        st_shift.astype(jnp.float32),
-        st_ff_bias.astype(jnp.float32),
-    )
+    stats = jnp.stack([jnp.broadcast_to(1.0 / count, (channels,)), time_row])
+    sffbias = st_ff_bias.astype(jnp.float32).reshape(1, -1)
     vocab_rows = embed_table.shape[0]
     local_ids = prompt_ids - lax.axis_index(("frame", "rows")) * vocab_rows
     ids_table = onehot(local_ids.reshape(-1), vocab_rows)
@@ -1354,122 +1530,89 @@
     prompt_row = jnp.broadcast_to(prompt_bias[None, :], (8, prompt_pad))
     prompt_col = jnp.broadcast_to(prompt_bias[:, None], (prompt_pad, 128))
 
-    def wide(row):
-        return jnp.broadcast_to(row[None, :], (8, row.shape[0]))
-
-    vec_one = stack_rows([rgain[0], rshift[0], rshift[2] + time_row, inv_count])
-    vec_two = stack_rows([rgain[1], rshift[1], rshift[3], inv_count])
     conv_one = conv_forward(
-        places_row, side, field, masks, vec_one, table, conv_all, 0, None
+        order_row, side, field, masks, res_gain, res_shift, stats, table, conv_all, 0, None,
+        [],
     )
     resid = conv_forward(
-        places_row, side, conv_one, masks, vec_two, table, conv_all, 1, [field]
-    )
-    vec_self = stack_rows(
-        [
-            sgain[0], sshift[0], sshift[4], sgain[1], sshift[1], sshift[5], sshift[5], inv_count,
-        ]
+        order_row, side, conv_one, masks, res_gain, res_shift, stats, table, conv_all, 1, [field],
+        [],
     )
     proj_one, query, key, value, proj_two = self_forward(
-        places_row, resid, masks, key_bias, vec_self, table, sproj_all, sattn_all
-    )
-    vec_cross = stack_rows(
-        [
-            sgain[2], sshift[2], sshift[6], sgain[3], sshift[3], sshift[7], sshift[8],
-            mgain[0], mshift[0], inv_count,
-        ]
+        order_row, resid, masks, key_bias, st_gain, st_shift, stats, table, sproj_all, sattn_all
     )
     cross_query, cross_key, cross_value, proj_three, st_out, motion_low = cross_forward(
-        places_row, proj_two, resid, context_low, masks, prompt_row, vec_cross, wide(sffbias),
-        table, sproj_all, sattn_all, cross_all, sffin_all, sffout_all,
-    )
-
-    moved = to_low(places.unit_to_columns([motion_low, to_low(st_out)]))
-    motion_in, st_columns = (moved[:, :channels], moved[:, channels:])
+        order_row, [grad_unit], proj_two, resid, context_low, masks, prompt_row, st_gain, st_shift, motion_rows,
+        stats, sffbias, table, sproj_all, sattn_all, cross_all, sffin_all, sffout_all,
+    )
+
+    motion_moved = places.unit_to_columns([motion_low])
+    st_moved = places.unit_to_columns([to_low(st_out)])
     frame_total = places.frames * frames_here
-    position = frame_table(jnp.arange(frame_total, dtype=jnp.int32), channels)
-    position = jnp.broadcast_to(
-        position[None], (places.share_total, frame_total, channels)
-    ).reshape(-1, channels)
+    position = jnp.asarray(np.tile(frame_table(frame_total, channels), (places.share_total, 1)))
     per_group = max(n for n in range(1, 14) if places.share_total % n == 0)
-    cell_of = jnp.arange(per_group * frame_total, dtype=jnp.int32) // frame_total
-    cell_bias = jnp.where(cell_of[:, None] == cell_of[None, :], 0.0, FAR)
-    vec_motion = stack_rows(
-        [mshift[4], mgain[1], mshift[1], mshift[5], mgain[2], mshift[2], mshift[6]]
-    )
+    cell_of = np.arange(per_group * frame_total) // frame_total
+    cell_bias = jnp.asarray(np.where(cell_of[:, None] == cell_of[None, :], 0.0, FAR).astype(np.float32))
     kept = motion_forward(
-        places_row, motion_in, position, cell_bias, vec_motion, mproj_pieces, mattn_pieces
-    )
-    zeds = kept[:3]
-    out_columns, grad_zed, d_proj_out, d_ff_in, d_ff_out, small_ff, wide_ff = motion_ff(
-        places_row, zeds[2], st_columns, grad_columns,
-        stack_rows([mgain[3], mshift[3], mshift[7], mshift[8]]), wide(mffbias),
-        mproj_pieces, mffin_pieces, mffout_pieces,
+        order_row, motion_moved, places.pick_table, position, cell_bias, motion_rows, mproj_all,
+        mattn_all,
+    )
+    zeds, motion_in = (kept[:3], kept[11])
+    out_columns, grad_zed, d_ff, small_sums, wide_sums = motion_ff(
+        order_row, zeds[2], st_moved, places.pick_table, grad_columns, motion_rows, mffbias, mproj_all, mffin_all,
+        mffout_all,
     )
     output = places.columns_to_blocks(out_columns)
-    d_attn = [None, None]
-    small_back = [None, None]
+    d_blocks = [None, None]
     for block in (1, 0):
-        results = motion_back(
-            places_row, block, grad_zed, zeds[block], *kept[3 + 4 * block : 7 + 4 * block],
-            motion_in if block == 0 else None, position, cell_bias,
-            stack_rows([mgain[1 + block], mshift[1 + block]]), mproj_pieces, mattn_pieces,
+        grad_zed, d_blocks[block], small_sums = motion_back(
+            order_row, block, grad_zed, zeds[block], *kept[3 + 4 * block : 7 + 4 * block],
+            motion_in if block == 0 else None, small_sums, position, cell_bias, motion_rows,
+            mproj_all, mattn_all,
         )
-        grad_zed, d_attn[block], small_back[block] = (results[0], results[1:5], results[5])
-    grad_motion, d_proj_in = (grad_zed, results[6])
-
-    def share_rows(gradients):
-        joined = jnp.concatenate(
-            [d.reshape(places.frames, -1, channels) for d in gradients], axis=1
-        )
-        mine = lax.psum_scatter(joined, "frame", scatter_dimension=0, tiled=False)
-        mine = lax.psum(mine, "rows").astype(jnp.float32)
-        shares = []
-        start = 0
-        for d in gradients:
-            size = d.size // places.frames // channels
-            shares.append(mine[start : start + size].reshape(-1, d.shape[1]))
-            start = start + size
-        return shares
-
-    ff_in_grad, ff_out_grad, share_out = share_rows([d_ff_in, d_ff_out, d_proj_out])
-    shares = share_rows([*d_attn[0], *d_attn[1], d_proj_in])
-    attn_grad = jnp.stack(shares[:8]).reshape(motion_attn.shape)
-    proj_grad = jnp.stack([shares[8], share_out])
-
+    grad_motion = grad_zed
+
+    small_rows = jnp.transpose(small_sums[:13].reshape(13, places.frames, own), (1, 0, 2))
+    small_rows = jnp.pad(small_rows, ((0, 0), (0, 0), (0, channels - own)))
+    bias_sums = wide_sums[0].reshape(places.frames, 1, channels)
+    tail = jnp.concatenate([small_rows, bias_sums, jnp.zeros_like(small_rows[:, :2])], axis=1)
+    d_first = lax.dynamic_update_slice(d_blocks[0], to_low(tail), (0, 5 * own, 0))
+
+    def over_frame(gradient):
+        return lax.psum_scatter(gradient, "frame", scatter_dimension=0, tiled=False)
+
+    ff_mine = over_frame(d_ff)
+    ff_sum = lax.psum(ff_mine, "rows").astype(jnp.float32)
+    ff_in_grad = jnp.concatenate([ff_sum[i * own : (i + 1) * own] for i in range(4)], axis=1)
+    ff_out_grad = ff_sum[4 * own : 8 * own]
     grad_gn = to_low(places.columns_to_unit(grad_motion))
-    grad_two, grad_st, small_gn = cross_backward(
-        places_row, grad_gn, grad_unit, st_out, proj_three, proj_two, cross_query, cross_key,
-        cross_value, masks, prompt_col, vec_cross, wide(sffbias), table, sproj_all, sattn_all,
-        sffin_all, sffout_all,
+    grad_two, grad_st = cross_backward(
+        order_row, grad_gn, grad_unit, st_out, proj_three, proj_two, cross_query, cross_key,
+        cross_value, masks, prompt_col, st_gain, st_shift, motion_rows, stats, sffbias, table,
+        sproj_all, sattn_all, sffin_all, sffout_all,
     )
     grad_res = self_backward(
-        places_row, grad_two, proj_one, query, key, value, resid, grad_st, masks, vec_self, table,
-        sproj_all, sattn_all,
+        order_row, [ff_mine], grad_two, proj_one, query, key, value, resid, grad_st, masks, st_gain, st_shift,
+        stats, table, sproj_all, sattn_all,
     )
     grad_conv = conv_backward(
-        places_row, side, grad_res, conv_one, masks, vec_two, table, conv_all, 1, []
+        order_row, side, grad_res, conv_one, masks, res_gain, res_shift, stats, table, conv_all, 1,
+        [],
     )
     grad_field = conv_backward(
-        places_row, side, grad_conv, field, masks, vec_one, table, conv_all, 0, [grad_res]
+        order_row, side, grad_conv, field, masks, res_gain, res_shift, stats, table, conv_all, 0,
+        [grad_res],
     )
     input_grad = places.unit_to_blocks(to_low(grad_field)).astype(jnp.float32)
 
-    gain_rows = [small_gn[0], small_back[0][1], small_back[1][1], small_ff[2]]
-    shift_rows = [
-        small_gn[1], small_back[0][2], small_back[1][2], small_ff[3], small_back[0][3],
-        small_back[0][0], small_back[1][0], small_ff[1], small_ff[0],
-    ]
-    small_grads = jnp.concatenate(
-        [
-            jnp.stack(gain_rows + shift_rows).reshape(13, places.frames, own),
-            jnp.transpose(wide_ff[0].reshape(places.frames, -1, own), (1, 0, 2)),
-        ]
-    )
-    small_grads = lax.psum(small_grads, ("frame", "rows"))
-    small_mine = lax.dynamic_index_in_dim(small_grads, places.frame, 1, keepdims=False)
-    gain_grad, shift_grad = (small_mine[:4], small_mine[4:13])
-    ff_bias_grad = small_mine[13:].reshape(-1)
+    d_first, grad_field = lax.optimization_barrier((d_first, grad_field))
+    attn_sum = reduce_all([d_first, d_blocks[1]], places.rows).astype(jnp.float32)
+    zero_sum, one_sum = (attn_sum[: 5 * own + 16], attn_sum[5 * own + 16 : 9 * own + 16])
+    attn_grad = jnp.concatenate([zero_sum[: 4 * own], one_sum]).reshape(motion_attn.shape)
+    proj_grad = jnp.stack([zero_sum[4 * own : 5 * own], ff_sum[8 * own :]])
+    small_sum = zero_sum[5 * own :]
+    gain_grad, shift_grad, ff_bias_grad = (small_sum[:4, :own], small_sum[4:13, :own], small_sum[13])
+
     return (
         output,
         input_grad,

time: 954 us -> 654 us (0.69)
  Pallas kernels: 534 us -> 434 us
  waiting for transfers between devices: 172 us -> 77.7 us
  local copies, waits for them, and re-layouts: 92.4 us -> 42.8 us
  blocking collectives: 42 us -> 0 us
    pallas_call x1 -> x2, Pallas kernels: 312 us -> 206 us  [the longest x1 116 us: gather_all(): pl.pallas_call(kernel, out_shape=outs, in_specs=[anywhere] * (count + 1),...]
    ppermute x16 -> x0, waiting for transfers between devices: 57.1 us -> none  [swap(): return lax.ppermute(value, axis, [(i, i ^ bit) for i in range(count)])]
    psum x1 -> x0, blocking collectives: 42 us -> none  [on_device(): small_grads = lax.psum(small_grads, ('frame', 'rows'))]
    reduce_scatter x2 -> x1, waiting for transfers between devices: 37.1 us -> 0.02 us  [over_frame(): return lax.psum_scatter(gradient, 'frame', scatter_dimension=0, tiled=False)]
    all_to_all x1 -> x2, waiting for transfers between devices: 0.01 us -> 27.9 us  [unit_to_columns(): received = lax.all_to_all(send, ('frame', 'rows'), 0, 0)]
    slice x28 -> x9, local copies, waits for them, and re-layouts: 23.3 us -> 4.34 us  [the longest x1 1.28 us: on_device(): ff_out_grad = ff_sum[4 * own:8 * own]]
    all_to_all x2, waiting for transfers between devices: 17.6 us -> 0.01 us  [blocks_to_unit(): received = lax.all_to_all(jnp.stack(pieces), 'rows', 0, 0)]
    psum x1, waiting for transfers between devices: 38.2 us -> 25.8 us  [on_device(): ff_sum = lax.psum(ff_mine, 'rows').astype(jnp.float32)]
  transfers between devices with their start and end apart: 27 -> 11, of which waited for: 8 -> 4; matrix products, arithmetic and copies ran while one was open for 10% -> 8% of each run, Pallas kernels for 50% -> 63%
where the time goes in v3:
time: 654 us; the launch traced here: 647 us
  Pallas kernels  434 us (66%)
  waiting for transfers between devices  77.7 us (12%)
  local copies, waits for them, and re-layouts  42.8 us (7%)
  starting transfers between devices  40.7 us (6%)
  between operations  20 us (3%)
  matrix products  17.4 us (3%)
  other arithmetic  14.7 us (2%)
    pallas_call x12, Pallas kernels, run_kernel(): pl.pallas_call(kernel, out_shape=outs, in_specs=[pl.BlockSpec(memory_spac...  228 us
    pallas_call x1, Pallas kernels, gather_all(): pl.pallas_call(kernel, out_shape=outs, in_specs=[anywhere] * (count + 1),...  116 us
    pallas_call x1, Pallas kernels, reduce_all(): pl.pallas_call(kernel, out_shape=b16(total, channels), in_specs=[pl.Block...  90.5 us
    all_to_all x2, waiting for transfers between devices, unit_to_columns(): received = lax.all_to_all(send, ('frame', 'rows'), 0, 0)  27.9 us
    psum x1, waiting for transfers between devices, on_device(): ff_sum = lax.psum(ff_mine, 'rows').astype(jnp.float32)  25.8 us
    all_to_all x1, waiting for transfers between devices, columns_to_unit(): received = lax.all_to_all(send, ('frame', 'rows'), 0, 0)  24 us
    unnamed x54, local copies, waits for them, and re-layouts  18.4 us
    all_to_all x2, starting transfers between devices, blocks_to_unit(): received = lax.all_to_all(jnp.stack(pieces), 'rows', 0, 0)  17.2 us
  transfers between devices with their start and end apart: 11, of which 4 were waited for; matrix products, arithmetic and copies ran while one was open for 8% of the time, Pallas kernels for 63%

profile of v3, /device:TPU:0, one launch (start us, length us, event | category | flops | bytes accessed | tf_op | source)
XLA Modules:
  0.0 647.3 jit_solution(6305923468290844009)
XLA Ops:
  7.2 1.0 slice_bitcast_fusion.15
  8.2 1.5 slice_dynamic-update-slice_fusion.7
  10.4 1.5 slice_dynamic-update-slice_fusion.6
  12.6 1.5 slice_dynamic-update-slice_fusion.5
  14.8 1.5 slice_dynamic-update-slice_fusion.4
  16.9 7.3 %all-to-all-start = ((bf16[8,72,640]{2,1,0:T(8,128)(2,1)}), bf16[8,72,640]{2,1,0:T(8,128)(2,1)}, u32[]{:S(2)}, u32[]{:S(2)}) async-start(bf16[8,72,640]{2,1,0:T(8,128)(2,1)} %bitcast_dynamic-update-slice_fusion.4), calls=%async_computation | async-start | bytes 1474560 | tf_op jit(solution)/shard_map/all_to_all | solution.py:148
  24.4 1.4 convolution_convert_fusion.1
  25.8 1.7 reshape.255
  30.8 115.9 %shard_map.349 = (bf16[18,640,640]{2,1,0:T(8,128)(2,1)}, bf16[2,640,640]{2,1,0:T(8,128)(2,1)}, bf16[6,640,640]{2,1,0:T(8,128)(2,1)}, bf16[2,768,640]{2,1,0:T(8,1...) custom-call(bf16[18,160,640]{2,1,0:T(8,128)(2,1)} %bitcast.114, ...), custom_call_target="tpu_custom_call" | custom-call | bytes 4096 | tf_op jit(solution)/shard_map/pallas_call | solution.py:1204
  146.7 0.9 slice_reduce_fusion
  155.4 9.9 %all-to-all-start.1 = ((bf16[8,72,640]{2,1,0:T(8,128)(2,1)}), bf16[8,72,640]{2,1,0:T(8,128)(2,1)S(1)}, u32[]{:S(2)}, u32[]{:S(2)}) async-start(bf16[8,72,640]{2,1,0:T(8,128)(2,1)} %bitcast_dynamic-update-slice_fusion), calls=%async_computation.1 | async-start | bytes 1474560 | tf_op jit(solution)/shard_map/all_to_all | solution.py:148
  165.3 1.1 maximum_bitcast_fusion
  166.5 1.0 convert_select_fusion.refs_2_.refs_4_.refs_9_.refs_8_.refs_3_
  172.6 1.0 fusion.38
  173.6 0.9 dynamic-slice_bitcast_fusion
  175.2 2.8 fusion.9.refs_1_.refs_7_.refs_2_
  178.0 12.6 %shard_map.350.refs_1_.refs_2_ = f32[576,640]{1,0:T(8,128)} custom-call(s32[4]{0:T(128)} %pad_add_fusion.refs_0_, bf16[576,640]{1,0:T(8,128)(2,1)} %fusion.9.refs_1_.refs_7_.refs_2_, f32[576,128]{1,0:T(8,128)} %convert_select_fusion.refs_2_.refs_4_.refs_9_.refs_8_.refs_3_, bf16[2,640]{1,0:T(2,128)(2,1)} %refs_4_.12, bf16[4,640]{1,0:T(4,128)(2,1)} %refs_5_.7, ...), custom_call_target="tpu_custom_call" | custom-call | flops 4246732 | bytes 4096 | tf_op jit(solution)/shard_map/pallas_call | solution.py:257
  190.6 13.5 %shard_map.351.refs_1_.refs_2_.refs_6_ = f32[576,640]{1,0:T(8,128)} custom-call(s32[4]{0:T(128)} %pad_add_fusion.refs_0_, f32[576,640]{1,0:T(8,128)} %shard_map.350.refs_1_.refs_2_, f32[576,128]{1,0:T(8,128)} %convert_select_fusion.refs_2_.refs_4_.refs_9_.refs_8_.refs_3_, bf16[2,640]{1,0:T(2,128)(2,1)} %refs_4_.12, bf16[4,640]{1,0:T(4,128)(2,1)} %refs_5_.7, ...), custom_call_target="tpu_custom_call" | custom-call | flops 4246732 | bytes 4096 | tf_op jit(solution)/shard_map/pallas_call | solution.py:257
  204.7 14.8 %shard_map.352 = (f32[576,640]{1,0:T(8,128)}, bf16[576,640]{1,0:T(8,128)(2,1)}, bf16[576,640]{1,0:T(8,128)(2,1)}, bf16[576,640]{1,0:T(8,128)(2,1)}, f32[576,640]{1,0:T(8,128)}) custom-call(s32[4]{0:T(128)} %pad_add_fusion.refs_0_, f32[576,640]{1,0:T(8,128)} %shard_map.351.refs_1_.refs_2_.refs_6_, ...), custom_call_target="tpu_custom_call" | custom-call | flops 3208642 | bytes 4096 | tf_op jit(solution)/shard_map/pallas_call | solution.py:257
  219.5 4.4 all-to-all-start.4
  224.0 1.8 fusion.10.refs_22_.refs_2_
  226.3 19.9 %shard_map.353 = (bf16[576,640]{1,0:T(8,128)(2,1)}, bf16[128,640]{1,0:T(8,128)(2,1)}, bf16[128,640]{1,0:T(8,128)(2,1)}, f32[576,640]{1,0:T(8,128)}, f32[576,640]{1,0:T(8,128)}, /*index=5*/bf16[576,640]{1,0:T(8,128)(2,1)}) custom-call(s32[4]{0:T(128)} %pad_add_fusion.refs_0_, f32[576,640]{1,0:T(8,128)} %get-tuple-element.61.refs_1_.refs_5_, ...), custom_call_target="tpu_custom_call" | custom-call | flops 7077888 | bytes 4096 | tf_op jit(solution)/shard_map/pallas_call | solution.py:257
  246.2 2.1 fusion.6
  248.4 1.2 reshape.260
  249.5 6.7 %all-to-all-start.2 = ((bf16[32,18,640]{2,1,0:T(8,128)(2,1)}), bf16[32,18,640]{2,1,0:T(8,128)(2,1)S(1)}, u32[]{:S(2)}, u32[]{:S(2)}) async-start(bf16[32,18,640]{2,1,0:T(8,128)(2,1)} %reshape.260), calls=%async_computation.2 | async-start | bytes 1966080 | tf_op jit(solution)/shard_map/all_to_all | solution.py:172
  256.2 2.4 fusion.7
  258.6 1.2 reshape.262
  259.8 22.6 %all-to-all-done.2 = bf16[32,18,640]{2,1,0:T(8,128)(2,1)S(1)} async-done(((bf16[32,18,640]{2,1,0:T(8,128)(2,1)}), bf16[32,18,640]{2,1,0:T(8,128)(2,1)S(1)}, u32[]{:S(2)}, u32[]{:S(2)}) %all-to-all-start.2) | async-done | bytes 737312 | tf_op jit(solution)/shard_map/all_to_all | solution.py:172
  282.4 2.6 all-to-all-start.3
  286.0 0.9 reshape.266
  286.9 1.1 reshape.261.refs_1_
  288.0 18.0 %shard_map.354 = (f32[416,640]{1,0:T(8,128)}, f32[416,640]{1,0:T(8,128)}, f32[416,640]{1,0:T(8,128)}, bf16[416,640]{1,0:T(8,128)(2,1)}, bf16[416,640]{1,0:T(8,12...) custom-call(s32[4]{0:T(128)} %pad_add_fusion.refs_0_, ...), custom_call_target="tpu_custom_call" | custom-call | flops 3067084 | bytes 4096 | tf_op jit(solution)/shard_map/pallas_call | solution.py:257
  306.0 5.3 all-to-all-done.3
  311.3 1.1 reshape.263.refs_2_
  312.3 25.2 %shard_map.355 = (bf16[416,640]{1,0:T(8,128)(2,1)}, f32[416,640]{1,0:T(8,128)}, bf16[4,1440,640]{2,1,0:T(8,128)(2,1)}, f32[8,640]{1,0:T(8,128)}, f32[8,2560]{1,0:T(8,128)}) custom-call(s32[4]{0:T(128)} %pad_add_fusion.refs_0_, f32[416,640]{1,0:T(8,128)} %get-tuple-element.68.refs_1_, bf16[576,640]{1,0:T(8,128)(2,1)} %reshape.263.refs_2_, ...), custom_call_target="tpu_custom_call" | custom-call | flops 8178892 | bytes 4096 | tf_op jit(solution)/shard_map/pallas_call | solution.py:257
  337.6 17.5 %shard_map.356 = (f32[416,640]{1,0:T(8,128)}, bf16[4,640,640]{2,1,0:T(8,128)(2,1)}, f32[16,640]{1,0:T(8,128)}) custom-call(s32[4]{0:T(128)} %pad_add_fusion.refs_0_, f32[416,640]{1,0:T(8,128)} %get-tuple-element.73.refs_1_, f32[416,640]{1,0:T(8,128)} %get-tuple-element.74.refs_2_, bf16[416,640]{1,0:T(8,128)(2,1)} %get-tuple-element.75.refs_3_, ...), custom_call_target="tpu_custom_call" | custom-call | flops 3067084 | bytes 4096 | tf_op jit(solution)/shard_map/pallas_call | solution.py:257
  355.1 20.0 %shard_map.357 = (bf16[416,640]{1,0:T(8,128)(2,1)}, bf16[4,816,640]{2,1,0:T(8,128)(2,1)}, f32[16,640]{1,0:T(8,128)}) custom-call(s32[4]{0:T(128)} %pad_add_fusion.refs_0_, f32[416,640]{1,0:T(8,128)} %get-tuple-element.80.refs_1_, f32[416,640]{1,0:T(8,128)} %get-tuple-element.81.refs_2_, bf16[416,640]{1,0:T(8,128)(2,1)} %get-tuple-element.82.refs_3_, ...), custom_call_target="tpu_custom_call" | custom-call | flops 3067084 | bytes 4096 | tf_op jit(solution)/shard_map/pallas_call | solution.py:257
  375.2 1.7 fusion.12
  376.9 1.2 reshape.273
  378.1 2.6 all-to-all-start.6
  380.9 0.9 slice.250
  382.0 1.0 copy.67
  383.0 24.0 %all-to-all-done.6 = bf16[32,18,640]{2,1,0:T(8,128)(2,1)S(1)} async-done(((bf16[32,18,640]{2,1,0:T(8,128)(2,1)}), bf16[32,18,640]{2,1,0:T(8,128)(2,1)S(1)}, u32[]{:S(2)}, u32[]{:S(2)}) %all-to-all-start.6) | async-done | bytes 737312 | tf_op jit(solution)/shard_map/all_to_all | solution.py:178
  406.9 3.5 all-to-all-start.5
  410.6 1.7 fusion.8.refs_1_
  413.0 28.3 %shard_map.358 = (f32[576,640]{1,0:T(8,128)}, f32[576,640]{1,0:T(8,128)}) custom-call(s32[4]{0:T(128)} %pad_add_fusion.refs_0_, bf16[576,640]{1,0:T(8,128)(2,1)} %fusion.8.refs_1_, bf16[576,640]{1,0:T(8,128)(2,1)} %fusion.10.refs_22_.refs_2_, f32[576,640]{1,0:T(8,128)} %get-tuple-element.69.refs_3_, f32[576,640]{1,0:T(8,128)} %get-tuple-element.89.refs_4_, ...), custom_call_target="tpu_custom_call" | custom-call | flops 12740198 | bytes 4096 | tf_op jit(solution)/shard_map/pallas_call | solution.py:257
  441.4 24.9 %shard_map.359.refs_1_.refs_8_ = f32[576,640]{1,0:T(8,128)} custom-call(s32[4]{0:T(128)} %pad_add_fusion.refs_0_, f32[576,640]{1,0:T(8,128)} %get-tuple-element.93.refs_1_, f32[576,640]{1,0:T(8,128)} %get-tuple-element.94.refs_2_, bf16[576,640]{1,0:T(8,128)(2,1)} %get-tuple-element.95.refs_3_, bf16[576,640]{1,0:T(8,128)(2,1)} %get-tuple-element.96.refs_4_, ...), custom_call_target="tpu_custom_call" | custom-call | flops 4482662 | bytes 4096 | tf_op jit(solution)/shard_map/pallas_call | solution.py:257
  466.2 16.4 %shard_map.360.refs_1_ = f32[576,640]{1,0:T(8,128)} custom-call(s32[4]{0:T(128)} %pad_add_fusion.refs_0_, f32[576,640]{1,0:T(8,128)} %shard_map.359.refs_1_.refs_8_, f32[576,640]{1,0:T(8,128)} %shard_map.350.refs_1_.refs_2_, f32[576,128]{1,0:T(8,128)} %convert_select_fusion.refs_2_.refs_4_.refs_9_.refs_8_.refs_3_, bf16[2,640]{1,0:T(2,128)(2,1)} %refs_4_.12, ...), custom_call_target="tpu_custom_call" | custom-call | flops 4246732 | bytes 4096 | tf_op jit(solution)/shard_map/pallas_call | solution.py:257
  482.6 16.5 %shard_map.361 = f32[576,640]{1,0:T(8,128)} custom-call(s32[4]{0:T(128)} %pad_add_fusion.refs_0_, f32[576,640]{1,0:T(8,128)} %shard_map.360.refs_1_, bf16[576,640]{1,0:T(8,128)(2,1)} %fusion.9.refs_1_.refs_7_.refs_2_, f32[576,128]{1,0:T(8,128)} %convert_select_fusion.refs_2_.refs_4_.refs_9_.refs_8_.refs_3_, bf16[2,640]{1,0:T(2,128)(2,1)} %refs_4_.12, ...), custom_call_target="tpu_custom_call" | custom-call | flops 4246732 | bytes 4096 | tf_op jit(solution)/shard_map/pallas_call | solution.py:257
  499.2 3.2 fusion.11
  502.4 3.5 all-to-all-start.7
  506.0 0.7 fusion.25.refs_0_
  507.4 0.9 copy.71
  508.3 2.2 copy-done.2
  510.5 1.9 copy-done.3
  512.4 90.5 %shard_map.362 = bf16[1536,640]{1,0:T(8,128)(2,1)S(1)} custom-call(bf16[4,816,640]{2,1,0:T(8,128)(2,1)S(1)} %copy-done.2, bf16[4,640,640]{2,1,0:T(8,128)(2,1)S(1)} %copy-done.3), custom_call_target="tpu_custom_call" | custom-call | bytes 4096 | tf_op jit(solution)/shard_map/pallas_call | solution.py:1399
  605.2 1.9 pad_maximum_fusion
  607.3 1.1 maximum_convert_fusion
  608.4 25.8 %all-reduce.17.cloned.1.call-done = bf16[1440,640]{1,0:T(8,128)(2,1)} async-done(((bf16[1440,640]{1,0:T(8,128)(2,1)}), bf16[1440,640]{1,0:T(8,128)(2,1)}) %all-reduce.17.cloned.1.call-update) | async-done | bytes 1843216 | tf_op jit(solution)/shard_map/psum | solution.py:1585
  634.2 1.7 convert_element_type.113
  636.0 1.0 pad_maximum_fusion.2
  637.0 0.8 copy-done.4
  637.9 1.3 pad_maximum_fusion.1
  639.2 1.3 slice.217
  (127 shorter events, 20.9 us)
Async XLA Ops:
  7.2 17.2 %copy-start = (bf16[1544,768]{1,0:T(8,128)(2,1)S(1)}, bf16[1544,768]{1,0:T(8,128)(2,1)}, u32[]{:S(2)}) copy-start(bf16[1544,768]{1,0:T(8,128)(2,1)} %param.34) | copy-start | bytes 7114756
  7.2 17.1 %copy-start.15 = (s32[2,77]{1,0:T(2,128)S(1)}, s32[2,77]{1,0:T(2,128)}, u32[]{:S(2)}) copy-start(s32[2,77]{1,0:T(2,128)} %param.33) | copy-start | bytes 1852
  16.9 138.4 %all-to-all-start = ((bf16[8,72,640]{2,1,0:T(8,128)(2,1)}), bf16[8,72,640]{2,1,0:T(8,128)(2,1)}, u32[]{:S(2)}, u32[]{:S(2)}) async-start(bf16[8,72,640]{2,1,0:T(8,128)(2,1)} %bitcast_dynamic-update-slice_fusion.4), calls=%async_computation | async-start | bytes 1474560 | tf_op jit(solution)/shard_map/all_to_all | solution.py:148
  24.2 149.4 %all-reduce.15.cloned.1.call-start = ((), (), s32[]{:S(2)}) async-start(), calls=%async_computation.9 | async-start | bytes 491520 | tf_op jit(solution)/shard_map/psum | solution.py:1524
  24.4 3.2 copy-start.18
  24.4 4.5 copy-start.6
  24.4 5.2 copy-start.16
  24.4 5.3 copy-start.8
  24.4 5.6 copy-start.12
  24.4 5.6 copy-start.13
  24.4 5.7 copy-start.14
  30.8 119.6 %slice-start = ((bf16[4,104,640]{2,1,0:T(8,128)(2,1)}), bf16[4,72,640]{2,1,0:T(8,128)(2,1)S(1)}, s32[]{:S(2)}) async-start(bf16[4,104,640]{2,1,0:T(8,128)(2,1)} %param.31), calls=%async_computation.12 | async-start | bytes 737280 | tf_op jit(solution)/shard_map/slice | solution.py:185
  146.7 3.8 slice-start.1
  152.1 14.3 %copy-start.9 = (f32[4,32,256]{2,1,0:T(8,128)S(1)}, f32[4,32,256]{2,1,0:T(8,128)}, u32[]{:S(2)}) copy-start(f32[4,32,256]{2,1,0:T(8,128)} %get-tuple-element.57) | copy-start | bytes 393220
  154.1 14.0 %copy-start.17 = (s32[2]{0:T(128)S(1)}, s32[2]{0:T(128)}, u32[]{:S(2)}) copy-start(s32[2]{0:T(128)} %constant.153.clone) | copy-start | bytes 28
  155.4 15.3 %copy-start.11 = (bf16[5120]{0:T(1024)(128)(2,1)S(1)}, bf16[5120]{0:T(1024)(128)(2,1)}, u32[]{:S(2)}) copy-start(bf16[5120]{0:T(1024)(128)(2,1)} %param.45) | copy-start | bytes 30724
  155.4 64.1 %all-to-all-start.1 = ((bf16[8,72,640]{2,1,0:T(8,128)(2,1)}), bf16[8,72,640]{2,1,0:T(8,128)(2,1)S(1)}, u32[]{:S(2)}, u32[]{:S(2)}) async-start(bf16[8,72,640]{2,1,0:T(8,128)(2,1)} %bitcast_dynamic-update-slice_fusion), calls=%async_computation.1 | async-start | bytes 1474560 | tf_op jit(solution)/shard_map/all_to_all | solution.py:148
  219.5 30.0 %all-to-all-start.4 = ((bf16[4,4,26,640]{3,1,2,0:T(4,128)(2,1)}), bf16[4,4,26,640]{3,1,2,0:T(4,128)(2,1)S(1)}, u32[]{:S(2)}, u32[]{:S(2)}) async-start(bf16[4,4,26,640]{3,1,2,0:T(4,128)(2,1)} %maximum_bitcast_fusion), calls=%async_computation.4 | async-start | bytes 1064960 | tf_op jit(solution)/shard_map/all_to_all | solution.py:189
  249.5 32.9 %all-to-all-start.2 = ((bf16[32,18,640]{2,1,0:T(8,128)(2,1)}), bf16[32,18,640]{2,1,0:T(8,128)(2,1)S(1)}, u32[]{:S(2)}, u32[]{:S(2)}) async-start(bf16[32,18,640]{2,1,0:T(8,128)(2,1)} %reshape.260), calls=%async_computation.2 | async-start | bytes 1966080 | tf_op jit(solution)/shard_map/all_to_all | solution.py:172
  282.4 28.8 %all-to-all-start.3 = ((bf16[32,18,640]{2,1,0:T(8,128)(2,1)}), bf16[32,18,640]{2,1,0:T(8,128)(2,1)S(1)}, u32[]{:S(2)}, u32[]{:S(2)}) async-start(bf16[32,18,640]{2,1,0:T(8,128)(2,1)} %reshape.262), calls=%async_computation.3 | async-start | bytes 1966080 | tf_op jit(solution)/shard_map/all_to_all | solution.py:172
  285.1 156.3 %reduce-scatter.2.cloned.1.call-start = ((), (), s32[]{:S(2)}) async-start(), calls=%async_computation.10 | async-start | bytes 9216000 | tf_op jit(solution)/shard_map/reduce_scatter | solution.py:1582
  355.1 20.0 %copy-start.5 = (bf16[416,576]{1,0:T(8,128)(2,1)S(1)}, bf16[416,576]{1,0:T(8,128)(2,1)}, u32[]{:S(2)}) copy-start(bf16[416,576]{1,0:T(8,128)(2,1)} %constant.154.clone.refs_2_.refs_3_) | copy-start | bytes 1437700
  376.9 3.9 copy-start.10
  376.9 4.9 copy-start.7
  378.1 28.8 %all-to-all-start.6 = ((bf16[32,18,640]{2,1,0:T(8,128)(2,1)}), bf16[32,18,640]{2,1,0:T(8,128)(2,1)S(1)}, u32[]{:S(2)}, u32[]{:S(2)}) async-start(bf16[32,18,640]{2,1,0:T(8,128)(2,1)} %reshape.273), calls=%async_computation.6 | async-start | bytes 1966080 | tf_op jit(solution)/shard_map/all_to_all | solution.py:178
  406.9 95.5 %all-to-all-start.5 = ((bf16[4,4,26,640]{3,1,2,0:T(4,128)(2,1)}), bf16[4,4,26,640]{3,1,2,0:T(4,128)(2,1)S(1)}, u32[]{:S(2)}, u32[]{:S(2)}) async-start(bf16[4,4,26,640]{3,1,2,0:T(4,128)(2,1)} %copy.67), calls=%async_computation.5 | async-start | bytes 1064960 | tf_op jit(solution)/shard_map/all_to_all | solution.py:196
  502.4 104.8 %all-to-all-start.7 = ((bf16[8,72,640]{2,1,0:T(8,128)(2,1)}), bf16[8,72,640]{2,1,0:T(8,128)(2,1)S(1)}, u32[]{:S(2)}, u32[]{:S(2)}) async-start(bf16[8,72,640]{2,1,0:T(8,128)(2,1)} %bitcast.42), calls=%async_computation.8 | async-start | bytes 1474560 | tf_op jit(solution)/shard_map/all_to_all | solution.py:154
  506.0 128.2 %all-reduce.17.cloned.1.call-start = ((), (), s32[]{:S(2)}) async-start(), calls=%async_computation.11 | async-start | bytes 3686400 | tf_op jit(solution)/shard_map/psum | solution.py:1585
  508.3 2.2 copy-start.2
  510.5 1.9 copy-start.3
  635.9 1.8 copy-start.4
  637.8 2.6 copy-start.1
Sparse Core Ops, SparseCore 0:
  31.1 128.5 all-reduce.14
  337.7 73.7 reduce-scatter.1
  510.9 123.2 all-reduce.16

commit v4 on v3

--- a/solution.py
+++ b/solution.py
@@ -22,6 +22,9 @@
 EPSILON = 1e-05
 FAR = -1e30
 MESH = pl.DeviceIdType.MESH
+RECORDING = []
+HOOK = []
+AHEAD = 32
 
 
 def to_low(value):
@@ -100,7 +103,7 @@
         assert self.units <= self.rows
         self.channels = channels
         self.side = max(entry[0] for entry in self.layout)
-        self.block_max = max(entry[1] * entry[2] for entry in self.layout)
+        self.block_max = -(-max(entry[1] * entry[2] for entry in self.layout) // 16) * 16
         self.shares = [-(-entry[1] * entry[2] // self.frames) for entry in self.layout]
         self.share_max = max(self.shares)
         self.share_total = sum(self.shares)
@@ -137,32 +140,25 @@
         slots = np.arange(self.frames * self.rows * self.share_max)
         self.pick_table = jnp.asarray((picks[:, None] == slots[None, :]).astype(jnp.bfloat16))
 
-    def blocks_to_unit(self, blocks):
+    def blocks_by_unit(self, blocks):
         pieces = []
-        for frame in range(self.frames_here):
-            for side, height, width, offset in self.layout:
-                piece = blocks[frame, offset : offset + height * width]
-                pieces.append(jnp.pad(piece, ((0, self.block_max - height * width), (0, 0))))
-        for _ in range(self.units, self.rows):
-            pieces.append(jnp.zeros_like(pieces[0]))
-        received = lax.all_to_all(jnp.stack(pieces), "rows", 0, 0)
-        return matmul(self.block_table, received.reshape(-1, self.channels))
-
-    def unit_to_blocks(self, field_low):
-        send = to_low(matmul_left(self.block_table, field_low))
-        send = send.reshape(self.rows, self.block_max, self.channels)
-        received = lax.all_to_all(send, "rows", 0, 0)
-        frames = []
-        for frame in range(self.frames_here):
-            frames.append(
-                jnp.concatenate(
-                    [
-                        received[frame * self.clips + number, : entry[1] * entry[2]]
-                        for number, entry in enumerate(self.layout)
-                    ]
-                )
-            )
-        return jnp.stack(frames)
+        for side, height, width, offset in self.layout:
+            piece = blocks[:, offset : offset + height * width]
+            pieces.append(jnp.pad(piece, ((0, 0), (0, self.block_max - height * width), (0, 0))))
+        packed = jnp.stack(pieces, axis=1).reshape(self.units, self.block_max, self.channels)
+        return jnp.pad(packed, ((0, self.rows - self.units), (0, 0), (0, 0)))
+
+    def blocks_from_units(self, received):
+        received = received[: self.units].reshape(
+            self.frames_here, self.clips, self.block_max, self.channels
+        )
+        return jnp.concatenate(
+            [
+                received[:, number, : entry[1] * entry[2]]
+                for number, entry in enumerate(self.layout)
+            ],
+            axis=1,
+        )
 
     def unit_to_columns(self, fields_low):
         width = sum(field.shape[-1] for field in fields_low)
@@ -237,6 +233,10 @@
 
 
 def run_kernel(body, order_row, arrays, groups, outs, scratch, flops):
+    if RECORDING:
+        slots = [Slot(out) for out in outs]
+        RECORDING[-1].append((body, arrays, groups, outs, scratch, slots))
+        return slots
     count, pieces = len(arrays), sum(len(group) for group in groups)
     out_count = len(outs)
 
@@ -267,6 +267,11 @@
     )(order_row, *arrays, *flat)
 
 
+def hook():
+    if HOOK:
+        HOOK[-1]()
+
+
 def rows_of(ref):
     value = ref[...].astype(jnp.float32)
     return [value[number : number + 1] for number in range(value.shape[0])]
@@ -367,6 +372,7 @@
         inverse = 1.0 / jnp.sum(powers, axis=1, keepdims=True)
         values = value_ref[rows if bias.shape[0] > 1 else slice(None), lanes] * mask
         out_ref[rows, lanes] += dot_nn(to_low(powers), values) * inverse
+        hook()
 
 
 def attend_back_into(query_ref, key_ref, value_ref, grad_ref, bias, outs, rows, key_rows):
@@ -394,6 +400,7 @@
         if len(outs) > 1:
             outs[1][key_rows, lanes] += dot_nn(grad_scores, queries) * scale
             outs[2][key_rows, lanes] += dot_nn(to_low(probs), grads)
+        hook()
 
 
 ALL = slice(None)
@@ -412,11 +419,10 @@
 
 def conv_rows(gains_ref, shifts_ref, stats_ref, which):
     gains, shifts, stats = rows_of(gains_ref), rows_of(shifts_ref), rows_of(stats_ref)
-    bias = shifts[2 + which] + stats[1] if which == 0 else shifts[2 + which]
-    return [gains[which], shifts[which], bias, stats[0]]
-
-
-def conv_forward(order_row, side, field, masks, gains, shifts, stats, table, weights, which, residual, early):
+    return [gains[which], shifts[which], shifts[2 + which], stats[0]]
+
+
+def conv_forward(order_row, side, field, masks, gains, shifts, stats, table, weights, which, residual, timed):
     cells, channels = field.shape
 
     def body(order_ref, ins, groups, outs, scratch):
@@ -433,30 +439,32 @@
         pre = normed * vec[0] + vec[1]
         act = pre / (1.0 + jnp.exp(-pre)) * valid
         fill_taps(act, masks, pads, side)
-        out_ref[...] = jnp.broadcast_to(vec[2], (cells, channels))
+        bias = vec[2]
+        if timed:
+            bias += ins[-1][pl.ds(timed[1] + lax.axis_index("rows") % timed[2], 1), :]
+        out_ref[...] = jnp.broadcast_to(bias, (cells, channels))
         if residual:
             out_ref[...] += field_resid(ins)
         finish_load(weight, sem.at[0])
 
-        def row_tap(step, carry):
-            rows = pl.ds(pl.multiple_of(step * side, 8), cells)
+        for step in range(3):
+            rows = pl.ds(step * side, cells)
             total = out_ref[...]
             for col in range(3):
                 total += dot_nn(to_low(pads[col, rows, :]), weight[step * 3 + col])
             out_ref[...] = total
-            return carry
-
-        lax.fori_loop(0, 3, row_tap, 0)
+            hook()
 
     def field_resid(ins):
         return ins[6][...].astype(jnp.float32)
 
     arrays = [field, masks, gains, shifts, stats, table] + ([residual[0]] if residual else [])
+    arrays += [timed[0]] if timed else []
     return run_kernel(
         body,
         order_row,
         arrays,
-        [weights, early],
+        [weights],
         [f32(cells, channels)],
         [
             pltpu.VMEM((9, channels, channels), jnp.bfloat16),
@@ -482,15 +490,13 @@
         total_ref[...] = jnp.zeros((cells, channels), jnp.float32)
         finish_load(weight, sem.at[0])
 
-        def row_tap(step, carry):
-            rows = pl.ds(pl.multiple_of(step * side, 8), cells)
+        for step in range(3):
+            rows = pl.ds(step * side, cells)
             total = total_ref[...]
             for col in range(3):
                 total += dot_nt(to_low(pads[col, rows, :]), weight[8 - (step * 3 + col)])
             total_ref[...] = total
-            return carry
-
-        lax.fori_loop(0, 3, row_tap, 0)
+            hook()
         normed, inv_std = group_normed(
             field_ref[...].astype(jnp.float32), valid, table_ref[...], vec[3]
         )
@@ -627,20 +633,18 @@
     ]
 
 
-def cross_forward(order_row, early, two, resid, context, masks, bias, gains, shifts, motion_rows, stats, wide_bias, table, proj, attn, cross, w_in_all, w_out_all):
+def cross_forward(order_row, two, resid, context, masks, bias, gains, shifts, motion_rows, stats, wide_bias, table, proj, attn, cross, w_in_all, w_out_all):
     cells, channels = resid.shape
     prompt, width = context.shape
 
     def body(order_ref, ins, groups, outs, scratch):
         two_ref, resid_ref, context_ref, masks_ref, bias_ref, gains_ref, shifts_ref, motion_rows_ref, stats_ref, wide_ref, table_ref = ins
         query_ref, key_ref, value_ref, three_ref, out_ref, motion_ref = outs
-        weight, kv, w_in, w_out, att, total, sem = scratch
+        weight, kv, w_in, w_out, att, low_in, total, sem = scratch
         for slot, lead in enumerate((6, 7, 1)):
             pair_load(order_ref, groups, lead, weight.at[slot], sem.at[slot])
         for slot in range(2):
             start_load(order_ref, groups[2], slot, kv.at[slot], sem.at[3 + slot])
-        start_load(order_ref, groups[3], None, w_in, sem.at[5])
-        start_load(order_ref, groups[4], None, w_out, sem.at[6])
         vec = cross_rows(gains_ref, shifts_ref, motion_rows_ref, stats_ref)
         normed, _ = layer_normed(two_ref[...])
         low = to_low(normed * vec[0] + vec[1])
@@ -650,6 +654,8 @@
             finish_load(kv.at[slot], sem.at[3 + slot])
             ref[...] = to_low(dot_nn(context_ref[...], kv[slot]))
         attend_into(query_ref, key_ref, value_ref, bias_ref[0:1, :], att, ALL)
+        start_load(order_ref, groups[3], None, w_in, sem.at[5])
+        start_load(order_ref, groups[4], None, w_out, sem.at[6])
         finish_load(weight.at[1], sem.at[1])
         three_ref[...] = two_ref[...] + dot_nn(to_low(att[...]), weight[1]) + vec[2]
         normed, _ = layer_normed(three_ref[...])
@@ -657,21 +663,16 @@
         finish_load(w_in, sem.at[5])
         finish_load(w_out, sem.at[6])
         total[...] = three_ref[...] + vec[5]
-
-        def chunk(step, carry):
-            lanes = pl.ds(pl.multiple_of(step * CHUNK, 128), CHUNK)
-            gates = pl.ds(pl.multiple_of(FF_ST + step * CHUNK, 128), CHUNK)
-            hidden = dot_nn(low_ref(att), w_in[:, lanes]) + wide_ref[0:1, lanes]
-            gate = dot_nn(low_ref(att), w_in[:, gates]) + wide_ref[0:1, gates]
+        low_in[...] = low
+
+        for step in range(FF_ST // CHUNK):
+            lanes = pl.ds(step * CHUNK, CHUNK)
+            gates = pl.ds(FF_ST + step * CHUNK, CHUNK)
+            hidden = dot_nn(low_in[...], w_in[:, lanes]) + wide_ref[0:1, lanes]
+            gate = dot_nn(low_in[...], w_in[:, gates]) + wide_ref[0:1, gates]
             act = to_low(hidden * (gate * half_erf(gate)))
             total[...] += dot_nn(act, w_out[lanes, :])
-            return carry
-
-        def low_ref(ref):
-            return to_low(ref[...])
-
-        att[...] = low.astype(jnp.float32)
-        lax.fori_loop(0, FF_ST // CHUNK, chunk, 0)
+            hook()
         finish_load(weight.at[2], sem.at[2])
         st_out = dot_nn(to_low(total[...]), weight[2]) + vec[6] + resid_ref[...]
         out_ref[...] = st_out
@@ -682,7 +683,7 @@
         body,
         order_row,
         [two, resid, context, masks, bias, gains, shifts, motion_rows, stats, wide_bias, table],
-        [proj, attn, cross, w_in_all, w_out_all, early],
+        [proj, attn, cross, w_in_all, w_out_all],
         [
             b16(cells, channels),
             b16(prompt, channels),
@@ -697,6 +698,7 @@
             pltpu.VMEM((channels, 2 * FF_ST), jnp.bfloat16),
             pltpu.VMEM((FF_ST, channels), jnp.bfloat16),
             pltpu.VMEM((cells, channels), jnp.float32),
+            pltpu.VMEM((cells, channels), jnp.bfloat16),
             pltpu.VMEM((cells, channels), jnp.float32),
             pltpu.SemaphoreType.DMA((7,)),
         ],
@@ -704,12 +706,12 @@
     )
 
 
-def cross_backward(order_row, grad_gn, grad_out, st_out, three, two, query, key, value, masks, bias_col, gains, shifts, motion_rows, stats, wide_bias, table, proj, attn, w_in_all, w_out_all):
+def cross_backward(order_row, grad_gn, cot_blocks, block_table, st_out, three, two, query, key, value, masks, bias_col, gains, shifts, motion_rows, stats, wide_bias, table, proj, attn, w_in_all, w_out_all):
     cells, channels = st_out.shape
     prompt = key.shape[0]
 
     def body(order_ref, ins, groups, outs, scratch):
-        gn_ref, cot_ref, st_ref, three_ref, two_ref, query_ref, key_ref, value_ref, masks_ref, bias_ref, gains_ref, shifts_ref, motion_rows_ref, stats_ref, wide_ref, table_ref = ins
+        gn_ref, cot_ref, blocks_ref, st_ref, three_ref, two_ref, query_ref, key_ref, value_ref, masks_ref, bias_ref, gains_ref, shifts_ref, motion_rows_ref, stats_ref, wide_ref, table_ref = ins
         grad_two_ref, grad_st_ref = outs
         weight, w_in, w_out, low, grad_low, total, grad_att, grad_q, sem = scratch
         pair_load(order_ref, groups, 1, weight.at[0], sem.at[0])
@@ -721,7 +723,7 @@
         valid = masks_ref[:, 0:1]
         grad_motion = gn_ref[...].astype(jnp.float32)
         normed, inv_std = group_normed(st_ref[...], valid, table_ref[...], vec[9])
-        grad_st_ref[...] = cot_ref[...].astype(jnp.float32) + group_back(
+        grad_st_ref[...] = dot_nn(blocks_ref[...], cot_ref[...]) + group_back(
             grad_motion, normed, inv_std, vec[7], valid, table_ref[...], vec[9]
         )
         finish_load(weight.at[0], sem.at[0])
@@ -761,7 +763,7 @@
     return run_kernel(
         body,
         order_row,
-        [grad_gn, grad_out, st_out, three, two, query, key, value, masks, bias_col, gains, shifts, motion_rows, stats, wide_bias, table],
+        [grad_gn, cot_blocks, block_table, st_out, three, two, query, key, value, masks, bias_col, gains, shifts, motion_rows, stats, wide_bias, table],
         [proj, attn, w_in_all, w_out_all],
         [f32(cells, channels), f32(cells, channels)],
         [
@@ -834,9 +836,8 @@
     )
 
 
-def motion_ff(order_row, zed, st_moved, picks, cotangent, vectors, wide_bias, proj, in_pieces, out_pieces):
+def motion_ff(order_row, zed, st_moved, picks, cotangent, vectors, bias_start, hidden_width, proj, in_pieces, out_pieces):
     tokens, channels = zed.shape
-    hidden_width = wide_bias.shape[1]
     frames = 4
     own = channels // frames
     joined = hidden_width // frames + own * (hidden_width // channels) + own
@@ -844,7 +845,7 @@
     assert hidden_width == frames * channels
 
     def body(order_ref, ins, groups, outs, scratch):
-        zed_ref, st_ref, picks_ref, cot_ref, vec_ref, wide_ref = ins
+        zed_ref, st_ref, picks_ref, cot_ref, vec_ref = ins
         out_ref, grad_ref, d_all, small_ref, wide_out = outs
         weight, w_in, w_out, pre, low, grad_low, total, sem = scratch
         start_load(order_ref, groups[1], None, w_in, sem.at[0])
@@ -860,7 +861,7 @@
 
         def forward(step, carry):
             lanes = pl.ds(pl.multiple_of(step * channels, 128), channels)
-            before = dot_nn(low[...], w_in[:, lanes]) + wide_ref[0:1, lanes]
+            before = dot_nn(low[...], w_in[:, lanes]) + vec_ref[pl.ds(bias_start + step, 1), :]
             pre[:, lanes] = before
             total[...] += dot_nn(to_low(before * half_erf(before)), w_out[lanes, :])
             return carry
@@ -909,7 +910,7 @@
     return run_kernel(
         body,
         order_row,
-        [zed, st_moved, picks, cotangent, vectors, wide_bias],
+        [zed, st_moved, picks, cotangent, vectors],
         [proj, in_pieces, out_pieces],
         [
             b16(tokens, channels),
@@ -932,7 +933,7 @@
     )
 
 
-def motion_back(order_row, block, grad_zed, zed, query, key, value, time_out, motion_in, small, position, bias, vectors, proj, attn):
+def motion_back(order_row, block, grad_zed, zed, query, key, value, time_out, motion_in, small, position, bias, vectors, proj, attn, early):
     tokens, channels = zed.shape
     group_len = bias.shape[0]
     leads = [5 + 4 * block, 2 + 4 * block, 3 + 4 * block, 4 + 4 * block] + ([0] if motion_in is not None else [])
@@ -1016,7 +1017,7 @@
         body,
         order_row,
         arrays,
-        [proj, attn],
+        [proj, attn, early],
         outs,
         [
             pltpu.VMEM((len(leads), channels, channels), jnp.bfloat16),
@@ -1041,7 +1042,10 @@
     plan = []
     for number, (shape, pieces) in enumerate(shards):
         if len(shape) == 2:
-            plan.append((number, None, None, part_rows(shape[0], len(plan))))
+            width = shape[1] // pieces
+            for piece in range(pieces):
+                lanes = (piece * width, width)
+                plan.append((number, None, lanes, part_rows(shape[0], len(plan))))
             continue
         step = shape[0] // pieces
         for piece in range(pieces):
@@ -1054,38 +1058,87 @@
     return plan
 
 
-def gather_all(shards, small):
+class Slot:
+    def __init__(self, like):
+        self.shape, self.dtype = like.shape, like.dtype
+        self.ndim, self.size = len(like.shape), math.prod(like.shape)
+
+
+def forward_all(places, shards, small, latent_blocks, block_table, build, plan_of_hooks):
     arrays = [array for array, _ in shards]
     plan = gather_plan([(array.shape, pieces) for array, pieces in shards])
-    frames = lax.axis_size("frame")
-    count = len(arrays)
-    steps = len(plan)
+    frames, row_devices = places.frames, places.rows
+    count, steps = len(arrays), len(plan)
+    channels = places.channels
+    cells = places.side * places.side
     roles = ((0, 1, 2), (1, 0, 2), (2, 1, 0), (2, 0, 1))
+    peers_count = row_devices - 1
+
+    wholes = [
+        Slot(b16(*array.shape[:-2], array.shape[-2] * frames, array.shape[-1])) for array in arrays
+    ]
+    field, params = Slot(b16(cells, channels)), Slot(f32(*small.shape))
+    RECORDING.append([])
+    kept = build(field, params, list(zip(wholes, arrays)))
+    stages = RECORDING.pop()
+
+    vmem_inputs = []
+    for _, stage_arrays, _, _, _, _ in stages:
+        for array in stage_arrays:
+            if not isinstance(array, Slot) and all(array is not seen for seen in vmem_inputs):
+                vmem_inputs.append(array)
+    vmem_outs = [field, params] + list(kept)
+    inner = []
+    for _, _, _, _, _, slots in stages:
+        for slot in slots:
+            if all(slot is not seen for seen in vmem_outs):
+                inner.append(slot)
 
     def kernel(*refs):
-        sources, small_ref = refs[:count], refs[count]
-        base = count + 1
-        targets, small_out = refs[base : base + count], refs[base + count]
-        send, recv, small_send, small_recv, own_sem = refs[base + count + 1 :]
+        refs = list(refs)
+
+        def take(number):
+            taken, refs[:] = refs[:number], refs[number:]
+            return taken
+
+        sources = take(count)
+        small_ref, latent_ref, table_ref = take(3)
+        in_refs = take(len(vmem_inputs))
+        targets = take(count)
+        out_refs = take(len(vmem_outs))
+        inner_refs = take(len(inner))
+        (
+            small_all, latent_all,
+            send, recv, small_send, small_recv, lat_send, lat_recv, own_sem,
+        ) = refs
         frame, row = lax.axis_index("frame"), lax.axis_index("rows")
         frame_bit, core_bit = frame // 2, frame % 2
         across = (1 - frame_bit) * 2 + core_bit
         beside = frame_bit * 2 + 1 - core_bit
         corner = (1 - frame_bit) * 2 + 1 - core_bit
         x_bit, z_bit = row % 2, row // 2 % 2
-        over_x = row + 1 - 2 * x_bit
-        over_z = row + 2 - 4 * z_bit
         over = {
             "y": (across, row),
             "core": (beside, row),
             "corner": (corner, row),
-            "x": (frame, over_x),
-            "z": (frame, over_z),
+            "x": (frame, row + 1 - 2 * x_bit),
+            "z": (frame, row + 2 - 4 * z_bit),
         }
+        peers = [(row + step) % row_devices for step in range(1, row_devices)]
+        def remote(source, target, send_sem, recv_sem, place):
+            return pltpu.make_async_remote_copy(
+                src_ref=source,
+                dst_ref=target,
+                send_sem=send_sem,
+                recv_sem=recv_sem,
+                device_id=place,
+                device_id_type=MESH,
+            )
+
         barrier = pltpu.get_barrier_semaphore()
-        for place in over.values():
+        greeted = [over["y"], over["core"], over["corner"]] + [(frame, peer) for peer in peers]
+        for place in greeted:
             pl.semaphore_signal(barrier, inc=1, device_id=place, device_id_type=MESH)
-        pl.semaphore_wait(barrier, len(over))
 
         def view(ref, step, part, shard):
             number, kind, leads, parts = plan[step]
@@ -1100,149 +1153,241 @@
             start, size = (0, rows) if part is None else parts[part]
             where = pl.ds(begin + start, size)
             if kind is None:
-                return ref.at[where]
+                return ref.at[where, pl.ds(*leads)]
             return ref.at[pl.ds(*leads), where]
 
-        def move(step, part, shard, source, target, way, slot):
-            number = plan[step][0]
-            return pltpu.make_async_remote_copy(
-                src_ref=source,
-                dst_ref=view(targets[number], step, part, shard),
-                send_sem=send.at[step, slot],
-                recv_sem=recv.at[step, slot],
-                device_id=over[way],
-                device_id_type=MESH,
+        def move(step, part, shard, source, way, slot):
+            return remote(
+                source, view(targets[plan[step][0]], step, part, shard), send.at[step, slot],
+                recv.at[step, slot], over[way],
             )
 
+        def fetched(step, part):
+            source = view(sources[plan[step][0]], step, part, None)
+            return move(step, part, frame, source, "y", 0)
+
+        def shared(step):
+            return move(step, None, frame, view(sources[plan[step][0]], step, None, None), "core", 3)
+
+        def passed(step, part, way, slot):
+            source = view(targets[plan[step][0]], step, part, across)
+            return move(step, part, across, source, way, slot)
+
+        def by_role(action):
+            for role in range(4):
+                pl.when((z_bit == role // 2) & (x_bit == role % 2))(functools.partial(action, role))
+
+        def start_fetch(role):
+            for step in range(min(AHEAD, steps)):
+                fetched(step, roles[role][0]).start()
+
+        def act(kind, step):
+            def over_y(role):
+                part = roles[role][0]
+                fetched(step, part).wait_recv()
+                if step + AHEAD < steps:
+                    fetched(step + AHEAD, part).start()
+                passed(step, part, "z", 2).start()
+                if role < 2:
+                    passed(step, part, "x", 1).start()
+                passed(step, part, "core", 4).start()
+                if step + AHEAD < steps:
+                    shared(step + AHEAD).start()
+
+            def over_z(role):
+                part = roles[role][2]
+                passed(step, part, "z", 2).wait_recv()
+                if role >= 2:
+                    passed(step, part, "x", 1).start()
+                passed(step, part, "core", 6).start()
+
+            def over_x(role):
+                part = roles[role][1]
+                passed(step, part, "x", 1).wait_recv()
+                passed(step, part, "core", 5).start()
+
+            def finish(role):
+                shared(step).wait_recv()
+                for part, slot in zip(roles[role], (4, 5, 6)):
+                    passed(step, part, "core", slot).wait_recv()
+
+            by_role({"y": over_y, "z": over_z, "x": over_x, "done": finish}[kind])
+
+        def end_sends(role):
+            part_y, part_x, part_z = roles[role]
+            for step in range(steps):
+                fetched(step, part_y).wait_send()
+                shared(step).wait_send()
+                passed(step, part_y, "z", 2).wait_send()
+                passed(step, part_y if role < 2 else part_z, "x", 1).wait_send()
+                for part, slot in ((part_y, 4), (part_x, 5), (part_z, 6)):
+                    passed(step, part, "core", slot).wait_send()
+
         smalls = [
-            pltpu.make_async_remote_copy(
-                src_ref=small_ref,
-                dst_ref=small_out.at[frame],
-                send_sem=small_send.at[slot],
-                recv_sem=small_recv.at[slot],
-                device_id=over[way],
-                device_id_type=MESH,
-            )
+            remote(small_ref, small_all.at[frame], small_send.at[slot], small_recv.at[slot], over[way])
             for slot, way in enumerate(("y", "core", "corner"))
         ]
-        small_own = pltpu.make_async_copy(small_ref, small_out.at[frame], own_sem.at[0])
-
-        def run(role):
-            part_y, part_x, part_z = roles[role]
-            forward = role >= 2
-
-            def first(step):
-                number = plan[step][0]
-                return [
-                    move(step, part_y, frame, view(sources[number], step, part_y, None), None, "y", 0),
-                    move(step, None, frame, view(sources[number], step, None, None), None, "core", 3),
-                ]
-
-            def passed(step, part, way, slot):
-                number = plan[step][0]
-                return move(
-                    step, part, across, view(targets[number], step, part, across), None, way, slot
+        latent_copies = [
+            remote(latent_ref.at[peer], latent_all.at[row], lat_send.at[step], lat_recv.at[step], (frame, peer))
+            for step, peer in enumerate(peers)
+        ]
+        owns = [
+            pltpu.make_async_copy(small_ref, small_all.at[frame], own_sem.at[0]),
+            pltpu.make_async_copy(latent_ref.at[row], latent_all.at[row], own_sem.at[1]),
+        ]
+        for copy in owns:
+            copy.start()
+        pl.semaphore_wait(barrier, len(greeted))
+        for copy in smalls + latent_copies:
+            copy.start()
+        by_role(start_fetch)
+        for step in range(min(AHEAD, steps)):
+            shared(step).start()
+
+        def run_actions(actions):
+            for action in actions:
+                act(*action)
+
+        for copy in smalls:
+            copy.wait_recv()
+        owns[0].wait()
+        field_ref, params_ref = out_refs[:2]
+        total = small_all[0]
+        for number in range(1, frames):
+            total += small_all[number]
+        params_ref[...] = total
+        for copy in latent_copies:
+            copy.wait_recv()
+        owns[1].wait()
+        blocks = latent_all[...].reshape(-1, channels)
+        field_ref[...] = to_low(dot_nn(table_ref[...], blocks))
+
+        order = [frame, across, beside, corner]
+        known = [(field, field_ref), (params, params_ref)]
+        known += list(zip(vmem_inputs, in_refs)) + list(zip(vmem_outs[2:], out_refs[2:]))
+        known += list(zip(inner, inner_refs)) + list(zip(wholes, targets)) + list(zip(arrays, sources))
+
+        def ref_of(array):
+            return next(ref for held, ref in known if held is array)
+
+        for number, (body, stage_arrays, groups, outs, scratch, slots) in enumerate(stages):
+            before, hooks = plan_of_hooks[number]
+            run_actions(before)
+            pending = list(hooks)
+
+            def hooked():
+                if pending:
+                    run_actions(pending.pop(0))
+
+            HOOK.append(hooked)
+
+            def stage(*scratch_refs):
+                body(
+                    order,
+                    [ref_of(array) for array in stage_arrays],
+                    [[ref_of(array) for array in group] for group in groups],
+                    [ref_of(slot) for slot in slots],
+                    scratch_refs,
                 )
 
-            started = [first(step) for step in range(steps)]
-            for step in range(steps):
-                started[step][0].start()
-            for copy in smalls:
-                copy.start()
-            small_own.start()
-            for step in range(steps):
-                started[step][1].start()
-            later = []
-            for turn in range(steps + 2):
-                if turn < steps:
-                    started[turn][0].wait_recv()
-                    sends = [passed(turn, part_y, "z", 2), passed(turn, part_y, "core", 4)]
-                    if not forward:
-                        sends.insert(1, passed(turn, part_y, "x", 1))
-                    for copy in sends:
-                        copy.start()
-                    later.append(sends)
-                if 1 <= turn <= steps:
-                    step = turn - 1
-                    arrival = passed(step, part_z, "z", 2)
-                    arrival.wait_recv()
-                    sends = [passed(step, part_z, "core", 6)]
-                    if forward:
-                        sends.insert(0, passed(step, part_z, "x", 1))
-                    for copy in sends:
-                        copy.start()
-                    later.append(sends)
-                if turn >= 2:
-                    step = turn - 2
-                    arrival = passed(step, part_x, "x", 1)
-                    arrival.wait_recv()
-                    sends = [passed(step, part_x, "core", 5)]
-                    for copy in sends:
-                        copy.start()
-                    later.append(sends)
-            for step in range(steps):
-                for copy in started[step]:
-                    copy.wait_send()
-                move(step, None, frame, view(sources[plan[step][0]], step, None, None), None, "core", 3).wait_recv()
-                for part, slot in ((part_y, 4), (part_x, 5), (part_z, 6)):
-                    passed(step, part, "core", slot).wait_recv()
-            for sends in later:
-                for copy in sends:
-                    copy.wait_send()
-            for copy in smalls + [small_own]:
-                copy.wait()
-
-        for role in range(4):
-            pl.when((z_bit == role // 2) & (x_bit == role % 2))(functools.partial(run, role))
+            pl.run_scoped(stage, *scratch)
+            HOOK.pop()
+            for rest in pending:
+                run_actions(rest)
+        run_actions(plan_of_hooks[len(stages)][0])
+        by_role(end_sends)
+        for copy in smalls + latent_copies:
+            copy.wait_send()
 
     anywhere = pl.BlockSpec(memory_space=pl.ANY)
-    outs = [
-        b16(*array.shape[:-2], array.shape[-2] * frames, array.shape[-1]) for array in arrays
-    ]
-    outs.append(jax.ShapeDtypeStruct((frames,) + small.shape, small.dtype))
+    whole_block = pl.BlockSpec(memory_space=pltpu.VMEM)
+    as_shape = lambda slot: jax.ShapeDtypeStruct(slot.shape, slot.dtype)
     dma = pltpu.SemaphoreType.DMA
     results = pl.pallas_call(
         kernel,
-        out_shape=outs,
-        in_specs=[anywhere] * (count + 1),
-        out_specs=[anywhere] * len(outs),
-        scratch_shapes=[
+        out_shape=[as_shape(slot) for slot in wholes] + [as_shape(slot) for slot in vmem_outs],
+        in_specs=[anywhere] * (count + 2) + [whole_block] * (1 + len(vmem_inputs)),
+        out_specs=[anywhere] * count + [whole_block] * len(vmem_outs),
+        scratch_shapes=[pltpu.VMEM(slot.shape, slot.dtype) for slot in inner]
+        + [
+            pltpu.VMEM((frames,) + small.shape, jnp.float32),
+            pltpu.VMEM(latent_blocks.shape, jnp.bfloat16),
             dma((steps, 7)),
             dma((steps, 7)),
             dma((3,)),
             dma((3,)),
-            dma((1,)),
+            dma((peers_count,)),
+            dma((peers_count,)),
+            dma((2,)),
         ],
-        compiler_params=pltpu.CompilerParams(collective_id=0, has_side_effects=True),
-        cost_estimate=pl.CostEstimate(
-            flops=0, bytes_accessed=4096, transcendentals=0
+        compiler_params=pltpu.CompilerParams(
+            collective_id=0, has_side_effects=True, vmem_limit_bytes=58 * 2**20
         ),
-    )(*arrays, small)
-    return ([(whole, own) for whole, own in zip(results[:count], arrays)], results[count])
+        cost_estimate=pl.CostEstimate(flops=0, bytes_accessed=4096, transcendentals=0),
+    )(*arrays, small, latent_blocks, block_table, *vmem_inputs)
+    wholes_out = list(zip(results[:count], arrays))
+    return (wholes_out, results[count], results[count + 1], results[count + 2 :])
 
 
 def reduce_piece(row_devices):
     return max(256, 16 * row_devices)
 
 
-def reduce_all(parts, row_devices):
+def reduce_all(parts, summed, row_devices, build, fused, plan_of_hooks, block_table, block_max):
     frames, channels = parts[0].shape[0], parts[0].shape[2]
     sizes = [part.shape[1] for part in parts]
     piece = reduce_piece(row_devices)
     count = -(-sum(sizes) // piece)
     total = count * piece
+    more = -(-summed.shape[0] // piece)
+    every = count + more
     group = row_devices // 2
     half = piece // 2
     share = half // group
+    stages = []
+    if fused:
+        RECORDING.append(stages)
+    (result,) = build()
+    if fused:
+        RECORDING.pop()
+    vmem_inputs, any_inputs, inner = ([] if fused else [result]), [], []
+
+    def note(array, seen):
+        if all(array is not other for other in seen):
+            seen.append(array)
+
+    for _, stage_arrays, groups, _, _, slots in stages:
+        for array in stage_arrays:
+            if not isinstance(array, Slot):
+                note(array, vmem_inputs)
+        for array in [array for held_group in groups for array in held_group]:
+            note(array, any_inputs)
+        inner += slots
 
     def kernel(*refs):
-        sources = refs[: len(parts)]
-        out_ref = refs[len(parts)]
+        refs = list(refs)
+
+        def take(number):
+            taken, refs[:] = refs[:number], refs[number:]
+            return taken
+
+        sources = take(len(parts))
+        any_refs = take(len(any_inputs))
+        (summed_ref, blocks_ref) = take(2)
+        in_refs = take(len(vmem_inputs))
+        out_ref, moved_ref = take(2)
+        inner_refs = take(len(inner))
+        known = list(zip(any_inputs, any_refs)) + list(zip(vmem_inputs, in_refs))
+        known += list(zip(inner, inner_refs))
+
+        def ref_of(array):
+            return next(ref for held_array, ref in known if held_array is array)
+
         (
-            held, from_core, from_y, from_x, halves, from_z,
+            held, ready, leaving, from_core, from_y, from_x, halves, from_z,
             load_sem, core_send, core_recv, y_send, y_recv, x_send, x_recv, z_send, z_recv,
-            back_send, back_recv, last_send, last_recv,
-        ) = refs[len(parts) + 1 :]
+            back_send, back_recv, last_send, last_recv, move_send, move_recv,
+        ) = refs
         frame, row = lax.axis_index("frame"), lax.axis_index("rows")
         frame_bit, core_bit = frame // 2, frame % 2
         across = (1 - frame_bit) * 2 + core_bit
@@ -1253,7 +1398,8 @@
         peers = [(level + step) % group for step in range(1, group)]
         barrier = pltpu.get_barrier_semaphore()
         places = [(beside, row), (across, row), over_x]
-        places += [(frame, peer * 2 + x_bit) for peer in peers]
+        row_peers = [(row + step) % row_devices for step in range(1, row_devices)]
+        places = places[:2] + [(frame, peer) for peer in row_peers]
         for place in places:
             pl.semaphore_signal(barrier, inc=1, device_id=place, device_id_type=MESH)
         loads = []
@@ -1266,6 +1412,16 @@
             )
             loads[-1].start()
             start = start + sizes[number]
+        loads.append(
+            pltpu.make_async_copy(
+                summed_ref, ready.at[pl.ds(0, summed.shape[0])], load_sem.at[len(sources)]
+            )
+        )
+        loads[-1].start()
+        if summed.shape[0] < more * piece:
+            ready[summed.shape[0] :, :] = jnp.zeros(
+                (more * piece - summed.shape[0], channels), jnp.bfloat16
+            )
         if start < total:
             held[:, start:, :] = jnp.zeros((frames, total - start, channels), jnp.bfloat16)
         for load in loads:
@@ -1309,9 +1465,14 @@
                 y_recv.at[number], (across, row),
             )
 
+        def own_rows(number, start):
+            if number < count:
+                return held.at[frame, pl.ds(number * piece + start, half)]
+            return ready.at[pl.ds((number - count) * piece + start, half)]
+
         def along_x(number):
             return send(
-                held.at[frame, pl.ds(number * piece + give_start, half)],
+                own_rows(number, give_start),
                 from_x.at[pl.ds(number * half, half)],
                 x_send.at[number],
                 x_recv.at[number],
@@ -1351,44 +1512,103 @@
         for number in range(count):
             for copy in over_core(number):
                 copy.start()
-        for turn in range(count + 4):
+
+        def stage_core(number):
+            for copy in over_core(number):
+                copy.wait_recv()
+            held[across, rows(number), :] = add(
+                held[across, rows(number), :], from_core[1, rows(number), :]
+            )
+            over_y(number).start()
+            held[frame, rows(number), :] = add(
+                held[frame, rows(number), :], from_core[0, rows(number), :]
+            )
+
+        def stage_y(number):
+            if number < count:
+                over_y(number).wait_recv()
+                held[frame, rows(number), :] = add(
+                    held[frame, rows(number), :], from_y[rows(number), :]
+                )
+            along_x(number).start()
+
+        def stage_x(number):
+            along_x(number).wait_recv()
+            where = pl.ds(number * half, half)
+            halves[where, :] = add(own_rows(number, keep_start)[...], from_x[where, :])
+            for step in range(group - 1):
+                along_z(number, step).start()
+
+        def stage_z(number):
+            start = pl.multiple_of(number * half + level * share, 16)
+            value = halves[pl.ds(start, share), :].astype(jnp.float32)
+            for step in range(group - 1):
+                along_z(number, step).wait_recv()
+                value += from_z[number, step].astype(jnp.float32)
+            out_ref[own_share(number), :] = to_low(value)
+            for step in range(group - 1):
+                back_z(number, step).start()
+
+        def stage_back(number):
+            for step in range(group - 1):
+                back_z(number, step).wait_recv()
+            back_x(number).start()
+
+        steps_on = (stage_y, stage_x, stage_z, stage_back)
+
+        def take_turn(turn):
             if turn < count:
-                for copy in over_core(turn):
-                    copy.wait_recv()
-                held[across, rows(turn), :] = add(held[across, rows(turn), :], from_core[1, rows(turn), :])
-                over_y(turn).start()
-                held[frame, rows(turn), :] = add(held[frame, rows(turn), :], from_core[0, rows(turn), :])
-            if 0 <= turn - 1 < count:
-                number = turn - 1
-                over_y(number).wait_recv()
-                held[frame, rows(number), :] = add(held[frame, rows(number), :], from_y[rows(number), :])
-                along_x(number).start()
-            if 0 <= turn - 2 < count:
-                number = turn - 2
-                along_x(number).wait_recv()
-                mine = held[frame, pl.ds(number * piece + keep_start, half), :]
-                where = pl.ds(number * half, half)
-                halves[where, :] = add(mine, from_x[where, :])
-                for step in range(group - 1):
-                    along_z(number, step).start()
-            if 0 <= turn - 3 < count:
-                number = turn - 3
-                start = pl.multiple_of(number * half + level * share, 16)
-                value = halves[pl.ds(start, share), :].astype(jnp.float32)
-                for step in range(group - 1):
-                    along_z(number, step).wait_recv()
-                    value += from_z[number, step].astype(jnp.float32)
-                out_ref[own_share(number), :] = to_low(value)
-                for step in range(group - 1):
-                    back_z(number, step).start()
-            if 0 <= turn - 4 < count:
-                number = turn - 4
-                for step in range(group - 1):
-                    back_z(number, step).wait_recv()
-                back_x(number).start()
+                stage_core(turn)
+            for late, step in enumerate(steps_on):
+                if 0 <= turn - late < more:
+                    step(count + turn - late)
+                if 0 <= turn - 1 - late < count:
+                    step(turn - 1 - late)
+
+        order = [frame, across, beside, corner]
+        turns = list(range(max(count + 4, more + 3)))
+        for number, (body, stage_arrays, groups, outs, scratch, slots) in enumerate(stages):
+            pending = list(plan_of_hooks[number])
+
+            def hooked():
+                if pending and pending.pop(0) and turns:
+                    take_turn(turns.pop(0))
+
+            HOOK.append(hooked)
+
+            def stage(*scratch_refs):
+                body(
+                    order,
+                    [ref_of(array) for array in stage_arrays],
+                    [[ref_of(array) for array in held_group] for held_group in groups],
+                    [ref_of(slot) for slot in slots],
+                    scratch_refs,
+                )
+
+            pl.run_scoped(stage, *scratch)
+            HOOK.pop()
+        values = to_low(dot_tn(blocks_ref[...], to_low(ref_of(result)[...])))
+        leaving[...] = values.reshape(row_devices, block_max, channels)
+        moves = [
+            send(
+                leaving.at[peer], moved_ref.at[row], move_send.at[step], move_recv.at[step],
+                (frame, peer),
+            )
+            for step, peer in enumerate(row_peers)
+        ]
+        for copy in moves:
+            copy.start()
+        moved_ref[row] = leaving[row]
+        for turn in turns:
+            take_turn(turn)
+        for copy in moves:
+            copy.wait()
         for number in range(count):
+            for copy in over_core(number) + [over_y(number)]:
+                copy.wait_send()
+        for number in range(every):
             back_x(number).wait_recv()
-            for copy in over_core(number) + [over_y(number), along_x(number), back_x(number)]:
+            for copy in [along_x(number), back_x(number)]:
                 copy.wait_send()
             for step in range(group - 1):
                 along_z(number, step).wait_send()
@@ -1396,37 +1616,46 @@
 
     dma = pltpu.SemaphoreType.DMA
     low_type = jnp.bfloat16
-    return pl.pallas_call(
+    anywhere = pl.BlockSpec(memory_space=pl.ANY)
+    whole_block = pl.BlockSpec(memory_space=pltpu.VMEM)
+    results = pl.pallas_call(
         kernel,
-        out_shape=b16(total, channels),
-        in_specs=[pl.BlockSpec(memory_space=pl.ANY)] * len(parts),
-        out_specs=pl.BlockSpec(memory_space=pltpu.VMEM),
-        scratch_shapes=[
+        out_shape=[b16(every * piece, channels), b16(row_devices, block_max, channels)],
+        in_specs=[anywhere] * (len(parts) + len(any_inputs) + 1)
+        + [whole_block] * (1 + len(vmem_inputs)),
+        out_specs=[whole_block] * 2,
+        scratch_shapes=[pltpu.VMEM(slot.shape, slot.dtype) for slot in inner]
+        + [
             pltpu.VMEM((frames, total, channels), low_type),
+            pltpu.VMEM((more * piece, channels), low_type),
+            pltpu.VMEM((row_devices, block_max, channels), low_type),
             pltpu.VMEM((2, total, channels), low_type),
             pltpu.VMEM((total, channels), low_type),
-            pltpu.VMEM((total // 2, channels), low_type),
-            pltpu.VMEM((total // 2, channels), low_type),
-            pltpu.VMEM((count, group - 1, share, channels), low_type),
-            dma((len(parts),)),
+            pltpu.VMEM((every * half, channels), low_type),
+            pltpu.VMEM((every * half, channels), low_type),
+            pltpu.VMEM((every, group - 1, share, channels), low_type),
+            dma((len(parts) + 1,)),
             dma((count, 2)),
             dma((count, 2)),
             dma((count,)),
             dma((count,)),
-            dma((count,)),
-            dma((count,)),
-            dma((count, group - 1)),
-            dma((count, group - 1)),
-            dma((count, group - 1)),
-            dma((count, group - 1)),
-            dma((count,)),
-            dma((count,)),
+            dma((every,)),
+            dma((every,)),
+            dma((every, group - 1)),
+            dma((every, group - 1)),
+            dma((every, group - 1)),
+            dma((every, group - 1)),
+            dma((every,)),
+            dma((every,)),
+            dma((row_devices - 1,)),
+            dma((row_devices - 1,)),
         ],
         compiler_params=pltpu.CompilerParams(
-            collective_id=1, has_side_effects=True, vmem_limit_bytes=40 * 2**20
+            collective_id=1, has_side_effects=True, vmem_limit_bytes=60 * 2**20
         ),
         cost_estimate=pl.CostEstimate(flops=0, bytes_accessed=4096, transcendentals=0),
-    )(*parts)
+    )(*parts, *any_inputs, summed, block_table, *vmem_inputs)
+    return (results[0][:total], results[0][total : total + summed.shape[0]], results[1])
 
 
 def on_device(
@@ -1477,18 +1706,63 @@
     time_low = to_low(jax.nn.silu(time_table(timesteps)))
     time_mine = lax.dynamic_slice_in_dim(time_low, places.frame * own_temb, own_temb, 1)
     time_part = matmul(time_mine, temb_weight)
+    own_lanes = jnp.arange(channels, dtype=jnp.int32) // own == places.frame
+    vectors = jnp.concatenate([motion_gain, motion_shift]).astype(jnp.float32)
+    bias_rows = motion_ff_bias.shape[0] * places.frames // channels
+    own_bias = jnp.arange(bias_rows)[:, None] == places.frame * (bias_rows // places.frames)
     small = jnp.concatenate(
         [
-            motion_gain.astype(jnp.float32),
-            motion_shift.astype(jnp.float32),
-            motion_ff_bias.astype(jnp.float32).reshape(-1, own),
-            time_part.reshape(-1, own),
+            jnp.where(own_lanes[None, :], jnp.tile(vectors, (1, places.frames)), 0.0),
+            jnp.where(own_bias, motion_ff_bias.astype(jnp.float32).reshape(1, channels), 0.0),
+            time_part,
         ]
     )
-    small_count = small.shape[0]
-    small = jnp.pad(small, ((0, -small_count % 8), (0, -own % 128)))
+    small = jnp.pad(small, ((0, -small.shape[0] % 8), (0, 0)))
     flat_attn = motion_attn.reshape((-1,) + motion_attn.shape[2:])
-    whole, small_all = gather_all(
+    stats = jnp.broadcast_to(1.0 / count, (8, channels))
+    sffbias = st_ff_bias.astype(jnp.float32).reshape(1, -1)
+    grad_columns = places.blocks_to_columns(cotangent)
+    cot_blocks = lax.all_to_all(places.blocks_by_unit(cotangent), "rows", 0, 0)
+
+    vocab_rows = embed_table.shape[0]
+    local_ids = prompt_ids - lax.axis_index(("frame", "rows")) * vocab_rows
+    ids_table = onehot(local_ids.reshape(-1), vocab_rows)
+    prompt_pad = -(-prompt_count // 16) * 16
+    context = lax.psum(to_low(matmul(ids_table, embed_table)), ("frame", "rows"))
+    context = context.reshape(clip_count, prompt_count, -1)
+    context_low = lax.dynamic_index_in_dim(context, places.clip, 0, keepdims=False)
+    context_low = jnp.pad(context_low, ((0, prompt_pad - prompt_count), (0, 0)))
+    prompt_bias = jnp.where(jnp.arange(prompt_pad) < prompt_count, 0.0, FAR)
+    prompt_row = jnp.broadcast_to(prompt_bias[None, :], (8, prompt_pad))
+    prompt_col = jnp.broadcast_to(prompt_bias[:, None], (prompt_pad, 128))
+
+    def build(field, params, whole):
+        conv_all, sproj_all, sattn_all, cross_all, sffin_all, sffout_all = whole[:6]
+        timed = (params, 13 + bias_rows, clip_count)
+        conv_one = conv_forward(
+            None, side, field, masks, res_gain, res_shift, stats, table, conv_all, 0, None, timed
+        )
+        resid = conv_forward(
+            None, side, conv_one, masks, res_gain, res_shift, stats, table, conv_all, 1, [field],
+            None,
+        )
+        proj_one, query, key, value, proj_two = self_forward(
+            None, resid, masks, key_bias, st_gain, st_shift, stats, table, sproj_all, sattn_all
+        )
+        return [conv_one, resid, proj_one, query, key, value, proj_two]
+
+    def acts(text):
+        ways = {"y": "y", "z": "z", "x": "x", "d": "done"}
+        return [(ways[word[0]], int(word[1:] or 0)) for word in text.split()]
+
+    hooks = [
+        (acts("y0 y1 z0") + acts("y2 x0 z1") + acts("d0"), [acts("y3 z2"), acts("y4 x2"), []]),
+        (acts("x1 z3 d1"), [acts("y5 z4"), [], acts("y6")]),
+        (acts("x3 d2 d3"), [acts("x4"), acts("y7"), acts("z5"), [], acts("z6"), acts("y8"), acts("x5"), []]),
+        (acts("x6 z7 d4") + acts("y9 x7 z8") + acts("y10 d5 z9") + acts("x8 z10 d6") + acts("d7 x9 x10") + acts("d8 d9 d10"), []),
+    ]
+    whole, field, params, kept = forward_all(
+        places,
         [
             (res_conv.reshape((-1,) + res_conv.shape[3:]), 2),
             (st_proj, 1),
@@ -1502,47 +1776,17 @@
             (motion_ff_out, 1),
         ],
         small,
+        places.blocks_by_unit(latents),
+        places.block_table,
+        build,
+        hooks,
     )
     conv_all, sproj_all, sattn_all, cross_all, sffin_all, sffout_all = whole[:6]
     mproj_all, mattn_all, mffin_all, mffout_all = whole[6:]
-    small_all = small_all[:, :small_count, :own]
-    bias_rows = motion_ff_bias.shape[0] // own
-    motion_rows = jnp.transpose(small_all[:, :13], (1, 0, 2)).reshape(13, channels)
-    mffbias = small_all[:, 13 : 13 + bias_rows].reshape(1, -1)
-    temb_proj = jnp.sum(small_all[:, 13 + bias_rows :], axis=0).reshape(clip_count, channels)
-    time_row = lax.dynamic_index_in_dim(temb_proj, places.clip, 0, keepdims=False)
-
-    field = to_low(places.blocks_to_unit(latents))
-    grad_unit = to_low(places.blocks_to_unit(cotangent))
-    grad_columns = places.blocks_to_columns(cotangent)
-
-    stats = jnp.stack([jnp.broadcast_to(1.0 / count, (channels,)), time_row])
-    sffbias = st_ff_bias.astype(jnp.float32).reshape(1, -1)
-    vocab_rows = embed_table.shape[0]
-    local_ids = prompt_ids - lax.axis_index(("frame", "rows")) * vocab_rows
-    ids_table = onehot(local_ids.reshape(-1), vocab_rows)
-    context = lax.psum(to_low(matmul(ids_table, embed_table)), ("frame", "rows"))
-    context = context.reshape(clip_count, prompt_count, -1)
-    context_low = lax.dynamic_index_in_dim(context, places.clip, 0, keepdims=False)
-    prompt_pad = -(-prompt_count // 128) * 128
-    context_low = jnp.pad(context_low, ((0, prompt_pad - prompt_count), (0, 0)))
-    prompt_bias = jnp.where(jnp.arange(prompt_pad) < prompt_count, 0.0, FAR)
-    prompt_row = jnp.broadcast_to(prompt_bias[None, :], (8, prompt_pad))
-    prompt_col = jnp.broadcast_to(prompt_bias[:, None], (prompt_pad, 128))
-
-    conv_one = conv_forward(
-        order_row, side, field, masks, res_gain, res_shift, stats, table, conv_all, 0, None,
-        [],
-    )
-    resid = conv_forward(
-        order_row, side, conv_one, masks, res_gain, res_shift, stats, table, conv_all, 1, [field],
-        [],
-    )
-    proj_one, query, key, value, proj_two = self_forward(
-        order_row, resid, masks, key_bias, st_gain, st_shift, stats, table, sproj_all, sattn_all
-    )
+    conv_one, resid, proj_one, query, key, value, proj_two = kept
+    motion_rows = params
     cross_query, cross_key, cross_value, proj_three, st_out, motion_low = cross_forward(
-        order_row, [grad_unit], proj_two, resid, context_low, masks, prompt_row, st_gain, st_shift, motion_rows,
+        order_row, proj_two, resid, context_low, masks, prompt_row, st_gain, st_shift, params,
         stats, sffbias, table, sproj_all, sattn_all, cross_all, sffin_all, sffout_all,
     )
 
@@ -1559,8 +1803,8 @@
     )
     zeds, motion_in = (kept[:3], kept[11])
     out_columns, grad_zed, d_ff, small_sums, wide_sums = motion_ff(
-        order_row, zeds[2], st_moved, places.pick_table, grad_columns, motion_rows, mffbias, mproj_all, mffin_all,
-        mffout_all,
+        order_row, zeds[2], st_moved, places.pick_table, grad_columns, motion_rows, 13, channels * bias_rows,
+        mproj_all, mffin_all, mffout_all,
     )
     output = places.columns_to_blocks(out_columns)
     d_blocks = [None, None]
@@ -1568,7 +1812,7 @@
         grad_zed, d_blocks[block], small_sums = motion_back(
             order_row, block, grad_zed, zeds[block], *kept[3 + 4 * block : 7 + 4 * block],
             motion_in if block == 0 else None, small_sums, position, cell_bias, motion_rows,
-            mproj_all, mattn_all,
+            mproj_all, mattn_all, [cot_blocks] if block == 1 else [],
         )
     grad_motion = grad_zed
 
@@ -1582,31 +1826,38 @@
         return lax.psum_scatter(gradient, "frame", scatter_dimension=0, tiled=False)
 
     ff_mine = over_frame(d_ff)
-    ff_sum = lax.psum(ff_mine, "rows").astype(jnp.float32)
-    ff_in_grad = jnp.concatenate([ff_sum[i * own : (i + 1) * own] for i in range(4)], axis=1)
-    ff_out_grad = ff_sum[4 * own : 8 * own]
     grad_gn = to_low(places.columns_to_unit(grad_motion))
     grad_two, grad_st = cross_backward(
-        order_row, grad_gn, grad_unit, st_out, proj_three, proj_two, cross_query, cross_key,
+        order_row, grad_gn, cot_blocks.reshape(-1, channels), places.block_table, st_out, proj_three, proj_two, cross_query, cross_key,
         cross_value, masks, prompt_col, st_gain, st_shift, motion_rows, stats, sffbias, table,
         sproj_all, sattn_all, sffin_all, sffout_all,
     )
-    grad_res = self_backward(
-        order_row, [ff_mine], grad_two, proj_one, query, key, value, resid, grad_st, masks, st_gain, st_shift,
-        stats, table, sproj_all, sattn_all,
+
+    def build_back():
+        grad_res = self_backward(
+            order_row, [], grad_two, proj_one, query, key, value, resid, grad_st, masks, st_gain,
+            st_shift, stats, table, sproj_all, sattn_all,
+        )
+        grad_conv = conv_backward(
+            order_row, side, grad_res, conv_one, masks, res_gain, res_shift, stats, table, conv_all, 1,
+            [],
+        )
+        return [
+            conv_backward(
+                order_row, side, grad_conv, field, masks, res_gain, res_shift, stats, table, conv_all,
+                0, [grad_res],
+            )
+        ]
+
+    turns_in = [[0, 1, 0, 0, 1, 0, 0, 1], [1, 1, 1], [1, 1, 1]]
+    attn_sum, ff_sum, moved = reduce_all(
+        [d_first, d_blocks[1]], ff_mine, places.rows, build_back, cells <= 640, turns_in,
+        places.block_table, places.block_max,
     )
-    grad_conv = conv_backward(
-        order_row, side, grad_res, conv_one, masks, res_gain, res_shift, stats, table, conv_all, 1,
-        [],
-    )
-    grad_field = conv_backward(
-        order_row, side, grad_conv, field, masks, res_gain, res_shift, stats, table, conv_all, 0,
-        [grad_res],
-    )
-    input_grad = places.unit_to_blocks(to_low(grad_field)).astype(jnp.float32)
-
-    d_first, grad_field = lax.optimization_barrier((d_first, grad_field))
-    attn_sum = reduce_all([d_first, d_blocks[1]], places.rows).astype(jnp.float32)
+    attn_sum, ff_sum = (attn_sum.astype(jnp.float32), ff_sum.astype(jnp.float32))
+    input_grad = places.blocks_from_units(moved).astype(jnp.float32)
+    ff_in_grad = jnp.concatenate([ff_sum[i * own : (i + 1) * own] for i in range(4)], axis=1)
+    ff_out_grad = ff_sum[4 * own : 8 * own]
     zero_sum, one_sum = (attn_sum[: 5 * own + 16], attn_sum[5 * own + 16 : 9 * own + 16])
     attn_grad = jnp.concatenate([zero_sum[: 4 * own], one_sum]).reshape(motion_attn.shape)
     proj_grad = jnp.stack([zero_sum[4 * own : 5 * own], ff_sum[8 * own :]])

time: 654 us -> 587 us (0.90)
  Pallas kernels: 434 us -> 400 us
  local copies, waits for them, and re-layouts: 42.8 us -> 25.8 us
  matrix products: 17.4 us -> 8.85 us
    pallas_call x12 -> x6, Pallas kernels: 228 us -> 128 us  [run_kernel(): pl.pallas_call(kernel, out_shape=outs, in_specs=[pl.BlockSpec(memory_spac...]
    pallas_call x2, Pallas kernels: 206 us -> 272 us  [the longest x1 137 us: forward_all(): pl.pallas_call(kernel, out_shape=[as_shape(slot) for slot in wholes] + [a...]
    psum x1 -> x0, waiting for transfers between devices: 25.8 us -> none  [on_device(): ff_sum = lax.psum(ff_mine, 'rows').astype(jnp.float32)]
    all_to_all x3 -> x1, waiting for transfers between devices: 0.01 us -> 19.8 us  [on_device(): cot_blocks = lax.all_to_all(places.blocks_by_unit(cotangent), 'rows', 0, 0)]
    all_to_all x3 -> x1, starting transfers between devices: 20.7 us -> 3.56 us  [on_device(): cot_blocks = lax.all_to_all(places.blocks_by_unit(cotangent), 'rows', 0, 0)]
    unnamed x54 -> x42, local copies, waits for them, and re-layouts: 18.4 us -> 4.29 us
    all_to_all x2, starting transfers between devices: 9.34 us -> 22.4 us  [unit_to_columns(): received = lax.all_to_all(send, ('frame', 'rows'), 0, 0)]
  transfers between devices with their start and end apart: 11 -> 8, of which waited for: 4 -> 4; matrix products, arithmetic and copies ran while one was open for 8% -> 6% of each run, Pallas kernels for 63% -> 41%
where the time goes in v4:
time: 587 us; the launch traced here: 582 us
  Pallas kernels  400 us (68%)
  waiting for transfers between devices  71.5 us (12%)
  starting transfers between devices  38.2 us (7%)
  local copies, waits for them, and re-layouts  25.8 us (4%)
  between operations  20.4 us (3%)
  other arithmetic  16.9 us (3%)
  matrix products  8.85 us (2%)
    pallas_call x1, Pallas kernels, forward_all(): pl.pallas_call(kernel, out_shape=[as_shape(slot) for slot in wholes] + [a...  137 us
    pallas_call x1, Pallas kernels, reduce_all(): pl.pallas_call(kernel, out_shape=[b16(every * piece, channels), b16(row_d...  135 us
    pallas_call x6, Pallas kernels, run_kernel(): pl.pallas_call(kernel, out_shape=outs, in_specs=[pl.BlockSpec(memory_spac...  128 us
    all_to_all x2, waiting for transfers between devices, unit_to_columns(): received = lax.all_to_all(send, ('frame', 'rows'), 0, 0)  28.8 us
    all_to_all x1, waiting for transfers between devices, columns_to_unit(): received = lax.all_to_all(send, ('frame', 'rows'), 0, 0)  22.8 us
    all_to_all x2, starting transfers between devices, unit_to_columns(): received = lax.all_to_all(send, ('frame', 'rows'), 0, 0)  22.4 us
    all_to_all x1, waiting for transfers between devices, on_device(): cot_blocks = lax.all_to_all(places.blocks_by_unit(cotangent), 'rows', 0, 0)  19.8 us
  transfers between devices with their start and end apart: 8, of which 4 were waited for; matrix products, arithmetic and copies ran while one was open for 6% of the time, Pallas kernels for 41%

profile of v4, /device:TPU:0, one launch (start us, length us, event | category | flops | bytes accessed | tf_op | source)
XLA Modules:
  0.0 581.7 jit_solution(15328301000981992847)
XLA Ops:
  7.2 0.8 broadcast_subtract_fusion
  8.2 0.7 copy-done
  8.9 0.7 convolution_convert_fusion.1
  9.6 0.7 reshape.275
  10.9 1.1 maximum_bitcast_fusion
  12.0 4.4 all-to-all-start.2
  22.9 1.0 fusion.29
  23.9 1.1 fusion.3.refs_12_.refs_3_.refs_9_
  25.4 1.0 select_bitcast_fusion
  26.7 0.7 select_maximum_fusion.refs_10_
  27.4 1.0 convert_select_fusion.refs_13_.refs_4_.refs_10_.refs_17_
  28.4 0.7 pad_add_fusion.refs_0_
  29.1 1.0 copy.75
  30.0 0.6 reshape.297
  30.7 0.6 broadcast_in_dim.131.refs_18_
  31.3 0.6 broadcast_in_dim.130.refs_16_.refs_9_.refs_15_.refs_20_
  31.9 137.1 %shard_map.349 = (bf16[18,640,640]{2,1,0:T(8,128)(2,1)}, bf16[2,640,640]{2,1,0:T(8,128)(2,1)}, bf16[6,640,640]{2,1,0:T(8,128)(2,1)}, bf16[2,768,640]{2,1,0:T(8,1...) custom-call(bf16[18,160,640]{2,1,0:T(8,128)(2,1)} %bitcast.75, ...), custom_call_target="tpu_custom_call" | custom-call | bytes 4096 | tf_op jit(solution)/shard_map/pallas_call | solution.py:1306
  169.0 0.9 dynamic-slice_bitcast_fusion
  170.0 0.7 pad.30.refs_3_
  170.6 0.6 broadcast_in_dim.134.refs_5_
  171.2 20.2 %shard_map.350 = (bf16[576,640]{1,0:T(8,128)(2,1)}, bf16[80,640]{1,0:T(8,128)(2,1)}, bf16[80,640]{1,0:T(8,128)(2,1)}, f32[576,640]{1,0:T(8,128)}, f32[576,640]{1,0:T(8,128)}, /*index=5*/bf16[576,640]{1,0:T(8,128)(2,1)}) custom-call(s32[4]{0:T(128)} %pad_add_fusion.refs_0_, f32[576,640]{1,0:T(8,128)} %get-tuple-element.61.refs_1_.refs_6_, ...), custom_call_target="tpu_custom_call" | custom-call | flops 7077888 | bytes 4096 | tf_op jit(solution)/shard_map/pallas_call | solution.py:257
  191.4 2.1 fusion.4
  193.6 1.2 reshape.278
  194.7 19.8 %all-to-all-start = ((bf16[32,18,640]{2,1,0:T(8,128)(2,1)}), bf16[32,18,640]{2,1,0:T(8,128)(2,1)S(1)}, u32[]{:S(2)}, u32[]{:S(2)}) async-start(bf16[32,18,640]{2,1,0:T(8,128)(2,1)} %reshape.278), calls=%async_computation | async-start | bytes 1966080 | tf_op jit(solution)/shard_map/all_to_all | solution.py:168
  214.5 2.4 fusion.5
  216.9 1.2 reshape.280
  218.1 22.6 %all-to-all-done = bf16[32,18,640]{2,1,0:T(8,128)(2,1)S(1)} async-done(((bf16[32,18,640]{2,1,0:T(8,128)(2,1)}), bf16[32,18,640]{2,1,0:T(8,128)(2,1)S(1)}, u32[]{:S(2)}, u32[]{:S(2)}) %all-to-all-start) | async-done | bytes 737312 | tf_op jit(solution)/shard_map/all_to_all | solution.py:168
  240.7 2.6 all-to-all-start.1
  243.6 0.9 reshape.284
  244.5 1.1 reshape.279.refs_1_
  245.6 17.7 %shard_map.351 = (f32[416,640]{1,0:T(8,128)}, f32[416,640]{1,0:T(8,128)}, f32[416,640]{1,0:T(8,128)}, bf16[416,640]{1,0:T(8,128)(2,1)}, bf16[416,640]{1,0:T(8,12...) custom-call(s32[4]{0:T(128)} %pad_add_fusion.refs_0_, ...), custom_call_target="tpu_custom_call" | custom-call | flops 3067084 | bytes 4096 | tf_op jit(solution)/shard_map/pallas_call | solution.py:257
  263.3 6.2 %all-to-all-done.1 = bf16[32,18,640]{2,1,0:T(8,128)(2,1)S(1)} async-done(((bf16[32,18,640]{2,1,0:T(8,128)(2,1)}), bf16[32,18,640]{2,1,0:T(8,128)(2,1)S(1)}, u32[]{:S(2)}, u32[]{:S(2)}) %all-to-all-start.1) | async-done | bytes 737312 | tf_op jit(solution)/shard_map/all_to_all | solution.py:168
  269.5 1.1 reshape.281.refs_2_
  270.6 25.2 %shard_map.352 = (bf16[416,640]{1,0:T(8,128)(2,1)}, f32[416,640]{1,0:T(8,128)}, bf16[4,1440,640]{2,1,0:T(8,128)(2,1)}, f32[8,640]{1,0:T(8,128)}, f32[8,2560]{1,0:T(8,128)}) custom-call(s32[4]{0:T(128)} %pad_add_fusion.refs_0_, f32[416,640]{1,0:T(8,128)} %get-tuple-element.72.refs_1_, bf16[576,640]{1,0:T(8,128)(2,1)} %reshape.281.refs_2_, ...), custom_call_target="tpu_custom_call" | custom-call | flops 8178892 | bytes 4096 | tf_op jit(solution)/shard_map/pallas_call | solution.py:257
  295.9 0.9 copy-done.6
  297.0 1.0 copy.82
  297.9 3.6 all-to-all-start.4
  301.6 1.0 copy.79
  302.6 19.8 %all-to-all-done.4.refs_15_ = bf16[8,80,640]{2,1,0:T(8,128)(2,1)S(1)} async-done(((bf16[8,80,640]{2,1,0:T(8,128)(2,1)}), bf16[8,80,640]{2,1,0:T(8,128)(2,1)S(1)}, u32[]{:S(2)}, u32[]{:S(2)}) %all-to-all-start.4) | async-done | bytes 819232 | tf_op jit(solution)/shard_map/all_to_all | solution.py:1725
  322.4 3.9 all-to-all-start.3
  326.3 17.1 %shard_map.353 = (f32[416,640]{1,0:T(8,128)}, bf16[4,640,640]{2,1,0:T(8,128)(2,1)}, f32[16,640]{1,0:T(8,128)}) custom-call(s32[4]{0:T(128)} %pad_add_fusion.refs_0_, f32[416,640]{1,0:T(8,128)} %get-tuple-element.77.refs_1_, f32[416,640]{1,0:T(8,128)} %get-tuple-element.78.refs_2_, bf16[416,640]{1,0:T(8,128)(2,1)} %get-tuple-element.79.refs_3_, ...), custom_call_target="tpu_custom_call" | custom-call | flops 3067084 | bytes 4096 | tf_op jit(solution)/shard_map/pallas_call | solution.py:257
  343.4 19.5 %shard_map.354 = (bf16[416,640]{1,0:T(8,128)(2,1)}, bf16[4,816,640]{2,1,0:T(8,128)(2,1)}, f32[16,640]{1,0:T(8,128)}) custom-call(s32[4]{0:T(128)} %pad_add_fusion.refs_0_, f32[416,640]{1,0:T(8,128)} %get-tuple-element.84.refs_1_, f32[416,640]{1,0:T(8,128)} %get-tuple-element.85.refs_2_, bf16[416,640]{1,0:T(8,128)(2,1)} %get-tuple-element.86.refs_3_, ...), custom_call_target="tpu_custom_call" | custom-call | flops 3067084 | bytes 4096 | tf_op jit(solution)/shard_map/pallas_call | solution.py:257
  363.0 1.7 fusion.7
  364.7 1.2 reshape.292
  365.9 3.9 all-to-all-start.5
  370.0 0.9 slice.143
  370.9 0.7 fusion.16.refs_0_
  372.3 0.9 copy.86
  373.1 22.8 %all-to-all-done.5 = bf16[32,18,640]{2,1,0:T(8,128)(2,1)S(1)} async-done(((bf16[32,18,640]{2,1,0:T(8,128)(2,1)}), bf16[32,18,640]{2,1,0:T(8,128)(2,1)S(1)}, u32[]{:S(2)}, u32[]{:S(2)}) %all-to-all-start.5) | async-done | bytes 737312 | tf_op jit(solution)/shard_map/all_to_all | solution.py:174
  396.2 1.7 fusion.6.refs_1_
  397.9 0.7 broadcast_in_dim.136.refs_11_
  398.6 28.4 %shard_map.355 = (f32[576,640]{1,0:T(8,128)}, f32[576,640]{1,0:T(8,128)}) custom-call(s32[4]{0:T(128)} %pad_add_fusion.refs_0_, bf16[576,640]{1,0:T(8,128)(2,1)} %fusion.6.refs_1_, bf16[640,640]{1,0:T(8,128)(2,1)} %bitcast.77, bf16[576,640]{1,0:T(8,128)(2,1)} %fusion.3.refs_12_.refs_3_.refs_9_, f32[576,640]{1,0:T(8,128)} %get-tuple-element.73.refs_4_, ...), custom_call_target="tpu_custom_call" | custom-call | flops 12740198 | bytes 4096 | tf_op jit(solution)/shard_map/pallas_call | solution.py:257
  427.0 134.8 %shard_map.356 = (bf16[3072,640]{1,0:T(8,128)(2,1)}, bf16[8,80,640]{2,1,0:T(8,128)(2,1)}) custom-call(bf16[4,816,640]{2,1,0:T(8,128)(2,1)} %fusion.16.refs_0_, bf16[4,640,640]{2,1,0:T(8,128)(2,1)} %get-tuple-element.95.refs_1_, bf16[2,640,640]{2,1,0:T(8,128)(2,1)} %get-tuple-element.64.refs_12_.refs_18_.refs_2_, bf16[2,160,640]{2,1,0:T(8,128)(2,1)} %refs_3_.5, ...), custom_call_target="tpu_custom_call" | custom-call | bytes 4096 | tf_op jit(solution)/shard_map/pallas_call | solution.py:1621
  561.8 1.9 slice_convert_fusion.1
  563.7 0.8 copy-done.3
  565.2 1.3 slice.130
  566.4 0.6 slice.120
  567.0 0.6 slice.119
  567.6 0.6 slice_reduce_fusion
  568.3 1.9 pad_maximum_fusion
  570.2 0.9 pad_maximum_fusion.4
  571.2 1.0 maximum_convert_fusion
  572.2 1.3 pad_maximum_fusion.1
  573.6 0.9 copy-done.1
  (93 shorter events, 4.9 us)
Async XLA Ops:
  7.2 1.7 copy-start
  7.2 161.8 %all-reduce.7.cloned.1.call-start = ((), (), s32[]{:S(2)}) async-start(), calls=%async_computation.7 | async-start | bytes 491520 | tf_op jit(solution)/shard_map/psum | solution.py:1731
  8.9 1.5 copy-start.5
  9.6 1.1 slice-start
  10.4 6.0 %copy-start.19 = (s32[2]{0:T(128)S(1)}, s32[2]{0:T(128)}, u32[]{:S(2)}) copy-start(s32[2]{0:T(128)} %constant.159.clone) | copy-start | bytes 28
  10.4 9.2 %copy-start.18 = (s32[2]{0:T(128)S(1)}, s32[2]{0:T(128)}, u32[]{:S(2)}) copy-start(s32[2]{0:T(128)} %constant.160.clone) | copy-start | bytes 28
  10.8 14.1 %copy-start.17 = (s32[2]{0:T(128)S(1)}, s32[2]{0:T(128)}, u32[]{:S(2)}) copy-start(s32[2]{0:T(128)} %param.32) | copy-start | bytes 28
  10.8 14.1 %copy-start.13 = (bf16[9,160]{1,0:T(8,128)(2,1)S(1)}, bf16[9,160]{1,0:T(8,128)(2,1)}, u32[]{:S(2)}) copy-start(bf16[9,160]{1,0:T(8,128)(2,1)} %param.48) | copy-start | bytes 8644
  10.8 14.1 %copy-start.15 = (bf16[4,160]{1,0:T(4,128)(2,1)S(1)}, bf16[4,160]{1,0:T(4,128)(2,1)}, u32[]{:S(2)}) copy-start(bf16[4,160]{1,0:T(4,128)(2,1)} %param.47) | copy-start | bytes 3844
  10.8 14.3 %copy-start.14 = (bf16[640]{0:T(1024)(128)(2,1)S(1)}, bf16[640]{0:T(1024)(128)(2,1)}, u32[]{:S(2)}) copy-start(bf16[640]{0:T(1024)(128)(2,1)} %param.52) | copy-start | bytes 3844
  10.9 14.5 %slice-start.1 = ((bf16[4,104,640]{2,1,0:T(8,128)(2,1)}), bf16[4,32,640]{2,1,0:T(8,128)(2,1)S(1)}, s32[]{:S(2)}) async-start(bf16[4,104,640]{2,1,0:T(8,128)(2,1)} %param.30), calls=%async_computation.10 | async-start | bytes 327680 | tf_op jit(solution)/shard_map/slice | solution.py:146
  10.9 14.5 %copy-start.16 = (pred[80]{0:T(512)(128)(4,1)S(1)}, pred[80]{0:T(512)(128)(4,1)}, u32[]{:S(2)}) copy-start(pred[80]{0:T(512)(128)(4,1)} %constant.148.clone.1) | copy-start | bytes 244
  12.0 13.4 %copy-start.7 = (bf16[4,104,640]{2,1,0:T(8,128)(2,1)S(1)}, bf16[4,104,640]{2,1,0:T(8,128)(2,1)}, u32[]{:S(2)}) copy-start(bf16[4,104,640]{2,1,0:T(8,128)(2,1)} %param.30) | copy-start | bytes 1597444
  12.0 182.7 %all-to-all-start.2 = ((bf16[4,4,26,640]{3,1,2,0:T(4,128)(2,1)}), bf16[4,4,26,640]{3,1,2,0:T(4,128)(2,1)S(1)}, u32[]{:S(2)}, u32[]{:S(2)}) async-start(bf16[4,4,26,640]{3,1,2,0:T(4,128)(2,1)} %maximum_bitcast_fusion), calls=%async_computation.2 | async-start | bytes 1064960 | tf_op jit(solution)/shard_map/all_to_all | solution.py:185
  25.4 1.1 copy-start.9
  26.5 3.6 copy-start.12
  194.7 46.0 %all-to-all-start = ((bf16[32,18,640]{2,1,0:T(8,128)(2,1)}), bf16[32,18,640]{2,1,0:T(8,128)(2,1)S(1)}, u32[]{:S(2)}, u32[]{:S(2)}) async-start(bf16[32,18,640]{2,1,0:T(8,128)(2,1)} %reshape.278), calls=%async_computation | async-start | bytes 1966080 | tf_op jit(solution)/shard_map/all_to_all | solution.py:168
  240.7 28.8 %all-to-all-start.1 = ((bf16[32,18,640]{2,1,0:T(8,128)(2,1)}), bf16[32,18,640]{2,1,0:T(8,128)(2,1)S(1)}, u32[]{:S(2)}, u32[]{:S(2)}) async-start(bf16[32,18,640]{2,1,0:T(8,128)(2,1)} %reshape.280), calls=%async_computation.1 | async-start | bytes 1966080 | tf_op jit(solution)/shard_map/all_to_all | solution.py:168
  243.3 183.7 %reduce-scatter.2.cloned.1.call-start = ((), (), s32[]{:S(2)}) async-start(), calls=%async_computation.8 | async-start | bytes 9216000 | tf_op jit(solution)/shard_map/reduce_scatter | solution.py:1826
  295.9 1.0 copy-start.6
  296.9 4.5 copy-start.8
  297.9 24.5 %all-to-all-start.4 = ((bf16[8,80,640]{2,1,0:T(8,128)(2,1)}), bf16[8,80,640]{2,1,0:T(8,128)(2,1)S(1)}, u32[]{:S(2)}, u32[]{:S(2)}) async-start(bf16[8,80,640]{2,1,0:T(8,128)(2,1)} %bitcast.26), calls=%async_computation.4 | async-start | bytes 1638400 | tf_op jit(solution)/shard_map/all_to_all | solution.py:1725
  322.4 3.9 copy-start.2
  322.4 43.5 %all-to-all-start.3 = ((bf16[4,4,26,640]{3,1,2,0:T(4,128)(2,1)}), bf16[4,4,26,640]{3,1,2,0:T(4,128)(2,1)S(1)}, u32[]{:S(2)}, u32[]{:S(2)}) async-start(bf16[4,4,26,640]{3,1,2,0:T(4,128)(2,1)} %copy.79), calls=%async_computation.3 | async-start | bytes 1064960 | tf_op jit(solution)/shard_map/all_to_all | solution.py:192
  343.4 19.6 %copy-start.4 = (bf16[416,576]{1,0:T(8,128)(2,1)S(1)}, bf16[416,576]{1,0:T(8,128)(2,1)}, u32[]{:S(2)}) copy-start(bf16[416,576]{1,0:T(8,128)(2,1)} %constant.161.clone.refs_2_.refs_3_) | copy-start | bytes 1437700
  364.7 5.2 copy-start.11
  365.9 30.1 %all-to-all-start.5 = ((bf16[32,18,640]{2,1,0:T(8,128)(2,1)}), bf16[32,18,640]{2,1,0:T(8,128)(2,1)S(1)}, u32[]{:S(2)}, u32[]{:S(2)}) async-start(bf16[32,18,640]{2,1,0:T(8,128)(2,1)} %reshape.292), calls=%async_computation.6 | async-start | bytes 1966080 | tf_op jit(solution)/shard_map/all_to_all | solution.py:174
  561.8 2.7 copy-start.3
  565.1 3.1 copy-start.10
  572.2 2.3 copy-start.1
Sparse Core Ops, SparseCore 0:
  14.1 139.8 all-reduce.6
  296.0 68.9 reduce-scatter.1

commit v5 on v4

--- a/solution.py
+++ b/solution.py
@@ -1064,7 +1064,7 @@
         self.ndim, self.size = len(like.shape), math.prod(like.shape)
 
 
-def forward_all(places, shards, small, latent_blocks, block_table, build, plan_of_hooks):
+def forward_all(places, shards, small, latent_blocks, cotangent_blocks, block_table, build, plan_of_hooks):
     arrays = [array for array, _ in shards]
     plan = gather_plan([(array.shape, pieces) for array, pieces in shards])
     frames, row_devices = places.frames, places.rows
@@ -1102,14 +1102,15 @@
             return taken
 
         sources = take(count)
-        small_ref, latent_ref, table_ref = take(3)
+        small_ref, latent_ref, cot_ref, table_ref = take(4)
         in_refs = take(len(vmem_inputs))
         targets = take(count)
+        (cot_out,) = take(1)
         out_refs = take(len(vmem_outs))
         inner_refs = take(len(inner))
         (
             small_all, latent_all,
-            send, recv, small_send, small_recv, lat_send, lat_recv, own_sem,
+            send, recv, small_send, small_recv, lat_send, lat_recv, cot_send, cot_recv, own_sem,
         ) = refs
         frame, row = lax.axis_index("frame"), lax.axis_index("rows")
         frame_bit, core_bit = frame // 2, frame % 2
@@ -1231,7 +1232,12 @@
             remote(latent_ref.at[peer], latent_all.at[row], lat_send.at[step], lat_recv.at[step], (frame, peer))
             for step, peer in enumerate(peers)
         ]
+        cot_copies = [
+            remote(cot_ref.at[peer], cot_out.at[row], cot_send.at[step], cot_recv.at[step], (frame, peer))
+            for step, peer in enumerate(peers)
+        ]
         owns = [
+            pltpu.make_async_copy(cot_ref.at[row], cot_out.at[row], own_sem.at[2]),
             pltpu.make_async_copy(small_ref, small_all.at[frame], own_sem.at[0]),
             pltpu.make_async_copy(latent_ref.at[row], latent_all.at[row], own_sem.at[1]),
         ]
@@ -1246,11 +1252,15 @@
 
         def run_actions(actions):
             for action in actions:
-                act(*action)
+                if action[0] == "cotangent":
+                    for copy in cot_copies:
+                        copy.start()
+                else:
+                    act(*action)
 
         for copy in smalls:
             copy.wait_recv()
-        owns[0].wait()
+        owns[1].wait()
         field_ref, params_ref = out_refs[:2]
         total = small_all[0]
         for number in range(1, frames):
@@ -1258,7 +1268,7 @@
         params_ref[...] = total
         for copy in latent_copies:
             copy.wait_recv()
-        owns[1].wait()
+        owns[2].wait()
         blocks = latent_all[...].reshape(-1, channels)
         field_ref[...] = to_low(dot_nn(table_ref[...], blocks))
 
@@ -1298,6 +1308,9 @@
         by_role(end_sends)
         for copy in smalls + latent_copies:
             copy.wait_send()
+        for copy in cot_copies:
+            copy.wait()
+        owns[0].wait()
 
     anywhere = pl.BlockSpec(memory_space=pl.ANY)
     whole_block = pl.BlockSpec(memory_space=pltpu.VMEM)
@@ -1305,9 +1318,9 @@
     dma = pltpu.SemaphoreType.DMA
     results = pl.pallas_call(
         kernel,
-        out_shape=[as_shape(slot) for slot in wholes] + [as_shape(slot) for slot in vmem_outs],
-        in_specs=[anywhere] * (count + 2) + [whole_block] * (1 + len(vmem_inputs)),
-        out_specs=[anywhere] * count + [whole_block] * len(vmem_outs),
+        out_shape=[as_shape(slot) for slot in wholes] + [b16(*cotangent_blocks.shape)] + [as_shape(slot) for slot in vmem_outs],
+        in_specs=[anywhere] * (count + 3) + [whole_block] * (1 + len(vmem_inputs)),
+        out_specs=[anywhere] * (count + 1) + [whole_block] * len(vmem_outs),
         scratch_shapes=[pltpu.VMEM(slot.shape, slot.dtype) for slot in inner]
         + [
             pltpu.VMEM((frames,) + small.shape, jnp.float32),
@@ -1318,15 +1331,17 @@
             dma((3,)),
             dma((peers_count,)),
             dma((peers_count,)),
-            dma((2,)),
+            dma((peers_count,)),
+            dma((peers_count,)),
+            dma((3,)),
         ],
         compiler_params=pltpu.CompilerParams(
             collective_id=0, has_side_effects=True, vmem_limit_bytes=58 * 2**20
         ),
         cost_estimate=pl.CostEstimate(flops=0, bytes_accessed=4096, transcendentals=0),
-    )(*arrays, small, latent_blocks, block_table, *vmem_inputs)
+    )(*arrays, small, latent_blocks, cotangent_blocks, block_table, *vmem_inputs)
     wholes_out = list(zip(results[:count], arrays))
-    return (wholes_out, results[count], results[count + 1], results[count + 2 :])
+    return (wholes_out, results[count], results[count + 1], results[count + 2], results[count + 3 :])
 
 
 def reduce_piece(row_devices):
@@ -1722,7 +1737,6 @@
     stats = jnp.broadcast_to(1.0 / count, (8, channels))
     sffbias = st_ff_bias.astype(jnp.float32).reshape(1, -1)
     grad_columns = places.blocks_to_columns(cotangent)
-    cot_blocks = lax.all_to_all(places.blocks_by_unit(cotangent), "rows", 0, 0)
 
     vocab_rows = embed_table.shape[0]
     local_ids = prompt_ids - lax.axis_index(("frame", "rows")) * vocab_rows
@@ -1752,16 +1766,16 @@
         return [conv_one, resid, proj_one, query, key, value, proj_two]
 
     def acts(text):
-        ways = {"y": "y", "z": "z", "x": "x", "d": "done"}
+        ways = {"y": "y", "z": "z", "x": "x", "d": "done", "c": "cotangent"}
         return [(ways[word[0]], int(word[1:] or 0)) for word in text.split()]
 
     hooks = [
         (acts("y0 y1 z0") + acts("y2 x0 z1") + acts("d0"), [acts("y3 z2"), acts("y4 x2"), []]),
         (acts("x1 z3 d1"), [acts("y5 z4"), [], acts("y6")]),
-        (acts("x3 d2 d3"), [acts("x4"), acts("y7"), acts("z5"), [], acts("z6"), acts("y8"), acts("x5"), []]),
+        (acts("x3 d2 d3") + acts("c"), [acts("x4"), acts("y7"), acts("z5"), [], acts("z6"), acts("y8"), acts("x5"), []]),
         (acts("x6 z7 d4") + acts("y9 x7 z8") + acts("y10 d5 z9") + acts("x8 z10 d6") + acts("d7 x9 x10") + acts("d8 d9 d10"), []),
     ]
-    whole, field, params, kept = forward_all(
+    whole, cot_blocks, field, params, kept = forward_all(
         places,
         [
             (res_conv.reshape((-1,) + res_conv.shape[3:]), 2),
@@ -1777,6 +1791,7 @@
         ],
         small,
         places.blocks_by_unit(latents),
+        places.blocks_by_unit(cotangent),
         places.block_table,
         build,
         hooks,
@@ -1812,7 +1827,7 @@
         grad_zed, d_blocks[block], small_sums = motion_back(
             order_row, block, grad_zed, zeds[block], *kept[3 + 4 * block : 7 + 4 * block],
             motion_in if block == 0 else None, small_sums, position, cell_bias, motion_rows,
-            mproj_all, mattn_all, [cot_blocks] if block == 1 else [],
+            mproj_all, mattn_all, [],
         )
     grad_motion = grad_zed
 

time: 587 us -> 571 us (0.973)
  waiting for transfers between devices: 71.5 us -> 51.7 us
  Pallas kernels: 400 us -> 414 us
  starting transfers between devices: 38.2 us -> 26.5 us
    all_to_all x1 -> x0, waiting for transfers between devices: 19.8 us -> none  [on_device(): cot_blocks = lax.all_to_all(places.blocks_by_unit(cotangent), 'rows', 0, 0)]
    pallas_call x1, Pallas kernels: 137 us -> 150 us  [forward_all(): pl.pallas_call(kernel, out_shape=[as_shape(slot) for slot in wholes] + [b...]
    all_to_all x2, starting transfers between devices: 22.4 us -> 15.2 us  [unit_to_columns(): received = lax.all_to_all(send, ('frame', 'rows'), 0, 0)]
  transfers between devices with their start and end apart: 8 -> 7, of which waited for: 4 -> 3; matrix products, arithmetic and copies ran while one was open for 6% -> 6% of each run, Pallas kernels for 41% -> 45%
where the time goes in v5:
time: 571 us; the launch traced here: 565 us
  Pallas kernels  414 us (73%)
  waiting for transfers between devices  51.7 us (9%)
  local copies, waits for them, and re-layouts  27.5 us (5%)
  starting transfers between devices  26.5 us (5%)
  between operations  20.3 us (4%)
  other arithmetic  16.1 us (3%)
  matrix products  8.84 us (2%)
    pallas_call x1, Pallas kernels, forward_all(): pl.pallas_call(kernel, out_shape=[as_shape(slot) for slot in wholes] + [b...  150 us
    pallas_call x1, Pallas kernels, reduce_all(): pl.pallas_call(kernel, out_shape=[b16(every * piece, channels), b16(row_d...  135 us
    pallas_call x6, Pallas kernels, run_kernel(): pl.pallas_call(kernel, out_shape=outs, in_specs=[pl.BlockSpec(memory_spac...  129 us
    all_to_all x2, waiting for transfers between devices, unit_to_columns(): received = lax.all_to_all(send, ('frame', 'rows'), 0, 0)  28.8 us
    all_to_all x1, waiting for transfers between devices, columns_to_unit(): received = lax.all_to_all(send, ('frame', 'rows'), 0, 0)  22.8 us
    all_to_all x2, starting transfers between devices, unit_to_columns(): received = lax.all_to_all(send, ('frame', 'rows'), 0, 0)  15.2 us
  transfers between devices with their start and end apart: 7, of which 3 were waited for; matrix products, arithmetic and copies ran while one was open for 6% of the time, Pallas kernels for 45%

profile of v5, /device:TPU:0, one launch (start us, length us, event | category | flops | bytes accessed | tf_op | source)
XLA Modules:
  0.0 565.3 jit_solution(16605822897812012917)
XLA Ops:
  7.2 0.8 broadcast_subtract_fusion
  8.2 0.7 copy-done
  8.9 0.7 convolution_convert_fusion.1
  9.6 0.7 reshape.276
  10.9 1.1 maximum_bitcast_fusion
  12.0 4.4 all-to-all-start.2
  19.6 0.6 dynamic_slice.16
  22.2 0.8 pad_bitcast_fusion
  23.7 1.0 fusion.29
  24.6 1.1 fusion.3.refs_13_.refs_3_.refs_9_
  26.5 0.6 copy-done.5
  27.7 0.7 select_maximum_fusion.refs_10_
  28.3 1.0 convert_select_fusion.refs_14_.refs_4_.refs_10_.refs_17_
  29.3 0.6 pad_add_fusion.refs_0_
  30.0 1.0 copy.75
  30.9 1.0 copy.76
  31.9 0.6 reshape.297
  32.5 0.6 broadcast_in_dim.131.refs_19_
  33.1 0.6 broadcast_in_dim.130.refs_17_.refs_9_.refs_15_.refs_20_
  33.7 150.5 %shard_map.349 = (bf16[18,640,640]{2,1,0:T(8,128)(2,1)}, bf16[2,640,640]{2,1,0:T(8,128)(2,1)}, bf16[6,640,640]{2,1,0:T(8,128)(2,1)}, bf16[2,768,640]{2,1,0:T(8,1...) custom-call(bf16[18,160,640]{2,1,0:T(8,128)(2,1)} %bitcast.75, ...), custom_call_target="tpu_custom_call" | custom-call | bytes 4096 | tf_op jit(solution)/shard_map/pallas_call | solution.py:1319
  184.2 0.9 dynamic-slice_bitcast_fusion
  185.2 0.7 pad.32.refs_3_
  185.8 0.6 broadcast_in_dim.134.refs_5_
  186.4 19.8 %shard_map.350 = (bf16[576,640]{1,0:T(8,128)(2,1)}, bf16[80,640]{1,0:T(8,128)(2,1)}, bf16[80,640]{1,0:T(8,128)(2,1)}, f32[576,640]{1,0:T(8,128)}, f32[576,640]{1,0:T(8,128)}, /*index=5*/bf16[576,640]{1,0:T(8,128)(2,1)}) custom-call(s32[4]{0:T(128)} %pad_add_fusion.refs_0_, f32[576,640]{1,0:T(8,128)} %get-tuple-element.62.refs_1_.refs_6_, ...), custom_call_target="tpu_custom_call" | custom-call | flops 7077888 | bytes 4096 | tf_op jit(solution)/shard_map/pallas_call | solution.py:257
  206.2 2.1 fusion.4
  208.3 1.2 reshape.279
  209.5 12.6 %all-to-all-start = ((bf16[32,18,640]{2,1,0:T(8,128)(2,1)}), bf16[32,18,640]{2,1,0:T(8,128)(2,1)S(1)}, u32[]{:S(2)}, u32[]{:S(2)}) async-start(bf16[32,18,640]{2,1,0:T(8,128)(2,1)} %reshape.279), calls=%async_computation | async-start | bytes 1966080 | tf_op jit(solution)/shard_map/all_to_all | solution.py:168
  222.1 2.4 fusion.5
  224.5 1.2 reshape.281
  225.7 22.6 %all-to-all-done = bf16[32,18,640]{2,1,0:T(8,128)(2,1)S(1)} async-done(((bf16[32,18,640]{2,1,0:T(8,128)(2,1)}), bf16[32,18,640]{2,1,0:T(8,128)(2,1)S(1)}, u32[]{:S(2)}, u32[]{:S(2)}) %all-to-all-start) | async-done | bytes 737312 | tf_op jit(solution)/shard_map/all_to_all | solution.py:168
  248.3 2.6 all-to-all-start.1
  251.2 0.9 reshape.285
  252.1 1.1 reshape.280.refs_1_
  253.2 17.7 %shard_map.351 = (f32[416,640]{1,0:T(8,128)}, f32[416,640]{1,0:T(8,128)}, f32[416,640]{1,0:T(8,128)}, bf16[416,640]{1,0:T(8,128)(2,1)}, bf16[416,640]{1,0:T(8,12...) custom-call(s32[4]{0:T(128)} %pad_add_fusion.refs_0_, ...), custom_call_target="tpu_custom_call" | custom-call | flops 3067084 | bytes 4096 | tf_op jit(solution)/shard_map/pallas_call | solution.py:257
  271.0 6.2 %all-to-all-done.1 = bf16[32,18,640]{2,1,0:T(8,128)(2,1)S(1)} async-done(((bf16[32,18,640]{2,1,0:T(8,128)(2,1)}), bf16[32,18,640]{2,1,0:T(8,128)(2,1)S(1)}, u32[]{:S(2)}, u32[]{:S(2)}) %all-to-all-start.1) | async-done | bytes 737312 | tf_op jit(solution)/shard_map/all_to_all | solution.py:168
  277.1 1.1 reshape.282.refs_2_
  278.2 25.2 %shard_map.352 = (bf16[416,640]{1,0:T(8,128)(2,1)}, f32[416,640]{1,0:T(8,128)}, bf16[4,1440,640]{2,1,0:T(8,128)(2,1)}, f32[8,640]{1,0:T(8,128)}, f32[8,2560]{1,0:T(8,128)}) custom-call(s32[4]{0:T(128)} %pad_add_fusion.refs_0_, f32[416,640]{1,0:T(8,128)} %get-tuple-element.73.refs_1_, bf16[576,640]{1,0:T(8,128)(2,1)} %reshape.282.refs_2_, ...), custom_call_target="tpu_custom_call" | custom-call | flops 8178892 | bytes 4096 | tf_op jit(solution)/shard_map/pallas_call | solution.py:257
  303.5 1.0 copy-done.7
  304.7 1.0 copy.80
  305.6 3.9 all-to-all-start.3
  309.5 18.4 %shard_map.353 = (f32[416,640]{1,0:T(8,128)}, bf16[4,640,640]{2,1,0:T(8,128)(2,1)}, f32[16,640]{1,0:T(8,128)}) custom-call(s32[4]{0:T(128)} %pad_add_fusion.refs_0_, f32[416,640]{1,0:T(8,128)} %get-tuple-element.78.refs_1_, f32[416,640]{1,0:T(8,128)} %get-tuple-element.79.refs_2_, bf16[416,640]{1,0:T(8,128)(2,1)} %get-tuple-element.80.refs_3_, ...), custom_call_target="tpu_custom_call" | custom-call | flops 3067084 | bytes 4096 | tf_op jit(solution)/shard_map/pallas_call | solution.py:257
  328.0 19.4 %shard_map.354 = (bf16[416,640]{1,0:T(8,128)(2,1)}, bf16[4,816,640]{2,1,0:T(8,128)(2,1)}, f32[16,640]{1,0:T(8,128)}) custom-call(s32[4]{0:T(128)} %pad_add_fusion.refs_0_, f32[416,640]{1,0:T(8,128)} %get-tuple-element.85.refs_1_, f32[416,640]{1,0:T(8,128)} %get-tuple-element.86.refs_2_, bf16[416,640]{1,0:T(8,128)(2,1)} %get-tuple-element.87.refs_3_, ...), custom_call_target="tpu_custom_call" | custom-call | flops 3067084 | bytes 4096 | tf_op jit(solution)/shard_map/pallas_call | solution.py:257
  347.4 1.7 fusion.7
  349.2 1.2 reshape.292
  350.3 2.9 all-to-all-start.4
  353.4 0.9 slice.143
  354.3 0.7 fusion.16.refs_0_
  355.7 0.9 copy.86
  356.6 22.8 %all-to-all-done.4 = bf16[32,18,640]{2,1,0:T(8,128)(2,1)S(1)} async-done(((bf16[32,18,640]{2,1,0:T(8,128)(2,1)}), bf16[32,18,640]{2,1,0:T(8,128)(2,1)S(1)}, u32[]{:S(2)}, u32[]{:S(2)}) %all-to-all-start.4) | async-done | bytes 737312 | tf_op jit(solution)/shard_map/all_to_all | solution.py:174
  379.6 1.7 fusion.6.refs_1_
  381.4 0.7 broadcast_in_dim.136.refs_11_
  382.1 28.4 %shard_map.355 = (f32[576,640]{1,0:T(8,128)}, f32[576,640]{1,0:T(8,128)}) custom-call(s32[4]{0:T(128)} %pad_add_fusion.refs_0_, bf16[576,640]{1,0:T(8,128)(2,1)} %fusion.6.refs_1_, bf16[640,640]{1,0:T(8,128)(2,1)} %bitcast.84, bf16[576,640]{1,0:T(8,128)(2,1)} %fusion.3.refs_13_.refs_3_.refs_9_, f32[576,640]{1,0:T(8,128)} %get-tuple-element.74.refs_4_, ...), custom_call_target="tpu_custom_call" | custom-call | flops 12740198 | bytes 4096 | tf_op jit(solution)/shard_map/pallas_call | solution.py:257
  410.5 134.8 %shard_map.356 = (bf16[3072,640]{1,0:T(8,128)(2,1)}, bf16[8,80,640]{2,1,0:T(8,128)(2,1)}) custom-call(bf16[4,816,640]{2,1,0:T(8,128)(2,1)} %fusion.16.refs_0_, bf16[4,640,640]{2,1,0:T(8,128)(2,1)} %get-tuple-element.96.refs_1_, bf16[2,640,640]{2,1,0:T(8,128)(2,1)} %get-tuple-element.65.refs_12_.refs_18_.refs_2_, bf16[2,160,640]{2,1,0:T(8,128)(2,1)} %refs_3_.5, ...), custom_call_target="tpu_custom_call" | custom-call | bytes 4096 | tf_op jit(solution)/shard_map/pallas_call | solution.py:1636
  545.3 1.9 slice_convert_fusion.1
  547.2 0.8 copy-done.2
  548.7 1.3 slice.130
  549.9 0.6 slice.120
  550.5 0.6 slice.119
  551.1 0.6 slice_reduce_fusion
  551.8 1.9 pad_maximum_fusion
  553.7 0.9 pad_maximum_fusion.4
  554.7 1.0 maximum_convert_fusion
  555.7 1.3 pad_maximum_fusion.1
  557.1 0.9 copy-done.1
  (89 shorter events, 4.7 us)
Async XLA Ops:
  7.2 1.7 copy-start
  7.2 177.0 %all-reduce.7.cloned.1.call-start = ((), (), s32[]{:S(2)}) async-start(), calls=%async_computation.6 | async-start | bytes 491520 | tf_op jit(solution)/shard_map/psum | solution.py:1745
  8.9 1.5 copy-start.4
  9.6 1.1 slice-start
  10.4 6.0 %copy-start.18 = (s32[2]{0:T(128)S(1)}, s32[2]{0:T(128)}, u32[]{:S(2)}) copy-start(s32[2]{0:T(128)} %constant.159.clone) | copy-start | bytes 28
  10.4 9.2 %copy-start.17 = (s32[2]{0:T(128)S(1)}, s32[2]{0:T(128)}, u32[]{:S(2)}) copy-start(s32[2]{0:T(128)} %constant.160.clone) | copy-start | bytes 28
  10.8 14.9 %copy-start.16 = (s32[2]{0:T(128)S(1)}, s32[2]{0:T(128)}, u32[]{:S(2)}) copy-start(s32[2]{0:T(128)} %param.32) | copy-start | bytes 28
  10.8 14.9 %copy-start.12 = (bf16[9,160]{1,0:T(8,128)(2,1)S(1)}, bf16[9,160]{1,0:T(8,128)(2,1)}, u32[]{:S(2)}) copy-start(bf16[9,160]{1,0:T(8,128)(2,1)} %param.48) | copy-start | bytes 8644
  10.8 14.9 %copy-start.14 = (bf16[4,160]{1,0:T(4,128)(2,1)S(1)}, bf16[4,160]{1,0:T(4,128)(2,1)}, u32[]{:S(2)}) copy-start(bf16[4,160]{1,0:T(4,128)(2,1)} %param.47) | copy-start | bytes 3844
  10.8 15.0 %copy-start.13 = (bf16[640]{0:T(1024)(128)(2,1)S(1)}, bf16[640]{0:T(1024)(128)(2,1)}, u32[]{:S(2)}) copy-start(bf16[640]{0:T(1024)(128)(2,1)} %param.52) | copy-start | bytes 3844
  12.0 14.1 %copy-start.6 = (bf16[4,104,640]{2,1,0:T(8,128)(2,1)S(1)}, bf16[4,104,640]{2,1,0:T(8,128)(2,1)}, u32[]{:S(2)}) copy-start(bf16[4,104,640]{2,1,0:T(8,128)(2,1)} %param.30) | copy-start | bytes 1597444
  12.0 14.1 %slice-start.1 = ((bf16[4,104,640]{2,1,0:T(8,128)(2,1)}), bf16[4,32,640]{2,1,0:T(8,128)(2,1)S(1)}, s32[]{:S(2)}) async-start(bf16[4,104,640]{2,1,0:T(8,128)(2,1)} %param.30), calls=%async_computation.9 | async-start | bytes 327680 | tf_op jit(solution)/shard_map/slice | solution.py:146
  12.0 14.1 %copy-start.15 = (pred[80]{0:T(512)(128)(4,1)S(1)}, pred[80]{0:T(512)(128)(4,1)}, u32[]{:S(2)}) copy-start(pred[80]{0:T(512)(128)(4,1)} %constant.148.clone.1) | copy-start | bytes 244
  12.0 197.5 %all-to-all-start.2 = ((bf16[4,4,26,640]{3,1,2,0:T(4,128)(2,1)}), bf16[4,4,26,640]{3,1,2,0:T(4,128)(2,1)S(1)}, u32[]{:S(2)}, u32[]{:S(2)}) async-start(bf16[4,4,26,640]{3,1,2,0:T(4,128)(2,1)} %maximum_bitcast_fusion), calls=%async_computation.2 | async-start | bytes 1064960 | tf_op jit(solution)/shard_map/all_to_all | solution.py:185
  26.2 1.0 copy-start.5
  26.4 1.0 copy-start.8
  30.0 1.9 copy-start.11
  209.5 38.8 %all-to-all-start = ((bf16[32,18,640]{2,1,0:T(8,128)(2,1)}), bf16[32,18,640]{2,1,0:T(8,128)(2,1)S(1)}, u32[]{:S(2)}, u32[]{:S(2)}) async-start(bf16[32,18,640]{2,1,0:T(8,128)(2,1)} %reshape.279), calls=%async_computation | async-start | bytes 1966080 | tf_op jit(solution)/shard_map/all_to_all | solution.py:168
  248.3 28.8 %all-to-all-start.1 = ((bf16[32,18,640]{2,1,0:T(8,128)(2,1)}), bf16[32,18,640]{2,1,0:T(8,128)(2,1)S(1)}, u32[]{:S(2)}, u32[]{:S(2)}) async-start(bf16[32,18,640]{2,1,0:T(8,128)(2,1)} %reshape.281), calls=%async_computation.1 | async-start | bytes 1966080 | tf_op jit(solution)/shard_map/all_to_all | solution.py:168
  251.0 159.5 %reduce-scatter.2.cloned.1.call-start = ((), (), s32[]{:S(2)}) async-start(), calls=%async_computation.7 | async-start | bytes 9216000 | tf_op jit(solution)/shard_map/reduce_scatter | solution.py:1841
  303.5 1.0 copy-start.7
  305.6 44.7 %all-to-all-start.3 = ((bf16[4,4,26,640]{3,1,2,0:T(4,128)(2,1)}), bf16[4,4,26,640]{3,1,2,0:T(4,128)(2,1)S(1)}, u32[]{:S(2)}, u32[]{:S(2)}) async-start(bf16[4,4,26,640]{3,1,2,0:T(4,128)(2,1)} %copy.80), calls=%async_computation.3 | async-start | bytes 1064960 | tf_op jit(solution)/shard_map/all_to_all | solution.py:192
  328.0 19.4 %copy-start.3 = (bf16[416,576]{1,0:T(8,128)(2,1)S(1)}, bf16[416,576]{1,0:T(8,128)(2,1)}, u32[]{:S(2)}) copy-start(bf16[416,576]{1,0:T(8,128)(2,1)} %constant.161.clone.refs_2_.refs_3_) | copy-start | bytes 1437700
  349.1 4.2 copy-start.10
  350.3 29.1 %all-to-all-start.4 = ((bf16[32,18,640]{2,1,0:T(8,128)(2,1)}), bf16[32,18,640]{2,1,0:T(8,128)(2,1)S(1)}, u32[]{:S(2)}, u32[]{:S(2)}) async-start(bf16[32,18,640]{2,1,0:T(8,128)(2,1)} %reshape.292), calls=%async_computation.5 | async-start | bytes 1966080 | tf_op jit(solution)/shard_map/all_to_all | solution.py:174
  545.3 2.7 copy-start.2
  548.7 3.1 copy-start.9
  555.7 2.3 copy-start.1
Sparse Core Ops, SparseCore 0:
  14.1 136.8 all-reduce.6
  303.6 73.4 reduce-scatter.1
